TPU v7x, 32 devices: a whole 2x2x4 slice. The times are simulated.
32 devices in a mesh: band: 2 (over y), grid: 16 (over z, x, core).
Axes of the slice: x: 2, y: 2, z: 4, core: 2. Of those that a mesh axis runs over, the one named last changes fastest.
Arguments:
- orbitals: float32 [2, 2, 192, 192, 192], P('band', None, 'grid'), may hold values from -6 to 6
- occupations: float32 [2], P('band'), may hold values from 0.5 to 2
- ion_potential: float32 [192, 192, 192], P('grid'), may hold values from -0.6 to 0.6
- hxc_potential: float32 [192, 192, 192], P('grid'), may hold values from -0.4 to 0.4
Outputs:
- new_orbitals: float32 [2, 2, 192, 192, 192], P('band', None, 'grid')
- new_potential: float32 [192, 192, 192], P('grid')
All inputs are finite; a program needn't handle non-finite values.
Results may differ from a plain program's by a relative error of at most 0.0003.
Values sent between devices are 32-bit elements; how exact they have to be, the bound alone decides.
No kernel may reach another device: no remote copies, remote signals or barrier semaphores. Data moves between devices by JAX's collectives and lax.ppermute only.
A program may use at most 128 MiB of HBM per device.

v0:
```python
import math

import jax
import jax.numpy as jnp
from jax import lax
from jax.sharding import PartitionSpec as P

BESSEL_ZERO = 0.8462873527504802
BESSEL_ONE = 0.36884204609417703
BESSEL_TWO = 0.07581776248
XC_FACTOR = 0.98474502


def tables(length):
    idx = jnp.arange(length, dtype=jnp.int32)
    angle = (idx[:, None] * idx[None, :] % length).astype(jnp.float32) * (2.0 * math.pi / length)
    return (jnp.cos(angle), jnp.sin(angle))


def transform(real_part, imag_part, form, inverse, length):
    cosine, sine = tables(length)
    high = lax.Precision.HIGHEST
    rc = jnp.einsum(form, real_part, cosine, precision=high)
    rs = jnp.einsum(form, real_part, sine, precision=high)
    ic = jnp.einsum(form, imag_part, cosine, precision=high)
    isn = jnp.einsum(form, imag_part, sine, precision=high)
    if inverse:
        scale = 1.0 / length
        return ((rc - isn) * scale, (ic + rs) * scale)
    return (rc + isn, ic - rs)


def along_z(real_part, imag_part, inverse):
    return transform(real_part, imag_part, "oxyn,nk->oxyk", inverse, real_part.shape[3])


def along_y(real_part, imag_part, inverse):
    return transform(real_part, imag_part, "oxnz,nk->oxkz", inverse, real_part.shape[2])


def along_x(real_part, imag_part, inverse):
    return transform(real_part, imag_part, "onyz,nk->okyz", inverse, real_part.shape[1])


def forward(real_part, imag_part):
    real_part, imag_part = along_z(real_part, imag_part, False)
    real_part, imag_part = along_y(real_part, imag_part, False)
    real_part, imag_part = (
        lax.all_to_all(real_part, "grid", split_axis=2, concat_axis=1, tiled=True),
        lax.all_to_all(imag_part, "grid", split_axis=2, concat_axis=1, tiled=True),
    )
    return along_x(real_part, imag_part, False)


def backward(real_part, imag_part):
    real_part, imag_part = along_x(real_part, imag_part, True)
    real_part, imag_part = (
        lax.all_to_all(real_part, "grid", split_axis=1, concat_axis=2, tiled=True),
        lax.all_to_all(imag_part, "grid", split_axis=1, concat_axis=2, tiled=True),
    )
    real_part, imag_part = along_y(real_part, imag_part, True)
    real_part, imag_part = along_z(real_part, imag_part, True)
    return (real_part, imag_part)


def frequency(idx, length):
    return jnp.where(idx < length // 2, idx, idx - length).astype(jnp.float32)


def squares_block(x_count, y_start, y_count, length):
    fx = frequency(jnp.arange(x_count, dtype=jnp.int32), length)
    fy = frequency(y_start + jnp.arange(y_count, dtype=jnp.int32), length)
    fz = frequency(jnp.arange(length, dtype=jnp.int32), length)
    return (fx * fx)[:, None, None] + (fy * fy)[None, :, None] + (fz * fz)[None, None, :]


def hartree_filter(squares, length):
    return jnp.where(squares > 0, length * math.sqrt(length) / 16.0 / (squares + 1.0), 0.0)


def local(orbitals, occupations, ion_potential, hxc_potential):
    length = orbitals.shape[-1]
    columns = length // lax.axis_size("grid")
    grid_pos = lax.axis_index("grid")
    squares = squares_block(length, grid_pos * columns, columns, length)
    kinetic = 2.0 * squares / (3.0 * (length / 2) ** 2) - 1.0
    potential = ion_potential + hxc_potential

    def hamilton(real_part, imag_part):
        fre, fim = forward(real_part, imag_part)
        back_re, back_im = backward(kinetic * fre, kinetic * fim)
        return (back_re + potential * real_part, back_im + potential * imag_part)

    psi_re = orbitals[:, 0]
    psi_im = orbitals[:, 1]
    first_re, first_im = hamilton(psi_re, psi_im)
    again_re, again_im = hamilton(first_re, first_im)
    second_re = 2.0 * again_re - psi_re
    second_im = 2.0 * again_im - psi_im
    fresh_re = BESSEL_ZERO * psi_re + 2.0 * BESSEL_ONE * first_im - 2.0 * BESSEL_TWO * second_re
    fresh_im = BESSEL_ZERO * psi_im - 2.0 * BESSEL_ONE * first_re - 2.0 * BESSEL_TWO * second_im
    new_orbitals = jnp.stack([fresh_re, fresh_im], axis=1)
    partial_value = jnp.sum(
        occupations[:, None, None, None] * (fresh_re * fresh_re + fresh_im * fresh_im), axis=0
    )
    density = lax.psum(partial_value, "band")
    fre, fim = forward(density[None], jnp.zeros_like(density)[None])
    kernel = hartree_filter(squares, length)
    hart_re, hart_im = backward(kernel * fre, kernel * fim)
    new_potential = hart_re[0] - XC_FACTOR * jnp.cbrt(density)
    return (new_orbitals, new_potential)


def solution(mesh):
    placed = (
        P("band", None, "grid", None, None),
        P("band"),
        P("grid", None, None),
        P("grid", None, None),
    )
    return jax.shard_map(
        local,
        mesh=mesh,
        in_specs=placed,
        out_specs=(P("band", None, "grid", None, None), P("grid", None, None)),
        check_vma=False,
    )
```

profile of v0, /device:TPU:0, one launch (start us, length us, event | category | flops | bytes accessed | tf_op | source)
XLA Modules:
  0.0 1059.1 jit_solution(10933783266553777765)
XLA Ops:
  7.2 7.2 fusion.35
  19.7 5.6 fusion.62
  30.7 5.6 fusion.59
  45.6 7.8 all-to-all-start
  53.4 7.0 fusion.27
  60.4 5.4 add_bitcast_fusion.2
  69.9 28.8 %all-to-all-done = f32[1,12,192,192]{3,0,1,2:T(1,128)} async-done(((f32[1,12,192,192]{3,0,1,2:T(1,128)}), f32[1,12,192,192]{3,0,1,2:T(1,128)}, u32[]{:S(2)}, u32[]{:S(2)}) %all-to-all-start) | async-done | bytes 1769504 | tf_op jit(solution)/shard_map/all_to_all | solution.py:50
  98.7 12.3 %all-to-all-start.1 = ((f32[1,12,192,192]{3,0,1,2:T(1,128)}), f32[1,12,192,192]{3,0,1,2:T(1,128)}, u32[]{:S(2)}, u32[]{:S(2)}) async-start(f32[1,12,192,192]{3,0,1,2:T(1,128)} %copy.250), calls=%async_computation.1 | async-start | bytes 4718592 | tf_op jit(solution)/shard_map/all_to_all | solution.py:49
  120.7 36.0 %all-to-all-done.1 = f32[1,12,192,192]{3,0,1,2:T(1,128)} async-done(((f32[1,12,192,192]{3,0,1,2:T(1,128)}), f32[1,12,192,192]{3,0,1,2:T(1,128)}, u32[]{:S(2)}, u32[]{:S(2)}) %all-to-all-start.1) | async-done | bytes 1769504 | tf_op jit(solution)/shard_map/all_to_all | solution.py:49
  194.4 12.5 %all-to-all-start.3 = ((f32[1,192,12,192]{3,0,2,1:T(1,128)}), f32[1,192,12,192]{3,0,2,1:T(1,128)}, u32[]{:S(2)}, u32[]{:S(2)}) async-start(f32[1,192,12,192]{3,0,2,1:T(1,128)} %copy.263), calls=%async_computation.3 | async-start | bytes 4718592 | tf_op jit(solution)/shard_map/all_to_all | solution.py:58
  218.5 34.2 %all-to-all-done.3 = f32[1,192,12,192]{3,0,2,1:T(1,128)} async-done(((f32[1,192,12,192]{3,0,2,1:T(1,128)}), f32[1,192,12,192]{3,0,2,1:T(1,128)}, u32[]{:S(2)}, u32[]{:S(2)}) %all-to-all-start.3) | async-done | bytes 1769504 | tf_op jit(solution)/shard_map/all_to_all | solution.py:58
  252.6 12.3 %all-to-all-start.2 = ((f32[1,192,12,192]{3,0,2,1:T(1,128)}), f32[1,192,12,192]{3,0,2,1:T(1,128)}, u32[]{:S(2)}, u32[]{:S(2)}) async-start(f32[1,192,12,192]{3,0,2,1:T(1,128)} %copy.258), calls=%async_computation.2 | async-start | bytes 4718592 | tf_op jit(solution)/shard_map/all_to_all | solution.py:59
  274.7 35.9 %all-to-all-done.2 = f32[1,192,12,192]{3,0,2,1:T(1,128)} async-done(((f32[1,192,12,192]{3,0,2,1:T(1,128)}), f32[1,192,12,192]{3,0,2,1:T(1,128)}, u32[]{:S(2)}, u32[]{:S(2)}) %all-to-all-start.2) | async-done | bytes 1769504 | tf_op jit(solution)/shard_map/all_to_all | solution.py:59
  366.2 12.6 %all-to-all-start.4 = ((f32[1,12,192,192]{3,0,1,2:T(1,128)}), f32[1,12,192,192]{3,0,1,2:T(1,128)}, u32[]{:S(2)}, u32[]{:S(2)}) async-start(f32[1,12,192,192]{3,0,1,2:T(1,128)} %copy.270), calls=%async_computation.4 | async-start | bytes 4718592 | tf_op jit(solution)/shard_map/all_to_all | solution.py:49
  390.5 34.0 %all-to-all-done.4 = f32[1,12,192,192]{3,0,1,2:T(1,128)} async-done(((f32[1,12,192,192]{3,0,1,2:T(1,128)}), f32[1,12,192,192]{3,0,1,2:T(1,128)}, u32[]{:S(2)}, u32[]{:S(2)}) %all-to-all-start.4) | async-done | bytes 1769504 | tf_op jit(solution)/shard_map/all_to_all | solution.py:49
  424.5 12.8 %all-to-all-start.5 = ((f32[1,12,192,192]{3,0,1,2:T(1,128)}), f32[1,12,192,192]{3,0,1,2:T(1,128)}, u32[]{:S(2)}, u32[]{:S(2)}) async-start(f32[1,12,192,192]{3,0,1,2:T(1,128)} %copy.276), calls=%async_computation.5 | async-start | bytes 4718592 | tf_op jit(solution)/shard_map/all_to_all | solution.py:50
  448.3 34.7 %all-to-all-done.5 = f32[1,12,192,192]{3,0,1,2:T(1,128)} async-done(((f32[1,12,192,192]{3,0,1,2:T(1,128)}), f32[1,12,192,192]{3,0,1,2:T(1,128)}, u32[]{:S(2)}, u32[]{:S(2)}) %all-to-all-start.5) | async-done | bytes 1769504 | tf_op jit(solution)/shard_map/all_to_all | solution.py:50
  519.0 12.7 %all-to-all-start.7 = ((f32[1,192,12,192]{3,0,2,1:T(1,128)}), f32[1,192,12,192]{3,0,2,1:T(1,128)}, u32[]{:S(2)}, u32[]{:S(2)}) async-start(f32[1,192,12,192]{3,0,2,1:T(1,128)} %copy.289), calls=%async_computation.7 | async-start | bytes 4718592 | tf_op jit(solution)/shard_map/all_to_all | solution.py:59
  543.5 34.0 %all-to-all-done.7 = f32[1,192,12,192]{3,0,2,1:T(1,128)} async-done(((f32[1,192,12,192]{3,0,2,1:T(1,128)}), f32[1,192,12,192]{3,0,2,1:T(1,128)}, u32[]{:S(2)}, u32[]{:S(2)}) %all-to-all-start.7) | async-done | bytes 1769504 | tf_op jit(solution)/shard_map/all_to_all | solution.py:59
  577.5 12.3 %all-to-all-start.6 = ((f32[1,192,12,192]{3,0,2,1:T(1,128)}), f32[1,192,12,192]{3,0,2,1:T(1,128)}, u32[]{:S(2)}, u32[]{:S(2)}) async-start(f32[1,192,12,192]{3,0,2,1:T(1,128)} %copy.284), calls=%async_computation.6 | async-start | bytes 4718592 | tf_op jit(solution)/shard_map/all_to_all | solution.py:58
  598.3 37.2 %all-to-all-done.6 = f32[1,192,12,192]{3,0,2,1:T(1,128)} async-done(((f32[1,192,12,192]{3,0,2,1:T(1,128)}), f32[1,192,12,192]{3,0,2,1:T(1,128)}, u32[]{:S(2)}, u32[]{:S(2)}) %all-to-all-start.6) | async-done | bytes 1769504 | tf_op jit(solution)/shard_map/all_to_all | solution.py:58
  667.3 6.5 add_multiply_fusion.2
  678.0 72.2 %all-reduce.2.cloned.1.call-done = f32[12,192,192]{2,1,0:T(8,128)} async-done(((f32[12,192,192]{2,1,0:T(8,128)}), f32[12,192,192]{2,1,0:T(8,128)}) %all-reduce.2.cloned.1.call-update) | async-done | bytes 1769488 | tf_op jit(solution)/shard_map/psum | solution.py:106
  770.4 5.9 all-to-all-start.9
  787.8 34.2 %all-to-all-done.9 = f32[1,12,192,192]{3,0,1,2:T(1,128)} async-done(((f32[1,12,192,192]{3,0,1,2:T(1,128)}), f32[1,12,192,192]{3,0,1,2:T(1,128)}, u32[]{:S(2)}, u32[]{:S(2)}) %all-to-all-start.9) | async-done | bytes 1769504 | tf_op jit(solution)/shard_map/all_to_all | solution.py:50
  822.0 12.7 %all-to-all-start.8 = ((f32[1,12,192,192]{3,0,1,2:T(1,128)}), f32[1,12,192,192]{3,0,1,2:T(1,128)}, u32[]{:S(2)}, u32[]{:S(2)}) async-start(f32[1,12,192,192]{3,0,1,2:T(1,128)} %copy.296), calls=%async_computation.8 | async-start | bytes 4718592 | tf_op jit(solution)/shard_map/all_to_all | solution.py:49
  841.6 38.8 %all-to-all-done.8 = f32[1,12,192,192]{3,0,1,2:T(1,128)} async-done(((f32[1,12,192,192]{3,0,1,2:T(1,128)}), f32[1,12,192,192]{3,0,1,2:T(1,128)}, u32[]{:S(2)}, u32[]{:S(2)}) %all-to-all-start.8) | async-done | bytes 1769504 | tf_op jit(solution)/shard_map/all_to_all | solution.py:49
  914.0 12.7 %all-to-all-start.11 = ((f32[1,192,12,192]{3,0,2,1:T(1,128)}), f32[1,192,12,192]{3,0,2,1:T(1,128)}, u32[]{:S(2)}, u32[]{:S(2)}) async-start(f32[1,192,12,192]{3,0,2,1:T(1,128)} %copy.315), calls=%async_computation.11 | async-start | bytes 4718592 | tf_op jit(solution)/shard_map/all_to_all | solution.py:59
  936.7 35.7 %all-to-all-done.11 = f32[1,192,12,192]{3,0,2,1:T(1,128)} async-done(((f32[1,192,12,192]{3,0,2,1:T(1,128)}), f32[1,192,12,192]{3,0,2,1:T(1,128)}, u32[]{:S(2)}, u32[]{:S(2)}) %all-to-all-start.11) | async-done | bytes 1769504 | tf_op jit(solution)/shard_map/all_to_all | solution.py:59
  972.4 12.5 %all-to-all-start.10 = ((f32[1,192,12,192]{3,0,2,1:T(1,128)}), f32[1,192,12,192]{3,0,2,1:T(1,128)}, u32[]{:S(2)}, u32[]{:S(2)}) async-start(f32[1,192,12,192]{3,0,2,1:T(1,128)} %copy.310), calls=%async_computation.10 | async-start | bytes 4718592 | tf_op jit(solution)/shard_map/all_to_all | solution.py:58
  1004.3 26.3 %all-to-all-done.10 = f32[1,192,12,192]{3,0,2,1:T(1,128)} async-done(((f32[1,192,12,192]{3,0,2,1:T(1,128)}), f32[1,192,12,192]{3,0,2,1:T(1,128)}, u32[]{:S(2)}, u32[]{:S(2)}) %all-to-all-start.10) | async-done | bytes 1769504 | tf_op jit(solution)/shard_map/all_to_all | solution.py:58
  1046.0 6.0 multiply_subtract_fusion
  (188 shorter events, 378.5 us)
Async XLA Ops:
  7.2 7.2 copy-start
  25.3 11.0 %copy-start.10 = (f32[192,12,192]{2,0,1:T(8,128)}, f32[192,12,192]{2,0,1:T(8,128)S(1)}, u32[]{:S(2)}) copy-start(f32[192,12,192]{2,0,1:T(8,128)S(1)} %fusion.62) | copy-start | bytes 5308420
  45.6 53.1 %all-to-all-start = ((f32[1,12,192,192]{3,0,1,2:T(1,128)}), f32[1,12,192,192]{3,0,1,2:T(1,128)}, u32[]{:S(2)}, u32[]{:S(2)}) async-start(f32[1,12,192,192]{3,0,1,2:T(1,128)} %copy.242), calls=%async_computation | async-start | bytes 4718592 | tf_op jit(solution)/shard_map/all_to_all | solution.py:50
  98.7 58.1 %all-to-all-start.1 = ((f32[1,12,192,192]{3,0,1,2:T(1,128)}), f32[1,12,192,192]{3,0,1,2:T(1,128)}, u32[]{:S(2)}, u32[]{:S(2)}) async-start(f32[1,12,192,192]{3,0,1,2:T(1,128)} %copy.250), calls=%async_computation.1 | async-start | bytes 4718592 | tf_op jit(solution)/shard_map/all_to_all | solution.py:49
  120.7 51.7 %copy-start.21 = (f32[192,12,192]{2,0,1:T(8,128)}, f32[192,12,192]{2,0,1:T(8,128)S(1)}, u32[]{:S(2)}) copy-start(f32[192,12,192]{2,0,1:T(8,128)S(1)} %reshape.430) | copy-start | bytes 5308420
  175.4 5.2 copy-start.23
  194.4 58.2 %all-to-all-start.3 = ((f32[1,192,12,192]{3,0,2,1:T(1,128)}), f32[1,192,12,192]{3,0,2,1:T(1,128)}, u32[]{:S(2)}, u32[]{:S(2)}) async-start(f32[1,192,12,192]{3,0,2,1:T(1,128)} %copy.263), calls=%async_computation.3 | async-start | bytes 4718592 | tf_op jit(solution)/shard_map/all_to_all | solution.py:58
  218.5 46.5 %copy-start.32 = (f32[12,192,192]{2,1,0:T(8,128)S(1)}, f32[12,192,192]{2,1,0:T(8,128)}, u32[]{:S(2)}) copy-start(f32[12,192,192]{2,1,0:T(8,128)} %param.6) | copy-start | bytes 5308420
  252.6 58.0 %all-to-all-start.2 = ((f32[1,192,12,192]{3,0,2,1:T(1,128)}), f32[1,192,12,192]{3,0,2,1:T(1,128)}, u32[]{:S(2)}, u32[]{:S(2)}) async-start(f32[1,192,12,192]{3,0,2,1:T(1,128)} %copy.258), calls=%async_computation.2 | async-start | bytes 4718592 | tf_op jit(solution)/shard_map/all_to_all | solution.py:59
  329.3 9.3 slice-start
  332.2 6.5 slice-start.1
  344.6 8.7 copy-start.1
  353.3 6.1 copy-start.5
  366.2 58.3 %all-to-all-start.4 = ((f32[1,12,192,192]{3,0,1,2:T(1,128)}), f32[1,12,192,192]{3,0,1,2:T(1,128)}, u32[]{:S(2)}, u32[]{:S(2)}) async-start(f32[1,12,192,192]{3,0,1,2:T(1,128)} %copy.270), calls=%async_computation.4 | async-start | bytes 4718592 | tf_op jit(solution)/shard_map/all_to_all | solution.py:49
  378.8 4.7 copy-start.7
  424.5 58.5 %all-to-all-start.5 = ((f32[1,12,192,192]{3,0,1,2:T(1,128)}), f32[1,12,192,192]{3,0,1,2:T(1,128)}, u32[]{:S(2)}, u32[]{:S(2)}) async-start(f32[1,12,192,192]{3,0,1,2:T(1,128)} %copy.276), calls=%async_computation.5 | async-start | bytes 4718592 | tf_op jit(solution)/shard_map/all_to_all | solution.py:50
  494.1 4.7 copy-start.22
  519.0 58.4 %all-to-all-start.7 = ((f32[1,192,12,192]{3,0,2,1:T(1,128)}), f32[1,192,12,192]{3,0,2,1:T(1,128)}, u32[]{:S(2)}, u32[]{:S(2)}) async-start(f32[1,192,12,192]{3,0,2,1:T(1,128)} %copy.289), calls=%async_computation.7 | async-start | bytes 4718592 | tf_op jit(solution)/shard_map/all_to_all | solution.py:59
  531.8 4.7 copy-start.15
  577.5 58.0 %all-to-all-start.6 = ((f32[1,192,12,192]{3,0,2,1:T(1,128)}), f32[1,192,12,192]{3,0,2,1:T(1,128)}, u32[]{:S(2)}, u32[]{:S(2)}) async-start(f32[1,192,12,192]{3,0,2,1:T(1,128)} %copy.284), calls=%async_computation.6 | async-start | bytes 4718592 | tf_op jit(solution)/shard_map/all_to_all | solution.py:58
  589.8 160.4 %all-reduce.2.cloned.1.call-start = ((), (), s32[]{:S(2)}) async-start(), calls=%async_computation.12 | async-start | bytes 4718592 | tf_op jit(solution)/shard_map/psum | solution.py:106
  643.4 4.7 copy-start.18
  654.3 9.1 slice-start.2
  657.2 6.2 slice-start.3
  667.3 6.5 copy-start.8
  757.5 6.0 copy-start.11
  770.4 51.6 %all-to-all-start.9 = ((f32[1,12,192,192]{3,0,1,2:T(1,128)}), f32[1,12,192,192]{3,0,1,2:T(1,128)}, u32[]{:S(2)}, u32[]{:S(2)}) async-start(f32[1,12,192,192]{3,0,1,2:T(1,128)} %copy.302), calls=%async_computation.9 | async-start | bytes 4718592 | tf_op jit(solution)/shard_map/all_to_all | solution.py:50
  822.0 58.4 %all-to-all-start.8 = ((f32[1,12,192,192]{3,0,1,2:T(1,128)}), f32[1,12,192,192]{3,0,1,2:T(1,128)}, u32[]{:S(2)}, u32[]{:S(2)}) async-start(f32[1,12,192,192]{3,0,1,2:T(1,128)} %copy.296), calls=%async_computation.8 | async-start | bytes 4718592 | tf_op jit(solution)/shard_map/all_to_all | solution.py:49
  887.5 4.7 copy-start.30
  914.0 58.4 %all-to-all-start.11 = ((f32[1,192,12,192]{3,0,2,1:T(1,128)}), f32[1,192,12,192]{3,0,2,1:T(1,128)}, u32[]{:S(2)}, u32[]{:S(2)}) async-start(f32[1,192,12,192]{3,0,2,1:T(1,128)} %copy.315), calls=%async_computation.11 | async-start | bytes 4718592 | tf_op jit(solution)/shard_map/all_to_all | solution.py:59
  936.7 48.2 %copy-start.9 = (f32[12,192,192]{2,1,0:T(8,128)S(1)}, f32[12,192,192]{2,1,0:T(8,128)}, u32[]{:S(2)}) copy-start(f32[12,192,192]{2,1,0:T(8,128)} %copy-done.8) | copy-start | bytes 5308420
  972.4 58.2 %all-to-all-start.10 = ((f32[1,192,12,192]{3,0,2,1:T(1,128)}), f32[1,192,12,192]{3,0,2,1:T(1,128)}, u32[]{:S(2)}, u32[]{:S(2)}) async-start(f32[1,192,12,192]{3,0,2,1:T(1,128)} %copy.310), calls=%async_computation.10 | async-start | bytes 4718592 | tf_op jit(solution)/shard_map/all_to_all | solution.py:58
  (18 other events, 54.5 us)
Sparse Core Ops, SparseCore 0:
  673.9 76.2 all-reduce.1
where the time goes:
time: 1080 us; the launch traced here: 1060 us
  waiting for transfers between devices  482 us (45%)
  matrix products  266 us (25%)
  local copies, waits for them, and re-layouts  148 us (14%)
  starting transfers between devices  139 us (13%)
  between operations  16.2 us (2%)
    all_to_all x3, waiting for transfers between devices, forward(): lax.all_to_all(real_part, 'grid', split_axis=2, concat_axis=1, tiled=True)  109 us
    all_to_all x3, waiting for transfers between devices, backward(): lax.all_to_all(imag_part, 'grid', split_axis=1, concat_axis=2, tiled=True)  106 us
    all_to_all x3, waiting for transfers between devices, forward(): lax.all_to_all(imag_part, 'grid', split_axis=2, concat_axis=1, tiled=True)  97.8 us
    all_to_all x3, waiting for transfers between devices, backward(): lax.all_to_all(real_part, 'grid', split_axis=1, concat_axis=2, tiled=True)  97.7 us
    dot_general x18, matrix products, transform(): rc = jnp.einsum(form, real_part, cosine, precision=high)  73 us
    psum x1, waiting for transfers between devices, local(): density = lax.psum(partial_value, 'band')  72.2 us
    dot_general x17, matrix products, transform(): ic = jnp.einsum(form, imag_part, cosine, precision=high)  68.2 us
    dot_general x18, matrix products, transform(): isn = jnp.einsum(form, imag_part, sine, precision=high)  66.3 us
  transfers between devices with their start and end apart: 13, of which 13 were waited for; matrix products, arithmetic and copies ran while one was open for 13% of the time, Pallas kernels for 0%

commit v1 on v0

v1 whole, which is shorter than its diff:
```python
import functools
import math

import jax
import jax.numpy as jnp
import numpy as np
from jax import lax
from jax.experimental import pallas as pl
from jax.experimental.pallas import tpu as pltpu
from jax.sharding import PartitionSpec as P

BESSEL_ZERO = 0.8462873527504802
BESSEL_ONE = 0.36884204609417703
BESSEL_TWO = 0.07581776248
XC_FACTOR = 0.98474502
PRECISION = lax.Precision.HIGH


def kinetic_matrix(length):
    idx = np.arange(length)
    freq = np.where(idx < length // 2, idx, idx - length).astype(np.float64)
    wave = np.cos(2.0 * math.pi * (np.outer(idx, idx) % length) / length)
    row = (wave @ (freq * freq)) / length * (2.0 / (3.0 * (length / 2) ** 2))
    return row[(idx[:, None] - idx[None, :]) % length].astype(np.float32)


def real_basis(length):
    half = length // 2
    idx = np.arange(length)
    order = np.concatenate([np.arange(half + 1), np.arange(1, half)])
    angle = 2.0 * math.pi * (np.outer(order, idx) % length) / length
    table = np.where((np.arange(length) <= half)[:, None], np.cos(angle), np.sin(angle))
    scale = np.where((order == 0) | (order == half), math.sqrt(1.0 / length), math.sqrt(2.0 / length))
    return (table * scale[:, None]).astype(np.float32), (order * order).astype(np.float32)


def dot(form, left, right):
    return jnp.einsum(form, left, right, precision=PRECISION)


def general(orbitals, occupations, ion_potential, hxc_potential):
    length = orbitals.shape[-1]
    planes = orbitals.shape[2]
    grid = lax.axis_size("grid")
    bands = lax.axis_size("band")
    cells = length * length
    columns = cells // grid
    share = cells // (grid * bands)
    kin = jnp.asarray(kinetic_matrix(length))
    kin_x = kin.reshape(length, grid, planes)
    basis_np, squares = real_basis(length)
    basis = jnp.asarray(basis_np)
    basis_x = basis.reshape(length, grid, planes)

    psi = orbitals[0]
    potential = ion_potential + hxc_potential

    def scatter(fields):
        parts = fields.reshape(fields.shape[0], planes, grid, columns).transpose(2, 1, 0, 3)
        return lax.all_to_all(parts, "grid", split_axis=0, concat_axis=0)

    def along_yz(field):
        return dot("cxyz,zk->cxyk", field, kin) + dot("cxyz,yk->cxkz", field, kin)

    moved = scatter(jnp.concatenate([psi, potential[None]], axis=0))
    local_kin = along_yz(psi) - psi
    applied = local_kin + potential * psi
    mixed = scatter(local_kin + applied)
    twice = along_yz(applied) - applied + potential * applied

    along = dot("ksp,spcn->ckn", kin_x, moved[:, :, :2])
    again = dot("ksp,spcn->ckn", kin_x, mixed) + dot("kx,cxn->ckn", kin, along)
    potential_cols = moved[:, :, 2].reshape(length, columns)
    again = again + potential_cols * along
    turned = jnp.stack([along[1], -along[0]])
    update = 2.0 * BESSEL_ONE * turned - 4.0 * BESSEL_TWO * again
    update = update.reshape(2, grid, planes, columns).transpose(1, 2, 0, 3)
    update = lax.all_to_all(update, "grid", split_axis=0, concat_axis=0)
    update = update.transpose(2, 1, 0, 3).reshape(psi.shape)

    turned = jnp.stack([applied[1], -applied[0]])
    fresh = (
        (BESSEL_ZERO + 2.0 * BESSEL_TWO) * psi
        + 2.0 * BESSEL_ONE * turned
        - 4.0 * BESSEL_TWO * twice
        + update
    )
    part = occupations[0] * (fresh[0] * fresh[0] + fresh[1] * fresh[1])
    density = lax.psum(part, "band")

    spectrum = dot("xyz,kz->xyk", part, basis)
    spectrum = dot("xyk,jy->xjk", spectrum, basis)
    spectrum = spectrum.reshape(planes, bands * grid, share).transpose(1, 0, 2)
    spectrum = lax.all_to_all(spectrum, ("band", "grid"), split_axis=0, concat_axis=0)
    spectrum = spectrum.reshape(bands, grid, planes, share).sum(axis=0)
    spectrum = dot("ksp,spn->kn", basis_x, spectrum)
    start = (lax.axis_index("band") * grid + lax.axis_index("grid")) * share
    cell = start + jnp.arange(share, dtype=jnp.int32)
    table = jnp.asarray(squares)
    total = table[:, None] + (table[cell // length] + table[cell % length])[None, :]
    kernel = jnp.where(total > 0, length * math.sqrt(length) / 16.0 / (total + 1.0), 0.0)
    spectrum = dot("kx,kn->xn", basis, kernel * spectrum)
    spectrum = spectrum.reshape(1, grid, planes, share)
    spectrum = jnp.broadcast_to(spectrum, (bands, grid, planes, share)).reshape(bands * grid, planes, share)
    spectrum = lax.all_to_all(spectrum, ("band", "grid"), split_axis=0, concat_axis=0)
    spectrum = spectrum.transpose(1, 0, 2).reshape(planes, length, length)
    spectrum = dot("xjk,jy->xyk", spectrum, basis)
    hartree = dot("xyk,kz->xyz", spectrum, basis)
    return (fresh[None], hartree - XC_FACTOR * jnp.cbrt(density))


LANES = 128


def product(left, right):
    return jnp.dot(left, right, precision=lax.Precision.HIGHEST, preferred_element_type=jnp.float32)


def split(array):
    high = array.astype(jnp.bfloat16)
    return high, (array - high.astype(jnp.float32)).astype(jnp.bfloat16)


def product_of_parts(left, right):
    total = jnp.dot(left[0], right[0], preferred_element_type=jnp.float32)
    total = total + jnp.dot(left[1], right[0], preferred_element_type=jnp.float32)
    return total + jnp.dot(left[0], right[1], preferred_element_type=jnp.float32)


def whole_tiles(rows):
    return -(-rows // 8) * 8


def chunk_rows(sizes):
    planes, _, rows, share = sizes
    return whole_tiles(planes * (2 * rows + share)), whole_tiles(planes * share)


def kinetic(plane, kin):
    return product(plane, kin) + product(kin, plane)


def pack(plane, packed):
    length = plane.shape[0]
    half = length // 2
    packed[:length, :] = plane[:, :LANES]
    packed[length:, :] = jnp.concatenate([plane[:half, LANES:], plane[half:, LANES:]], axis=1)


def unpack(packed, length):
    side = length - LANES
    tail = packed[length:, :]
    right = jnp.concatenate([tail[:, :side], tail[:, side:]], axis=0)
    return jnp.concatenate([packed[:length, :], right], axis=1)


def fill(out_ref, count, chunk, used):
    if used < chunk:

        @pl.when(pl.program_id(0) == 0)
        def _():
            for to in range(count):
                out_ref[pl.ds(to * chunk + used, chunk - used), :] = jnp.zeros((chunk - used, LANES), jnp.float32)


def pack_kernel(sizes, band_ref, psi_ref, ion_ref, hxc_ref, out_ref, packed):
    planes, grid, rows, share = sizes
    plane = pl.program_id(0)
    stride = 2 * rows + share
    chunk = chunk_rows(sizes)[0]
    fill(out_ref, grid, chunk, planes * stride)
    for part in range(2):
        pack(psi_ref[0, part, 0], packed)
        for to in range(grid):
            start = to * chunk + plane * stride + part * rows
            out_ref[pl.ds(start, rows), :] = packed[pl.ds(to * rows, rows), :]
    pack(ion_ref[0] + hxc_ref[0], packed)
    band = band_ref[0]
    for to in range(grid):
        start = to * chunk + plane * stride + 2 * rows
        out_ref[pl.ds(start, share), :] = packed[pl.ds(to * rows + band * share, share), :]


def plane_kernel(sizes, psi_ref, ion_ref, hxc_ref, kin_ref, out_ref, base_ref, packed):
    planes, grid, rows, share = sizes
    plane = pl.program_id(0)
    kin = kin_ref[...]
    potential = ion_ref[0] + hxc_ref[0]
    applied = []
    for part in range(2):
        field = psi_ref[0, part, 0]
        bare = kinetic(field, kin) - field
        applied.append(bare + potential * field)
        pack(bare + applied[part], packed)
        for to in range(grid):
            start = ((to * planes + plane) * 2 + part) * rows
            out_ref[pl.ds(start, rows), :] = packed[pl.ds(to * rows, rows), :]
    for part in range(2):
        twice = kinetic(applied[part], kin) + (potential - 1.0) * applied[part]
        turned = applied[1] if part == 0 else -applied[0]
        base_ref[part, 0] = (
            (BESSEL_ZERO + 2.0 * BESSEL_TWO) * psi_ref[0, part, 0]
            + 2.0 * BESSEL_ONE * turned
            - 4.0 * BESSEL_TWO * twice
        )


def share_kernel(sizes, moved_ref, out_ref):
    planes, grid, rows, share = sizes
    length = planes * grid
    stride = 2 * rows + share
    chunk = chunk_rows(sizes)[0]
    for row in range(share):
        for source in range(grid):
            start = source * chunk + 2 * rows + row
            out_ref[pl.ds(row * length + source * planes, planes), :] = moved_ref[pl.ds(start, planes, stride=stride), :]


def along_kernel(sizes, moved_ref, kin_ref, out_ref, lines):
    planes, grid, rows, share = sizes
    stride = 2 * rows + share
    chunk = chunk_rows(sizes)[0]
    row = pl.program_id(0)
    for source in range(grid):
        for part in range(2):
            start = source * chunk + part * rows + row
            lines[pl.ds(source * planes, planes), part * LANES : (part + 1) * LANES] = moved_ref[
                pl.ds(start, planes, stride=stride), :
            ]
    out_ref[...] = product(kin_ref[...], lines[...])


def update_kernel(sizes, steps, band_ref, mixed_ref, along_ref, own_ref, other_ref, kin_ref, out_ref):
    planes, grid, rows, share = sizes
    length = planes * grid
    kin = split(kin_ref[...])
    step = pl.program_id(0)
    mine_here = band_ref[0] == step // (steps // 2)
    for inner in range(rows // steps):
        row = step * (rows // steps) + inner
        here = slice(inner * length, (inner + 1) * length)
        along = along_ref[here, :]
        mixed = jnp.concatenate(
            [mixed_ref[pl.ds(part * rows + row, length, stride=2 * rows), :] for part in range(2)], axis=1
        )
        again = product_of_parts(kin, split(mixed + along))
        potential = jnp.where(mine_here, own_ref[here, :], other_ref[here, :])
        for part in range(2):
            mine = along[:, part * LANES : (part + 1) * LANES]
            turned = along[:, LANES:] if part == 0 else -along[:, :LANES]
            twice = again[:, part * LANES : (part + 1) * LANES] + potential * mine
            out_ref[pl.ds(part * rows + row, length, stride=2 * rows), :] = (
                2.0 * BESSEL_ONE * turned - 4.0 * BESSEL_TWO * twice
            )


def fresh_kernel(sizes, occ_ref, update_ref, base_ref, basis_ref, turn_ref, fresh_ref, part_ref, out_ref, packed):
    planes, grid, rows, share = sizes
    plane = pl.program_id(0)
    length = planes * grid
    part_sum = None
    for part in range(2):
        for source in range(grid):
            start = ((source * planes + plane) * 2 + part) * rows
            packed[pl.ds(source * rows, rows), :] = update_ref[pl.ds(start, rows), :]
        fresh = base_ref[part, 0] + unpack(packed, length)
        fresh_ref[0, part, 0] = fresh
        part_sum = fresh * fresh if part_sum is None else part_sum + fresh * fresh
    part_sum = occ_ref[0] * part_sum
    pack(part_sum, packed)
    part_ref[...] = packed[...]
    pack(product(product(basis_ref[...], part_sum), turn_ref[...]), packed)
    chunk = chunk_rows(sizes)[1]
    fill(out_ref, 2 * grid, chunk, planes * share)
    for to in range(2 * grid):
        out_ref[pl.ds(to * chunk + plane * share, share), :] = packed[pl.ds(to * share, share), :]


def filter_kernel(sizes, spec_ref, cells_ref, squares_ref, basis_ref, turn_ref, out_ref, lines):
    planes, grid, rows, share = sizes
    length = planes * grid
    chunk = chunk_rows(sizes)[1]

    def places():
        for source in range(grid):
            for row in range(share):
                first, second = (
                    pl.ds((band * grid + source) * chunk + row, planes, stride=share) for band in range(2)
                )
                here = (pl.ds(source * planes, planes), slice(row * LANES, (row + 1) * LANES))
                yield first, second, here

    for first, second, here in places():
        lines[here] = spec_ref[first, :] + spec_ref[second, :]
    total = squares_ref[...] + cells_ref[...]
    scale = length * math.sqrt(length) / 16.0
    kernel = jnp.where(total > 0.0, scale / (total + 1.0), 0.0)
    field = kernel * product(basis_ref[...], lines[...])
    lines[...] = product_of_parts(split(turn_ref[...]), split(field))
    for first, second, here in places():
        piece = lines[here]
        out_ref[first, :] = piece
        out_ref[second, :] = piece
    used = planes * share
    if used < chunk:
        for to in range(2 * grid):
            out_ref[pl.ds(to * chunk + used, chunk - used), :] = jnp.zeros((chunk - used, LANES), jnp.float32)


def last_kernel(sizes, spec_ref, root_ref, basis_ref, turn_ref, out_ref, packed):
    planes, grid, rows, share = sizes
    plane = pl.program_id(0)
    length = planes * grid
    chunk = chunk_rows(sizes)[1]
    for source in range(2 * grid):
        start = source * chunk + plane * share
        packed[pl.ds(source * share, share), :] = spec_ref[pl.ds(start, share), :]
    hartree = product_of_parts(split(turn_ref[...]), split(unpack(packed, length)))
    hartree = product_of_parts(split(hartree), split(basis_ref[...]))
    out_ref[0] = hartree - unpack(root_ref, length)


def shape(*dims):
    return jax.ShapeDtypeStruct(dims, jnp.float32)


def whole(*dims):
    return pl.BlockSpec(dims, lambda *_: (0,) * len(dims))


PARAMS = pltpu.CompilerParams(vmem_limit_bytes=56 << 20)


def cost(flops, moved):
    return pl.CostEstimate(flops=flops, bytes_accessed=moved, transcendentals=0)


def packed_path(orbitals, occupations, ion_potential, hxc_potential):
    length = orbitals.shape[-1]
    planes = orbitals.shape[2]
    grid = lax.axis_size("grid")
    cell_rows = length * length // LANES
    rows = cell_rows // grid
    share = rows // 2
    sizes = (planes, grid, rows, share)
    field = planes * cell_rows
    work = 2 * planes * length**3
    band = lax.axis_index("band").astype(jnp.int32).reshape(1)
    kin = jnp.asarray(kinetic_matrix(length))
    basis_np, squares_np = real_basis(length)
    basis, turn = jnp.asarray(basis_np), jnp.asarray(basis_np.T.copy())
    smem = pl.BlockSpec(memory_space=pltpu.SMEM)
    vmem = pl.BlockSpec(memory_space=pltpu.VMEM)
    psi_spec = pl.BlockSpec((1, 2, 1, length, length), lambda i: (0, 0, i, 0, 0))
    plane_spec = pl.BlockSpec((1, length, length), lambda i: (i, 0, 0))
    pair_spec = pl.BlockSpec((2, 1, length, length), lambda i: (0, i, 0, 0))
    square = whole(length, length)
    scratch = [pltpu.VMEM((cell_rows, LANES), jnp.float32)]

    def swap(array):
        flat = array.reshape(grid, -1, LANES)
        return lax.all_to_all(flat, "grid", split_axis=0, concat_axis=0).reshape(array.shape)

    def swap_all(array):
        flat = array.reshape(2 * grid, -1, LANES)
        return lax.all_to_all(flat, ("band", "grid"), split_axis=0, concat_axis=0).reshape(array.shape)

    moved_rows, spec_rows = (count * grid for count in chunk_rows(sizes))
    spec_rows = 2 * spec_rows
    steps = 6 if rows % 6 == 0 and share % (rows // 6) == 0 else 2
    moved = pl.pallas_call(
        functools.partial(pack_kernel, sizes),
        grid=(planes,),
        in_specs=[smem, psi_spec, plane_spec, plane_spec],
        out_specs=whole(moved_rows, LANES),
        out_shape=shape(moved_rows, LANES),
        scratch_shapes=scratch,
        compiler_params=PARAMS,
        cost_estimate=cost(0, 15 << 20),
    )(band, orbitals, ion_potential, hxc_potential)
    moved = swap(moved)
    mixed, base = pl.pallas_call(
        functools.partial(plane_kernel, sizes),
        grid=(planes,),
        in_specs=[psi_spec, plane_spec, plane_spec, square],
        out_specs=[whole(2 * field, LANES), pair_spec],
        out_shape=[shape(2 * field, LANES), shape(2, planes, length, length)],
        scratch_shapes=scratch,
        compiler_params=PARAMS,
        cost_estimate=cost(8 * 6 * work, 20 << 20),
    )(orbitals, ion_potential, hxc_potential, kin)
    mixed = swap(mixed)

    own = pl.pallas_call(
        functools.partial(share_kernel, sizes),
        in_specs=[vmem],
        out_specs=vmem,
        out_shape=shape(share * length, LANES),
        compiler_params=PARAMS,
        cost_estimate=cost(0, 6 << 20),
    )(moved)
    other = lax.ppermute(own, "band", [(0, 1), (1, 0)])
    along = pl.pallas_call(
        functools.partial(along_kernel, sizes),
        grid=(rows,),
        in_specs=[whole(moved_rows, LANES), square],
        out_specs=pl.BlockSpec((length, 2 * LANES), lambda i: (i, 0)),
        out_shape=shape(rows * length, 2 * LANES),
        scratch_shapes=[pltpu.VMEM((length, 2 * LANES), jnp.float32)],
        compiler_params=PARAMS,
        cost_estimate=cost(2 * 6 * work, 10 << 20),
    )(moved, kin)
    half_spec = pl.BlockSpec((rows // steps * length, LANES), lambda i: (i % (steps // 2), 0))
    update = pl.pallas_call(
        functools.partial(update_kernel, sizes, steps),
        grid=(steps,),
        in_specs=[
            smem,
            whole(2 * field, LANES),
            pl.BlockSpec((rows // steps * length, 2 * LANES), lambda i: (i, 0)),
            half_spec,
            half_spec,
            square,
        ],
        out_specs=whole(2 * field, LANES),
        out_shape=shape(2 * field, LANES),
        compiler_params=PARAMS,
        cost_estimate=cost(2 * 3 * work, 14 << 20),
    )(band, mixed, along, own, other, kin)
    update = swap(update)

    fresh, part, spectrum = pl.pallas_call(
        functools.partial(fresh_kernel, sizes),
        grid=(planes,),
        in_specs=[smem, whole(2 * field, LANES), pair_spec, square, square],
        out_specs=[
            psi_spec,
            pl.BlockSpec((cell_rows, LANES), lambda i: (i, 0)),
            whole(spec_rows, LANES),
        ],
        out_shape=[shape(*orbitals.shape), shape(field, LANES), shape(spec_rows, LANES)],
        scratch_shapes=scratch,
        compiler_params=PARAMS,
        cost_estimate=cost(2 * 6 * work, 16 << 20),
    )(occupations, update, base, basis, turn)
    density = part + lax.ppermute(part, "band", [(0, 1), (1, 0)])
    root = XC_FACTOR * jnp.cbrt(density)

    spectrum = swap_all(spectrum)
    cells_np = squares_np[:, None] + squares_np[None, :]
    half = length // 2
    cells_np = np.concatenate(
        [cells_np[:, :LANES], np.concatenate([cells_np[:half, LANES:], cells_np[half:, LANES:]], axis=1)]
    )
    device = lax.axis_index("band") * grid + lax.axis_index("grid")
    cells = lax.dynamic_slice_in_dim(jnp.asarray(cells_np), device * share, share, axis=0)
    spectrum = pl.pallas_call(
        functools.partial(filter_kernel, sizes),
        in_specs=[vmem] * 5,
        out_specs=vmem,
        out_shape=shape(spec_rows, LANES),
        scratch_shapes=[pltpu.VMEM((length, share * LANES), jnp.float32)],
        compiler_params=PARAMS,
        cost_estimate=cost(6 * work, 5 << 20),
    )(spectrum, cells.reshape(1, share * LANES), jnp.asarray(squares_np)[:, None], basis, turn)
    spectrum, root = lax.optimization_barrier((spectrum, root))
    spectrum = swap_all(spectrum)
    potential = pl.pallas_call(
        functools.partial(last_kernel, sizes),
        grid=(planes,),
        in_specs=[
            whole(spec_rows, LANES),
            pl.BlockSpec((cell_rows, LANES), lambda i: (i, 0)),
            square,
            square,
        ],
        out_specs=plane_spec,
        out_shape=shape(planes, length, length),
        scratch_shapes=scratch,
        compiler_params=PARAMS,
        cost_estimate=cost(2 * 6 * work, 6 << 20),
    )(spectrum, root, basis, turn)
    return (fresh, potential)


def local(orbitals, occupations, ion_potential, hxc_potential):
    length = orbitals.shape[-1]
    parts = 2 * lax.axis_size("grid") * LANES
    fits = length == LANES + LANES // 2 and lax.axis_size("band") == 2 and length * length % parts == 0
    path = packed_path if fits else general
    return path(orbitals, occupations, ion_potential, hxc_potential)


def solution(mesh):
    placed = (
        P("band", None, "grid", None, None),
        P("band"),
        P("grid", None, None),
        P("grid", None, None),
    )
    return jax.shard_map(
        local,
        mesh=mesh,
        in_specs=placed,
        out_specs=(P("band", None, "grid", None, None), P("grid", None, None)),
        check_vma=False,
    )
```

time: 1080 us -> 450 us (0.42); the launches traced: 1060 us -> 449 us
  matrix products: 266 us -> 0 us
  waiting for transfers between devices: 482 us -> 232 us
  local copies, waits for them, and re-layouts: 148 us -> 6.1 us
  Pallas kernels: 0 us -> 90.5 us
  starting transfers between devices: 139 us -> 65.4 us
  blocking collectives: 0 us -> 48.7 us
  between operations: 16.2 us -> 1.33 us
    dot_general x70 -> x0, matrix products: 266 us -> none  [the longest x18 73 us: transform(): rc = jnp.einsum(form, real_part, cosine, precision=high)]
    all_to_all x12 -> x4, waiting for transfers between devices: 410 us -> 174 us  [the longest x3 174 us: swap(): lax.all_to_all(flat, 'grid', split_axis=0, concat_axis=0)]
    pallas_call x0 -> x8, Pallas kernels: none -> 90.5 us  [the longest x1 23 us: packed_path(): pl.pallas_call(functools.partial(plane_kernel, sizes), grid=(planes,), in...]
    all_to_all x12 -> x4, starting transfers between devices: 139 us -> 62 us  [the longest x3 45.1 us: swap(): lax.all_to_all(flat, 'grid', split_axis=0, concat_axis=0)]
    psum x1 -> x0, waiting for transfers between devices: 72.2 us -> none  [local(): density = lax.psum(partial_value, 'band')]
    all_to_all x18 -> x0, local copies, waits for them, and re-layouts: 61 us -> none  [the longest x6 19.2 us: forward(): lax.all_to_all(imag_part, 'grid', split_axis=2, concat_axis=1, tiled=True)]
    ppermute x0 -> x2, waiting for transfers between devices: none -> 57.4 us  [the longest x1 57.4 us: packed_path(): density = part + lax.ppermute(part, 'band', [(0, 1), (1, 0)])]
    all_to_all x0 -> x1, blocking collectives: none -> 48.7 us  [swap_all(): lax.all_to_all(flat, ('band', 'grid'), split_axis=0, concat_axis=0)]
  transfers between devices with their start and end apart: 13 -> 6, of which waited for: 13 -> 4; matrix products, arithmetic and copies ran while one was open for 13% -> 1% of each run, Pallas kernels for 0% -> 8%
where the time goes in v1:
time: 450 us; the launch traced here: 449 us
  waiting for transfers between devices  232 us (52%)
  Pallas kernels  90.5 us (20%)
  starting transfers between devices  65.4 us (15%)
  blocking collectives  48.7 us (11%)
  local copies, waits for them, and re-layouts  6.1 us (1%)
  other arithmetic  4.7 us (1%)
    all_to_all x3, waiting for transfers between devices, swap(): lax.all_to_all(flat, 'grid', split_axis=0, concat_axis=0)  174 us
    ppermute x1, waiting for transfers between devices, packed_path(): density = part + lax.ppermute(part, 'band', [(0, 1), (1, 0)])  57.4 us
    all_to_all x1, blocking collectives, swap_all(): lax.all_to_all(flat, ('band', 'grid'), split_axis=0, concat_axis=0)  48.7 us
    all_to_all x3, starting transfers between devices, swap(): lax.all_to_all(flat, 'grid', split_axis=0, concat_axis=0)  45.1 us
    pallas_call x1, Pallas kernels, packed_path(): pl.pallas_call(functools.partial(plane_kernel, sizes), grid=(planes,), in...  23 us
    pallas_call x1, Pallas kernels, packed_path(): pl.pallas_call(functools.partial(fresh_kernel, sizes), grid=(planes,), in...  17 us
    all_to_all x1, starting transfers between devices, swap_all(): lax.all_to_all(flat, ('band', 'grid'), split_axis=0, concat_axis=0)  17 us
    pallas_call x1, Pallas kernels, packed_path(): pl.pallas_call(functools.partial(along_kernel, sizes), grid=(rows,), in_s...  11.8 us
  transfers between devices with their start and end apart: 6, of which 4 were waited for; matrix products, arithmetic and copies ran while one was open for 1% of the time, Pallas kernels for 8%

profile of v1, /device:TPU:0, one launch (start us, length us, event | category | flops | bytes accessed | tf_op | source)
XLA Modules:
  0.0 448.5 jit_solution(18258917059532634616)
XLA Ops:
  0.6 10.1 %shard_map.105 = f32[8704,128]{1,0:T(8,128)} custom-call(s32[1]{0:T(128)} %bitcast.band_ref, f32[1,2,12,192,192]{4,3,2,1,0:T(8,128)} %psi_ref.3, f32[12,192,192]{2,1,0:T(8,128)} %ion_ref.3, f32[12,192,192]{2,1,0:T(8,128)} %hxc_ref.3), custom_call_target="tpu_custom_call" | custom-call | bytes 15728640 | tf_op jit(solution)/shard_map/pallas_call | solution.py:371
  10.8 7.4 %all-to-all-start.1 = ((f32[16,544,128]{2,1,0:T(8,128)}), f32[16,544,128]{2,1,0:T(8,128)}, u32[]{:S(2)}, u32[]{:S(2)}) async-start(f32[16,544,128]{2,1,0:T(8,128)} %bitcast.17), calls=%async_computation.1 | async-start | bytes 8912896 | tf_op jit(solution)/shard_map/all_to_all | solution.py:362
  18.2 23.0 %shard_map.104 = (f32[6912,128]{1,0:T(8,128)}, f32[2,12,192,192]{3,2,1,0:T(8,128)}) custom-call(f32[1,2,12,192,192]{4,3,2,1,0:T(8,128)} %psi_ref.3, f32[12,192,192]{2,1,0:T(8,128)} %ion_ref.3, f32[12,192,192]{2,1,0:T(8,128)} %hxc_ref.3, f32[192,192]{1,0:T(8,128)} %constant.29.clone.kin_ref), custom_call_target="tpu_custom_call" | custom-call | flops 8153726976 | bytes 20971520 | tf_op jit(solution)/shard_map/pallas_call | solution.py:382
  41.2 59.3 %all-to-all-done.1 = f32[16,544,128]{2,1,0:T(8,128)} async-done(((f32[16,544,128]{2,1,0:T(8,128)}), f32[16,544,128]{2,1,0:T(8,128)}, u32[]{:S(2)}, u32[]{:S(2)}) %all-to-all-start.1) | async-done | bytes 4456480 | tf_op jit(solution)/shard_map/all_to_all | solution.py:362
  100.4 20.7 %all-to-all-start = ((f32[16,432,128]{2,1,0:T(8,128)}), f32[16,432,128]{2,1,0:T(8,128)S(1)}, u32[]{:S(2)}, u32[]{:S(2)}) async-start(f32[16,432,128]{2,1,0:T(8,128)} %bitcast.23), calls=%async_computation | async-start | bytes 7077888 | tf_op jit(solution)/shard_map/all_to_all | solution.py:362
  121.1 3.3 shard_map.107.own_ref
  124.4 1.5 collective-permute-start
  125.9 11.8 %shard_map.106.along_ref = f32[3456,256]{1,0:T(8,128)} custom-call(f32[8704,128]{1,0:T(8,128)} %bitcast.4.moved_ref, f32[192,192]{1,0:T(8,128)} %constant.29.clone.kin_ref), custom_call_target="tpu_custom_call" | custom-call | flops 2038431744 | bytes 10485760 | tf_op jit(solution)/shard_map/pallas_call | solution.py:403
  137.8 49.6 %all-to-all-done = f32[16,432,128]{2,1,0:T(8,128)S(1)} async-done(((f32[16,432,128]{2,1,0:T(8,128)}), f32[16,432,128]{2,1,0:T(8,128)S(1)}, u32[]{:S(2)}, u32[]{:S(2)}) %all-to-all-start) | async-done | bytes 3538976 | tf_op jit(solution)/shard_map/all_to_all | solution.py:362
  187.3 0.0 copy-start
  187.3 0.0 collective-permute-done.other_ref
  187.3 1.8 copy-done
  189.1 8.6 %shard_map.108 = f32[6912,128]{1,0:T(8,128)} custom-call(s32[1]{0:T(128)} %bitcast.band_ref, f32[6912,128]{1,0:T(8,128)} %bitcast.18, f32[3456,256]{1,0:T(8,128)} %shard_map.106.along_ref, f32[1728,128]{1,0:T(8,128)} %shard_map.107.own_ref, f32[1728,128]{1,0:T(8,128)} %collective-permute-done.other_ref, f32[192,192]{1,0:T(8,128)} %constant.29.clone.kin_ref), custom_call_target="tpu_custom_call" | custom-call | flops 1019215872 | bytes 14680064 | tf_op jit(solution)/shard_map/pallas_call | solution.py:414
  197.8 17.0 %all-to-all-start.2 = ((f32[16,432,128]{2,1,0:T(8,128)}), f32[16,432,128]{2,1,0:T(8,128)S(1)}, u32[]{:S(2)}, u32[]{:S(2)}) async-start(f32[16,432,128]{2,1,0:T(8,128)} %bitcast.20), calls=%async_computation.2 | async-start | bytes 7077888 | tf_op jit(solution)/shard_map/all_to_all | solution.py:362
  215.4 65.6 %all-to-all-done.2 = f32[16,432,128]{2,1,0:T(8,128)S(1)} async-done(((f32[16,432,128]{2,1,0:T(8,128)}), f32[16,432,128]{2,1,0:T(8,128)S(1)}, u32[]{:S(2)}, u32[]{:S(2)}) %all-to-all-start.2) | async-done | bytes 3538976 | tf_op jit(solution)/shard_map/all_to_all | solution.py:362
  281.0 0.0 copy-start.1
  281.0 1.8 copy-done.1
  282.8 17.0 %shard_map.109 = (f32[1,2,12,192,192]{4,3,2,1,0:T(8,128)}, f32[3456,128]{1,0:T(8,128)}, f32[3584,128]{1,0:T(8,128)}) custom-call(f32[1]{0:T(128)S(6)} %copy.14.occ_ref, f32[6912,128]{1,0:T(8,128)} %bitcast.19, f32[2,12,192,192]{3,2,1,0:T(8,128)} %get-tuple-element.10.base_ref, f32[192,192]{1,0:T(8,128)} %constant.30.clone.basis_ref, ...), custom_call_target="tpu_custom_call" | custom-call | flops 2038431744 | bytes 16777216 | tf_op jit(solution)/shard_map/pallas_call | solution.py:432
  299.8 17.0 %all-to-all-start.3 = ((f32[32,112,128]{2,1,0:T(8,128)}), f32[32,112,128]{2,1,0:T(8,128)S(1)}, u32[]{:S(2)}, u32[]{:S(2)}) async-start(f32[32,112,128]{2,1,0:T(8,128)} %bitcast.24), calls=%async_computation.3 | async-start | bytes 3670016 | tf_op jit(solution)/shard_map/all_to_all | solution.py:366
  316.7 1.8 collective-permute-start.1
  318.6 0.7 dynamic-slice_bitcast_fusion
  319.3 0.6 copy.13
  319.9 57.4 %collective-permute-done.1 = f32[3456,128]{1,0:T(8,128)} collective-permute-done((f32[3456,128]{1,0:T(8,128)}, f32[3456,128]{1,0:T(8,128)}, u32[]{:S(2)}, u32[]{:S(2)}) %collective-permute-start.1) | collective-permute-done | bytes 1769504 | tf_op jit(solution)/shard_map/ppermute | solution.py:446
  377.3 4.7 %cbrt_multiply_fusion.root_ref = f32[3456,128]{1,0:T(8,128)} fusion(f32[3456,128]{1,0:T(8,128)} %get-tuple-element.13, f32[3456,128]{1,0:T(8,128)} %collective-permute-done.1), kind=kLoop, calls=%fused_computation | loop fusion | flops 884736 | bytes 5308416 | tf_op jit(solution)/shard_map/mul | solution.py:447
  382.0 0.0 all-to-all-done.3
  382.0 0.0 copy-start.2
  382.0 1.2 copy-done.2
  383.2 5.1 %shard_map.110 = f32[3584,128]{1,0:T(8,128)} custom-call(f32[3584,128]{1,0:T(8,128)} %bitcast.21, f32[1,1152]{1,0:T(1,128)} %bitcast.26, f32[192,1]{1,0:T(8,128)} %constant.38.squares_ref, f32[192,192]{1,0:T(8,128)} %constant.30.clone.basis_ref, f32[192,192]{1,0:T(8,128)} %constant.31.clone.turn_ref), custom_call_target="tpu_custom_call" | custom-call | flops 1019215872 | bytes 5242880 | tf_op jit(solution)/shard_map/pallas_call | solution.py:457
  388.3 48.7 %all_to_all.25 = f32[32,112,128]{2,1,0:T(8,128)} all-to-all(f32[32,112,128]{2,1,0:T(8,128)} %bitcast.22), channel_id=1, replica_groups=mesh['band'=2,'grid'=16] {'band','grid'}, dimensions={0} | all-to-all | bytes 3670016 | tf_op jit(solution)/shard_map/all_to_all | solution.py:366
  437.0 11.5 %shard_map.111 = f32[12,192,192]{2,1,0:T(8,128)} custom-call(f32[3584,128]{1,0:T(8,128)} %bitcast.25, f32[3456,128]{1,0:T(8,128)} %cbrt_multiply_fusion.root_ref, f32[192,192]{1,0:T(8,128)} %constant.30.clone.basis_ref, f32[192,192]{1,0:T(8,128)} %constant.31.clone.turn_ref), custom_call_target="tpu_custom_call" | custom-call | flops 2038431744 | bytes 6291456 | tf_op jit(solution)/shard_map/pallas_call | solution.py:468
Async XLA Ops:
  10.8 89.7 %all-to-all-start.1 = ((f32[16,544,128]{2,1,0:T(8,128)}), f32[16,544,128]{2,1,0:T(8,128)}, u32[]{:S(2)}, u32[]{:S(2)}) async-start(f32[16,544,128]{2,1,0:T(8,128)} %bitcast.17), calls=%async_computation.1 | async-start | bytes 8912896 | tf_op jit(solution)/shard_map/all_to_all | solution.py:362
  100.4 86.9 %all-to-all-start = ((f32[16,432,128]{2,1,0:T(8,128)}), f32[16,432,128]{2,1,0:T(8,128)S(1)}, u32[]{:S(2)}, u32[]{:S(2)}) async-start(f32[16,432,128]{2,1,0:T(8,128)} %bitcast.23), calls=%async_computation | async-start | bytes 7077888 | tf_op jit(solution)/shard_map/all_to_all | solution.py:362
  124.4 62.9 %collective-permute-start = (f32[1728,128]{1,0:T(8,128)}, f32[1728,128]{1,0:T(8,128)}, u32[]{:S(2)}, u32[]{:S(2)}) collective-permute-start(f32[1728,128]{1,0:T(8,128)} %shard_map.107.own_ref), channel_id=1, source_target_pairs={{0,16},{16,0},{1,17},{17,1},{2,18},{18,2},{3,19},{19,3},{4,20},{20... | collective-permute-start | bytes 2654216 | tf_op jit(solution)/shard_map/ppermute | solution.py:402
  187.3 1.8 copy-start
  197.8 83.2 %all-to-all-start.2 = ((f32[16,432,128]{2,1,0:T(8,128)}), f32[16,432,128]{2,1,0:T(8,128)S(1)}, u32[]{:S(2)}, u32[]{:S(2)}) async-start(f32[16,432,128]{2,1,0:T(8,128)} %bitcast.20), calls=%async_computation.2 | async-start | bytes 7077888 | tf_op jit(solution)/shard_map/all_to_all | solution.py:362
  281.0 1.8 copy-start.1
  299.8 82.2 %all-to-all-start.3 = ((f32[32,112,128]{2,1,0:T(8,128)}), f32[32,112,128]{2,1,0:T(8,128)S(1)}, u32[]{:S(2)}, u32[]{:S(2)}) async-start(f32[32,112,128]{2,1,0:T(8,128)} %bitcast.24), calls=%async_computation.3 | async-start | bytes 3670016 | tf_op jit(solution)/shard_map/all_to_all | solution.py:366
  316.7 60.6 %collective-permute-start.1 = (f32[3456,128]{1,0:T(8,128)}, f32[3456,128]{1,0:T(8,128)}, u32[]{:S(2)}, u32[]{:S(2)}) collective-permute-start(f32[3456,128]{1,0:T(8,128)} %get-tuple-element.13), channel_id=1, source_target_pairs={{0,16},{16,0},{1,17},{17,1},{2,18},{18,2},{3,19},{19,3},{4,20},{20... | collective-permute-start | bytes 5308424 | tf_op jit(solution)/shard_map/ppermute | solution.py:446
  382.0 1.2 copy-start.2

commit v2 on v1

--- a/solution.py
+++ b/solution.py
@@ -163,46 +163,51 @@
                 out_ref[pl.ds(to * chunk + used, chunk - used), :] = jnp.zeros((chunk - used, LANES), jnp.float32)
 
 
-def pack_kernel(sizes, band_ref, psi_ref, ion_ref, hxc_ref, out_ref, packed):
-    planes, grid, rows, share = sizes
-    plane = pl.program_id(0)
+def pack_kernel(sizes, bunch, band_ref, psi_ref, ion_ref, hxc_ref, out_ref, packed):
+    planes, grid, rows, share = sizes
     stride = 2 * rows + share
     chunk = chunk_rows(sizes)[0]
     fill(out_ref, grid, chunk, planes * stride)
-    for part in range(2):
-        pack(psi_ref[0, part, 0], packed)
+    band = band_ref[0]
+    for inner in range(bunch):
+        plane = pl.program_id(0) * bunch + inner
+        for part in range(2):
+            slot = packed.at[inner * 3 + part]
+            pack(psi_ref[0, part, inner], slot)
+            for to in range(grid):
+                start = to * chunk + plane * stride + part * rows
+                out_ref[pl.ds(start, rows), :] = slot[pl.ds(to * rows, rows), :]
+        slot = packed.at[inner * 3 + 2]
+        pack(ion_ref[inner] + hxc_ref[inner], slot)
         for to in range(grid):
-            start = to * chunk + plane * stride + part * rows
-            out_ref[pl.ds(start, rows), :] = packed[pl.ds(to * rows, rows), :]
-    pack(ion_ref[0] + hxc_ref[0], packed)
-    band = band_ref[0]
-    for to in range(grid):
-        start = to * chunk + plane * stride + 2 * rows
-        out_ref[pl.ds(start, share), :] = packed[pl.ds(to * rows + band * share, share), :]
-
-
-def plane_kernel(sizes, psi_ref, ion_ref, hxc_ref, kin_ref, out_ref, base_ref, packed):
-    planes, grid, rows, share = sizes
-    plane = pl.program_id(0)
+            start = to * chunk + plane * stride + 2 * rows
+            out_ref[pl.ds(start, share), :] = slot[pl.ds(to * rows + band * share, share), :]
+
+
+def plane_kernel(sizes, bunch, psi_ref, ion_ref, hxc_ref, kin_ref, out_ref, base_ref, packed):
+    planes, grid, rows, share = sizes
     kin = kin_ref[...]
-    potential = ion_ref[0] + hxc_ref[0]
-    applied = []
-    for part in range(2):
-        field = psi_ref[0, part, 0]
-        bare = kinetic(field, kin) - field
-        applied.append(bare + potential * field)
-        pack(bare + applied[part], packed)
-        for to in range(grid):
-            start = ((to * planes + plane) * 2 + part) * rows
-            out_ref[pl.ds(start, rows), :] = packed[pl.ds(to * rows, rows), :]
-    for part in range(2):
-        twice = kinetic(applied[part], kin) + (potential - 1.0) * applied[part]
-        turned = applied[1] if part == 0 else -applied[0]
-        base_ref[part, 0] = (
-            (BESSEL_ZERO + 2.0 * BESSEL_TWO) * psi_ref[0, part, 0]
-            + 2.0 * BESSEL_ONE * turned
-            - 4.0 * BESSEL_TWO * twice
-        )
+    for inner in range(bunch):
+        plane = pl.program_id(0) * bunch + inner
+        potential = ion_ref[inner] + hxc_ref[inner]
+        applied = []
+        for part in range(2):
+            field = psi_ref[0, part, inner]
+            bare = kinetic(field, kin) - field
+            applied.append(bare + potential * field)
+            slot = packed.at[inner * 2 + part]
+            pack(bare + applied[part], slot)
+            for to in range(grid):
+                start = ((to * planes + plane) * 2 + part) * rows
+                out_ref[pl.ds(start, rows), :] = slot[pl.ds(to * rows, rows), :]
+        for part in range(2):
+            twice = kinetic(applied[part], kin) + (potential - 1.0) * applied[part]
+            turned = applied[1] if part == 0 else -applied[0]
+            base_ref[part, inner] = (
+                (BESSEL_ZERO + 2.0 * BESSEL_TWO) * psi_ref[0, part, inner]
+                + 2.0 * BESSEL_ONE * turned
+                - 4.0 * BESSEL_TWO * twice
+            )
 
 
 def share_kernel(sizes, moved_ref, out_ref):
@@ -254,26 +259,35 @@
             )
 
 
-def fresh_kernel(sizes, occ_ref, update_ref, base_ref, basis_ref, turn_ref, fresh_ref, part_ref, out_ref, packed):
-    planes, grid, rows, share = sizes
-    plane = pl.program_id(0)
+def fresh_kernel(
+    sizes, bunch, occ_ref, update_ref, base_ref, basis_ref, turn_ref, fresh_ref, upper_ref, lower_ref, out_ref, packed
+):
+    planes, grid, rows, share = sizes
     length = planes * grid
-    part_sum = None
-    for part in range(2):
-        for source in range(grid):
-            start = ((source * planes + plane) * 2 + part) * rows
-            packed[pl.ds(source * rows, rows), :] = update_ref[pl.ds(start, rows), :]
-        fresh = base_ref[part, 0] + unpack(packed, length)
-        fresh_ref[0, part, 0] = fresh
-        part_sum = fresh * fresh if part_sum is None else part_sum + fresh * fresh
-    part_sum = occ_ref[0] * part_sum
-    pack(part_sum, packed)
-    part_ref[...] = packed[...]
-    pack(product(product(basis_ref[...], part_sum), turn_ref[...]), packed)
     chunk = chunk_rows(sizes)[1]
+    cell_rows = rows * grid
+    half = cell_rows // 2
     fill(out_ref, 2 * grid, chunk, planes * share)
-    for to in range(2 * grid):
-        out_ref[pl.ds(to * chunk + plane * share, share), :] = packed[pl.ds(to * share, share), :]
+    for inner in range(bunch):
+        plane = pl.program_id(0) * bunch + inner
+        part_sum = None
+        for part in range(2):
+            slot = packed.at[inner * 4 + part]
+            for source in range(grid):
+                start = ((source * planes + plane) * 2 + part) * rows
+                slot[pl.ds(source * rows, rows), :] = update_ref[pl.ds(start, rows), :]
+            fresh = base_ref[part, inner] + unpack(slot, length)
+            fresh_ref[0, part, inner] = fresh
+            part_sum = fresh * fresh if part_sum is None else part_sum + fresh * fresh
+        part_sum = occ_ref[0] * part_sum
+        slot = packed.at[inner * 4 + 2]
+        pack(part_sum, slot)
+        upper_ref[inner * half : (inner + 1) * half, :] = slot[:half, :]
+        lower_ref[inner * half : (inner + 1) * half, :] = slot[half:, :]
+        slot = packed.at[inner * 4 + 3]
+        pack(product(product(basis_ref[...], part_sum), turn_ref[...]), slot)
+        for to in range(2 * grid):
+            out_ref[pl.ds(to * chunk + plane * share, share), :] = slot[pl.ds(to * share, share), :]
 
 
 def filter_kernel(sizes, spec_ref, cells_ref, squares_ref, basis_ref, turn_ref, out_ref, lines):
@@ -307,17 +321,28 @@
             out_ref[pl.ds(to * chunk + used, chunk - used), :] = jnp.zeros((chunk - used, LANES), jnp.float32)
 
 
-def last_kernel(sizes, spec_ref, root_ref, basis_ref, turn_ref, out_ref, packed):
-    planes, grid, rows, share = sizes
-    plane = pl.program_id(0)
+def last_kernel(
+    sizes, bunch, spec_ref, upper_ref, lower_ref, upper_other, lower_other, basis_ref, turn_ref, out_ref, packed
+):
+    planes, grid, rows, share = sizes
     length = planes * grid
+    half = rows * grid // 2
     chunk = chunk_rows(sizes)[1]
-    for source in range(2 * grid):
-        start = source * chunk + plane * share
-        packed[pl.ds(source * share, share), :] = spec_ref[pl.ds(start, share), :]
-    hartree = product_of_parts(split(turn_ref[...]), split(unpack(packed, length)))
-    hartree = product_of_parts(split(hartree), split(basis_ref[...]))
-    out_ref[0] = hartree - unpack(root_ref, length)
+    turn, basis = split(turn_ref[...]), split(basis_ref[...])
+    for inner in range(bunch):
+        plane = pl.program_id(0) * bunch + inner
+        slot = packed.at[inner * 2]
+        for source in range(2 * grid):
+            start = source * chunk + plane * share
+            slot[pl.ds(source * share, share), :] = spec_ref[pl.ds(start, share), :]
+        hartree = product_of_parts(turn, split(unpack(slot, length)))
+        hartree = product_of_parts(split(hartree), basis)
+        slot = packed.at[inner * 2 + 1]
+        here = slice(inner * half, (inner + 1) * half)
+        slot[:half, :] = upper_ref[here, :] + upper_other[here, :]
+        slot[half:, :] = lower_ref[here, :] + lower_other[here, :]
+        root = jnp.exp(jnp.log(unpack(slot, length)) * (1.0 / 3.0))
+        out_ref[inner] = hartree - XC_FACTOR * root
 
 
 def shape(*dims):
@@ -351,11 +376,15 @@
     basis, turn = jnp.asarray(basis_np), jnp.asarray(basis_np.T.copy())
     smem = pl.BlockSpec(memory_space=pltpu.SMEM)
     vmem = pl.BlockSpec(memory_space=pltpu.VMEM)
-    psi_spec = pl.BlockSpec((1, 2, 1, length, length), lambda i: (0, 0, i, 0, 0))
-    plane_spec = pl.BlockSpec((1, length, length), lambda i: (i, 0, 0))
-    pair_spec = pl.BlockSpec((2, 1, length, length), lambda i: (0, i, 0, 0))
+    bunch = next(count for count in (3, 2, 1) if planes % count == 0)
+    psi_spec = pl.BlockSpec((1, 2, bunch, length, length), lambda i: (0, 0, i, 0, 0))
+    plane_spec = pl.BlockSpec((bunch, length, length), lambda i: (i, 0, 0))
+    pair_spec = pl.BlockSpec((2, bunch, length, length), lambda i: (0, i, 0, 0))
+    half_rows = pl.BlockSpec((bunch * cell_rows // 2, LANES), lambda i: (i, 0))
     square = whole(length, length)
-    scratch = [pltpu.VMEM((cell_rows, LANES), jnp.float32)]
+
+    def scratch(count):
+        return [pltpu.VMEM((count * bunch, cell_rows, LANES), jnp.float32)]
 
     def swap(array):
         flat = array.reshape(grid, -1, LANES)
@@ -369,23 +398,23 @@
     spec_rows = 2 * spec_rows
     steps = 6 if rows % 6 == 0 and share % (rows // 6) == 0 else 2
     moved = pl.pallas_call(
-        functools.partial(pack_kernel, sizes),
-        grid=(planes,),
+        functools.partial(pack_kernel, sizes, bunch),
+        grid=(planes // bunch,),
         in_specs=[smem, psi_spec, plane_spec, plane_spec],
         out_specs=whole(moved_rows, LANES),
         out_shape=shape(moved_rows, LANES),
-        scratch_shapes=scratch,
+        scratch_shapes=scratch(3),
         compiler_params=PARAMS,
         cost_estimate=cost(0, 15 << 20),
     )(band, orbitals, ion_potential, hxc_potential)
     moved = swap(moved)
     mixed, base = pl.pallas_call(
-        functools.partial(plane_kernel, sizes),
-        grid=(planes,),
+        functools.partial(plane_kernel, sizes, bunch),
+        grid=(planes // bunch,),
         in_specs=[psi_spec, plane_spec, plane_spec, square],
         out_specs=[whole(2 * field, LANES), pair_spec],
         out_shape=[shape(2 * field, LANES), shape(2, planes, length, length)],
-        scratch_shapes=scratch,
+        scratch_shapes=scratch(2),
         compiler_params=PARAMS,
         cost_estimate=cost(8 * 6 * work, 20 << 20),
     )(orbitals, ion_potential, hxc_potential, kin)
@@ -429,22 +458,28 @@
     )(band, mixed, along, own, other, kin)
     update = swap(update)
 
-    fresh, part, spectrum = pl.pallas_call(
-        functools.partial(fresh_kernel, sizes),
-        grid=(planes,),
+    fresh, upper, lower, spectrum = pl.pallas_call(
+        functools.partial(fresh_kernel, sizes, bunch),
+        grid=(planes // bunch,),
         in_specs=[smem, whole(2 * field, LANES), pair_spec, square, square],
         out_specs=[
             psi_spec,
-            pl.BlockSpec((cell_rows, LANES), lambda i: (i, 0)),
+            half_rows,
+            half_rows,
             whole(spec_rows, LANES),
         ],
-        out_shape=[shape(*orbitals.shape), shape(field, LANES), shape(spec_rows, LANES)],
-        scratch_shapes=scratch,
+        out_shape=[
+            shape(*orbitals.shape),
+            shape(field // 2, LANES),
+            shape(field // 2, LANES),
+            shape(spec_rows, LANES),
+        ],
+        scratch_shapes=scratch(4),
         compiler_params=PARAMS,
         cost_estimate=cost(2 * 6 * work, 16 << 20),
     )(occupations, update, base, basis, turn)
-    density = part + lax.ppermute(part, "band", [(0, 1), (1, 0)])
-    root = XC_FACTOR * jnp.cbrt(density)
+    upper_other = lax.ppermute(upper, "band", [(0, 1), (1, 0)])
+    lower_other = lax.ppermute(lower, "band", [(0, 1), (1, 0)])
 
     spectrum = swap_all(spectrum)
     cells_np = squares_np[:, None] + squares_np[None, :]
@@ -463,23 +498,26 @@
         compiler_params=PARAMS,
         cost_estimate=cost(6 * work, 5 << 20),
     )(spectrum, cells.reshape(1, share * LANES), jnp.asarray(squares_np)[:, None], basis, turn)
-    spectrum, root = lax.optimization_barrier((spectrum, root))
+    spectrum, upper_other = lax.optimization_barrier((spectrum, upper_other))
     spectrum = swap_all(spectrum)
     potential = pl.pallas_call(
-        functools.partial(last_kernel, sizes),
-        grid=(planes,),
+        functools.partial(last_kernel, sizes, bunch),
+        grid=(planes // bunch,),
         in_specs=[
             whole(spec_rows, LANES),
-            pl.BlockSpec((cell_rows, LANES), lambda i: (i, 0)),
+            half_rows,
+            half_rows,
+            half_rows,
+            half_rows,
             square,
             square,
         ],
         out_specs=plane_spec,
         out_shape=shape(planes, length, length),
-        scratch_shapes=scratch,
+        scratch_shapes=scratch(2),
         compiler_params=PARAMS,
         cost_estimate=cost(2 * 6 * work, 6 << 20),
-    )(spectrum, root, basis, turn)
+    )(spectrum, upper, lower, upper_other, lower_other, basis, turn)
     return (fresh, potential)
 
 

time: 450 us -> 414 us (0.920)
  blocking collectives: 48.7 us -> 0 us
  waiting for transfers between devices: 232 us -> 259 us
  Pallas kernels: 90.5 us -> 76.2 us
  other arithmetic: 4.7 us -> 0 us
  starting transfers between devices: 65.4 us -> 69.9 us
    all_to_all x1 -> x0, blocking collectives: 48.7 us -> none  [swap_all(): lax.all_to_all(flat, ('band', 'grid'), split_axis=0, concat_axis=0)]
    all_to_all x1 -> x2, waiting for transfers between devices: 0.01 us -> 45.5 us  [swap_all(): lax.all_to_all(flat, ('band', 'grid'), split_axis=0, concat_axis=0)]
    ppermute x1 -> x2, waiting for transfers between devices: 57.4 us -> 37.8 us  [the longest x1 37.8 us: packed_path(): lower_other = lax.ppermute(lower, 'band', [(0, 1), (1, 0)])]
    pallas_call x4, Pallas kernels: 61.6 us -> 47.4 us  [the longest x1 22 us: packed_path(): pl.pallas_call(functools.partial(plane_kernel, sizes, bunch), grid=(plane...]
    mul x1 -> x0, other arithmetic: 4.7 us -> none  [packed_path(): root = XC_FACTOR * jnp.cbrt(density)]
    all_to_all x1 -> x2, starting transfers between devices: 17 us -> 19.7 us  [swap_all(): lax.all_to_all(flat, ('band', 'grid'), split_axis=0, concat_axis=0)]
  transfers between devices with their start and end apart: 6 -> 8, of which waited for: 4 -> 6; matrix products, arithmetic and copies ran while one was open for 1% -> 0% of each run, Pallas kernels for 8% -> 10%
where the time goes in v2:
time: 414 us; the launch traced here: 413 us
  waiting for transfers between devices  259 us (63%)
  Pallas kernels  76.2 us (18%)
  starting transfers between devices  69.9 us (17%)
  local copies, waits for them, and re-layouts  7.35 us (2%)
    all_to_all x3, waiting for transfers between devices, swap(): lax.all_to_all(flat, 'grid', split_axis=0, concat_axis=0)  175 us
    all_to_all x2, waiting for transfers between devices, swap_all(): lax.all_to_all(flat, ('band', 'grid'), split_axis=0, concat_axis=0)  45.5 us
    all_to_all x3, starting transfers between devices, swap(): lax.all_to_all(flat, 'grid', split_axis=0, concat_axis=0)  45.1 us
    ppermute x1, waiting for transfers between devices, packed_path(): lower_other = lax.ppermute(lower, 'band', [(0, 1), (1, 0)])  37.8 us
    pallas_call x1, Pallas kernels, packed_path(): pl.pallas_call(functools.partial(plane_kernel, sizes, bunch), grid=(plane...  22 us
    all_to_all x2, starting transfers between devices, swap_all(): lax.all_to_all(flat, ('band', 'grid'), split_axis=0, concat_axis=0)  19.7 us
    pallas_call x1, Pallas kernels, packed_path(): pl.pallas_call(functools.partial(along_kernel, sizes), grid=(rows,), in_s...  11.9 us
    pallas_call x1, Pallas kernels, packed_path(): pl.pallas_call(functools.partial(fresh_kernel, sizes, bunch), grid=(plane...  11.5 us
  transfers between devices with their start and end apart: 8, of which 6 were waited for; matrix products, arithmetic and copies ran while one was open for 0% of the time, Pallas kernels for 10%

profile of v2, /device:TPU:0, one launch (start us, length us, event | category | flops | bytes accessed | tf_op | source)
XLA Modules:
  0.0 413.5 jit_solution(197271319133715894)
XLA Ops:
  0.6 6.8 %shard_map.105 = f32[8704,128]{1,0:T(8,128)} custom-call(s32[1]{0:T(128)} %bitcast.band_ref, f32[1,2,12,192,192]{4,3,2,1,0:T(8,128)} %psi_ref.3, f32[12,192,192]{2,1,0:T(8,128)} %ion_ref.3, f32[12,192,192]{2,1,0:T(8,128)} %hxc_ref.3), custom_call_target="tpu_custom_call" | custom-call | bytes 15728640 | tf_op jit(solution)/shard_map/pallas_call | solution.py:400
  7.4 7.4 %all-to-all-start.1 = ((f32[16,544,128]{2,1,0:T(8,128)}), f32[16,544,128]{2,1,0:T(8,128)}, u32[]{:S(2)}, u32[]{:S(2)}) async-start(f32[16,544,128]{2,1,0:T(8,128)} %bitcast.17), calls=%async_computation.1 | async-start | bytes 8912896 | tf_op jit(solution)/shard_map/all_to_all | solution.py:391
  14.8 22.0 %shard_map.104 = (f32[6912,128]{1,0:T(8,128)}, f32[2,12,192,192]{3,2,1,0:T(8,128)}) custom-call(f32[1,2,12,192,192]{4,3,2,1,0:T(8,128)} %psi_ref.3, f32[12,192,192]{2,1,0:T(8,128)} %ion_ref.3, f32[12,192,192]{2,1,0:T(8,128)} %hxc_ref.3, f32[192,192]{1,0:T(8,128)} %constant.27.clone.kin_ref), custom_call_target="tpu_custom_call" | custom-call | flops 8153726976 | bytes 20971520 | tf_op jit(solution)/shard_map/pallas_call | solution.py:411
  36.8 60.3 %all-to-all-done.1 = f32[16,544,128]{2,1,0:T(8,128)} async-done(((f32[16,544,128]{2,1,0:T(8,128)}), f32[16,544,128]{2,1,0:T(8,128)}, u32[]{:S(2)}, u32[]{:S(2)}) %all-to-all-start.1) | async-done | bytes 4456480 | tf_op jit(solution)/shard_map/all_to_all | solution.py:391
  97.1 20.7 %all-to-all-start = ((f32[16,432,128]{2,1,0:T(8,128)}), f32[16,432,128]{2,1,0:T(8,128)S(1)}, u32[]{:S(2)}, u32[]{:S(2)}) async-start(f32[16,432,128]{2,1,0:T(8,128)} %bitcast.24), calls=%async_computation | async-start | bytes 7077888 | tf_op jit(solution)/shard_map/all_to_all | solution.py:391
  117.8 3.3 shard_map.107.own_ref
  121.0 1.5 collective-permute-start
  122.6 11.9 %shard_map.106.along_ref = f32[3456,256]{1,0:T(8,128)} custom-call(f32[8704,128]{1,0:T(8,128)} %bitcast.4.moved_ref, f32[192,192]{1,0:T(8,128)} %constant.27.clone.kin_ref), custom_call_target="tpu_custom_call" | custom-call | flops 2038431744 | bytes 10485760 | tf_op jit(solution)/shard_map/pallas_call | solution.py:432
  134.4 49.5 %all-to-all-done = f32[16,432,128]{2,1,0:T(8,128)S(1)} async-done(((f32[16,432,128]{2,1,0:T(8,128)}), f32[16,432,128]{2,1,0:T(8,128)S(1)}, u32[]{:S(2)}, u32[]{:S(2)}) %all-to-all-start) | async-done | bytes 3538976 | tf_op jit(solution)/shard_map/all_to_all | solution.py:391
  184.0 0.0 collective-permute-done.other_ref
  184.0 1.8 copy-done
  185.8 8.6 %shard_map.108 = f32[6912,128]{1,0:T(8,128)} custom-call(s32[1]{0:T(128)} %bitcast.band_ref, f32[6912,128]{1,0:T(8,128)} %bitcast.18, f32[3456,256]{1,0:T(8,128)} %shard_map.106.along_ref, f32[1728,128]{1,0:T(8,128)} %shard_map.107.own_ref, f32[1728,128]{1,0:T(8,128)} %collective-permute-done.other_ref, f32[192,192]{1,0:T(8,128)} %constant.27.clone.kin_ref), custom_call_target="tpu_custom_call" | custom-call | flops 1019215872 | bytes 14680064 | tf_op jit(solution)/shard_map/pallas_call | solution.py:443
  194.4 17.0 %all-to-all-start.2 = ((f32[16,432,128]{2,1,0:T(8,128)}), f32[16,432,128]{2,1,0:T(8,128)S(1)}, u32[]{:S(2)}, u32[]{:S(2)}) async-start(f32[16,432,128]{2,1,0:T(8,128)} %bitcast.20), calls=%async_computation.2 | async-start | bytes 7077888 | tf_op jit(solution)/shard_map/all_to_all | solution.py:391
  212.1 65.6 %all-to-all-done.2 = f32[16,432,128]{2,1,0:T(8,128)S(1)} async-done(((f32[16,432,128]{2,1,0:T(8,128)}), f32[16,432,128]{2,1,0:T(8,128)S(1)}, u32[]{:S(2)}, u32[]{:S(2)}) %all-to-all-start.2) | async-done | bytes 3538976 | tf_op jit(solution)/shard_map/all_to_all | solution.py:391
  277.6 1.8 copy-done.1
  279.4 11.5 %shard_map.109 = (f32[1,2,12,192,192]{4,3,2,1,0:T(8,128)}, f32[1728,128]{1,0:T(8,128)}, f32[1728,128]{1,0:T(8,128)}, f32[3584,128]{1,0:T(8,128)}) custom-call(f32[1]{0:T(128)S(6)} %copy.14.occ_ref, f32[6912,128]{1,0:T(8,128)} %bitcast.19, f32[2,12,192,192]{3,2,1,0:T(8,128)} %get-tuple-element.11.base_ref, f32[192,192]{1,0:T(8,128)} %constant.28.clone.basis_ref, ...), custom_call_target="tpu_custom_call" | custom-call | flops 2038431744 | bytes 16777216 | tf_op jit(solution)/shard_map/pallas_call | solution.py:461
  290.9 0.0 copy-start.4
  290.9 17.0 %all-to-all-start.3 = ((f32[32,112,128]{2,1,0:T(8,128)}), f32[32,112,128]{2,1,0:T(8,128)S(1)}, u32[]{:S(2)}, u32[]{:S(2)}) async-start(f32[32,112,128]{2,1,0:T(8,128)} %bitcast.25), calls=%async_computation.3 | async-start | bytes 3670016 | tf_op jit(solution)/shard_map/all_to_all | solution.py:395
  307.9 1.8 collective-permute-start.1
  309.7 0.7 dynamic-slice_bitcast_fusion
  310.4 0.6 copy.13
  311.0 40.9 %all-to-all-done.3 = f32[32,112,128]{2,1,0:T(8,128)S(1)} async-done(((f32[32,112,128]{2,1,0:T(8,128)}), f32[32,112,128]{2,1,0:T(8,128)S(1)}, u32[]{:S(2)}, u32[]{:S(2)}) %all-to-all-start.3) | async-done | bytes 1835040 | tf_op jit(solution)/shard_map/all_to_all | solution.py:395
  352.0 1.2 copy-done.2
  353.2 5.1 %shard_map.110 = f32[3584,128]{1,0:T(8,128)} custom-call(f32[3584,128]{1,0:T(8,128)} %bitcast.21, f32[1,1152]{1,0:T(1,128)} %bitcast.26, f32[192,1]{1,0:T(8,128)} %constant.36.squares_ref, f32[192,192]{1,0:T(8,128)} %constant.28.clone.basis_ref, f32[192,192]{1,0:T(8,128)} %constant.29.clone.turn_ref), custom_call_target="tpu_custom_call" | custom-call | flops 1019215872 | bytes 5242880 | tf_op jit(solution)/shard_map/pallas_call | solution.py:492
  358.3 0.0 collective-permute-done.1.upper_other
  358.3 2.7 all-to-all-start.4
  361.0 1.7 collective-permute-start.2
  362.7 37.8 %collective-permute-done.2.lower_other = f32[1728,128]{1,0:T(8,128)S(1)} collective-permute-done((f32[1728,128]{1,0:T(8,128)}, f32[1728,128]{1,0:T(8,128)S(1)}, u32[]{:S(2)}, u32[]{:S(2)}) %collective-permute-start.2) | collective-permute-done | bytes 884768 | tf_op jit(solution)/shard_map/ppermute | solution.py:482
  400.6 4.6 %all-to-all-done.4 = f32[32,112,128]{2,1,0:T(8,128)S(1)} async-done(((f32[32,112,128]{2,1,0:T(8,128)}), f32[32,112,128]{2,1,0:T(8,128)S(1)}, u32[]{:S(2)}, u32[]{:S(2)}) %all-to-all-start.4) | async-done | bytes 1835040 | tf_op jit(solution)/shard_map/all_to_all | solution.py:395
  405.1 0.0 copy-done.5
  405.1 1.2 copy-done.3
  406.4 7.1 %shard_map.111 = f32[12,192,192]{2,1,0:T(8,128)} custom-call(f32[3584,128]{1,0:T(8,128)} %bitcast.23, f32[1728,128]{1,0:T(8,128)} %get-tuple-element.14.upper_ref, f32[1728,128]{1,0:T(8,128)} %get-tuple-element.16.lower_ref, f32[1728,128]{1,0:T(8,128)} %collective-permute-done.1.upper_other, f32[1728,128]{1,0:T(8,128)} %copy-done.5, ...), custom_call_target="tpu_custom_call" | custom-call | flops 2038431744 | bytes 6291456 | tf_op jit(solution)/shard_map/pallas_call | solution.py:503
  (6 shorter events, 0.0 us)
Async XLA Ops:
  7.4 89.7 %all-to-all-start.1 = ((f32[16,544,128]{2,1,0:T(8,128)}), f32[16,544,128]{2,1,0:T(8,128)}, u32[]{:S(2)}, u32[]{:S(2)}) async-start(f32[16,544,128]{2,1,0:T(8,128)} %bitcast.17), calls=%async_computation.1 | async-start | bytes 8912896 | tf_op jit(solution)/shard_map/all_to_all | solution.py:391
  97.1 86.9 %all-to-all-start = ((f32[16,432,128]{2,1,0:T(8,128)}), f32[16,432,128]{2,1,0:T(8,128)S(1)}, u32[]{:S(2)}, u32[]{:S(2)}) async-start(f32[16,432,128]{2,1,0:T(8,128)} %bitcast.24), calls=%async_computation | async-start | bytes 7077888 | tf_op jit(solution)/shard_map/all_to_all | solution.py:391
  121.0 62.9 %collective-permute-start = (f32[1728,128]{1,0:T(8,128)}, f32[1728,128]{1,0:T(8,128)}, u32[]{:S(2)}, u32[]{:S(2)}) collective-permute-start(f32[1728,128]{1,0:T(8,128)} %shard_map.107.own_ref), channel_id=1, source_target_pairs={{0,16},{16,0},{1,17},{17,1},{2,18},{18,2},{3,19},{19,3},{4,20},{20... | collective-permute-start | bytes 2654216 | tf_op jit(solution)/shard_map/ppermute | solution.py:431
  184.0 1.8 copy-start
  194.4 83.2 %all-to-all-start.2 = ((f32[16,432,128]{2,1,0:T(8,128)}), f32[16,432,128]{2,1,0:T(8,128)S(1)}, u32[]{:S(2)}, u32[]{:S(2)}) async-start(f32[16,432,128]{2,1,0:T(8,128)} %bitcast.20), calls=%async_computation.2 | async-start | bytes 7077888 | tf_op jit(solution)/shard_map/all_to_all | solution.py:391
  277.6 1.8 copy-start.1
  290.9 17.0 %copy-start.4 = (f32[1728,128]{1,0:T(8,128)S(1)}, f32[1728,128]{1,0:T(8,128)}, u32[]{:S(2)}) copy-start(f32[1728,128]{1,0:T(8,128)} %get-tuple-element.14.upper_ref) | copy-start | bytes 2654212
  290.9 61.1 %all-to-all-start.3 = ((f32[32,112,128]{2,1,0:T(8,128)}), f32[32,112,128]{2,1,0:T(8,128)S(1)}, u32[]{:S(2)}, u32[]{:S(2)}) async-start(f32[32,112,128]{2,1,0:T(8,128)} %bitcast.25), calls=%async_computation.3 | async-start | bytes 3670016 | tf_op jit(solution)/shard_map/all_to_all | solution.py:395
  307.9 50.4 %collective-permute-start.1 = (f32[1728,128]{1,0:T(8,128)S(1)}, f32[1728,128]{1,0:T(8,128)}, u32[]{:S(2)}, u32[]{:S(2)}) collective-permute-start(f32[1728,128]{1,0:T(8,128)S(1)} %copy-done.4), channel_id=1, source_target_pairs={{0,16},{16,0},{1,17},{17,1},{2,18},{18,2},{3,19},{19,3},{4,20},{20... | collective-permute-start | bytes 2654216 | tf_op jit(solution)/shard_map/ppermute | solution.py:481
  352.0 1.2 copy-start.2
  358.3 46.8 %all-to-all-start.4 = ((f32[32,112,128]{2,1,0:T(8,128)}), f32[32,112,128]{2,1,0:T(8,128)S(1)}, u32[]{:S(2)}, u32[]{:S(2)}) async-start(f32[32,112,128]{2,1,0:T(8,128)} %bitcast.22), calls=%async_computation.4 | async-start | bytes 3670016 | tf_op jit(solution)/shard_map/all_to_all | solution.py:395
  361.0 39.5 %collective-permute-start.2 = (f32[1728,128]{1,0:T(8,128)}, f32[1728,128]{1,0:T(8,128)S(1)}, u32[]{:S(2)}, u32[]{:S(2)}) collective-permute-start(f32[1728,128]{1,0:T(8,128)} %get-tuple-element.16.lower_ref), channel_id=1, source_target_pairs={{0,16},{16,0},{1,17},{17,1},{2,18},{18,2},{3,19},{19,3},{4,20},{20... | collective-permute-start | bytes 2654216 | tf_op jit(solution)/shard_map/ppermute | solution.py:482
  400.6 4.6 %copy-start.5 = (f32[1728,128]{1,0:T(8,128)}, f32[1728,128]{1,0:T(8,128)S(1)}, u32[]{:S(2)}) copy-start(f32[1728,128]{1,0:T(8,128)S(1)} %collective-permute-done.2.lower_other) | copy-start | bytes 2654212
  405.1 1.2 copy-start.3

commit v3 on v2

--- a/solution.py
+++ b/solution.py
@@ -163,29 +163,32 @@
                 out_ref[pl.ds(to * chunk + used, chunk - used), :] = jnp.zeros((chunk - used, LANES), jnp.float32)
 
 
-def pack_kernel(sizes, bunch, band_ref, psi_ref, ion_ref, hxc_ref, out_ref, packed):
-    planes, grid, rows, share = sizes
+def pack_kernel(sizes, bunch, place_ref, psi_ref, ion_ref, hxc_ref, *refs):
+    planes, grid, rows, share = sizes
+    *out_refs, packed = refs
     stride = 2 * rows + share
-    chunk = chunk_rows(sizes)[0]
-    fill(out_ref, grid, chunk, planes * stride)
-    band = band_ref[0]
+    band, mine = place_ref[0], place_ref[1]
+    for out_ref in out_refs:
+        fill(out_ref, 1, chunk_rows(sizes)[0], planes * stride)
     for inner in range(bunch):
-        plane = pl.program_id(0) * bunch + inner
+        first = (pl.program_id(0) * bunch + inner) * stride
         for part in range(2):
             slot = packed.at[inner * 3 + part]
             pack(psi_ref[0, part, inner], slot)
-            for to in range(grid):
-                start = to * chunk + plane * stride + part * rows
-                out_ref[pl.ds(start, rows), :] = slot[pl.ds(to * rows, rows), :]
+            for turn, out_ref in enumerate(out_refs):
+                start = (mine ^ turn) * rows
+                out_ref[pl.ds(first + part * rows, rows), :] = slot[pl.ds(start, rows), :]
         slot = packed.at[inner * 3 + 2]
         pack(ion_ref[inner] + hxc_ref[inner], slot)
-        for to in range(grid):
-            start = to * chunk + plane * stride + 2 * rows
-            out_ref[pl.ds(start, share), :] = slot[pl.ds(to * rows + band * share, share), :]
-
-
-def plane_kernel(sizes, bunch, psi_ref, ion_ref, hxc_ref, kin_ref, out_ref, base_ref, packed):
-    planes, grid, rows, share = sizes
+        for turn, out_ref in enumerate(out_refs):
+            start = (mine ^ turn) * rows + band * share
+            out_ref[pl.ds(first + 2 * rows, share), :] = slot[pl.ds(start, share), :]
+
+
+def plane_kernel(sizes, bunch, place_ref, psi_ref, ion_ref, hxc_ref, kin_ref, *refs):
+    planes, grid, rows, share = sizes
+    *out_refs, base_ref, packed = refs
+    mine = place_ref[1]
     kin = kin_ref[...]
     for inner in range(bunch):
         plane = pl.program_id(0) * bunch + inner
@@ -197,9 +200,9 @@
             applied.append(bare + potential * field)
             slot = packed.at[inner * 2 + part]
             pack(bare + applied[part], slot)
-            for to in range(grid):
-                start = ((to * planes + plane) * 2 + part) * rows
-                out_ref[pl.ds(start, rows), :] = slot[pl.ds(to * rows, rows), :]
+            for turn, out_ref in enumerate(out_refs):
+                start = (mine ^ turn) * rows
+                out_ref[pl.ds((plane * 2 + part) * rows, rows), :] = slot[pl.ds(start, rows), :]
         for part in range(2):
             twice = kinetic(applied[part], kin) + (potential - 1.0) * applied[part]
             turned = applied[1] if part == 0 else -applied[0]
@@ -210,59 +213,62 @@
             )
 
 
-def share_kernel(sizes, moved_ref, out_ref):
-    planes, grid, rows, share = sizes
+def share_kernel(sizes, place_ref, *refs):
+    planes, grid, rows, share = sizes
+    *moved_refs, out_ref = refs
     length = planes * grid
     stride = 2 * rows + share
-    chunk = chunk_rows(sizes)[0]
-    for row in range(share):
-        for source in range(grid):
-            start = source * chunk + 2 * rows + row
-            out_ref[pl.ds(row * length + source * planes, planes), :] = moved_ref[pl.ds(start, planes, stride=stride), :]
-
-
-def along_kernel(sizes, moved_ref, kin_ref, out_ref, lines):
-    planes, grid, rows, share = sizes
+    for turn, moved_ref in enumerate(moved_refs):
+        first = (place_ref[1] ^ turn) * planes
+        for row in range(share):
+            out_ref[pl.ds(row * length + first, planes), :] = moved_ref[pl.ds(2 * rows + row, planes, stride=stride), :]
+
+
+def along_kernel(sizes, place_ref, *refs):
+    planes, grid, rows, share = sizes
+    *moved_refs, kin_ref, out_ref, lines = refs
     stride = 2 * rows + share
-    chunk = chunk_rows(sizes)[0]
     row = pl.program_id(0)
-    for source in range(grid):
+    for turn, moved_ref in enumerate(moved_refs):
+        first = (place_ref[1] ^ turn) * planes
         for part in range(2):
-            start = source * chunk + part * rows + row
-            lines[pl.ds(source * planes, planes), part * LANES : (part + 1) * LANES] = moved_ref[
-                pl.ds(start, planes, stride=stride), :
-            ]
-    out_ref[...] = product(kin_ref[...], lines[...])
-
-
-def update_kernel(sizes, steps, band_ref, mixed_ref, along_ref, own_ref, other_ref, kin_ref, out_ref):
-    planes, grid, rows, share = sizes
+            lines[part, pl.ds(first, planes), :] = moved_ref[pl.ds(part * rows + row, planes, stride=stride), :]
+    out_ref[...] = product(kin_ref[...], jnp.concatenate([lines[0], lines[1]], axis=1))
+
+
+def update_kernel(sizes, steps, place_ref, along_ref, own_ref, other_ref, kin_ref, *refs):
+    planes, grid, rows, share = sizes
+    mixed_refs, out_refs, lines = refs[:grid], refs[grid : 2 * grid], refs[-1]
     length = planes * grid
     kin = split(kin_ref[...])
     step = pl.program_id(0)
-    mine_here = band_ref[0] == step // (steps // 2)
+    mine_here = place_ref[0] == step // (steps // 2)
     for inner in range(rows // steps):
         row = step * (rows // steps) + inner
         here = slice(inner * length, (inner + 1) * length)
+        slot = lines.at[inner]
+        for turn, mixed_ref in enumerate(mixed_refs):
+            first = (place_ref[1] ^ turn) * planes
+            for part in range(2):
+                slot[part, pl.ds(first, planes), :] = mixed_ref[pl.ds(part * rows + row, planes, stride=2 * rows), :]
         along = along_ref[here, :]
-        mixed = jnp.concatenate(
-            [mixed_ref[pl.ds(part * rows + row, length, stride=2 * rows), :] for part in range(2)], axis=1
-        )
-        again = product_of_parts(kin, split(mixed + along))
+        again = product_of_parts(kin, split(jnp.concatenate([slot[0], slot[1]], axis=1) + along))
         potential = jnp.where(mine_here, own_ref[here, :], other_ref[here, :])
         for part in range(2):
             mine = along[:, part * LANES : (part + 1) * LANES]
             turned = along[:, LANES:] if part == 0 else -along[:, :LANES]
             twice = again[:, part * LANES : (part + 1) * LANES] + potential * mine
-            out_ref[pl.ds(part * rows + row, length, stride=2 * rows), :] = (
-                2.0 * BESSEL_ONE * turned - 4.0 * BESSEL_TWO * twice
-            )
-
-
-def fresh_kernel(
-    sizes, bunch, occ_ref, update_ref, base_ref, basis_ref, turn_ref, fresh_ref, upper_ref, lower_ref, out_ref, packed
-):
-    planes, grid, rows, share = sizes
+            slot[part] = 2.0 * BESSEL_ONE * turned - 4.0 * BESSEL_TWO * twice
+        for turn, out_ref in enumerate(out_refs):
+            first = (place_ref[1] ^ turn) * planes
+            for part in range(2):
+                out_ref[pl.ds(part * rows + row, planes, stride=2 * rows), :] = slot[part, pl.ds(first, planes), :]
+
+
+def fresh_kernel(sizes, bunch, place_ref, occ_ref, base_ref, basis_ref, turn_ref, *refs):
+    planes, grid, rows, share = sizes
+    update_refs = refs[:grid]
+    fresh_ref, upper_ref, lower_ref, out_ref, packed = refs[grid:]
     length = planes * grid
     chunk = chunk_rows(sizes)[1]
     cell_rows = rows * grid
@@ -273,9 +279,9 @@
         part_sum = None
         for part in range(2):
             slot = packed.at[inner * 4 + part]
-            for source in range(grid):
-                start = ((source * planes + plane) * 2 + part) * rows
-                slot[pl.ds(source * rows, rows), :] = update_ref[pl.ds(start, rows), :]
+            for turn, update_ref in enumerate(update_refs):
+                start = (place_ref[1] ^ turn) * rows
+                slot[pl.ds(start, rows), :] = update_ref[pl.ds((plane * 2 + part) * rows, rows), :]
             fresh = base_ref[part, inner] + unpack(slot, length)
             fresh_ref[0, part, inner] = fresh
             part_sum = fresh * fresh if part_sum is None else part_sum + fresh * fresh
@@ -370,7 +376,7 @@
     sizes = (planes, grid, rows, share)
     field = planes * cell_rows
     work = 2 * planes * length**3
-    band = lax.axis_index("band").astype(jnp.int32).reshape(1)
+    place = jnp.stack([lax.axis_index("band"), lax.axis_index("grid")]).astype(jnp.int32)
     kin = jnp.asarray(kinetic_matrix(length))
     basis_np, squares_np = real_basis(length)
     basis, turn = jnp.asarray(basis_np), jnp.asarray(basis_np.T.copy())
@@ -386,82 +392,87 @@
     def scratch(count):
         return [pltpu.VMEM((count * bunch, cell_rows, LANES), jnp.float32)]
 
-    def swap(array):
-        flat = array.reshape(grid, -1, LANES)
-        return lax.all_to_all(flat, "grid", split_axis=0, concat_axis=0).reshape(array.shape)
+    def swap(pieces):
+        swapped = list(pieces)
+        for turn in sorted(range(1, grid), key=lambda k: -k):
+            pairs = [(place, place ^ turn) for place in range(grid)]
+            swapped[turn] = lax.ppermute(pieces[turn], "grid", pairs)
+        return swapped
 
     def swap_all(array):
         flat = array.reshape(2 * grid, -1, LANES)
         return lax.all_to_all(flat, ("band", "grid"), split_axis=0, concat_axis=0).reshape(array.shape)
 
-    moved_rows, spec_rows = (count * grid for count in chunk_rows(sizes))
-    spec_rows = 2 * spec_rows
+    moved_rows, spec_rows = chunk_rows(sizes)
+    spec_rows = 2 * grid * spec_rows
+    mixed_rows = 2 * planes * rows
     steps = 6 if rows % 6 == 0 and share % (rows // 6) == 0 else 2
     moved = pl.pallas_call(
         functools.partial(pack_kernel, sizes, bunch),
         grid=(planes // bunch,),
         in_specs=[smem, psi_spec, plane_spec, plane_spec],
-        out_specs=whole(moved_rows, LANES),
-        out_shape=shape(moved_rows, LANES),
+        out_specs=[whole(moved_rows, LANES)] * grid,
+        out_shape=[shape(moved_rows, LANES)] * grid,
         scratch_shapes=scratch(3),
         compiler_params=PARAMS,
         cost_estimate=cost(0, 15 << 20),
-    )(band, orbitals, ion_potential, hxc_potential)
+    )(place, orbitals, ion_potential, hxc_potential)
     moved = swap(moved)
-    mixed, base = pl.pallas_call(
+    *mixed, base = pl.pallas_call(
         functools.partial(plane_kernel, sizes, bunch),
         grid=(planes // bunch,),
-        in_specs=[psi_spec, plane_spec, plane_spec, square],
-        out_specs=[whole(2 * field, LANES), pair_spec],
-        out_shape=[shape(2 * field, LANES), shape(2, planes, length, length)],
+        in_specs=[smem, psi_spec, plane_spec, plane_spec, square],
+        out_specs=[whole(mixed_rows, LANES)] * grid + [pair_spec],
+        out_shape=[shape(mixed_rows, LANES)] * grid + [shape(2, planes, length, length)],
         scratch_shapes=scratch(2),
         compiler_params=PARAMS,
         cost_estimate=cost(8 * 6 * work, 20 << 20),
-    )(orbitals, ion_potential, hxc_potential, kin)
+    )(place, orbitals, ion_potential, hxc_potential, kin)
     mixed = swap(mixed)
 
     own = pl.pallas_call(
         functools.partial(share_kernel, sizes),
-        in_specs=[vmem],
+        in_specs=[smem] + [vmem] * grid,
         out_specs=vmem,
         out_shape=shape(share * length, LANES),
         compiler_params=PARAMS,
         cost_estimate=cost(0, 6 << 20),
-    )(moved)
+    )(place, *moved)
     other = lax.ppermute(own, "band", [(0, 1), (1, 0)])
     along = pl.pallas_call(
         functools.partial(along_kernel, sizes),
         grid=(rows,),
-        in_specs=[whole(moved_rows, LANES), square],
+        in_specs=[smem] + [whole(moved_rows, LANES)] * grid + [square],
         out_specs=pl.BlockSpec((length, 2 * LANES), lambda i: (i, 0)),
         out_shape=shape(rows * length, 2 * LANES),
-        scratch_shapes=[pltpu.VMEM((length, 2 * LANES), jnp.float32)],
+        scratch_shapes=[pltpu.VMEM((2, length, LANES), jnp.float32)],
         compiler_params=PARAMS,
         cost_estimate=cost(2 * 6 * work, 10 << 20),
-    )(moved, kin)
+    )(place, *moved, kin)
     half_spec = pl.BlockSpec((rows // steps * length, LANES), lambda i: (i % (steps // 2), 0))
     update = pl.pallas_call(
         functools.partial(update_kernel, sizes, steps),
         grid=(steps,),
         in_specs=[
             smem,
-            whole(2 * field, LANES),
             pl.BlockSpec((rows // steps * length, 2 * LANES), lambda i: (i, 0)),
             half_spec,
             half_spec,
             square,
-        ],
-        out_specs=whole(2 * field, LANES),
-        out_shape=shape(2 * field, LANES),
+        ]
+        + [whole(mixed_rows, LANES)] * grid,
+        out_specs=[whole(mixed_rows, LANES)] * grid,
+        out_shape=[shape(mixed_rows, LANES)] * grid,
+        scratch_shapes=[pltpu.VMEM((rows // steps, 2, length, LANES), jnp.float32)],
         compiler_params=PARAMS,
         cost_estimate=cost(2 * 3 * work, 14 << 20),
-    )(band, mixed, along, own, other, kin)
+    )(place, along, own, other, kin, *mixed)
     update = swap(update)
 
     fresh, upper, lower, spectrum = pl.pallas_call(
         functools.partial(fresh_kernel, sizes, bunch),
         grid=(planes // bunch,),
-        in_specs=[smem, whole(2 * field, LANES), pair_spec, square, square],
+        in_specs=[smem, smem, pair_spec, square, square] + [whole(mixed_rows, LANES)] * grid,
         out_specs=[
             psi_spec,
             half_rows,
@@ -477,7 +488,7 @@
         scratch_shapes=scratch(4),
         compiler_params=PARAMS,
         cost_estimate=cost(2 * 6 * work, 16 << 20),
-    )(occupations, update, base, basis, turn)
+    )(place, occupations, base, basis, turn, *update)
     upper_other = lax.ppermute(upper, "band", [(0, 1), (1, 0)])
     lower_other = lax.ppermute(lower, "band", [(0, 1), (1, 0)])
 
@@ -524,7 +535,8 @@
 def local(orbitals, occupations, ion_potential, hxc_potential):
     length = orbitals.shape[-1]
     parts = 2 * lax.axis_size("grid") * LANES
-    fits = length == LANES + LANES // 2 and lax.axis_size("band") == 2 and length * length % parts == 0
+    fits = lax.axis_size("grid") & (lax.axis_size("grid") - 1) == 0
+    fits = fits and length == LANES + LANES // 2 and lax.axis_size("band") == 2 and length * length % parts == 0
     path = packed_path if fits else general
     return path(orbitals, occupations, ion_potential, hxc_potential)
 

time: 414 us -> 445 us (1.075)
  starting transfers between devices: 69.9 us -> 151 us
  waiting for transfers between devices: 259 us -> 199 us
  Pallas kernels: 76.2 us -> 85 us
    all_to_all x3 -> x0, waiting for transfers between devices: 175 us -> none  [swap(): lax.all_to_all(flat, 'grid', split_axis=0, concat_axis=0)]
    ppermute x0 -> x45, starting transfers between devices: none -> 122 us  [swap(): swapped[turn] = lax.ppermute(pieces[turn], 'grid', pairs)]
    ppermute x0 -> x45, waiting for transfers between devices: none -> 116 us  [swap(): swapped[turn] = lax.ppermute(pieces[turn], 'grid', pairs)]
    all_to_all x3 -> x0, starting transfers between devices: 45.1 us -> none  [swap(): lax.all_to_all(flat, 'grid', split_axis=0, concat_axis=0)]
    pallas_call x1, Pallas kernels: 11.5 us -> 17.1 us  [packed_path(): pl.pallas_call(functools.partial(fresh_kernel, sizes, bunch), grid=(plane...]
    all_to_all x2, starting transfers between devices: 19.7 us -> 24.3 us  [swap_all(): lax.all_to_all(flat, ('band', 'grid'), split_axis=0, concat_axis=0)]
  transfers between devices with their start and end apart: 8 -> 50, of which waited for: 6 -> 17; matrix products, arithmetic and copies ran while one was open for 0% -> 0% of each run, Pallas kernels for 10% -> 10%
where the time goes in v3:
time: 445 us
  waiting for transfers between devices  199 us (45%)
  starting transfers between devices  151 us (34%)
  Pallas kernels  85 us (19%)
  local copies, waits for them, and re-layouts  6.41 us (1%)
    ppermute x45, starting transfers between devices, swap(): swapped[turn] = lax.ppermute(pieces[turn], 'grid', pairs)  122 us
    ppermute x45, waiting for transfers between devices, swap(): swapped[turn] = lax.ppermute(pieces[turn], 'grid', pairs)  116 us
    all_to_all x2, waiting for transfers between devices, swap_all(): lax.all_to_all(flat, ('band', 'grid'), split_axis=0, concat_axis=0)  45.4 us
    ppermute x1, waiting for transfers between devices, packed_path(): lower_other = lax.ppermute(lower, 'band', [(0, 1), (1, 0)])  37.9 us
    all_to_all x2, starting transfers between devices, swap_all(): lax.all_to_all(flat, ('band', 'grid'), split_axis=0, concat_axis=0)  24.3 us
    pallas_call x1, Pallas kernels, packed_path(): pl.pallas_call(functools.partial(plane_kernel, sizes, bunch), grid=(plane...  22.3 us
    pallas_call x1, Pallas kernels, packed_path(): pl.pallas_call(functools.partial(fresh_kernel, sizes, bunch), grid=(plane...  17.1 us
    pallas_call x1, Pallas kernels, packed_path(): pl.pallas_call(functools.partial(along_kernel, sizes), grid=(rows,), in_s...  12 us
  transfers between devices with their start and end apart: 50, of which 17 were waited for; matrix products, arithmetic and copies ran while one was open for 0% of the time, Pallas kernels for 10%

profile of v3, /device:TPU:0, one launch (start us, length us, event | category | flops | bytes accessed | tf_op | source)
XLA Modules:
  0.0 444.6 jit_solution(13370481432854744926)
XLA Ops:
  1.3 6.9 %shard_map.105 = (f32[544,128]{1,0:T(8,128)}, f32[544,128]{1,0:T(8,128)}, f32[544,128]{1,0:T(8,128)}, f32[544,128]{1,0:T(8,128)}, f32[544,128]{1,0:T(8,128)}, /*...) custom-call(s32[2]{0:T(128)} %pad_add_fusion.place_ref, ...), custom_call_target="tpu_custom_call" | custom-call | bytes 15728640 | tf_op jit(solution)/shard_map/pallas_call | solution.py:410
  22.9 28.9 %collective-permute-done.10.refs_11_ = f32[544,128]{1,0:T(8,128)S(1)} collective-permute-done((f32[544,128]{1,0:T(8,128)}, f32[544,128]{1,0:T(8,128)S(1)}, u32[]{:S(2)}, u32[]{:S(2)}) %collective-permute-start.10) | collective-permute-done | bytes 278560 | tf_op jit(solution)/shard_map/ppermute | solution.py:399
  52.3 5.7 %collective-permute-start.3 = (f32[544,128]{1,0:T(8,128)}, f32[544,128]{1,0:T(8,128)S(1)}, u32[]{:S(2)}, u32[]{:S(2)}) collective-permute-start(f32[544,128]{1,0:T(8,128)} %get-tuple-element.62), channel_id=1, source_target_pairs={{0,4},{1,5},{2,6},{3,7},{4,0},{5,1},{6,2},{7,3},{8,12},{9,13},{10,... | collective-permute-start | bytes 835592 | tf_op jit(solution)/shard_map/ppermute | solution.py:399
  57.9 5.6 %collective-permute-start.4 = (f32[544,128]{1,0:T(8,128)}, f32[544,128]{1,0:T(8,128)S(1)}, u32[]{:S(2)}, u32[]{:S(2)}) collective-permute-start(f32[544,128]{1,0:T(8,128)} %get-tuple-element.63), channel_id=1, source_target_pairs={{0,5},{1,4},{2,7},{3,6},{4,1},{5,0},{6,3},{7,2},{8,13},{9,12},{10,... | collective-permute-start | bytes 835592 | tf_op jit(solution)/shard_map/ppermute | solution.py:399
  63.6 7.2 %collective-permute-start.5 = (f32[544,128]{1,0:T(8,128)}, f32[544,128]{1,0:T(8,128)S(1)}, u32[]{:S(2)}, u32[]{:S(2)}) collective-permute-start(f32[544,128]{1,0:T(8,128)} %get-tuple-element.64), channel_id=1, source_target_pairs={{0,6},{1,7},{2,4},{3,5},{4,2},{5,3},{6,0},{7,1},{8,14},{9,15},{10,... | collective-permute-start | bytes 835592 | tf_op jit(solution)/shard_map/ppermute | solution.py:399
  70.8 6.8 %collective-permute-start.6 = (f32[544,128]{1,0:T(8,128)}, f32[544,128]{1,0:T(8,128)S(1)}, u32[]{:S(2)}, u32[]{:S(2)}) collective-permute-start(f32[544,128]{1,0:T(8,128)} %get-tuple-element.65), channel_id=1, source_target_pairs={{0,7},{1,6},{2,5},{3,4},{4,3},{5,2},{6,1},{7,0},{8,15},{9,14},{10,... | collective-permute-start | bytes 835592 | tf_op jit(solution)/shard_map/ppermute | solution.py:399
  82.9 22.3 %shard_map.104 = (f32[432,128]{1,0:T(8,128)}, f32[432,128]{1,0:T(8,128)}, f32[432,128]{1,0:T(8,128)}, f32[432,128]{1,0:T(8,128)}, f32[432,128]{1,0:T(8,128)}, /*...) custom-call(s32[2]{0:T(128)} %pad_add_fusion.place_ref, ...), custom_call_target="tpu_custom_call" | custom-call | flops 8153726976 | bytes 20971520 | tf_op jit(solution)/shard_map/pallas_call | solution.py:421
  107.5 3.4 collective-permute-done.8.refs_9_
  110.9 8.2 %collective-permute-done.9.refs_10_ = f32[544,128]{1,0:T(8,128)S(1)} collective-permute-done((f32[544,128]{1,0:T(8,128)}, f32[544,128]{1,0:T(8,128)S(1)}, u32[]{:S(2)}, u32[]{:S(2)}) %collective-permute-start.9) | collective-permute-done | bytes 278560 | tf_op jit(solution)/shard_map/ppermute | solution.py:399
  119.9 3.4 shard_map.107.own_ref
  129.4 3.8 collective-permute-done.19.refs_4_
  135.5 4.4 collective-permute-start.24
  139.9 9.8 %collective-permute-done.21.refs_6_ = f32[432,128]{1,0:T(8,128)S(1)} collective-permute-done((f32[432,128]{1,0:T(8,128)S(1)}, f32[432,128]{1,0:T(8,128)S(1)}, u32[]{:S(2)}, u32[]{:S(2)}) %collective-permute-start.21) | collective-permute-done | bytes 221216 | tf_op jit(solution)/shard_map/ppermute | solution.py:399
  155.3 20.2 %collective-permute-start.28 = (f32[432,128]{1,0:T(8,128)S(1)}, f32[432,128]{1,0:T(8,128)S(1)}, u32[]{:S(2)}, u32[]{:S(2)}) collective-permute-start(f32[432,128]{1,0:T(8,128)S(1)} %copy-done.52), channel_id=1, source_target_pairs={{0,13},{1,12},{2,15},{3,14},{4,9},{5,8},{6,11},{7,10},{8,5},{9,4},... | collective-permute-start | bytes 663560 | tf_op jit(solution)/shard_map/ppermute | solution.py:399
  175.5 11.8 %collective-permute-done.25.refs_10_ = f32[432,128]{1,0:T(8,128)S(1)} collective-permute-done((f32[432,128]{1,0:T(8,128)S(1)}, f32[432,128]{1,0:T(8,128)S(1)}, u32[]{:S(2)}, u32[]{:S(2)}) %collective-permute-start.25) | collective-permute-done | bytes 221216 | tf_op jit(solution)/shard_map/ppermute | solution.py:399
  188.3 4.7 %collective-permute-start.30 = (f32[432,128]{1,0:T(8,128)S(1)}, f32[432,128]{1,0:T(8,128)S(1)}, u32[]{:S(2)}, u32[]{:S(2)}) collective-permute-start(f32[432,128]{1,0:T(8,128)S(1)} %copy-done.50), channel_id=1, source_target_pairs={{0,15},{1,14},{2,13},{3,12},{4,11},{5,10},{6,9},{7,8},{8,7},{9,6},... | collective-permute-start | bytes 663560 | tf_op jit(solution)/shard_map/ppermute | solution.py:399
  193.0 12.0 %shard_map.106.along_ref = f32[3456,256]{1,0:T(8,128)} custom-call(s32[2]{0:T(128)} %pad_add_fusion.place_ref, f32[544,128]{1,0:T(8,128)} %get-tuple-element.58.refs_0_, f32[544,128]{1,0:T(8,128)} %copy-done.2, f32[544,128]{1,0:T(8,128)} %copy-done.3, f32[544,128]{1,0:T(8,128)} %copy-done.9, f32[544,128]{1,0:T(8,128)} %copy-done.10, f32[544,128]{1,0:T(8,128)} %copy-done.11, ...), custom_call_target="tpu_custom_call" | custom-call | flops 2038431744 | bytes 10485760 | tf_op jit(solution)/shard_map/pallas_call | solution.py:442
  206.4 11.1 %shard_map.108 = (f32[432,128]{1,0:T(8,128)}, f32[432,128]{1,0:T(8,128)}, f32[432,128]{1,0:T(8,128)}, f32[432,128]{1,0:T(8,128)}, f32[432,128]{1,0:T(8,128)}, /*...) custom-call(s32[2]{0:T(128)} %pad_add_fusion.place_ref, ...), custom_call_target="tpu_custom_call" | custom-call | flops 1019215872 | bytes 14680064 | tf_op jit(solution)/shard_map/pallas_call | solution.py:453
  219.4 11.2 %collective-permute-start.34 = (f32[432,128]{1,0:T(8,128)}, f32[432,128]{1,0:T(8,128)S(1)}, u32[]{:S(2)}, u32[]{:S(2)}) collective-permute-start(f32[432,128]{1,0:T(8,128)} %get-tuple-element.94), channel_id=1, source_target_pairs={{0,4},{1,5},{2,6},{3,7},{4,0},{5,1},{6,2},{7,3},{8,12},{9,13},{10,... | collective-permute-start | bytes 663560 | tf_op jit(solution)/shard_map/ppermute | solution.py:399
  236.5 4.0 collective-permute-start.38
  243.2 14.1 %collective-permute-done.36.refs_6_ = f32[432,128]{1,0:T(8,128)S(1)} collective-permute-done((f32[432,128]{1,0:T(8,128)}, f32[432,128]{1,0:T(8,128)S(1)}, u32[]{:S(2)}, u32[]{:S(2)}) %collective-permute-start.36) | collective-permute-done | bytes 221216 | tf_op jit(solution)/shard_map/ppermute | solution.py:399
  257.3 4.8 %collective-permute-done.37.refs_7_ = f32[432,128]{1,0:T(8,128)S(1)} collective-permute-done((f32[432,128]{1,0:T(8,128)}, f32[432,128]{1,0:T(8,128)S(1)}, u32[]{:S(2)}, u32[]{:S(2)}) %collective-permute-start.37) | collective-permute-done | bytes 221216 | tf_op jit(solution)/shard_map/ppermute | solution.py:399
  266.2 23.1 %collective-permute-done.40.refs_10_ = f32[432,128]{1,0:T(8,128)S(1)} collective-permute-done((f32[432,128]{1,0:T(8,128)}, f32[432,128]{1,0:T(8,128)S(1)}, u32[]{:S(2)}, u32[]{:S(2)}) %collective-permute-start.40) | collective-permute-done | bytes 221216 | tf_op jit(solution)/shard_map/ppermute | solution.py:399
  289.3 3.4 collective-permute-start.45
  294.2 5.5 %collective-permute-done.45.refs_15_ = f32[432,128]{1,0:T(8,128)S(1)} collective-permute-done((f32[432,128]{1,0:T(8,128)}, f32[432,128]{1,0:T(8,128)S(1)}, u32[]{:S(2)}, u32[]{:S(2)}) %collective-permute-start.45) | collective-permute-done | bytes 221216 | tf_op jit(solution)/shard_map/ppermute | solution.py:399
  300.4 17.1 %shard_map.109 = (f32[1,2,12,192,192]{4,3,2,1,0:T(8,128)}, f32[1728,128]{1,0:T(8,128)}, f32[1728,128]{1,0:T(8,128)}, f32[3584,128]{1,0:T(8,128)}) custom-call(s32[2]{0:T(128)} %pad_add_fusion.place_ref, f32[1]{0:T(128)S(6)} %copy.14.occ_ref, f32[2,12,192,192]{3,2,1,0:T(8,128)} %get-tuple-element.57.base_ref, f32[192,192]{1,0:T(8,128)} %constant.28.clone.basis_ref, ...), custom_call_target="tpu_custom_call" | custom-call | flops 2038431744 | bytes 16777216 | tf_op jit(solution)/shard_map/pallas_call | solution.py:472
  317.5 21.4 %all-to-all-start = ((f32[32,112,128]{2,1,0:T(8,128)}), f32[32,112,128]{2,1,0:T(8,128)S(1)}, u32[]{:S(2)}, u32[]{:S(2)}) async-start(f32[32,112,128]{2,1,0:T(8,128)} %bitcast.15), calls=%async_computation | async-start | bytes 3670016 | tf_op jit(solution)/shard_map/all_to_all | solution.py:404
  342.1 40.9 %all-to-all-done = f32[32,112,128]{2,1,0:T(8,128)S(1)} async-done(((f32[32,112,128]{2,1,0:T(8,128)}), f32[32,112,128]{2,1,0:T(8,128)S(1)}, u32[]{:S(2)}, u32[]{:S(2)}) %all-to-all-start) | async-done | bytes 1835040 | tf_op jit(solution)/shard_map/all_to_all | solution.py:404
  384.2 5.1 %shard_map.110 = f32[3584,128]{1,0:T(8,128)} custom-call(f32[3584,128]{1,0:T(8,128)} %bitcast.12, f32[1,1152]{1,0:T(1,128)} %bitcast.16, f32[192,1]{1,0:T(8,128)} %constant.36.squares_ref, f32[192,192]{1,0:T(8,128)} %constant.28.clone.basis_ref, f32[192,192]{1,0:T(8,128)} %constant.29.clone.turn_ref), custom_call_target="tpu_custom_call" | custom-call | flops 1019215872 | bytes 5242880 | tf_op jit(solution)/shard_map/pallas_call | solution.py:503
  393.9 37.9 %collective-permute-done.47.lower_other = f32[1728,128]{1,0:T(8,128)} collective-permute-done((f32[1728,128]{1,0:T(8,128)S(1)}, f32[1728,128]{1,0:T(8,128)}, u32[]{:S(2)}, u32[]{:S(2)}) %collective-permute-start.47) | collective-permute-done | bytes 884768 | tf_op jit(solution)/shard_map/ppermute | solution.py:493
  431.8 4.4 %all-to-all-done.1 = f32[32,112,128]{2,1,0:T(8,128)S(1)} async-done(((f32[32,112,128]{2,1,0:T(8,128)}), f32[32,112,128]{2,1,0:T(8,128)S(1)}, u32[]{:S(2)}, u32[]{:S(2)}) %all-to-all-start.1) | async-done | bytes 1835040 | tf_op jit(solution)/shard_map/all_to_all | solution.py:404
  437.5 7.1 %shard_map.111 = f32[12,192,192]{2,1,0:T(8,128)} custom-call(f32[3584,128]{1,0:T(8,128)} %bitcast.14, f32[1728,128]{1,0:T(8,128)} %get-tuple-element.108.upper_ref, f32[1728,128]{1,0:T(8,128)} %get-tuple-element.110.lower_ref, f32[1728,128]{1,0:T(8,128)} %collective-permute-done.46.upper_other, f32[1728,128]{1,0:T(8,128)} %collective-permute-done.47.lower_other, ...), custom_call_target="tpu_custom_call" | custom-call | flops 2038431744 | bytes 6291456 | tf_op jit(solution)/shard_map/pallas_call | solution.py:514
  (203 shorter events, 66.4 us)
Async XLA Ops:
  11.3 40.6 %collective-permute-start.10 = (f32[544,128]{1,0:T(8,128)}, f32[544,128]{1,0:T(8,128)S(1)}, u32[]{:S(2)}, u32[]{:S(2)}) collective-permute-start(f32[544,128]{1,0:T(8,128)} %get-tuple-element.69), channel_id=1, source_target_pairs={{0,11},{1,10},{2,9},{3,8},{4,15},{5,14},{6,13},{7,12},{8,3},{9,2},... | collective-permute-start | bytes 835592 | tf_op jit(solution)/shard_map/ppermute | solution.py:399
  13.6 38.6 %collective-permute-start.11 = (f32[544,128]{1,0:T(8,128)}, f32[544,128]{1,0:T(8,128)S(1)}, u32[]{:S(2)}, u32[]{:S(2)}) collective-permute-start(f32[544,128]{1,0:T(8,128)} %get-tuple-element.70), channel_id=1, source_target_pairs={{0,12},{1,13},{2,14},{3,15},{4,8},{5,9},{6,10},{7,11},{8,4},{9,5},... | collective-permute-start | bytes 835592 | tf_op jit(solution)/shard_map/ppermute | solution.py:399
  14.9 43.0 %collective-permute-start.12 = (f32[544,128]{1,0:T(8,128)}, f32[544,128]{1,0:T(8,128)S(1)}, u32[]{:S(2)}, u32[]{:S(2)}) collective-permute-start(f32[544,128]{1,0:T(8,128)} %get-tuple-element.71), channel_id=1, source_target_pairs={{0,13},{1,12},{2,15},{3,14},{4,9},{5,8},{6,11},{7,10},{8,5},{9,4},... | collective-permute-start | bytes 835592 | tf_op jit(solution)/shard_map/ppermute | solution.py:399
  17.1 46.5 %collective-permute-start.13 = (f32[544,128]{1,0:T(8,128)}, f32[544,128]{1,0:T(8,128)S(1)}, u32[]{:S(2)}, u32[]{:S(2)}) collective-permute-start(f32[544,128]{1,0:T(8,128)} %get-tuple-element.72), channel_id=1, source_target_pairs={{0,14},{1,15},{2,12},{3,13},{4,10},{5,11},{6,8},{7,9},{8,6},{9,7},... | collective-permute-start | bytes 835592 | tf_op jit(solution)/shard_map/ppermute | solution.py:399
  19.8 51.0 %collective-permute-start.14 = (f32[544,128]{1,0:T(8,128)}, f32[544,128]{1,0:T(8,128)S(1)}, u32[]{:S(2)}, u32[]{:S(2)}) collective-permute-start(f32[544,128]{1,0:T(8,128)} %get-tuple-element.73), channel_id=1, source_target_pairs={{0,15},{1,14},{2,13},{3,12},{4,11},{5,10},{6,9},{7,8},{8,7},{9,6},... | collective-permute-start | bytes 835592 | tf_op jit(solution)/shard_map/ppermute | solution.py:399
  51.8 25.8 %collective-permute-start.2 = (f32[544,128]{1,0:T(8,128)}, f32[544,128]{1,0:T(8,128)S(1)}, u32[]{:S(2)}, u32[]{:S(2)}) collective-permute-start(f32[544,128]{1,0:T(8,128)} %get-tuple-element.61), channel_id=1, source_target_pairs={{0,3},{1,2},{2,1},{3,0},{4,7},{5,6},{6,5},{7,4},{8,11},{9,10},{10,... | collective-permute-start | bytes 835592 | tf_op jit(solution)/shard_map/ppermute | solution.py:399
  52.3 28.5 %collective-permute-start.3 = (f32[544,128]{1,0:T(8,128)}, f32[544,128]{1,0:T(8,128)S(1)}, u32[]{:S(2)}, u32[]{:S(2)}) collective-permute-start(f32[544,128]{1,0:T(8,128)} %get-tuple-element.62), channel_id=1, source_target_pairs={{0,4},{1,5},{2,6},{3,7},{4,0},{5,1},{6,2},{7,3},{8,12},{9,13},{10,... | collective-permute-start | bytes 835592 | tf_op jit(solution)/shard_map/ppermute | solution.py:399
  63.6 41.6 %collective-permute-start.5 = (f32[544,128]{1,0:T(8,128)}, f32[544,128]{1,0:T(8,128)S(1)}, u32[]{:S(2)}, u32[]{:S(2)}) collective-permute-start(f32[544,128]{1,0:T(8,128)} %get-tuple-element.64), channel_id=1, source_target_pairs={{0,6},{1,7},{2,4},{3,5},{4,2},{5,3},{6,0},{7,1},{8,14},{9,15},{10,... | collective-permute-start | bytes 835592 | tf_op jit(solution)/shard_map/ppermute | solution.py:399
  70.8 35.2 %collective-permute-start.6 = (f32[544,128]{1,0:T(8,128)}, f32[544,128]{1,0:T(8,128)S(1)}, u32[]{:S(2)}, u32[]{:S(2)}) collective-permute-start(f32[544,128]{1,0:T(8,128)} %get-tuple-element.65), channel_id=1, source_target_pairs={{0,7},{1,6},{2,5},{3,4},{4,3},{5,2},{6,1},{7,0},{8,15},{9,14},{10,... | collective-permute-start | bytes 835592 | tf_op jit(solution)/shard_map/ppermute | solution.py:399
  77.6 29.9 %collective-permute-start.7 = (f32[544,128]{1,0:T(8,128)}, f32[544,128]{1,0:T(8,128)S(1)}, u32[]{:S(2)}, u32[]{:S(2)}) collective-permute-start(f32[544,128]{1,0:T(8,128)} %get-tuple-element.66), channel_id=1, source_target_pairs={{0,8},{1,9},{2,10},{3,11},{4,12},{5,13},{6,14},{7,15},{8,0},{9,1},... | collective-permute-start | bytes 835592 | tf_op jit(solution)/shard_map/ppermute | solution.py:399
  80.8 30.1 %collective-permute-start.8 = (f32[544,128]{1,0:T(8,128)}, f32[544,128]{1,0:T(8,128)S(1)}, u32[]{:S(2)}, u32[]{:S(2)}) collective-permute-start(f32[544,128]{1,0:T(8,128)} %get-tuple-element.67), channel_id=1, source_target_pairs={{0,9},{1,8},{2,11},{3,10},{4,13},{5,12},{6,15},{7,14},{8,1},{9,0},... | collective-permute-start | bytes 835592 | tf_op jit(solution)/shard_map/ppermute | solution.py:399
  80.8 38.3 %collective-permute-start.9 = (f32[544,128]{1,0:T(8,128)}, f32[544,128]{1,0:T(8,128)S(1)}, u32[]{:S(2)}, u32[]{:S(2)}) collective-permute-start(f32[544,128]{1,0:T(8,128)} %get-tuple-element.68), channel_id=1, source_target_pairs={{0,10},{1,11},{2,8},{3,9},{4,14},{5,15},{6,12},{7,13},{8,2},{9,3},... | collective-permute-start | bytes 835592 | tf_op jit(solution)/shard_map/ppermute | solution.py:399
  123.3 81.9 %collective-permute-start.15 = (f32[1728,128]{1,0:T(8,128)}, f32[1728,128]{1,0:T(8,128)S(1)}, u32[]{:S(2)}, u32[]{:S(2)}) collective-permute-start(f32[1728,128]{1,0:T(8,128)} %shard_map.107.own_ref), channel_id=1, source_target_pairs={{0,16},{16,0},{1,17},{17,1},{2,18},{18,2},{3,19},{19,3},{4,20},{20... | collective-permute-start | bytes 2654216 | tf_op jit(solution)/shard_map/ppermute | solution.py:441
  125.2 24.5 %collective-permute-start.21 = (f32[432,128]{1,0:T(8,128)S(1)}, f32[432,128]{1,0:T(8,128)S(1)}, u32[]{:S(2)}, u32[]{:S(2)}) collective-permute-start(f32[432,128]{1,0:T(8,128)S(1)} %copy-done.59), channel_id=1, source_target_pairs={{0,6},{1,7},{2,4},{3,5},{4,2},{5,3},{6,0},{7,1},{8,14},{9,15},{10,... | collective-permute-start | bytes 663560 | tf_op jit(solution)/shard_map/ppermute | solution.py:399
  126.8 24.7 %collective-permute-start.22 = (f32[432,128]{1,0:T(8,128)S(1)}, f32[432,128]{1,0:T(8,128)S(1)}, u32[]{:S(2)}, u32[]{:S(2)}) collective-permute-start(f32[432,128]{1,0:T(8,128)S(1)} %copy-done.58), channel_id=1, source_target_pairs={{0,7},{1,6},{2,5},{3,4},{4,3},{5,2},{6,1},{7,0},{8,15},{9,14},{10,... | collective-permute-start | bytes 663560 | tf_op jit(solution)/shard_map/ppermute | solution.py:399
  149.7 37.6 %collective-permute-start.25 = (f32[432,128]{1,0:T(8,128)S(1)}, f32[432,128]{1,0:T(8,128)S(1)}, u32[]{:S(2)}, u32[]{:S(2)}) collective-permute-start(f32[432,128]{1,0:T(8,128)S(1)} %copy-done.55), channel_id=1, source_target_pairs={{0,10},{1,11},{2,8},{3,9},{4,14},{5,15},{6,12},{7,13},{8,2},{9,3},... | collective-permute-start | bytes 663560 | tf_op jit(solution)/shard_map/ppermute | solution.py:399
  151.5 36.8 %collective-permute-start.26 = (f32[432,128]{1,0:T(8,128)S(1)}, f32[432,128]{1,0:T(8,128)S(1)}, u32[]{:S(2)}, u32[]{:S(2)}) collective-permute-start(f32[432,128]{1,0:T(8,128)S(1)} %copy-done.54), channel_id=1, source_target_pairs={{0,11},{1,10},{2,9},{3,8},{4,15},{5,14},{6,13},{7,12},{8,3},{9,2},... | collective-permute-start | bytes 663560 | tf_op jit(solution)/shard_map/ppermute | solution.py:399
  153.0 52.1 %collective-permute-start.27 = (f32[432,128]{1,0:T(8,128)S(1)}, f32[432,128]{1,0:T(8,128)S(1)}, u32[]{:S(2)}, u32[]{:S(2)}) collective-permute-start(f32[432,128]{1,0:T(8,128)S(1)} %copy-done.53), channel_id=1, source_target_pairs={{0,12},{1,13},{2,14},{3,15},{4,8},{5,9},{6,10},{7,11},{8,4},{9,5},... | collective-permute-start | bytes 663560 | tf_op jit(solution)/shard_map/ppermute | solution.py:399
  155.3 49.8 %collective-permute-start.28 = (f32[432,128]{1,0:T(8,128)S(1)}, f32[432,128]{1,0:T(8,128)S(1)}, u32[]{:S(2)}, u32[]{:S(2)}) collective-permute-start(f32[432,128]{1,0:T(8,128)S(1)} %copy-done.52), channel_id=1, source_target_pairs={{0,13},{1,12},{2,15},{3,14},{4,9},{5,8},{6,11},{7,10},{8,5},{9,4},... | collective-permute-start | bytes 663560 | tf_op jit(solution)/shard_map/ppermute | solution.py:399
  230.6 26.7 %collective-permute-start.36 = (f32[432,128]{1,0:T(8,128)}, f32[432,128]{1,0:T(8,128)S(1)}, u32[]{:S(2)}, u32[]{:S(2)}) collective-permute-start(f32[432,128]{1,0:T(8,128)} %get-tuple-element.96), channel_id=1, source_target_pairs={{0,6},{1,7},{2,4},{3,5},{4,2},{5,3},{6,0},{7,1},{8,14},{9,15},{10,... | collective-permute-start | bytes 663560 | tf_op jit(solution)/shard_map/ppermute | solution.py:399
  233.5 28.6 %collective-permute-start.37 = (f32[432,128]{1,0:T(8,128)}, f32[432,128]{1,0:T(8,128)S(1)}, u32[]{:S(2)}, u32[]{:S(2)}) collective-permute-start(f32[432,128]{1,0:T(8,128)} %get-tuple-element.97), channel_id=1, source_target_pairs={{0,7},{1,6},{2,5},{3,4},{4,3},{5,2},{6,1},{7,0},{8,15},{9,14},{10,... | collective-permute-start | bytes 663560 | tf_op jit(solution)/shard_map/ppermute | solution.py:399
  236.5 25.6 %collective-permute-start.38 = (f32[432,128]{1,0:T(8,128)}, f32[432,128]{1,0:T(8,128)S(1)}, u32[]{:S(2)}, u32[]{:S(2)}) collective-permute-start(f32[432,128]{1,0:T(8,128)} %get-tuple-element.98), channel_id=1, source_target_pairs={{0,8},{1,9},{2,10},{3,11},{4,12},{5,13},{6,14},{7,15},{8,0},{9,1},... | collective-permute-start | bytes 663560 | tf_op jit(solution)/shard_map/ppermute | solution.py:399
  240.5 24.9 %collective-permute-start.39 = (f32[432,128]{1,0:T(8,128)}, f32[432,128]{1,0:T(8,128)S(1)}, u32[]{:S(2)}, u32[]{:S(2)}) collective-permute-start(f32[432,128]{1,0:T(8,128)} %get-tuple-element.99), channel_id=1, source_target_pairs={{0,9},{1,8},{2,11},{3,10},{4,13},{5,12},{6,15},{7,14},{8,1},{9,0},... | collective-permute-start | bytes 663560 | tf_op jit(solution)/shard_map/ppermute | solution.py:399
  241.4 47.8 %collective-permute-start.40 = (f32[432,128]{1,0:T(8,128)}, f32[432,128]{1,0:T(8,128)S(1)}, u32[]{:S(2)}, u32[]{:S(2)}) collective-permute-start(f32[432,128]{1,0:T(8,128)} %get-tuple-element.100), channel_id=1, source_target_pairs={{0,10},{1,11},{2,8},{3,9},{4,14},{5,15},{6,12},{7,13},{8,2},{9,3},... | collective-permute-start | bytes 663560 | tf_op jit(solution)/shard_map/ppermute | solution.py:399
  257.3 36.8 %collective-permute-start.41 = (f32[432,128]{1,0:T(8,128)}, f32[432,128]{1,0:T(8,128)S(1)}, u32[]{:S(2)}, u32[]{:S(2)}) collective-permute-start(f32[432,128]{1,0:T(8,128)} %get-tuple-element.101), channel_id=1, source_target_pairs={{0,11},{1,10},{2,9},{3,8},{4,15},{5,14},{6,13},{7,12},{8,3},{9,2},... | collective-permute-start | bytes 663560 | tf_op jit(solution)/shard_map/ppermute | solution.py:399
  262.1 32.1 %collective-permute-start.42 = (f32[432,128]{1,0:T(8,128)}, f32[432,128]{1,0:T(8,128)S(1)}, u32[]{:S(2)}, u32[]{:S(2)}) collective-permute-start(f32[432,128]{1,0:T(8,128)} %get-tuple-element.102), channel_id=1, source_target_pairs={{0,12},{1,13},{2,14},{3,15},{4,8},{5,9},{6,10},{7,11},{8,4},{9,5},... | collective-permute-start | bytes 663560 | tf_op jit(solution)/shard_map/ppermute | solution.py:399
  262.1 32.1 %collective-permute-start.43 = (f32[432,128]{1,0:T(8,128)}, f32[432,128]{1,0:T(8,128)S(1)}, u32[]{:S(2)}, u32[]{:S(2)}) collective-permute-start(f32[432,128]{1,0:T(8,128)} %get-tuple-element.103), channel_id=1, source_target_pairs={{0,13},{1,12},{2,15},{3,14},{4,9},{5,8},{6,11},{7,10},{8,5},{9,4},... | collective-permute-start | bytes 663560 | tf_op jit(solution)/shard_map/ppermute | solution.py:399
  265.4 28.9 %collective-permute-start.44 = (f32[432,128]{1,0:T(8,128)}, f32[432,128]{1,0:T(8,128)S(1)}, u32[]{:S(2)}, u32[]{:S(2)}) collective-permute-start(f32[432,128]{1,0:T(8,128)} %get-tuple-element.104), channel_id=1, source_target_pairs={{0,14},{1,15},{2,12},{3,13},{4,10},{5,11},{6,8},{7,9},{8,6},{9,7},... | collective-permute-start | bytes 663560 | tf_op jit(solution)/shard_map/ppermute | solution.py:399
  317.5 65.5 %all-to-all-start = ((f32[32,112,128]{2,1,0:T(8,128)}), f32[32,112,128]{2,1,0:T(8,128)S(1)}, u32[]{:S(2)}, u32[]{:S(2)}) async-start(f32[32,112,128]{2,1,0:T(8,128)} %bitcast.15), calls=%async_computation | async-start | bytes 3670016 | tf_op jit(solution)/shard_map/all_to_all | solution.py:404
  338.9 50.4 %collective-permute-start.46 = (f32[1728,128]{1,0:T(8,128)S(1)}, f32[1728,128]{1,0:T(8,128)}, u32[]{:S(2)}, u32[]{:S(2)}) collective-permute-start(f32[1728,128]{1,0:T(8,128)S(1)} %copy-done.18), channel_id=1, source_target_pairs={{0,16},{16,0},{1,17},{17,1},{2,18},{18,2},{3,19},{19,3},{4,20},{20... | collective-permute-start | bytes 2654216 | tf_op jit(solution)/shard_map/ppermute | solution.py:492
  389.3 46.9 %all-to-all-start.1 = ((f32[32,112,128]{2,1,0:T(8,128)}), f32[32,112,128]{2,1,0:T(8,128)S(1)}, u32[]{:S(2)}, u32[]{:S(2)}) async-start(f32[32,112,128]{2,1,0:T(8,128)} %bitcast.13), calls=%async_computation.1 | async-start | bytes 3670016 | tf_op jit(solution)/shard_map/all_to_all | solution.py:404
  392.2 39.6 %collective-permute-start.47 = (f32[1728,128]{1,0:T(8,128)S(1)}, f32[1728,128]{1,0:T(8,128)}, u32[]{:S(2)}, u32[]{:S(2)}) collective-permute-start(f32[1728,128]{1,0:T(8,128)S(1)} %copy-done.19), channel_id=1, source_target_pairs={{0,16},{16,0},{1,17},{17,1},{2,18},{18,2},{3,19},{19,3},{4,20},{20... | collective-permute-start | bytes 2654216 | tf_op jit(solution)/shard_map/ppermute | solution.py:493
  (80 other events, 2285.4 us)

commit v4 on v3

--- a/solution.py
+++ b/solution.py
@@ -137,7 +137,8 @@
 
 
 def kinetic(plane, kin):
-    return product(plane, kin) + product(kin, plane)
+    plane = split(plane)
+    return product_of_parts(plane, kin) + product_of_parts(kin, plane)
 
 
 def pack(plane, packed):
@@ -163,7 +164,7 @@
                 out_ref[pl.ds(to * chunk + used, chunk - used), :] = jnp.zeros((chunk - used, LANES), jnp.float32)
 
 
-def pack_kernel(sizes, bunch, place_ref, psi_ref, ion_ref, hxc_ref, *refs):
+def pack_kernel(sizes, bunch, turns, place_ref, psi_ref, ion_ref, hxc_ref, *refs):
     planes, grid, rows, share = sizes
     *out_refs, packed = refs
     stride = 2 * rows + share
@@ -175,21 +176,21 @@
         for part in range(2):
             slot = packed.at[inner * 3 + part]
             pack(psi_ref[0, part, inner], slot)
-            for turn, out_ref in enumerate(out_refs):
+            for turn, out_ref in zip(turns, out_refs):
                 start = (mine ^ turn) * rows
                 out_ref[pl.ds(first + part * rows, rows), :] = slot[pl.ds(start, rows), :]
         slot = packed.at[inner * 3 + 2]
         pack(ion_ref[inner] + hxc_ref[inner], slot)
-        for turn, out_ref in enumerate(out_refs):
+        for turn, out_ref in zip(turns, out_refs):
             start = (mine ^ turn) * rows + band * share
             out_ref[pl.ds(first + 2 * rows, share), :] = slot[pl.ds(start, share), :]
 
 
-def plane_kernel(sizes, bunch, place_ref, psi_ref, ion_ref, hxc_ref, kin_ref, *refs):
+def plane_kernel(sizes, bunch, turns, place_ref, psi_ref, ion_ref, hxc_ref, kin_ref, *refs):
     planes, grid, rows, share = sizes
     *out_refs, base_ref, packed = refs
     mine = place_ref[1]
-    kin = kin_ref[...]
+    kin = split(kin_ref[...])
     for inner in range(bunch):
         plane = pl.program_id(0) * bunch + inner
         potential = ion_ref[inner] + hxc_ref[inner]
@@ -200,7 +201,7 @@
             applied.append(bare + potential * field)
             slot = packed.at[inner * 2 + part]
             pack(bare + applied[part], slot)
-            for turn, out_ref in enumerate(out_refs):
+            for turn, out_ref in zip(turns, out_refs):
                 start = (mine ^ turn) * rows
                 out_ref[pl.ds((plane * 2 + part) * rows, rows), :] = slot[pl.ds(start, rows), :]
         for part in range(2):
@@ -213,32 +214,32 @@
             )
 
 
-def share_kernel(sizes, place_ref, *refs):
+def share_kernel(sizes, turns, place_ref, *refs):
     planes, grid, rows, share = sizes
     *moved_refs, out_ref = refs
     length = planes * grid
     stride = 2 * rows + share
-    for turn, moved_ref in enumerate(moved_refs):
+    for turn, moved_ref in zip(turns, moved_refs):
         first = (place_ref[1] ^ turn) * planes
         for row in range(share):
             out_ref[pl.ds(row * length + first, planes), :] = moved_ref[pl.ds(2 * rows + row, planes, stride=stride), :]
 
 
-def along_kernel(sizes, place_ref, *refs):
+def along_kernel(sizes, turns, place_ref, *refs):
     planes, grid, rows, share = sizes
     *moved_refs, kin_ref, out_ref, lines = refs
     stride = 2 * rows + share
     row = pl.program_id(0)
-    for turn, moved_ref in enumerate(moved_refs):
+    for turn, moved_ref in zip(turns, moved_refs):
         first = (place_ref[1] ^ turn) * planes
         for part in range(2):
             lines[part, pl.ds(first, planes), :] = moved_ref[pl.ds(part * rows + row, planes, stride=stride), :]
     out_ref[...] = product(kin_ref[...], jnp.concatenate([lines[0], lines[1]], axis=1))
 
 
-def update_kernel(sizes, steps, place_ref, along_ref, own_ref, other_ref, kin_ref, *refs):
-    planes, grid, rows, share = sizes
-    mixed_refs, out_refs, lines = refs[:grid], refs[grid : 2 * grid], refs[-1]
+def update_kernel(sizes, steps, turns, place_ref, along_ref, own_ref, other_ref, kin_ref, *refs):
+    planes, grid, rows, share = sizes
+    *mixed_refs, out_ref, lines = refs
     length = planes * grid
     kin = split(kin_ref[...])
     step = pl.program_id(0)
@@ -247,7 +248,7 @@
         row = step * (rows // steps) + inner
         here = slice(inner * length, (inner + 1) * length)
         slot = lines.at[inner]
-        for turn, mixed_ref in enumerate(mixed_refs):
+        for turn, mixed_ref in zip(turns, mixed_refs):
             first = (place_ref[1] ^ turn) * planes
             for part in range(2):
                 slot[part, pl.ds(first, planes), :] = mixed_ref[pl.ds(part * rows + row, planes, stride=2 * rows), :]
@@ -258,17 +259,15 @@
             mine = along[:, part * LANES : (part + 1) * LANES]
             turned = along[:, LANES:] if part == 0 else -along[:, :LANES]
             twice = again[:, part * LANES : (part + 1) * LANES] + potential * mine
-            slot[part] = 2.0 * BESSEL_ONE * turned - 4.0 * BESSEL_TWO * twice
-        for turn, out_ref in enumerate(out_refs):
-            first = (place_ref[1] ^ turn) * planes
-            for part in range(2):
-                out_ref[pl.ds(part * rows + row, planes, stride=2 * rows), :] = slot[part, pl.ds(first, planes), :]
-
-
-def fresh_kernel(sizes, bunch, place_ref, occ_ref, base_ref, basis_ref, turn_ref, *refs):
-    planes, grid, rows, share = sizes
-    update_refs = refs[:grid]
-    fresh_ref, upper_ref, lower_ref, out_ref, packed = refs[grid:]
+            out_ref[pl.ds(part * rows + row, length, stride=2 * rows), :] = (
+                2.0 * BESSEL_ONE * turned - 4.0 * BESSEL_TWO * twice
+            )
+
+
+def fresh_kernel(
+    sizes, bunch, occ_ref, update_ref, base_ref, basis_ref, turn_ref, fresh_ref, upper_ref, lower_ref, out_ref, packed
+):
+    planes, grid, rows, share = sizes
     length = planes * grid
     chunk = chunk_rows(sizes)[1]
     cell_rows = rows * grid
@@ -279,9 +278,9 @@
         part_sum = None
         for part in range(2):
             slot = packed.at[inner * 4 + part]
-            for turn, update_ref in enumerate(update_refs):
-                start = (place_ref[1] ^ turn) * rows
-                slot[pl.ds(start, rows), :] = update_ref[pl.ds((plane * 2 + part) * rows, rows), :]
+            for source in range(grid):
+                start = ((source * planes + plane) * 2 + part) * rows
+                slot[pl.ds(source * rows, rows), :] = update_ref[pl.ds(start, rows), :]
             fresh = base_ref[part, inner] + unpack(slot, length)
             fresh_ref[0, part, inner] = fresh
             part_sum = fresh * fresh if part_sum is None else part_sum + fresh * fresh
@@ -364,6 +363,13 @@
 
 def cost(flops, moved):
     return pl.CostEstimate(flops=flops, bytes_accessed=moved, transcendentals=0)
+
+
+def turn_order(grid):
+    order = [0]
+    for near in range(grid // 2):
+        order += [near + grid // 2] if near == 0 else [near, near + grid // 2]
+    return order
 
 
 def packed_path(orbitals, occupations, ion_potential, hxc_potential):
@@ -392,23 +398,27 @@
     def scratch(count):
         return [pltpu.VMEM((count * bunch, cell_rows, LANES), jnp.float32)]
 
-    def swap(pieces):
-        swapped = list(pieces)
-        for turn in sorted(range(1, grid), key=lambda k: -k):
-            pairs = [(place, place ^ turn) for place in range(grid)]
-            swapped[turn] = lax.ppermute(pieces[turn], "grid", pairs)
-        return swapped
+    def swap_pieces(turns, pieces):
+        return [
+            lax.ppermute(piece, "grid", [(place, place ^ turn) for place in range(grid)]) if turn else piece
+            for turn, piece in zip(turns, pieces)
+        ]
+
+    def swap(array):
+        flat = array.reshape(grid, -1, LANES)
+        return lax.all_to_all(flat, "grid", split_axis=0, concat_axis=0).reshape(array.shape)
 
     def swap_all(array):
         flat = array.reshape(2 * grid, -1, LANES)
         return lax.all_to_all(flat, ("band", "grid"), split_axis=0, concat_axis=0).reshape(array.shape)
 
+    turns = turn_order(grid)
     moved_rows, spec_rows = chunk_rows(sizes)
     spec_rows = 2 * grid * spec_rows
     mixed_rows = 2 * planes * rows
     steps = 6 if rows % 6 == 0 and share % (rows // 6) == 0 else 2
     moved = pl.pallas_call(
-        functools.partial(pack_kernel, sizes, bunch),
+        functools.partial(pack_kernel, sizes, bunch, turns),
         grid=(planes // bunch,),
         in_specs=[smem, psi_spec, plane_spec, plane_spec],
         out_specs=[whole(moved_rows, LANES)] * grid,
@@ -417,21 +427,27 @@
         compiler_params=PARAMS,
         cost_estimate=cost(0, 15 << 20),
     )(place, orbitals, ion_potential, hxc_potential)
-    moved = swap(moved)
     *mixed, base = pl.pallas_call(
-        functools.partial(plane_kernel, sizes, bunch),
+        functools.partial(plane_kernel, sizes, bunch, turns),
         grid=(planes // bunch,),
         in_specs=[smem, psi_spec, plane_spec, plane_spec, square],
         out_specs=[whole(mixed_rows, LANES)] * grid + [pair_spec],
         out_shape=[shape(mixed_rows, LANES)] * grid + [shape(2, planes, length, length)],
         scratch_shapes=scratch(2),
         compiler_params=PARAMS,
-        cost_estimate=cost(8 * 6 * work, 20 << 20),
+        cost_estimate=cost(8 * 3 * work, 20 << 20),
     )(place, orbitals, ion_potential, hxc_potential, kin)
-    mixed = swap(mixed)
+    late = range(6, grid)
+    held = lax.optimization_barrier(([moved[k] for k in late], base))
+    base = held[1]
+    moved = list(moved)
+    for k, piece in zip(late, held[0]):
+        moved[k] = piece
+    moved = swap_pieces(turns, moved)
+    mixed = swap_pieces(turns, mixed)
 
     own = pl.pallas_call(
-        functools.partial(share_kernel, sizes),
+        functools.partial(share_kernel, sizes, turns),
         in_specs=[smem] + [vmem] * grid,
         out_specs=vmem,
         out_shape=shape(share * length, LANES),
@@ -440,7 +456,7 @@
     )(place, *moved)
     other = lax.ppermute(own, "band", [(0, 1), (1, 0)])
     along = pl.pallas_call(
-        functools.partial(along_kernel, sizes),
+        functools.partial(along_kernel, sizes, turns),
         grid=(rows,),
         in_specs=[smem] + [whole(moved_rows, LANES)] * grid + [square],
         out_specs=pl.BlockSpec((length, 2 * LANES), lambda i: (i, 0)),
@@ -451,7 +467,7 @@
     )(place, *moved, kin)
     half_spec = pl.BlockSpec((rows // steps * length, LANES), lambda i: (i % (steps // 2), 0))
     update = pl.pallas_call(
-        functools.partial(update_kernel, sizes, steps),
+        functools.partial(update_kernel, sizes, steps, turns),
         grid=(steps,),
         in_specs=[
             smem,
@@ -461,8 +477,8 @@
             square,
         ]
         + [whole(mixed_rows, LANES)] * grid,
-        out_specs=[whole(mixed_rows, LANES)] * grid,
-        out_shape=[shape(mixed_rows, LANES)] * grid,
+        out_specs=whole(2 * field, LANES),
+        out_shape=shape(2 * field, LANES),
         scratch_shapes=[pltpu.VMEM((rows // steps, 2, length, LANES), jnp.float32)],
         compiler_params=PARAMS,
         cost_estimate=cost(2 * 3 * work, 14 << 20),
@@ -472,7 +488,7 @@
     fresh, upper, lower, spectrum = pl.pallas_call(
         functools.partial(fresh_kernel, sizes, bunch),
         grid=(planes // bunch,),
-        in_specs=[smem, smem, pair_spec, square, square] + [whole(mixed_rows, LANES)] * grid,
+        in_specs=[smem, whole(2 * field, LANES), pair_spec, square, square],
         out_specs=[
             psi_spec,
             half_rows,
@@ -488,7 +504,7 @@
         scratch_shapes=scratch(4),
         compiler_params=PARAMS,
         cost_estimate=cost(2 * 6 * work, 16 << 20),
-    )(place, occupations, base, basis, turn, *update)
+    )(occupations, update, base, basis, turn)
     upper_other = lax.ppermute(upper, "band", [(0, 1), (1, 0)])
     lower_other = lax.ppermute(lower, "band", [(0, 1), (1, 0)])
 

time: 445 us -> 407 us (0.915)
  starting transfers between devices: 151 us -> 111 us
  waiting for transfers between devices: 199 us -> 216 us
  Pallas kernels: 85 us -> 69.2 us
    all_to_all x0 -> x1, waiting for transfers between devices: none -> 65.6 us  [swap(): lax.all_to_all(flat, 'grid', split_axis=0, concat_axis=0)]
    ppermute x45 -> x30, waiting for transfers between devices: 116 us -> 66.7 us  [swap_pieces(): lax.ppermute(piece, 'grid', [(place, place ^ turn) for place in range(gri...]
    ppermute x45 -> x30, starting transfers between devices: 122 us -> 81.6 us  [swap_pieces(): lax.ppermute(piece, 'grid', [(place, place ^ turn) for place in range(gri...]
    pallas_call x5, Pallas kernels: 55.7 us -> 45.5 us  [the longest x1 13.9 us: packed_path(): pl.pallas_call(functools.partial(plane_kernel, sizes, bunch, turns), grid...]
    pallas_call x1, Pallas kernels: 17.1 us -> 11.5 us  [packed_path(): pl.pallas_call(functools.partial(fresh_kernel, sizes, bunch), grid=(plane...]
    all_to_all x0 -> x1, starting transfers between devices: none -> 4.87 us  [swap(): lax.all_to_all(flat, 'grid', split_axis=0, concat_axis=0)]
    all_to_all x2, starting transfers between devices: 24.3 us -> 19.8 us  [swap_all(): lax.all_to_all(flat, ('band', 'grid'), split_axis=0, concat_axis=0)]
  transfers between devices with their start and end apart: 50 -> 36, of which waited for: 17 -> 17; matrix products, arithmetic and copies ran while one was open for 0% -> 0% of each run, Pallas kernels for 10% -> 8%
where the time goes in v4:
time: 407 us; the launch traced here: 406 us
  waiting for transfers between devices  216 us (53%)
  starting transfers between devices  111 us (27%)
  Pallas kernels  69.2 us (17%)
  local copies, waits for them, and re-layouts  7.49 us (2%)
    ppermute x30, starting transfers between devices, swap_pieces(): lax.ppermute(piece, 'grid', [(place, place ^ turn) for place in range(gri...  81.6 us
    ppermute x30, waiting for transfers between devices, swap_pieces(): lax.ppermute(piece, 'grid', [(place, place ^ turn) for place in range(gri...  66.7 us
    all_to_all x1, waiting for transfers between devices, swap(): lax.all_to_all(flat, 'grid', split_axis=0, concat_axis=0)  65.6 us
    all_to_all x2, waiting for transfers between devices, swap_all(): lax.all_to_all(flat, ('band', 'grid'), split_axis=0, concat_axis=0)  45.4 us
    ppermute x1, waiting for transfers between devices, packed_path(): lower_other = lax.ppermute(lower, 'band', [(0, 1), (1, 0)])  37.9 us
    all_to_all x2, starting transfers between devices, swap_all(): lax.all_to_all(flat, ('band', 'grid'), split_axis=0, concat_axis=0)  19.8 us
    pallas_call x1, Pallas kernels, packed_path(): pl.pallas_call(functools.partial(plane_kernel, sizes, bunch, turns), grid...  13.9 us
    pallas_call x1, Pallas kernels, packed_path(): pl.pallas_call(functools.partial(along_kernel, sizes, turns), grid=(rows,...  12 us
  transfers between devices with their start and end apart: 36, of which 17 were waited for; matrix products, arithmetic and copies ran while one was open for 0% of the time, Pallas kernels for 8%

profile of v4, /device:TPU:0, one launch (start us, length us, event | category | flops | bytes accessed | tf_op | source)
XLA Modules:
  0.0 406.1 jit_solution(9368980710429496145)
XLA Ops:
  1.3 7.0 %shard_map.104 = (f32[544,128]{1,0:T(8,128)}, f32[544,128]{1,0:T(8,128)}, f32[544,128]{1,0:T(8,128)}, f32[544,128]{1,0:T(8,128)}, f32[544,128]{1,0:T(8,128)}, /*...) custom-call(s32[2]{0:T(128)} %pad_add_fusion.place_ref, ...), custom_call_target="tpu_custom_call" | custom-call | bytes 15728640 | tf_op jit(solution)/shard_map/pallas_call | solution.py:420
  8.3 4.0 collective-permute-start
  17.0 13.9 %shard_map.105 = (f32[432,128]{1,0:T(8,128)}, f32[432,128]{1,0:T(8,128)}, f32[432,128]{1,0:T(8,128)}, f32[432,128]{1,0:T(8,128)}, f32[432,128]{1,0:T(8,128)}, /*...) custom-call(s32[2]{0:T(128)} %pad_add_fusion.place_ref, ...), custom_call_target="tpu_custom_call" | custom-call | flops 4076863488 | bytes 20971520 | tf_op jit(solution)/shard_map/pallas_call | solution.py:430
  30.8 7.1 %collective-permute-done.refs_1_ = f32[544,128]{1,0:T(8,128)S(1)} collective-permute-done((f32[544,128]{1,0:T(8,128)}, f32[544,128]{1,0:T(8,128)S(1)}, u32[]{:S(2)}, u32[]{:S(2)}) %collective-permute-start) | collective-permute-done | bytes 278560 | tf_op jit(solution)/shard_map/ppermute | solution.py:403
  38.8 3.4 collective-permute-done.2.refs_3_
  42.2 7.7 %collective-permute-start.7 = (f32[544,128]{1,0:T(8,128)S(1)}, f32[544,128]{1,0:T(8,128)S(1)}, u32[]{:S(2)}, u32[]{:S(2)}) collective-permute-start(f32[544,128]{1,0:T(8,128)S(1)} %copy-done.43), channel_id=1, source_target_pairs={{0,4},{1,5},{2,6},{3,7},{4,0},{5,1},{6,2},{7,3},{8,12},{9,13},{10,... | collective-permute-start | bytes 835592 | tf_op jit(solution)/shard_map/ppermute | solution.py:403
  52.6 4.6 %collective-permute-done.4.refs_5_ = f32[544,128]{1,0:T(8,128)S(1)} collective-permute-done((f32[544,128]{1,0:T(8,128)}, f32[544,128]{1,0:T(8,128)S(1)}, u32[]{:S(2)}, u32[]{:S(2)}) %collective-permute-start.4) | collective-permute-done | bytes 278560 | tf_op jit(solution)/shard_map/ppermute | solution.py:403
  59.2 7.6 %collective-permute-done.6.refs_7_ = f32[544,128]{1,0:T(8,128)S(1)} collective-permute-done((f32[544,128]{1,0:T(8,128)S(1)}, f32[544,128]{1,0:T(8,128)S(1)}, u32[]{:S(2)}, u32[]{:S(2)}) %collective-permute-start.6) | collective-permute-done | bytes 278560 | tf_op jit(solution)/shard_map/ppermute | solution.py:403
  68.7 10.1 %collective-permute-done.7.refs_8_ = f32[544,128]{1,0:T(8,128)S(1)} collective-permute-done((f32[544,128]{1,0:T(8,128)S(1)}, f32[544,128]{1,0:T(8,128)S(1)}, u32[]{:S(2)}, u32[]{:S(2)}) %collective-permute-start.7) | collective-permute-done | bytes 278560 | tf_op jit(solution)/shard_map/ppermute | solution.py:403
  78.8 4.6 %collective-permute-start.12 = (f32[544,128]{1,0:T(8,128)S(1)}, f32[544,128]{1,0:T(8,128)S(1)}, u32[]{:S(2)}, u32[]{:S(2)}) collective-permute-start(f32[544,128]{1,0:T(8,128)S(1)} %copy-done.38), channel_id=1, source_target_pairs={{0,14},{1,15},{2,12},{3,13},{4,10},{5,11},{6,8},{7,9},{8,6},{9,7},... | collective-permute-start | bytes 835592 | tf_op jit(solution)/shard_map/ppermute | solution.py:403
  83.5 7.2 %collective-permute-done.9.refs_10_ = f32[544,128]{1,0:T(8,128)S(1)} collective-permute-done((f32[544,128]{1,0:T(8,128)S(1)}, f32[544,128]{1,0:T(8,128)S(1)}, u32[]{:S(2)}, u32[]{:S(2)}) %collective-permute-start.9) | collective-permute-done | bytes 278560 | tf_op jit(solution)/shard_map/ppermute | solution.py:403
  90.7 4.4 %collective-permute-start.14 = (f32[544,128]{1,0:T(8,128)S(1)}, f32[544,128]{1,0:T(8,128)S(1)}, u32[]{:S(2)}, u32[]{:S(2)}) collective-permute-start(f32[544,128]{1,0:T(8,128)S(1)} %copy-done.36), channel_id=1, source_target_pairs={{0,15},{1,14},{2,13},{3,12},{4,11},{5,10},{6,9},{7,8},{8,7},{9,6},... | collective-permute-start | bytes 835592 | tf_op jit(solution)/shard_map/ppermute | solution.py:403
  95.1 8.0 %collective-permute-done.11.refs_12_ = f32[544,128]{1,0:T(8,128)S(1)} collective-permute-done((f32[544,128]{1,0:T(8,128)S(1)}, f32[544,128]{1,0:T(8,128)S(1)}, u32[]{:S(2)}, u32[]{:S(2)}) %collective-permute-start.11) | collective-permute-done | bytes 278560 | tf_op jit(solution)/shard_map/ppermute | solution.py:403
  103.3 10.0 %collective-permute-start.18 = (f32[432,128]{1,0:T(8,128)}, f32[432,128]{1,0:T(8,128)S(1)}, u32[]{:S(2)}, u32[]{:S(2)}) collective-permute-start(f32[432,128]{1,0:T(8,128)} %get-tuple-element.82), channel_id=1, source_target_pairs={{0,9},{1,8},{2,11},{3,10},{4,13},{5,12},{6,15},{7,14},{8,1},{9,0},... | collective-permute-start | bytes 663560 | tf_op jit(solution)/shard_map/ppermute | solution.py:403
  120.4 5.5 %collective-permute-done.16.refs_1_ = f32[432,128]{1,0:T(8,128)S(1)} collective-permute-done((f32[432,128]{1,0:T(8,128)}, f32[432,128]{1,0:T(8,128)S(1)}, u32[]{:S(2)}, u32[]{:S(2)}) %collective-permute-start.16) | collective-permute-done | bytes 221216 | tf_op jit(solution)/shard_map/ppermute | solution.py:403
  125.9 5.7 %collective-permute-start.20 = (f32[432,128]{1,0:T(8,128)S(1)}, f32[432,128]{1,0:T(8,128)S(1)}, u32[]{:S(2)}, u32[]{:S(2)}) collective-permute-start(f32[432,128]{1,0:T(8,128)S(1)} %copy-done.56), channel_id=1, source_target_pairs={{0,10},{1,11},{2,8},{3,9},{4,14},{5,15},{6,12},{7,13},{8,2},{9,3},... | collective-permute-start | bytes 663560 | tf_op jit(solution)/shard_map/ppermute | solution.py:403
  132.7 13.2 %collective-permute-start.23 = (f32[432,128]{1,0:T(8,128)S(1)}, f32[432,128]{1,0:T(8,128)S(1)}, u32[]{:S(2)}, u32[]{:S(2)}) collective-permute-start(f32[432,128]{1,0:T(8,128)S(1)} %copy-done.53), channel_id=1, source_target_pairs={{0,4},{1,5},{2,6},{3,7},{4,0},{5,1},{6,2},{7,3},{8,12},{9,13},{10,... | collective-permute-start | bytes 663560 | tf_op jit(solution)/shard_map/ppermute | solution.py:403
  150.6 7.1 %collective-permute-start.26 = (f32[432,128]{1,0:T(8,128)S(1)}, f32[432,128]{1,0:T(8,128)S(1)}, u32[]{:S(2)}, u32[]{:S(2)}) collective-permute-start(f32[432,128]{1,0:T(8,128)S(1)} %copy-done.50), channel_id=1, source_target_pairs={{0,13},{1,12},{2,15},{3,14},{4,9},{5,8},{6,11},{7,10},{8,5},{9,4},... | collective-permute-start | bytes 663560 | tf_op jit(solution)/shard_map/ppermute | solution.py:403
  157.7 3.5 collective-permute-done.23.refs_8_
  164.6 4.9 %collective-permute-done.25.refs_10_ = f32[432,128]{1,0:T(8,128)S(1)} collective-permute-done((f32[432,128]{1,0:T(8,128)S(1)}, f32[432,128]{1,0:T(8,128)S(1)}, u32[]{:S(2)}, u32[]{:S(2)}) %collective-permute-start.25) | collective-permute-done | bytes 221216 | tf_op jit(solution)/shard_map/ppermute | solution.py:403
  169.6 4.0 collective-permute-start.30
  173.6 12.0 %shard_map.106.along_ref = f32[3456,256]{1,0:T(8,128)} custom-call(s32[2]{0:T(128)} %pad_add_fusion.place_ref, f32[544,128]{1,0:T(8,128)} %get-tuple-element.52.refs_0_, f32[544,128]{1,0:T(8,128)} %copy-done.3, f32[544,128]{1,0:T(8,128)} %copy-done.4, f32[544,128]{1,0:T(8,128)} %copy-done.5, f32[544,128]{1,0:T(8,128)} %copy-done.6, f32[544,128]{1,0:T(8,128)} %copy-done.7, ...), custom_call_target="tpu_custom_call" | custom-call | flops 2038431744 | bytes 10485760 | tf_op jit(solution)/shard_map/pallas_call | solution.py:458
  189.8 9.2 %shard_map.108 = f32[6912,128]{1,0:T(8,128)} custom-call(s32[2]{0:T(128)} %pad_add_fusion.place_ref, f32[3456,256]{1,0:T(8,128)} %shard_map.106.along_ref, f32[1728,128]{1,0:T(8,128)} %shard_map.107.own_ref, f32[1728,128]{1,0:T(8,128)} %copy-done.18, f32[192,192]{1,0:T(8,128)} %constant.27.clone.kin_ref.refs_16_, f32[432,128]{1,0:T(8,128)} %get-tuple-element.79.refs_0_, ...), custom_call_target="tpu_custom_call" | custom-call | flops 1019215872 | bytes 14680064 | tf_op jit(solution)/shard_map/pallas_call | solution.py:469
  199.0 4.9 %all-to-all-start = ((f32[16,432,128]{2,1,0:T(8,128)}), f32[16,432,128]{2,1,0:T(8,128)S(1)}, u32[]{:S(2)}, u32[]{:S(2)}) async-start(f32[16,432,128]{2,1,0:T(8,128)} %bitcast.14), calls=%async_computation | async-start | bytes 7077888 | tf_op jit(solution)/shard_map/all_to_all | solution.py:409
  204.5 65.6 %all-to-all-done = f32[16,432,128]{2,1,0:T(8,128)S(1)} async-done(((f32[16,432,128]{2,1,0:T(8,128)}), f32[16,432,128]{2,1,0:T(8,128)S(1)}, u32[]{:S(2)}, u32[]{:S(2)}) %all-to-all-start) | async-done | bytes 3538976 | tf_op jit(solution)/shard_map/all_to_all | solution.py:409
  271.9 11.5 %shard_map.109 = (f32[1,2,12,192,192]{4,3,2,1,0:T(8,128)}, f32[1728,128]{1,0:T(8,128)}, f32[1728,128]{1,0:T(8,128)}, f32[3584,128]{1,0:T(8,128)}) custom-call(f32[1]{0:T(128)S(6)} %copy.14.occ_ref, f32[6912,128]{1,0:T(8,128)} %bitcast.15, f32[2,12,192,192]{3,2,1,0:T(8,128)} %get-tuple-element.95.base_ref, f32[192,192]{1,0:T(8,128)} %constant.28.clone.basis_ref, ...), custom_call_target="tpu_custom_call" | custom-call | flops 2038431744 | bytes 16777216 | tf_op jit(solution)/shard_map/pallas_call | solution.py:488
  283.5 17.0 %all-to-all-start.1 = ((f32[32,112,128]{2,1,0:T(8,128)}), f32[32,112,128]{2,1,0:T(8,128)S(1)}, u32[]{:S(2)}, u32[]{:S(2)}) async-start(f32[32,112,128]{2,1,0:T(8,128)} %bitcast.19), calls=%async_computation.1 | async-start | bytes 3670016 | tf_op jit(solution)/shard_map/all_to_all | solution.py:413
  303.6 40.9 %all-to-all-done.1 = f32[32,112,128]{2,1,0:T(8,128)S(1)} async-done(((f32[32,112,128]{2,1,0:T(8,128)}), f32[32,112,128]{2,1,0:T(8,128)S(1)}, u32[]{:S(2)}, u32[]{:S(2)}) %all-to-all-start.1) | async-done | bytes 1835040 | tf_op jit(solution)/shard_map/all_to_all | solution.py:413
  345.7 5.1 %shard_map.110 = f32[3584,128]{1,0:T(8,128)} custom-call(f32[3584,128]{1,0:T(8,128)} %bitcast.16, f32[1,1152]{1,0:T(1,128)} %bitcast.20, f32[192,1]{1,0:T(8,128)} %constant.36.squares_ref, f32[192,192]{1,0:T(8,128)} %constant.28.clone.basis_ref, f32[192,192]{1,0:T(8,128)} %constant.29.clone.turn_ref), custom_call_target="tpu_custom_call" | custom-call | flops 1019215872 | bytes 5242880 | tf_op jit(solution)/shard_map/pallas_call | solution.py:519
  355.4 37.9 %collective-permute-done.32.lower_other = f32[1728,128]{1,0:T(8,128)} collective-permute-done((f32[1728,128]{1,0:T(8,128)S(1)}, f32[1728,128]{1,0:T(8,128)}, u32[]{:S(2)}, u32[]{:S(2)}) %collective-permute-start.32) | collective-permute-done | bytes 884768 | tf_op jit(solution)/shard_map/ppermute | solution.py:509
  393.3 4.4 %all-to-all-done.2 = f32[32,112,128]{2,1,0:T(8,128)S(1)} async-done(((f32[32,112,128]{2,1,0:T(8,128)}), f32[32,112,128]{2,1,0:T(8,128)S(1)}, u32[]{:S(2)}, u32[]{:S(2)}) %all-to-all-start.2) | async-done | bytes 1835040 | tf_op jit(solution)/shard_map/all_to_all | solution.py:413
  398.9 7.1 %shard_map.111 = f32[12,192,192]{2,1,0:T(8,128)} custom-call(f32[3584,128]{1,0:T(8,128)} %bitcast.18, f32[1728,128]{1,0:T(8,128)} %get-tuple-element.98.upper_ref, f32[1728,128]{1,0:T(8,128)} %get-tuple-element.100.lower_ref, f32[1728,128]{1,0:T(8,128)} %collective-permute-done.31.upper_other, f32[1728,128]{1,0:T(8,128)} %collective-permute-done.32.lower_other, ...), custom_call_target="tpu_custom_call" | custom-call | flops 2038431744 | bytes 6291456 | tf_op jit(solution)/shard_map/pallas_call | solution.py:530
  (167 shorter events, 45.1 us)
Async XLA Ops:
  8.3 29.7 %collective-permute-start = (f32[544,128]{1,0:T(8,128)}, f32[544,128]{1,0:T(8,128)S(1)}, u32[]{:S(2)}, u32[]{:S(2)}) collective-permute-start(f32[544,128]{1,0:T(8,128)} %get-tuple-element.53), channel_id=1, source_target_pairs={{0,8},{1,9},{2,10},{3,11},{4,12},{5,13},{6,14},{7,15},{8,0},{9,1},... | collective-permute-start | bytes 835592 | tf_op jit(solution)/shard_map/ppermute | solution.py:403
  12.3 25.6 %collective-permute-start.1 = (f32[544,128]{1,0:T(8,128)}, f32[544,128]{1,0:T(8,128)S(1)}, u32[]{:S(2)}, u32[]{:S(2)}) collective-permute-start(f32[544,128]{1,0:T(8,128)} %get-tuple-element.54), channel_id=1, source_target_pairs={{0,1},{1,0},{2,3},{3,2},{4,5},{5,4},{6,7},{7,6},{8,9},{9,8},{10,11... | collective-permute-start | bytes 835592 | tf_op jit(solution)/shard_map/ppermute | solution.py:403
  12.3 29.9 %collective-permute-start.2 = (f32[544,128]{1,0:T(8,128)}, f32[544,128]{1,0:T(8,128)S(1)}, u32[]{:S(2)}, u32[]{:S(2)}) collective-permute-start(f32[544,128]{1,0:T(8,128)} %get-tuple-element.55), channel_id=1, source_target_pairs={{0,9},{1,8},{2,11},{3,10},{4,13},{5,12},{6,15},{7,14},{8,1},{9,0},... | collective-permute-start | bytes 835592 | tf_op jit(solution)/shard_map/ppermute | solution.py:403
  12.5 37.4 %collective-permute-start.3 = (f32[544,128]{1,0:T(8,128)}, f32[544,128]{1,0:T(8,128)S(1)}, u32[]{:S(2)}, u32[]{:S(2)}) collective-permute-start(f32[544,128]{1,0:T(8,128)} %get-tuple-element.56), channel_id=1, source_target_pairs={{0,2},{1,3},{2,0},{3,1},{4,6},{5,7},{6,4},{7,5},{8,10},{9,11},{10,... | collective-permute-start | bytes 835592 | tf_op jit(solution)/shard_map/ppermute | solution.py:403
  14.3 42.9 %collective-permute-start.4 = (f32[544,128]{1,0:T(8,128)}, f32[544,128]{1,0:T(8,128)S(1)}, u32[]{:S(2)}, u32[]{:S(2)}) collective-permute-start(f32[544,128]{1,0:T(8,128)} %get-tuple-element.57), channel_id=1, source_target_pairs={{0,10},{1,11},{2,8},{3,9},{4,14},{5,15},{6,12},{7,13},{8,2},{9,3},... | collective-permute-start | bytes 835592 | tf_op jit(solution)/shard_map/ppermute | solution.py:403
  37.9 19.3 %collective-permute-start.5 = (f32[544,128]{1,0:T(8,128)S(1)}, f32[544,128]{1,0:T(8,128)S(1)}, u32[]{:S(2)}, u32[]{:S(2)}) collective-permute-start(f32[544,128]{1,0:T(8,128)S(1)} %copy-done.45), channel_id=1, source_target_pairs={{0,3},{1,2},{2,1},{3,0},{4,7},{5,6},{6,5},{7,4},{8,11},{9,10},{10,... | collective-permute-start | bytes 835592 | tf_op jit(solution)/shard_map/ppermute | solution.py:403
  38.0 28.9 %collective-permute-start.6 = (f32[544,128]{1,0:T(8,128)S(1)}, f32[544,128]{1,0:T(8,128)S(1)}, u32[]{:S(2)}, u32[]{:S(2)}) collective-permute-start(f32[544,128]{1,0:T(8,128)S(1)} %copy-done.44), channel_id=1, source_target_pairs={{0,11},{1,10},{2,9},{3,8},{4,15},{5,14},{6,13},{7,12},{8,3},{9,2},... | collective-permute-start | bytes 835592 | tf_op jit(solution)/shard_map/ppermute | solution.py:403
  42.2 36.6 %collective-permute-start.7 = (f32[544,128]{1,0:T(8,128)S(1)}, f32[544,128]{1,0:T(8,128)S(1)}, u32[]{:S(2)}, u32[]{:S(2)}) collective-permute-start(f32[544,128]{1,0:T(8,128)S(1)} %copy-done.43), channel_id=1, source_target_pairs={{0,4},{1,5},{2,6},{3,7},{4,0},{5,1},{6,2},{7,3},{8,12},{9,13},{10,... | collective-permute-start | bytes 835592 | tf_op jit(solution)/shard_map/ppermute | solution.py:403
  50.0 33.4 %collective-permute-start.8 = (f32[544,128]{1,0:T(8,128)S(1)}, f32[544,128]{1,0:T(8,128)S(1)}, u32[]{:S(2)}, u32[]{:S(2)}) collective-permute-start(f32[544,128]{1,0:T(8,128)S(1)} %copy-done.42), channel_id=1, source_target_pairs={{0,12},{1,13},{2,14},{3,15},{4,8},{5,9},{6,10},{7,11},{8,4},{9,5},... | collective-permute-start | bytes 835592 | tf_op jit(solution)/shard_map/ppermute | solution.py:403
  57.2 33.4 %collective-permute-start.9 = (f32[544,128]{1,0:T(8,128)S(1)}, f32[544,128]{1,0:T(8,128)S(1)}, u32[]{:S(2)}, u32[]{:S(2)}) collective-permute-start(f32[544,128]{1,0:T(8,128)S(1)} %copy-done.41), channel_id=1, source_target_pairs={{0,5},{1,4},{2,7},{3,6},{4,1},{5,0},{6,3},{7,2},{8,13},{9,12},{10,... | collective-permute-start | bytes 835592 | tf_op jit(solution)/shard_map/ppermute | solution.py:403
  57.3 37.8 %collective-permute-start.10 = (f32[544,128]{1,0:T(8,128)S(1)}, f32[544,128]{1,0:T(8,128)S(1)}, u32[]{:S(2)}, u32[]{:S(2)}) collective-permute-start(f32[544,128]{1,0:T(8,128)S(1)} %copy-done.40), channel_id=1, source_target_pairs={{0,13},{1,12},{2,15},{3,14},{4,9},{5,8},{6,11},{7,10},{8,5},{9,4},... | collective-permute-start | bytes 835592 | tf_op jit(solution)/shard_map/ppermute | solution.py:403
  66.9 36.2 %collective-permute-start.11 = (f32[544,128]{1,0:T(8,128)S(1)}, f32[544,128]{1,0:T(8,128)S(1)}, u32[]{:S(2)}, u32[]{:S(2)}) collective-permute-start(f32[544,128]{1,0:T(8,128)S(1)} %copy-done.39), channel_id=1, source_target_pairs={{0,6},{1,7},{2,4},{3,5},{4,2},{5,3},{6,0},{7,1},{8,14},{9,15},{10,... | collective-permute-start | bytes 835592 | tf_op jit(solution)/shard_map/ppermute | solution.py:403
  78.8 24.5 %collective-permute-start.12 = (f32[544,128]{1,0:T(8,128)S(1)}, f32[544,128]{1,0:T(8,128)S(1)}, u32[]{:S(2)}, u32[]{:S(2)}) collective-permute-start(f32[544,128]{1,0:T(8,128)S(1)} %copy-done.38), channel_id=1, source_target_pairs={{0,14},{1,15},{2,12},{3,13},{4,10},{5,11},{6,8},{7,9},{8,6},{9,7},... | collective-permute-start | bytes 835592 | tf_op jit(solution)/shard_map/ppermute | solution.py:403
  83.4 29.9 %collective-permute-start.13 = (f32[544,128]{1,0:T(8,128)S(1)}, f32[544,128]{1,0:T(8,128)S(1)}, u32[]{:S(2)}, u32[]{:S(2)}) collective-permute-start(f32[544,128]{1,0:T(8,128)S(1)} %copy-done.37), channel_id=1, source_target_pairs={{0,7},{1,6},{2,5},{3,4},{4,3},{5,2},{6,1},{7,0},{8,15},{9,14},{10,... | collective-permute-start | bytes 835592 | tf_op jit(solution)/shard_map/ppermute | solution.py:403
  90.7 22.6 %collective-permute-start.14 = (f32[544,128]{1,0:T(8,128)S(1)}, f32[544,128]{1,0:T(8,128)S(1)}, u32[]{:S(2)}, u32[]{:S(2)}) collective-permute-start(f32[544,128]{1,0:T(8,128)S(1)} %copy-done.36), channel_id=1, source_target_pairs={{0,15},{1,14},{2,13},{3,12},{4,11},{5,10},{6,9},{7,8},{8,7},{9,6},... | collective-permute-start | bytes 835592 | tf_op jit(solution)/shard_map/ppermute | solution.py:403
  95.1 30.8 %collective-permute-start.16 = (f32[432,128]{1,0:T(8,128)}, f32[432,128]{1,0:T(8,128)S(1)}, u32[]{:S(2)}, u32[]{:S(2)}) collective-permute-start(f32[432,128]{1,0:T(8,128)} %get-tuple-element.80), channel_id=1, source_target_pairs={{0,8},{1,9},{2,10},{3,11},{4,12},{5,13},{6,14},{7,15},{8,0},{9,1},... | collective-permute-start | bytes 663560 | tf_op jit(solution)/shard_map/ppermute | solution.py:403
  103.1 28.5 %collective-permute-start.17 = (f32[432,128]{1,0:T(8,128)}, f32[432,128]{1,0:T(8,128)S(1)}, u32[]{:S(2)}, u32[]{:S(2)}) collective-permute-start(f32[432,128]{1,0:T(8,128)} %get-tuple-element.81), channel_id=1, source_target_pairs={{0,1},{1,0},{2,3},{3,2},{4,5},{5,4},{6,7},{7,6},{8,9},{9,8},{10,11... | collective-permute-start | bytes 663560 | tf_op jit(solution)/shard_map/ppermute | solution.py:403
  103.3 28.4 %collective-permute-start.18 = (f32[432,128]{1,0:T(8,128)}, f32[432,128]{1,0:T(8,128)S(1)}, u32[]{:S(2)}, u32[]{:S(2)}) collective-permute-start(f32[432,128]{1,0:T(8,128)} %get-tuple-element.82), channel_id=1, source_target_pairs={{0,9},{1,8},{2,11},{3,10},{4,13},{5,12},{6,15},{7,14},{8,1},{9,0},... | collective-permute-start | bytes 663560 | tf_op jit(solution)/shard_map/ppermute | solution.py:403
  117.6 71.1 %collective-permute-start.15 = (f32[1728,128]{1,0:T(8,128)}, f32[1728,128]{1,0:T(8,128)S(1)}, u32[]{:S(2)}, u32[]{:S(2)}) collective-permute-start(f32[1728,128]{1,0:T(8,128)} %shard_map.107.own_ref), channel_id=1, source_target_pairs={{0,16},{16,0},{1,17},{17,1},{2,18},{18,2},{3,19},{19,3},{4,20},{20... | collective-permute-start | bytes 2654216 | tf_op jit(solution)/shard_map/ppermute | solution.py:457
  125.9 20.8 %collective-permute-start.20 = (f32[432,128]{1,0:T(8,128)S(1)}, f32[432,128]{1,0:T(8,128)S(1)}, u32[]{:S(2)}, u32[]{:S(2)}) collective-permute-start(f32[432,128]{1,0:T(8,128)S(1)} %copy-done.56), channel_id=1, source_target_pairs={{0,10},{1,11},{2,8},{3,9},{4,14},{5,15},{6,12},{7,13},{8,2},{9,3},... | collective-permute-start | bytes 663560 | tf_op jit(solution)/shard_map/ppermute | solution.py:403
  132.7 28.5 %collective-permute-start.23 = (f32[432,128]{1,0:T(8,128)S(1)}, f32[432,128]{1,0:T(8,128)S(1)}, u32[]{:S(2)}, u32[]{:S(2)}) collective-permute-start(f32[432,128]{1,0:T(8,128)S(1)} %copy-done.53), channel_id=1, source_target_pairs={{0,4},{1,5},{2,6},{3,7},{4,0},{5,1},{6,2},{7,3},{8,12},{9,13},{10,... | collective-permute-start | bytes 663560 | tf_op jit(solution)/shard_map/ppermute | solution.py:403
  149.6 19.9 %collective-permute-start.25 = (f32[432,128]{1,0:T(8,128)S(1)}, f32[432,128]{1,0:T(8,128)S(1)}, u32[]{:S(2)}, u32[]{:S(2)}) collective-permute-start(f32[432,128]{1,0:T(8,128)S(1)} %copy-done.51), channel_id=1, source_target_pairs={{0,5},{1,4},{2,7},{3,6},{4,1},{5,0},{6,3},{7,2},{8,13},{9,12},{10,... | collective-permute-start | bytes 663560 | tf_op jit(solution)/shard_map/ppermute | solution.py:403
  150.6 19.0 %collective-permute-start.26 = (f32[432,128]{1,0:T(8,128)S(1)}, f32[432,128]{1,0:T(8,128)S(1)}, u32[]{:S(2)}, u32[]{:S(2)}) collective-permute-start(f32[432,128]{1,0:T(8,128)S(1)} %copy-done.50), channel_id=1, source_target_pairs={{0,13},{1,12},{2,15},{3,14},{4,9},{5,8},{6,11},{7,10},{8,5},{9,4},... | collective-permute-start | bytes 663560 | tf_op jit(solution)/shard_map/ppermute | solution.py:403
  161.2 24.5 %collective-permute-start.27 = (f32[432,128]{1,0:T(8,128)S(1)}, f32[432,128]{1,0:T(8,128)S(1)}, u32[]{:S(2)}, u32[]{:S(2)}) collective-permute-start(f32[432,128]{1,0:T(8,128)S(1)} %copy-done.49), channel_id=1, source_target_pairs={{0,6},{1,7},{2,4},{3,5},{4,2},{5,3},{6,0},{7,1},{8,14},{9,15},{10,... | collective-permute-start | bytes 663560 | tf_op jit(solution)/shard_map/ppermute | solution.py:403
  161.3 24.5 %collective-permute-start.28 = (f32[432,128]{1,0:T(8,128)S(1)}, f32[432,128]{1,0:T(8,128)S(1)}, u32[]{:S(2)}, u32[]{:S(2)}) collective-permute-start(f32[432,128]{1,0:T(8,128)S(1)} %copy-done.48), channel_id=1, source_target_pairs={{0,14},{1,15},{2,12},{3,13},{4,10},{5,11},{6,8},{7,9},{8,6},{9,7},... | collective-permute-start | bytes 663560 | tf_op jit(solution)/shard_map/ppermute | solution.py:403
  169.6 19.2 %collective-permute-start.29 = (f32[432,128]{1,0:T(8,128)S(1)}, f32[432,128]{1,0:T(8,128)S(1)}, u32[]{:S(2)}, u32[]{:S(2)}) collective-permute-start(f32[432,128]{1,0:T(8,128)S(1)} %copy-done.47), channel_id=1, source_target_pairs={{0,7},{1,6},{2,5},{3,4},{4,3},{5,2},{6,1},{7,0},{8,15},{9,14},{10,... | collective-permute-start | bytes 663560 | tf_op jit(solution)/shard_map/ppermute | solution.py:403
  169.6 19.2 %collective-permute-start.30 = (f32[432,128]{1,0:T(8,128)S(1)}, f32[432,128]{1,0:T(8,128)S(1)}, u32[]{:S(2)}, u32[]{:S(2)}) collective-permute-start(f32[432,128]{1,0:T(8,128)S(1)} %copy-done.46), channel_id=1, source_target_pairs={{0,15},{1,14},{2,13},{3,12},{4,11},{5,10},{6,9},{7,8},{8,7},{9,6},... | collective-permute-start | bytes 663560 | tf_op jit(solution)/shard_map/ppermute | solution.py:403
  199.0 71.1 %all-to-all-start = ((f32[16,432,128]{2,1,0:T(8,128)}), f32[16,432,128]{2,1,0:T(8,128)S(1)}, u32[]{:S(2)}, u32[]{:S(2)}) async-start(f32[16,432,128]{2,1,0:T(8,128)} %bitcast.14), calls=%async_computation | async-start | bytes 7077888 | tf_op jit(solution)/shard_map/all_to_all | solution.py:409
  283.5 61.0 %all-to-all-start.1 = ((f32[32,112,128]{2,1,0:T(8,128)}), f32[32,112,128]{2,1,0:T(8,128)S(1)}, u32[]{:S(2)}, u32[]{:S(2)}) async-start(f32[32,112,128]{2,1,0:T(8,128)} %bitcast.19), calls=%async_computation.1 | async-start | bytes 3670016 | tf_op jit(solution)/shard_map/all_to_all | solution.py:413
  300.4 50.4 %collective-permute-start.31 = (f32[1728,128]{1,0:T(8,128)S(1)}, f32[1728,128]{1,0:T(8,128)}, u32[]{:S(2)}, u32[]{:S(2)}) collective-permute-start(f32[1728,128]{1,0:T(8,128)S(1)} %copy-done.19), channel_id=1, source_target_pairs={{0,16},{16,0},{1,17},{17,1},{2,18},{18,2},{3,19},{19,3},{4,20},{20... | collective-permute-start | bytes 2654216 | tf_op jit(solution)/shard_map/ppermute | solution.py:508
  350.8 46.9 %all-to-all-start.2 = ((f32[32,112,128]{2,1,0:T(8,128)}), f32[32,112,128]{2,1,0:T(8,128)S(1)}, u32[]{:S(2)}, u32[]{:S(2)}) async-start(f32[32,112,128]{2,1,0:T(8,128)} %bitcast.17), calls=%async_computation.2 | async-start | bytes 3670016 | tf_op jit(solution)/shard_map/all_to_all | solution.py:413
  353.7 39.6 %collective-permute-start.32 = (f32[1728,128]{1,0:T(8,128)S(1)}, f32[1728,128]{1,0:T(8,128)}, u32[]{:S(2)}, u32[]{:S(2)}) collective-permute-start(f32[1728,128]{1,0:T(8,128)S(1)} %copy-done.20), channel_id=1, source_target_pairs={{0,16},{16,0},{1,17},{17,1},{2,18},{18,2},{3,19},{19,3},{4,20},{20... | collective-permute-start | bytes 2654216 | tf_op jit(solution)/shard_map/ppermute | solution.py:509
  (62 other events, 1920.6 us)

commit v5 on v4

--- a/solution.py
+++ b/solution.py
@@ -168,7 +168,7 @@
     planes, grid, rows, share = sizes
     *out_refs, packed = refs
     stride = 2 * rows + share
-    band, mine = place_ref[0], place_ref[1]
+    band, mine = place_ref[0] // grid, place_ref[0] % grid
     for out_ref in out_refs:
         fill(out_ref, 1, chunk_rows(sizes)[0], planes * stride)
     for inner in range(bunch):
@@ -189,7 +189,7 @@
 def plane_kernel(sizes, bunch, turns, place_ref, psi_ref, ion_ref, hxc_ref, kin_ref, *refs):
     planes, grid, rows, share = sizes
     *out_refs, base_ref, packed = refs
-    mine = place_ref[1]
+    mine = place_ref[0] % grid
     kin = split(kin_ref[...])
     for inner in range(bunch):
         plane = pl.program_id(0) * bunch + inner
@@ -220,7 +220,7 @@
     length = planes * grid
     stride = 2 * rows + share
     for turn, moved_ref in zip(turns, moved_refs):
-        first = (place_ref[1] ^ turn) * planes
+        first = (place_ref[0] % grid ^ turn) * planes
         for row in range(share):
             out_ref[pl.ds(row * length + first, planes), :] = moved_ref[pl.ds(2 * rows + row, planes, stride=stride), :]
 
@@ -231,7 +231,7 @@
     stride = 2 * rows + share
     row = pl.program_id(0)
     for turn, moved_ref in zip(turns, moved_refs):
-        first = (place_ref[1] ^ turn) * planes
+        first = (place_ref[0] % grid ^ turn) * planes
         for part in range(2):
             lines[part, pl.ds(first, planes), :] = moved_ref[pl.ds(part * rows + row, planes, stride=stride), :]
     out_ref[...] = product(kin_ref[...], jnp.concatenate([lines[0], lines[1]], axis=1))
@@ -243,13 +243,13 @@
     length = planes * grid
     kin = split(kin_ref[...])
     step = pl.program_id(0)
-    mine_here = place_ref[0] == step // (steps // 2)
+    mine_here = place_ref[0] // grid == step // (steps // 2)
     for inner in range(rows // steps):
         row = step * (rows // steps) + inner
         here = slice(inner * length, (inner + 1) * length)
         slot = lines.at[inner]
         for turn, mixed_ref in zip(turns, mixed_refs):
-            first = (place_ref[1] ^ turn) * planes
+            first = (place_ref[0] % grid ^ turn) * planes
             for part in range(2):
                 slot[part, pl.ds(first, planes), :] = mixed_ref[pl.ds(part * rows + row, planes, stride=2 * rows), :]
         along = along_ref[here, :]
@@ -265,7 +265,7 @@
 
 
 def fresh_kernel(
-    sizes, bunch, occ_ref, update_ref, base_ref, basis_ref, turn_ref, fresh_ref, upper_ref, lower_ref, out_ref, packed
+    sizes, bunch, occ_ref, update_ref, base_ref, tables_ref, fresh_ref, upper_ref, lower_ref, out_ref, packed
 ):
     planes, grid, rows, share = sizes
     length = planes * grid
@@ -290,12 +290,12 @@
         upper_ref[inner * half : (inner + 1) * half, :] = slot[:half, :]
         lower_ref[inner * half : (inner + 1) * half, :] = slot[half:, :]
         slot = packed.at[inner * 4 + 3]
-        pack(product(product(basis_ref[...], part_sum), turn_ref[...]), slot)
+        pack(product(product(tables_ref[0], part_sum), tables_ref[1]), slot)
         for to in range(2 * grid):
             out_ref[pl.ds(to * chunk + plane * share, share), :] = slot[pl.ds(to * share, share), :]
 
 
-def filter_kernel(sizes, spec_ref, cells_ref, squares_ref, basis_ref, turn_ref, out_ref, lines):
+def filter_kernel(sizes, spec_ref, cells_ref, tables_ref, out_ref, lines):
     planes, grid, rows, share = sizes
     length = planes * grid
     chunk = chunk_rows(sizes)[1]
@@ -311,11 +311,13 @@
 
     for first, second, here in places():
         lines[here] = spec_ref[first, :] + spec_ref[second, :]
-    total = squares_ref[...] + cells_ref[...]
+    index = lax.broadcasted_iota(jnp.int32, lines.shape, 0)
+    order = jnp.where(index <= length // 2, index, index - length // 2).astype(jnp.float32)
+    total = order * order + cells_ref[...]
     scale = length * math.sqrt(length) / 16.0
     kernel = jnp.where(total > 0.0, scale / (total + 1.0), 0.0)
-    field = kernel * product(basis_ref[...], lines[...])
-    lines[...] = product_of_parts(split(turn_ref[...]), split(field))
+    field = kernel * product(tables_ref[0], lines[...])
+    lines[...] = product_of_parts(split(tables_ref[1]), split(field))
     for first, second, here in places():
         piece = lines[here]
         out_ref[first, :] = piece
@@ -327,13 +329,13 @@
 
 
 def last_kernel(
-    sizes, bunch, spec_ref, upper_ref, lower_ref, upper_other, lower_other, basis_ref, turn_ref, out_ref, packed
+    sizes, bunch, spec_ref, upper_ref, lower_ref, upper_other, lower_other, tables_ref, out_ref, packed
 ):
     planes, grid, rows, share = sizes
     length = planes * grid
     half = rows * grid // 2
     chunk = chunk_rows(sizes)[1]
-    turn, basis = split(turn_ref[...]), split(basis_ref[...])
+    turn, basis = split(tables_ref[1]), split(tables_ref[0])
     for inner in range(bunch):
         plane = pl.program_id(0) * bunch + inner
         slot = packed.at[inner * 2]
@@ -358,18 +360,25 @@
     return pl.BlockSpec(dims, lambda *_: (0,) * len(dims))
 
 
-PARAMS = pltpu.CompilerParams(vmem_limit_bytes=56 << 20)
+SMALL = pltpu.CompilerParams(vmem_limit_bytes=24 << 20)
+PARAMS = pltpu.CompilerParams(vmem_limit_bytes=54 << 20)
 
 
 def cost(flops, moved):
     return pl.CostEstimate(flops=flops, bytes_accessed=moved, transcendentals=0)
 
 
-def turn_order(grid):
-    order = [0]
-    for near in range(grid // 2):
-        order += [near + grid // 2] if near == 0 else [near, near + grid // 2]
-    return order
+def turn_orders(grid):
+    half = grid // 2
+    near, far = list(range(1, half)), list(range(half, grid))
+    first, second = [], far[:3]
+    for index in range(half):
+        first += far[index : index + 1] + (near[index : index + 1] if index < half - 4 else [])
+    first += near[half - 4 :]
+    for index in range(3, half):
+        second += near[index - 3 : index - 2] + far[index : index + 1]
+    second = second[:-1] + near[half - 3 :] + second[-1:]
+    return [0] + first, [0] + second
 
 
 def packed_path(orbitals, occupations, ion_potential, hxc_potential):
@@ -382,10 +391,10 @@
     sizes = (planes, grid, rows, share)
     field = planes * cell_rows
     work = 2 * planes * length**3
-    place = jnp.stack([lax.axis_index("band"), lax.axis_index("grid")]).astype(jnp.int32)
+    place = lax.axis_index(("band", "grid")).astype(jnp.int32).reshape(1)
     kin = jnp.asarray(kinetic_matrix(length))
     basis_np, squares_np = real_basis(length)
-    basis, turn = jnp.asarray(basis_np), jnp.asarray(basis_np.T.copy())
+    tables = jnp.asarray(np.stack([basis_np, basis_np.T]))
     smem = pl.BlockSpec(memory_space=pltpu.SMEM)
     vmem = pl.BlockSpec(memory_space=pltpu.VMEM)
     bunch = next(count for count in (3, 2, 1) if planes % count == 0)
@@ -394,6 +403,7 @@
     pair_spec = pl.BlockSpec((2, bunch, length, length), lambda i: (0, i, 0, 0))
     half_rows = pl.BlockSpec((bunch * cell_rows // 2, LANES), lambda i: (i, 0))
     square = whole(length, length)
+    table_spec = whole(2, length, length)
 
     def scratch(count):
         return [pltpu.VMEM((count * bunch, cell_rows, LANES), jnp.float32)]
@@ -412,13 +422,13 @@
         flat = array.reshape(2 * grid, -1, LANES)
         return lax.all_to_all(flat, ("band", "grid"), split_axis=0, concat_axis=0).reshape(array.shape)
 
-    turns = turn_order(grid)
+    first_turns, turns = turn_orders(grid)
     moved_rows, spec_rows = chunk_rows(sizes)
     spec_rows = 2 * grid * spec_rows
     mixed_rows = 2 * planes * rows
     steps = 6 if rows % 6 == 0 and share % (rows // 6) == 0 else 2
     moved = pl.pallas_call(
-        functools.partial(pack_kernel, sizes, bunch, turns),
+        functools.partial(pack_kernel, sizes, bunch, first_turns),
         grid=(planes // bunch,),
         in_specs=[smem, psi_spec, plane_spec, plane_spec],
         out_specs=[whole(moved_rows, LANES)] * grid,
@@ -443,11 +453,10 @@
     moved = list(moved)
     for k, piece in zip(late, held[0]):
         moved[k] = piece
-    moved = swap_pieces(turns, moved)
-    mixed = swap_pieces(turns, mixed)
+    moved = swap_pieces(first_turns, moved)
 
     own = pl.pallas_call(
-        functools.partial(share_kernel, sizes, turns),
+        functools.partial(share_kernel, sizes, first_turns),
         in_specs=[smem] + [vmem] * grid,
         out_specs=vmem,
         out_shape=shape(share * length, LANES),
@@ -456,7 +465,7 @@
     )(place, *moved)
     other = lax.ppermute(own, "band", [(0, 1), (1, 0)])
     along = pl.pallas_call(
-        functools.partial(along_kernel, sizes, turns),
+        functools.partial(along_kernel, sizes, first_turns),
         grid=(rows,),
         in_specs=[smem] + [whole(moved_rows, LANES)] * grid + [square],
         out_specs=pl.BlockSpec((length, 2 * LANES), lambda i: (i, 0)),
@@ -465,6 +474,12 @@
         compiler_params=PARAMS,
         cost_estimate=cost(2 * 6 * work, 10 << 20),
     )(place, *moved, kin)
+    late = range(5, grid)
+    held = lax.optimization_barrier(([mixed[k] for k in late], along))
+    along = held[1]
+    for k, piece in zip(late, held[0]):
+        mixed[k] = piece
+    mixed = swap_pieces(turns, mixed)
     half_spec = pl.BlockSpec((rows // steps * length, LANES), lambda i: (i % (steps // 2), 0))
     update = pl.pallas_call(
         functools.partial(update_kernel, sizes, steps, turns),
@@ -488,7 +503,7 @@
     fresh, upper, lower, spectrum = pl.pallas_call(
         functools.partial(fresh_kernel, sizes, bunch),
         grid=(planes // bunch,),
-        in_specs=[smem, whole(2 * field, LANES), pair_spec, square, square],
+        in_specs=[smem, vmem, pair_spec, table_spec],
         out_specs=[
             psi_spec,
             half_rows,
@@ -502,9 +517,9 @@
             shape(spec_rows, LANES),
         ],
         scratch_shapes=scratch(4),
-        compiler_params=PARAMS,
+        compiler_params=SMALL,
         cost_estimate=cost(2 * 6 * work, 16 << 20),
-    )(occupations, update, base, basis, turn)
+    )(occupations, update, base, tables)
     upper_other = lax.ppermute(upper, "band", [(0, 1), (1, 0)])
     lower_other = lax.ppermute(lower, "band", [(0, 1), (1, 0)])
 
@@ -518,33 +533,32 @@
     cells = lax.dynamic_slice_in_dim(jnp.asarray(cells_np), device * share, share, axis=0)
     spectrum = pl.pallas_call(
         functools.partial(filter_kernel, sizes),
-        in_specs=[vmem] * 5,
+        in_specs=[vmem] * 3,
         out_specs=vmem,
         out_shape=shape(spec_rows, LANES),
         scratch_shapes=[pltpu.VMEM((length, share * LANES), jnp.float32)],
-        compiler_params=PARAMS,
+        compiler_params=SMALL,
         cost_estimate=cost(6 * work, 5 << 20),
-    )(spectrum, cells.reshape(1, share * LANES), jnp.asarray(squares_np)[:, None], basis, turn)
+    )(spectrum, cells.reshape(1, share * LANES), tables)
     spectrum, upper_other = lax.optimization_barrier((spectrum, upper_other))
     spectrum = swap_all(spectrum)
     potential = pl.pallas_call(
         functools.partial(last_kernel, sizes, bunch),
         grid=(planes // bunch,),
         in_specs=[
-            whole(spec_rows, LANES),
+            vmem,
             half_rows,
             half_rows,
             half_rows,
             half_rows,
-            square,
-            square,
+            table_spec,
         ],
         out_specs=plane_spec,
         out_shape=shape(planes, length, length),
         scratch_shapes=scratch(2),
         compiler_params=PARAMS,
         cost_estimate=cost(2 * 6 * work, 6 << 20),
-    )(spectrum, upper, lower, upper_other, lower_other, basis, turn)
+    )(spectrum, upper, lower, upper_other, lower_other, tables)
     return (fresh, potential)
 
 

time: 407 us -> 417 us (1.025)
  starting transfers between devices: 111 us -> 120 us
  Pallas kernels: 69.2 us -> 63.2 us
  waiting for transfers between devices: 216 us -> 221 us
    ppermute x30, starting transfers between devices: 81.6 us -> 88.2 us  [swap_pieces(): lax.ppermute(piece, 'grid', [(place, place ^ turn) for place in range(gri...]
    ppermute x30, waiting for transfers between devices: 66.7 us -> 71.7 us  [swap_pieces(): lax.ppermute(piece, 'grid', [(place, place ^ turn) for place in range(gri...]
    unnamed x118 -> x128, local copies, waits for them, and re-layouts: 7.49 us -> 10.1 us
  transfers between devices with their start and end apart: 36 -> 36, of which waited for: 17 -> 18; matrix products, arithmetic and copies ran while one was open for 0% -> 0% of each run, Pallas kernels for 8% -> 8%
where the time goes in v5:
time: 417 us; the launch traced here: 416 us
  waiting for transfers between devices  221 us (53%)
  starting transfers between devices  120 us (29%)
  Pallas kernels  63.2 us (15%)
  local copies, waits for them, and re-layouts  10.1 us (2%)
    ppermute x30, starting transfers between devices, swap_pieces(): lax.ppermute(piece, 'grid', [(place, place ^ turn) for place in range(gri...  88.2 us
    ppermute x30, waiting for transfers between devices, swap_pieces(): lax.ppermute(piece, 'grid', [(place, place ^ turn) for place in range(gri...  71.7 us
    all_to_all x1, waiting for transfers between devices, swap(): lax.all_to_all(flat, 'grid', split_axis=0, concat_axis=0)  65.6 us
    all_to_all x2, waiting for transfers between devices, swap_all(): lax.all_to_all(flat, ('band', 'grid'), split_axis=0, concat_axis=0)  46.2 us
    ppermute x1, waiting for transfers between devices, packed_path(): lower_other = lax.ppermute(lower, 'band', [(0, 1), (1, 0)])  37.8 us
    all_to_all x2, starting transfers between devices, swap_all(): lax.all_to_all(flat, ('band', 'grid'), split_axis=0, concat_axis=0)  20.5 us
    pallas_call x1, Pallas kernels, packed_path(): pl.pallas_call(functools.partial(plane_kernel, sizes, bunch, turns), grid...  13.8 us
    pallas_call x1, Pallas kernels, packed_path(): pl.pallas_call(functools.partial(along_kernel, sizes, first_turns), grid=...  12.3 us
  transfers between devices with their start and end apart: 36, of which 18 were waited for; matrix products, arithmetic and copies ran while one was open for 0% of the time, Pallas kernels for 8%

profile of v5, /device:TPU:0, one launch (start us, length us, event | category | flops | bytes accessed | tf_op | source)
XLA Modules:
  0.0 416.5 jit_solution(10006306292008735971)
XLA Ops:
  0.6 7.0 %shard_map.87 = (f32[544,128]{1,0:T(8,128)}, f32[544,128]{1,0:T(8,128)}, f32[544,128]{1,0:T(8,128)}, f32[544,128]{1,0:T(8,128)}, f32[544,128]{1,0:T(8,128)}, /*i...) custom-call(s32[1]{0:T(128)} %bitcast.place_ref, ...), custom_call_target="tpu_custom_call" | custom-call | bytes 15728640 | tf_op jit(solution)/shard_map/pallas_call | solution.py:430
  7.6 4.0 collective-permute-start
  16.3 13.8 %shard_map.86 = (f32[432,128]{1,0:T(8,128)}, f32[432,128]{1,0:T(8,128)}, f32[432,128]{1,0:T(8,128)}, f32[432,128]{1,0:T(8,128)}, f32[432,128]{1,0:T(8,128)}, /*i...) custom-call(s32[1]{0:T(128)} %bitcast.place_ref, ...), custom_call_target="tpu_custom_call" | custom-call | flops 4076863488 | bytes 20971520 | tf_op jit(solution)/shard_map/pallas_call | solution.py:440
  30.0 7.2 %collective-permute-done.refs_1_ = f32[544,128]{1,0:T(8,128)S(1)} collective-permute-done((f32[544,128]{1,0:T(8,128)}, f32[544,128]{1,0:T(8,128)S(1)}, u32[]{:S(2)}, u32[]{:S(2)}) %collective-permute-start) | collective-permute-done | bytes 278560 | tf_op jit(solution)/shard_map/ppermute | solution.py:413
  38.1 3.4 collective-permute-done.2.refs_3_
  41.6 7.7 %collective-permute-start.7 = (f32[544,128]{1,0:T(8,128)S(1)}, f32[544,128]{1,0:T(8,128)S(1)}, u32[]{:S(2)}, u32[]{:S(2)}) collective-permute-start(f32[544,128]{1,0:T(8,128)S(1)} %copy-done.48), channel_id=1, source_target_pairs={{0,4},{1,5},{2,6},{3,7},{4,0},{5,1},{6,2},{7,3},{8,12},{9,13},{10,... | collective-permute-start | bytes 835592 | tf_op jit(solution)/shard_map/ppermute | solution.py:413
  51.9 4.6 %collective-permute-done.4.refs_5_ = f32[544,128]{1,0:T(8,128)S(1)} collective-permute-done((f32[544,128]{1,0:T(8,128)}, f32[544,128]{1,0:T(8,128)S(1)}, u32[]{:S(2)}, u32[]{:S(2)}) %collective-permute-start.4) | collective-permute-done | bytes 278560 | tf_op jit(solution)/shard_map/ppermute | solution.py:413
  59.1 19.1 %collective-permute-done.6.refs_7_ = f32[544,128]{1,0:T(8,128)S(1)} collective-permute-done((f32[544,128]{1,0:T(8,128)S(1)}, f32[544,128]{1,0:T(8,128)S(1)}, u32[]{:S(2)}, u32[]{:S(2)}) %collective-permute-start.6) | collective-permute-done | bytes 278560 | tf_op jit(solution)/shard_map/ppermute | solution.py:413
  78.1 4.2 %collective-permute-start.11 = (f32[544,128]{1,0:T(8,128)S(1)}, f32[544,128]{1,0:T(8,128)S(1)}, u32[]{:S(2)}, u32[]{:S(2)}) collective-permute-start(f32[544,128]{1,0:T(8,128)S(1)} %copy-done.44), channel_id=1, source_target_pairs={{0,15},{1,14},{2,13},{3,12},{4,11},{5,10},{6,9},{7,8},{8,7},{9,6},... | collective-permute-start | bytes 835592 | tf_op jit(solution)/shard_map/ppermute | solution.py:413
  82.3 7.8 %collective-permute-done.7.refs_8_ = f32[544,128]{1,0:T(8,128)S(1)} collective-permute-done((f32[544,128]{1,0:T(8,128)S(1)}, f32[544,128]{1,0:T(8,128)S(1)}, u32[]{:S(2)}, u32[]{:S(2)}) %collective-permute-start.7) | collective-permute-done | bytes 278560 | tf_op jit(solution)/shard_map/ppermute | solution.py:413
  92.9 5.7 %collective-permute-start.14 = (f32[544,128]{1,0:T(8,128)S(1)}, f32[544,128]{1,0:T(8,128)S(1)}, u32[]{:S(2)}, u32[]{:S(2)}) collective-permute-start(f32[544,128]{1,0:T(8,128)S(1)} %copy-done.41), channel_id=1, source_target_pairs={{0,7},{1,6},{2,5},{3,4},{4,3},{5,2},{6,1},{7,0},{8,15},{9,14},{10,... | collective-permute-start | bytes 835592 | tf_op jit(solution)/shard_map/ppermute | solution.py:413
  98.6 11.2 %collective-permute-start.16 = (f32[432,128]{1,0:T(8,128)}, f32[432,128]{1,0:T(8,128)S(1)}, u32[]{:S(2)}, u32[]{:S(2)}) collective-permute-start(f32[432,128]{1,0:T(8,128)} %get-tuple-element.104), channel_id=1, source_target_pairs={{0,8},{1,9},{2,10},{3,11},{4,12},{5,13},{6,14},{7,15},{8,0},{9,1},... | collective-permute-start | bytes 663560 | tf_op jit(solution)/shard_map/ppermute | solution.py:413
  109.7 11.2 %collective-permute-start.17 = (f32[432,128]{1,0:T(8,128)}, f32[432,128]{1,0:T(8,128)S(1)}, u32[]{:S(2)}, u32[]{:S(2)}) collective-permute-start(f32[432,128]{1,0:T(8,128)} %get-tuple-element.105), channel_id=1, source_target_pairs={{0,9},{1,8},{2,11},{3,10},{4,13},{5,12},{6,15},{7,14},{8,1},{9,0},... | collective-permute-start | bytes 663560 | tf_op jit(solution)/shard_map/ppermute | solution.py:413
  127.2 12.3 %shard_map.88.along_ref = f32[3456,256]{1,0:T(8,128)} custom-call(s32[1]{0:T(128)} %bitcast.place_ref, f32[544,128]{1,0:T(8,128)} %get-tuple-element.75.refs_0_, f32[544,128]{1,0:T(8,128)} %copy-done.9, f32[544,128]{1,0:T(8,128)} %copy-done.10, f32[544,128]{1,0:T(8,128)} %copy-done.11, f32[544,128]{1,0:T(8,128)} %copy-done.12, f32[544,128]{1,0:T(8,128)} %copy-done.13, ...), custom_call_target="tpu_custom_call" | custom-call | flops 2038431744 | bytes 10485760 | tf_op jit(solution)/shard_map/pallas_call | solution.py:467
  143.5 7.7 %collective-permute-done.18.refs_3_ = f32[432,128]{1,0:T(8,128)S(1)} collective-permute-done((f32[432,128]{1,0:T(8,128)}, f32[432,128]{1,0:T(8,128)S(1)}, u32[]{:S(2)}, u32[]{:S(2)}) %collective-permute-start.18) | collective-permute-done | bytes 221216 | tf_op jit(solution)/shard_map/ppermute | solution.py:413
  155.4 12.8 %collective-permute-start.24 = (f32[432,128]{1,0:T(8,128)S(1)}, f32[432,128]{1,0:T(8,128)S(1)}, u32[]{:S(2)}, u32[]{:S(2)}) collective-permute-start(f32[432,128]{1,0:T(8,128)S(1)} %copy-done.57), channel_id=1, source_target_pairs={{0,13},{1,12},{2,15},{3,14},{4,9},{5,8},{6,11},{7,10},{8,5},{9,4},... | collective-permute-start | bytes 663560 | tf_op jit(solution)/shard_map/ppermute | solution.py:413
  168.4 4.2 %collective-permute-start.27 = (f32[432,128]{1,0:T(8,128)S(1)}, f32[432,128]{1,0:T(8,128)S(1)}, u32[]{:S(2)}, u32[]{:S(2)}) collective-permute-start(f32[432,128]{1,0:T(8,128)S(1)} %copy-done.54), channel_id=1, source_target_pairs={{0,5},{1,4},{2,7},{3,6},{4,1},{5,0},{6,3},{7,2},{8,13},{9,12},{10,... | collective-permute-start | bytes 663560 | tf_op jit(solution)/shard_map/ppermute | solution.py:413
  174.3 5.9 %collective-permute-start.28 = (f32[432,128]{1,0:T(8,128)S(1)}, f32[432,128]{1,0:T(8,128)S(1)}, u32[]{:S(2)}, u32[]{:S(2)}) collective-permute-start(f32[432,128]{1,0:T(8,128)S(1)} %copy-done.53), channel_id=1, source_target_pairs={{0,6},{1,7},{2,4},{3,5},{4,2},{5,3},{6,0},{7,1},{8,14},{9,15},{10,... | collective-permute-start | bytes 663560 | tf_op jit(solution)/shard_map/ppermute | solution.py:413
  181.9 4.7 %collective-permute-done.27.refs_12_ = f32[432,128]{1,0:T(8,128)S(1)} collective-permute-done((f32[432,128]{1,0:T(8,128)S(1)}, f32[432,128]{1,0:T(8,128)S(1)}, u32[]{:S(2)}, u32[]{:S(2)}) %collective-permute-start.27) | collective-permute-done | bytes 221216 | tf_op jit(solution)/shard_map/ppermute | solution.py:413
  186.6 4.7 %collective-permute-done.28.refs_13_ = f32[432,128]{1,0:T(8,128)S(1)} collective-permute-done((f32[432,128]{1,0:T(8,128)S(1)}, f32[432,128]{1,0:T(8,128)S(1)}, u32[]{:S(2)}, u32[]{:S(2)}) %collective-permute-start.28) | collective-permute-done | bytes 221216 | tf_op jit(solution)/shard_map/ppermute | solution.py:413
  191.4 4.6 %collective-permute-done.29.refs_14_ = f32[432,128]{1,0:T(8,128)S(1)} collective-permute-done((f32[432,128]{1,0:T(8,128)S(1)}, f32[432,128]{1,0:T(8,128)S(1)}, u32[]{:S(2)}, u32[]{:S(2)}) %collective-permute-start.29) | collective-permute-done | bytes 221216 | tf_op jit(solution)/shard_map/ppermute | solution.py:413
  196.0 3.7 collective-permute-done.30.refs_15_
  200.7 9.0 %shard_map.90 = f32[6912,128]{1,0:T(8,128)} custom-call(s32[1]{0:T(128)} %bitcast.place_ref, f32[3456,256]{1,0:T(8,128)} %shard_map.88.along_ref, f32[1728,128]{1,0:T(8,128)} %shard_map.89.own_ref, f32[1728,128]{1,0:T(8,128)} %copy-done.24, f32[192,192]{1,0:T(8,128)} %constant.23.clone.kin_ref.refs_16_, f32[432,128]{1,0:T(8,128)} %get-tuple-element.103.refs_0_, ...), custom_call_target="tpu_custom_call" | custom-call | flops 1019215872 | bytes 14680064 | tf_op jit(solution)/shard_map/pallas_call | solution.py:484
  209.6 6.4 %all-to-all-start = ((f32[16,432,128]{2,1,0:T(8,128)}), f32[16,432,128]{2,1,0:T(8,128)S(1)}, u32[]{:S(2)}, u32[]{:S(2)}) async-start(f32[16,432,128]{2,1,0:T(8,128)} %bitcast.18), calls=%async_computation | async-start | bytes 7077888 | tf_op jit(solution)/shard_map/all_to_all | solution.py:419
  216.7 65.6 %all-to-all-done = f32[16,432,128]{2,1,0:T(8,128)S(1)} async-done(((f32[16,432,128]{2,1,0:T(8,128)}), f32[16,432,128]{2,1,0:T(8,128)S(1)}, u32[]{:S(2)}, u32[]{:S(2)}) %all-to-all-start) | async-done | bytes 3538976 | tf_op jit(solution)/shard_map/all_to_all | solution.py:419
  285.6 8.6 %shard_map.91 = (f32[1,2,12,192,192]{4,3,2,1,0:T(8,128)}, f32[1728,128]{1,0:T(8,128)S(1)}, f32[1728,128]{1,0:T(8,128)S(1)}, f32[3584,128]{1,0:T(8,128)S(1)}) custom-call(f32[1]{0:T(128)S(6)} %copy.12.occ_ref, f32[6912,128]{1,0:T(8,128)S(1)} %bitcast.13, f32[2,12,192,192]{3,2,1,0:T(8,128)S(1)} %copy-done.1, f32[2,192,192]{2,1,0:T(8,128)S(1)} %copy-done.2), custom_call_target="tpu_custom_call" | custom-call | flops 2038431744 | bytes 16777216 | tf_op jit(solution)/shard_map/pallas_call | solution.py:503
  297.2 16.9 %all-to-all-start.1 = ((f32[32,112,128]{2,1,0:T(8,128)}), f32[32,112,128]{2,1,0:T(8,128)S(1)}, u32[]{:S(2)}, u32[]{:S(2)}) async-start(f32[32,112,128]{2,1,0:T(8,128)} %bitcast.16), calls=%async_computation.1 | async-start | bytes 3670016 | tf_op jit(solution)/shard_map/all_to_all | solution.py:423
  316.8 41.5 %all-to-all-done.1 = f32[32,112,128]{2,1,0:T(8,128)S(1)} async-done(((f32[32,112,128]{2,1,0:T(8,128)}), f32[32,112,128]{2,1,0:T(8,128)S(1)}, u32[]{:S(2)}, u32[]{:S(2)}) %all-to-all-start.1) | async-done | bytes 1835040 | tf_op jit(solution)/shard_map/all_to_all | solution.py:423
  361.7 3.6 all-to-all-start.2
  367.0 37.8 %collective-permute-done.32.lower_other = f32[1728,128]{1,0:T(8,128)S(1)} collective-permute-done((f32[1728,128]{1,0:T(8,128)S(1)}, f32[1728,128]{1,0:T(8,128)S(1)}, u32[]{:S(2)}, u32[]{:S(2)}) %collective-permute-start.32) | collective-permute-done | bytes 884768 | tf_op jit(solution)/shard_map/ppermute | solution.py:524
  404.7 4.7 %all-to-all-done.2 = f32[32,112,128]{2,1,0:T(8,128)} async-done(((f32[32,112,128]{2,1,0:T(8,128)}), f32[32,112,128]{2,1,0:T(8,128)}, u32[]{:S(2)}, u32[]{:S(2)}) %all-to-all-start.2) | async-done | bytes 1835040 | tf_op jit(solution)/shard_map/all_to_all | solution.py:423
  409.4 7.1 %shard_map.93 = f32[12,192,192]{2,1,0:T(8,128)} custom-call(f32[3584,128]{1,0:T(8,128)} %bitcast.6.spec_ref, f32[1728,128]{1,0:T(8,128)} %copy-done.5, f32[1728,128]{1,0:T(8,128)} %copy-done.7, f32[1728,128]{1,0:T(8,128)} %collective-permute-done.31.upper_other, f32[1728,128]{1,0:T(8,128)} %copy-done.25, f32[2,192,192]{2,1,0:T(8,128)} %constant.24.clone.tables_ref), custom_call_target="tpu_custom_call" | custom-call | flops 2038431744 | bytes 6291456 | tf_op jit(solution)/shard_map/pallas_call | solution.py:545
  (176 shorter events, 46.2 us)
Async XLA Ops:
  7.6 29.6 %collective-permute-start = (f32[544,128]{1,0:T(8,128)}, f32[544,128]{1,0:T(8,128)S(1)}, u32[]{:S(2)}, u32[]{:S(2)}) collective-permute-start(f32[544,128]{1,0:T(8,128)} %get-tuple-element.76), channel_id=1, source_target_pairs={{0,8},{1,9},{2,10},{3,11},{4,12},{5,13},{6,14},{7,15},{8,0},{9,1},... | collective-permute-start | bytes 835592 | tf_op jit(solution)/shard_map/ppermute | solution.py:413
  11.6 25.6 %collective-permute-start.1 = (f32[544,128]{1,0:T(8,128)}, f32[544,128]{1,0:T(8,128)S(1)}, u32[]{:S(2)}, u32[]{:S(2)}) collective-permute-start(f32[544,128]{1,0:T(8,128)} %get-tuple-element.77), channel_id=1, source_target_pairs={{0,1},{1,0},{2,3},{3,2},{4,5},{5,4},{6,7},{7,6},{8,9},{9,8},{10,11... | collective-permute-start | bytes 835592 | tf_op jit(solution)/shard_map/ppermute | solution.py:413
  11.6 29.9 %collective-permute-start.2 = (f32[544,128]{1,0:T(8,128)}, f32[544,128]{1,0:T(8,128)S(1)}, u32[]{:S(2)}, u32[]{:S(2)}) collective-permute-start(f32[544,128]{1,0:T(8,128)} %get-tuple-element.78), channel_id=1, source_target_pairs={{0,9},{1,8},{2,11},{3,10},{4,13},{5,12},{6,15},{7,14},{8,1},{9,0},... | collective-permute-start | bytes 835592 | tf_op jit(solution)/shard_map/ppermute | solution.py:413
  11.8 37.4 %collective-permute-start.3 = (f32[544,128]{1,0:T(8,128)}, f32[544,128]{1,0:T(8,128)S(1)}, u32[]{:S(2)}, u32[]{:S(2)}) collective-permute-start(f32[544,128]{1,0:T(8,128)} %get-tuple-element.79), channel_id=1, source_target_pairs={{0,2},{1,3},{2,0},{3,1},{4,6},{5,7},{6,4},{7,5},{8,10},{9,11},{10,... | collective-permute-start | bytes 835592 | tf_op jit(solution)/shard_map/ppermute | solution.py:413
  13.7 42.9 %collective-permute-start.4 = (f32[544,128]{1,0:T(8,128)}, f32[544,128]{1,0:T(8,128)S(1)}, u32[]{:S(2)}, u32[]{:S(2)}) collective-permute-start(f32[544,128]{1,0:T(8,128)} %get-tuple-element.80), channel_id=1, source_target_pairs={{0,10},{1,11},{2,8},{3,9},{4,14},{5,15},{6,12},{7,13},{8,2},{9,3},... | collective-permute-start | bytes 835592 | tf_op jit(solution)/shard_map/ppermute | solution.py:413
  37.2 21.2 %collective-permute-start.5 = (f32[544,128]{1,0:T(8,128)S(1)}, f32[544,128]{1,0:T(8,128)S(1)}, u32[]{:S(2)}, u32[]{:S(2)}) collective-permute-start(f32[544,128]{1,0:T(8,128)S(1)} %copy-done.50), channel_id=1, source_target_pairs={{0,3},{1,2},{2,1},{3,0},{4,7},{5,6},{6,5},{7,4},{8,11},{9,10},{10,... | collective-permute-start | bytes 835592 | tf_op jit(solution)/shard_map/ppermute | solution.py:413
  37.3 40.9 %collective-permute-start.6 = (f32[544,128]{1,0:T(8,128)S(1)}, f32[544,128]{1,0:T(8,128)S(1)}, u32[]{:S(2)}, u32[]{:S(2)}) collective-permute-start(f32[544,128]{1,0:T(8,128)S(1)} %copy-done.49), channel_id=1, source_target_pairs={{0,11},{1,10},{2,9},{3,8},{4,15},{5,14},{6,13},{7,12},{8,3},{9,2},... | collective-permute-start | bytes 835592 | tf_op jit(solution)/shard_map/ppermute | solution.py:413
  41.6 48.5 %collective-permute-start.7 = (f32[544,128]{1,0:T(8,128)S(1)}, f32[544,128]{1,0:T(8,128)S(1)}, u32[]{:S(2)}, u32[]{:S(2)}) collective-permute-start(f32[544,128]{1,0:T(8,128)S(1)} %copy-done.48), channel_id=1, source_target_pairs={{0,4},{1,5},{2,6},{3,7},{4,0},{5,1},{6,2},{7,3},{8,12},{9,13},{10,... | collective-permute-start | bytes 835592 | tf_op jit(solution)/shard_map/ppermute | solution.py:413
  49.3 40.8 %collective-permute-start.8 = (f32[544,128]{1,0:T(8,128)S(1)}, f32[544,128]{1,0:T(8,128)S(1)}, u32[]{:S(2)}, u32[]{:S(2)}) collective-permute-start(f32[544,128]{1,0:T(8,128)S(1)} %copy-done.47), channel_id=1, source_target_pairs={{0,12},{1,13},{2,14},{3,15},{4,8},{5,9},{6,10},{7,11},{8,4},{9,5},... | collective-permute-start | bytes 835592 | tf_op jit(solution)/shard_map/ppermute | solution.py:413
  56.5 36.3 %collective-permute-start.9 = (f32[544,128]{1,0:T(8,128)S(1)}, f32[544,128]{1,0:T(8,128)S(1)}, u32[]{:S(2)}, u32[]{:S(2)}) collective-permute-start(f32[544,128]{1,0:T(8,128)S(1)} %copy-done.46), channel_id=1, source_target_pairs={{0,13},{1,12},{2,15},{3,14},{4,9},{5,8},{6,11},{7,10},{8,5},{9,4},... | collective-permute-start | bytes 835592 | tf_op jit(solution)/shard_map/ppermute | solution.py:413
  58.5 40.1 %collective-permute-start.10 = (f32[544,128]{1,0:T(8,128)S(1)}, f32[544,128]{1,0:T(8,128)S(1)}, u32[]{:S(2)}, u32[]{:S(2)}) collective-permute-start(f32[544,128]{1,0:T(8,128)S(1)} %copy-done.45), channel_id=1, source_target_pairs={{0,14},{1,15},{2,12},{3,13},{4,10},{5,11},{6,8},{7,9},{8,6},{9,7},... | collective-permute-start | bytes 835592 | tf_op jit(solution)/shard_map/ppermute | solution.py:413
  78.1 31.6 %collective-permute-start.11 = (f32[544,128]{1,0:T(8,128)S(1)}, f32[544,128]{1,0:T(8,128)S(1)}, u32[]{:S(2)}, u32[]{:S(2)}) collective-permute-start(f32[544,128]{1,0:T(8,128)S(1)} %copy-done.44), channel_id=1, source_target_pairs={{0,15},{1,14},{2,13},{3,12},{4,11},{5,10},{6,9},{7,8},{8,7},{9,6},... | collective-permute-start | bytes 835592 | tf_op jit(solution)/shard_map/ppermute | solution.py:413
  90.1 30.9 %collective-permute-start.12 = (f32[544,128]{1,0:T(8,128)S(1)}, f32[544,128]{1,0:T(8,128)S(1)}, u32[]{:S(2)}, u32[]{:S(2)}) collective-permute-start(f32[544,128]{1,0:T(8,128)S(1)} %copy-done.43), channel_id=1, source_target_pairs={{0,5},{1,4},{2,7},{3,6},{4,1},{5,0},{6,3},{7,2},{8,13},{9,12},{10,... | collective-permute-start | bytes 835592 | tf_op jit(solution)/shard_map/ppermute | solution.py:413
  90.1 31.3 %collective-permute-start.13 = (f32[544,128]{1,0:T(8,128)S(1)}, f32[544,128]{1,0:T(8,128)S(1)}, u32[]{:S(2)}, u32[]{:S(2)}) collective-permute-start(f32[544,128]{1,0:T(8,128)S(1)} %copy-done.42), channel_id=1, source_target_pairs={{0,6},{1,7},{2,4},{3,5},{4,2},{5,3},{6,0},{7,1},{8,14},{9,15},{10,... | collective-permute-start | bytes 835592 | tf_op jit(solution)/shard_map/ppermute | solution.py:413
  92.9 28.5 %collective-permute-start.14 = (f32[544,128]{1,0:T(8,128)S(1)}, f32[544,128]{1,0:T(8,128)S(1)}, u32[]{:S(2)}, u32[]{:S(2)}) collective-permute-start(f32[544,128]{1,0:T(8,128)S(1)} %copy-done.41), channel_id=1, source_target_pairs={{0,7},{1,6},{2,5},{3,4},{4,3},{5,2},{6,1},{7,0},{8,15},{9,14},{10,... | collective-permute-start | bytes 835592 | tf_op jit(solution)/shard_map/ppermute | solution.py:413
  98.6 40.9 %collective-permute-start.16 = (f32[432,128]{1,0:T(8,128)}, f32[432,128]{1,0:T(8,128)S(1)}, u32[]{:S(2)}, u32[]{:S(2)}) collective-permute-start(f32[432,128]{1,0:T(8,128)} %get-tuple-element.104), channel_id=1, source_target_pairs={{0,8},{1,9},{2,10},{3,11},{4,12},{5,13},{6,14},{7,15},{8,0},{9,1},... | collective-permute-start | bytes 663560 | tf_op jit(solution)/shard_map/ppermute | solution.py:413
  109.7 33.1 %collective-permute-start.17 = (f32[432,128]{1,0:T(8,128)}, f32[432,128]{1,0:T(8,128)S(1)}, u32[]{:S(2)}, u32[]{:S(2)}) collective-permute-start(f32[432,128]{1,0:T(8,128)} %get-tuple-element.105), channel_id=1, source_target_pairs={{0,9},{1,8},{2,11},{3,10},{4,13},{5,12},{6,15},{7,14},{8,1},{9,0},... | collective-permute-start | bytes 663560 | tf_op jit(solution)/shard_map/ppermute | solution.py:413
  121.0 30.3 %collective-permute-start.18 = (f32[432,128]{1,0:T(8,128)}, f32[432,128]{1,0:T(8,128)S(1)}, u32[]{:S(2)}, u32[]{:S(2)}) collective-permute-start(f32[432,128]{1,0:T(8,128)} %get-tuple-element.106), channel_id=1, source_target_pairs={{0,10},{1,11},{2,8},{3,9},{4,14},{5,15},{6,12},{7,13},{8,2},{9,3},... | collective-permute-start | bytes 663560 | tf_op jit(solution)/shard_map/ppermute | solution.py:413
  125.5 74.2 %collective-permute-start.15 = (f32[1728,128]{1,0:T(8,128)}, f32[1728,128]{1,0:T(8,128)S(1)}, u32[]{:S(2)}, u32[]{:S(2)}) collective-permute-start(f32[1728,128]{1,0:T(8,128)} %shard_map.89.own_ref), channel_id=1, source_target_pairs={{0,16},{16,0},{1,17},{17,1},{2,18},{18,2},{3,19},{19,3},{4,20},{20... | collective-permute-start | bytes 2654216 | tf_op jit(solution)/shard_map/ppermute | solution.py:466
  127.1 27.5 %collective-permute-start.19 = (f32[432,128]{1,0:T(8,128)S(1)}, f32[432,128]{1,0:T(8,128)S(1)}, u32[]{:S(2)}, u32[]{:S(2)}) collective-permute-start(f32[432,128]{1,0:T(8,128)S(1)} %copy-done.62), channel_id=1, source_target_pairs={{0,1},{1,0},{2,3},{3,2},{4,5},{5,4},{6,7},{7,6},{8,9},{9,8},{10,11... | collective-permute-start | bytes 663560 | tf_op jit(solution)/shard_map/ppermute | solution.py:413
  139.5 15.9 %collective-permute-start.20 = (f32[432,128]{1,0:T(8,128)S(1)}, f32[432,128]{1,0:T(8,128)S(1)}, u32[]{:S(2)}, u32[]{:S(2)}) collective-permute-start(f32[432,128]{1,0:T(8,128)S(1)} %copy-done.61), channel_id=1, source_target_pairs={{0,11},{1,10},{2,9},{3,8},{4,15},{5,14},{6,13},{7,12},{8,3},{9,2},... | collective-permute-start | bytes 663560 | tf_op jit(solution)/shard_map/ppermute | solution.py:413
  142.8 25.3 %collective-permute-start.21 = (f32[432,128]{1,0:T(8,128)S(1)}, f32[432,128]{1,0:T(8,128)S(1)}, u32[]{:S(2)}, u32[]{:S(2)}) collective-permute-start(f32[432,128]{1,0:T(8,128)S(1)} %copy-done.60), channel_id=1, source_target_pairs={{0,2},{1,3},{2,0},{3,1},{4,6},{5,7},{6,4},{7,5},{8,10},{9,11},{10,... | collective-permute-start | bytes 663560 | tf_op jit(solution)/shard_map/ppermute | solution.py:413
  151.3 17.0 %collective-permute-start.22 = (f32[432,128]{1,0:T(8,128)S(1)}, f32[432,128]{1,0:T(8,128)S(1)}, u32[]{:S(2)}, u32[]{:S(2)}) collective-permute-start(f32[432,128]{1,0:T(8,128)S(1)} %copy-done.59), channel_id=1, source_target_pairs={{0,12},{1,13},{2,14},{3,15},{4,8},{5,9},{6,10},{7,11},{8,4},{9,5},... | collective-permute-start | bytes 663560 | tf_op jit(solution)/shard_map/ppermute | solution.py:413
  155.4 19.0 %collective-permute-start.24 = (f32[432,128]{1,0:T(8,128)S(1)}, f32[432,128]{1,0:T(8,128)S(1)}, u32[]{:S(2)}, u32[]{:S(2)}) collective-permute-start(f32[432,128]{1,0:T(8,128)S(1)} %copy-done.57), channel_id=1, source_target_pairs={{0,13},{1,12},{2,15},{3,14},{4,9},{5,8},{6,11},{7,10},{8,5},{9,4},... | collective-permute-start | bytes 663560 | tf_op jit(solution)/shard_map/ppermute | solution.py:413
  168.4 18.3 %collective-permute-start.27 = (f32[432,128]{1,0:T(8,128)S(1)}, f32[432,128]{1,0:T(8,128)S(1)}, u32[]{:S(2)}, u32[]{:S(2)}) collective-permute-start(f32[432,128]{1,0:T(8,128)S(1)} %copy-done.54), channel_id=1, source_target_pairs={{0,5},{1,4},{2,7},{3,6},{4,1},{5,0},{6,3},{7,2},{8,13},{9,12},{10,... | collective-permute-start | bytes 663560 | tf_op jit(solution)/shard_map/ppermute | solution.py:413
  174.3 17.0 %collective-permute-start.28 = (f32[432,128]{1,0:T(8,128)S(1)}, f32[432,128]{1,0:T(8,128)S(1)}, u32[]{:S(2)}, u32[]{:S(2)}) collective-permute-start(f32[432,128]{1,0:T(8,128)S(1)} %copy-done.53), channel_id=1, source_target_pairs={{0,6},{1,7},{2,4},{3,5},{4,2},{5,3},{6,0},{7,1},{8,14},{9,15},{10,... | collective-permute-start | bytes 663560 | tf_op jit(solution)/shard_map/ppermute | solution.py:413
  181.9 17.8 %collective-permute-start.30 = (f32[432,128]{1,0:T(8,128)S(1)}, f32[432,128]{1,0:T(8,128)S(1)}, u32[]{:S(2)}, u32[]{:S(2)}) collective-permute-start(f32[432,128]{1,0:T(8,128)S(1)} %copy-done.51), channel_id=1, source_target_pairs={{0,15},{1,14},{2,13},{3,12},{4,11},{5,10},{6,9},{7,8},{8,7},{9,6},... | collective-permute-start | bytes 663560 | tf_op jit(solution)/shard_map/ppermute | solution.py:413
  209.6 72.6 %all-to-all-start = ((f32[16,432,128]{2,1,0:T(8,128)}), f32[16,432,128]{2,1,0:T(8,128)S(1)}, u32[]{:S(2)}, u32[]{:S(2)}) async-start(f32[16,432,128]{2,1,0:T(8,128)} %bitcast.18), calls=%async_computation | async-start | bytes 7077888 | tf_op jit(solution)/shard_map/all_to_all | solution.py:419
  297.2 61.0 %all-to-all-start.1 = ((f32[32,112,128]{2,1,0:T(8,128)}), f32[32,112,128]{2,1,0:T(8,128)S(1)}, u32[]{:S(2)}, u32[]{:S(2)}) async-start(f32[32,112,128]{2,1,0:T(8,128)} %bitcast.16), calls=%async_computation.1 | async-start | bytes 3670016 | tf_op jit(solution)/shard_map/all_to_all | solution.py:423
  314.2 47.5 %collective-permute-start.31 = (f32[1728,128]{1,0:T(8,128)S(1)}, f32[1728,128]{1,0:T(8,128)}, u32[]{:S(2)}, u32[]{:S(2)}) collective-permute-start(f32[1728,128]{1,0:T(8,128)S(1)} %copy-done.6), channel_id=1, source_target_pairs={{0,16},{16,0},{1,17},{17,1},{2,18},{18,2},{3,19},{19,3},{4,20},{20... | collective-permute-start | bytes 2654216 | tf_op jit(solution)/shard_map/ppermute | solution.py:523
  361.7 47.7 %all-to-all-start.2 = ((f32[32,112,128]{2,1,0:T(8,128)}), f32[32,112,128]{2,1,0:T(8,128)}, u32[]{:S(2)}, u32[]{:S(2)}) async-start(f32[32,112,128]{2,1,0:T(8,128)} %bitcast.15), calls=%async_computation.2 | async-start | bytes 3670016 | tf_op jit(solution)/shard_map/all_to_all | solution.py:423
  365.3 39.4 %collective-permute-start.32 = (f32[1728,128]{1,0:T(8,128)S(1)}, f32[1728,128]{1,0:T(8,128)S(1)}, u32[]{:S(2)}, u32[]{:S(2)}) collective-permute-start(f32[1728,128]{1,0:T(8,128)S(1)} %copy-done.8), channel_id=1, source_target_pairs={{0,16},{16,0},{1,17},{17,1},{2,18},{18,2},{3,19},{19,3},{4,20},{20... | collective-permute-start | bytes 2654216 | tf_op jit(solution)/shard_map/ppermute | solution.py:524
  (67 other events, 2095.4 us)

commit v6 on v5

--- a/solution.py
+++ b/solution.py
@@ -273,6 +273,7 @@
     cell_rows = rows * grid
     half = cell_rows // 2
     fill(out_ref, 2 * grid, chunk, planes * share)
+    means, parts = [], []
     for inner in range(bunch):
         plane = pl.program_id(0) * bunch + inner
         part_sum = None
@@ -289,8 +290,17 @@
         pack(part_sum, slot)
         upper_ref[inner * half : (inner + 1) * half, :] = slot[:half, :]
         lower_ref[inner * half : (inner + 1) * half, :] = slot[half:, :]
+        means.append(jnp.sum(part_sum) * (1.0 / length**2))
+        parts.append(part_sum - means[inner])
+    basis, turn = split(tables_ref[0]), split(tables_ref[1])
+    along_z = product_of_parts(split(jnp.concatenate(parts, axis=0)), turn)
+    first = (lax.broadcasted_iota(jnp.int32, (length, length), axis) == 0 for axis in range(2))
+    first = jnp.logical_and(*first)
+    for inner in range(bunch):
+        plane = pl.program_id(0) * bunch + inner
+        spectrum = product_of_parts(basis, split(along_z[inner * length : (inner + 1) * length, :]))
         slot = packed.at[inner * 4 + 3]
-        pack(product(product(tables_ref[0], part_sum), tables_ref[1]), slot)
+        pack(spectrum + jnp.where(first, means[inner] * length, 0.0), slot)
         for to in range(2 * grid):
             out_ref[pl.ds(to * chunk + plane * share, share), :] = slot[pl.ds(to * share, share), :]
 
@@ -336,20 +346,22 @@
     half = rows * grid // 2
     chunk = chunk_rows(sizes)[1]
     turn, basis = split(tables_ref[1]), split(tables_ref[0])
+    lines = []
     for inner in range(bunch):
         plane = pl.program_id(0) * bunch + inner
         slot = packed.at[inner * 2]
         for source in range(2 * grid):
             start = source * chunk + plane * share
             slot[pl.ds(source * share, share), :] = spec_ref[pl.ds(start, share), :]
-        hartree = product_of_parts(turn, split(unpack(slot, length)))
-        hartree = product_of_parts(split(hartree), basis)
+        lines.append(product_of_parts(turn, split(unpack(slot, length))))
+    hartree = product_of_parts(split(jnp.concatenate(lines, axis=0)), basis)
+    for inner in range(bunch):
         slot = packed.at[inner * 2 + 1]
         here = slice(inner * half, (inner + 1) * half)
         slot[:half, :] = upper_ref[here, :] + upper_other[here, :]
         slot[half:, :] = lower_ref[here, :] + lower_other[here, :]
         root = jnp.exp(jnp.log(unpack(slot, length)) * (1.0 / 3.0))
-        out_ref[inner] = hartree - XC_FACTOR * root
+        out_ref[inner] = hartree[inner * length : (inner + 1) * length, :] - XC_FACTOR * root
 
 
 def shape(*dims):
@@ -377,7 +389,7 @@
     first += near[half - 4 :]
     for index in range(3, half):
         second += near[index - 3 : index - 2] + far[index : index + 1]
-    second = second[:-1] + near[half - 3 :] + second[-1:]
+    second += near[half - 3 :]
     return [0] + first, [0] + second
 
 
@@ -474,11 +486,6 @@
         compiler_params=PARAMS,
         cost_estimate=cost(2 * 6 * work, 10 << 20),
     )(place, *moved, kin)
-    late = range(5, grid)
-    held = lax.optimization_barrier(([mixed[k] for k in late], along))
-    along = held[1]
-    for k, piece in zip(late, held[0]):
-        mixed[k] = piece
     mixed = swap_pieces(turns, mixed)
     half_spec = pl.BlockSpec((rows // steps * length, LANES), lambda i: (i % (steps // 2), 0))
     update = pl.pallas_call(
@@ -517,7 +524,7 @@
             shape(spec_rows, LANES),
         ],
         scratch_shapes=scratch(4),
-        compiler_params=SMALL,
+        compiler_params=PARAMS,
         cost_estimate=cost(2 * 6 * work, 16 << 20),
     )(occupations, update, base, tables)
     upper_other = lax.ppermute(upper, "band", [(0, 1), (1, 0)])

time: 417 us -> 420 us (level)
    unnamed x128 -> x120, local copies, waits for them, and re-layouts: 10.1 us -> 7 us
  transfers between devices with their start and end apart: 36 -> 36, of which waited for: 18 -> 15; matrix products, arithmetic and copies ran while one was open for 0% -> 0% of each run, Pallas kernels for 8% -> 7%
where the time goes in v6:
time: 420 us; the launch traced here: 419 us
  waiting for transfers between devices  222 us (53%)
  starting transfers between devices  123 us (29%)
  Pallas kernels  65.2 us (16%)
  local copies, waits for them, and re-layouts  7 us (2%)
    ppermute x30, starting transfers between devices, swap_pieces(): lax.ppermute(piece, 'grid', [(place, place ^ turn) for place in range(gri...  90.9 us
    ppermute x30, waiting for transfers between devices, swap_pieces(): lax.ppermute(piece, 'grid', [(place, place ^ turn) for place in range(gri...  73 us
    all_to_all x1, waiting for transfers between devices, swap(): lax.all_to_all(flat, 'grid', split_axis=0, concat_axis=0)  65.6 us
    all_to_all x2, waiting for transfers between devices, swap_all(): lax.all_to_all(flat, ('band', 'grid'), split_axis=0, concat_axis=0)  46 us
    ppermute x1, waiting for transfers between devices, packed_path(): lower_other = lax.ppermute(lower, 'band', [(0, 1), (1, 0)])  37.9 us
    all_to_all x2, starting transfers between devices, swap_all(): lax.all_to_all(flat, ('band', 'grid'), split_axis=0, concat_axis=0)  19.8 us
    pallas_call x1, Pallas kernels, packed_path(): pl.pallas_call(functools.partial(plane_kernel, sizes, bunch, turns), grid...  13.8 us
    pallas_call x1, Pallas kernels, packed_path(): pl.pallas_call(functools.partial(along_kernel, sizes, first_turns), grid=...  11.9 us
  transfers between devices with their start and end apart: 36, of which 15 were waited for; matrix products, arithmetic and copies ran while one was open for 0% of the time, Pallas kernels for 7%

profile of v6, /device:TPU:0, one launch (start us, length us, event | category | flops | bytes accessed | tf_op | source)
XLA Modules:
  0.0 419.3 jit_solution(17816084659359407660)
XLA Ops:
  0.6 7.0 %shard_map.86 = (f32[544,128]{1,0:T(8,128)}, f32[544,128]{1,0:T(8,128)}, f32[544,128]{1,0:T(8,128)}, f32[544,128]{1,0:T(8,128)}, f32[544,128]{1,0:T(8,128)}, /*i...) custom-call(s32[1]{0:T(128)} %bitcast.place_ref, ...), custom_call_target="tpu_custom_call" | custom-call | bytes 15728640 | tf_op jit(solution)/shard_map/pallas_call | solution.py:442
  7.6 4.0 collective-permute-start
  16.3 13.8 %shard_map.87 = (f32[432,128]{1,0:T(8,128)}, f32[432,128]{1,0:T(8,128)}, f32[432,128]{1,0:T(8,128)}, f32[432,128]{1,0:T(8,128)}, f32[432,128]{1,0:T(8,128)}, /*i...) custom-call(s32[1]{0:T(128)} %bitcast.place_ref, ...), custom_call_target="tpu_custom_call" | custom-call | flops 4076863488 | bytes 20971520 | tf_op jit(solution)/shard_map/pallas_call | solution.py:452
  30.1 7.1 %collective-permute-done.refs_1_ = f32[544,128]{1,0:T(8,128)S(1)} collective-permute-done((f32[544,128]{1,0:T(8,128)}, f32[544,128]{1,0:T(8,128)S(1)}, u32[]{:S(2)}, u32[]{:S(2)}) %collective-permute-start) | collective-permute-done | bytes 278560 | tf_op jit(solution)/shard_map/ppermute | solution.py:425
  38.2 3.4 collective-permute-done.2.refs_3_
  41.6 7.7 %collective-permute-start.7 = (f32[544,128]{1,0:T(8,128)S(1)}, f32[544,128]{1,0:T(8,128)S(1)}, u32[]{:S(2)}, u32[]{:S(2)}) collective-permute-start(f32[544,128]{1,0:T(8,128)S(1)} %copy-done.44), channel_id=1, source_target_pairs={{0,4},{1,5},{2,6},{3,7},{4,0},{5,1},{6,2},{7,3},{8,12},{9,13},{10,... | collective-permute-start | bytes 835592 | tf_op jit(solution)/shard_map/ppermute | solution.py:425
  51.9 4.6 %collective-permute-done.4.refs_5_ = f32[544,128]{1,0:T(8,128)S(1)} collective-permute-done((f32[544,128]{1,0:T(8,128)}, f32[544,128]{1,0:T(8,128)S(1)}, u32[]{:S(2)}, u32[]{:S(2)}) %collective-permute-start.4) | collective-permute-done | bytes 278560 | tf_op jit(solution)/shard_map/ppermute | solution.py:425
  59.1 19.1 %collective-permute-done.6.refs_7_ = f32[544,128]{1,0:T(8,128)S(1)} collective-permute-done((f32[544,128]{1,0:T(8,128)S(1)}, f32[544,128]{1,0:T(8,128)S(1)}, u32[]{:S(2)}, u32[]{:S(2)}) %collective-permute-start.6) | collective-permute-done | bytes 278560 | tf_op jit(solution)/shard_map/ppermute | solution.py:425
  78.2 4.2 collective-permute-start.11
  82.3 7.8 %collective-permute-done.7.refs_8_ = f32[544,128]{1,0:T(8,128)S(1)} collective-permute-done((f32[544,128]{1,0:T(8,128)S(1)}, f32[544,128]{1,0:T(8,128)S(1)}, u32[]{:S(2)}, u32[]{:S(2)}) %collective-permute-start.7) | collective-permute-done | bytes 278560 | tf_op jit(solution)/shard_map/ppermute | solution.py:425
  92.9 5.7 %collective-permute-start.14 = (f32[544,128]{1,0:T(8,128)S(1)}, f32[544,128]{1,0:T(8,128)S(1)}, u32[]{:S(2)}, u32[]{:S(2)}) collective-permute-start(f32[544,128]{1,0:T(8,128)S(1)} %copy-done.37), channel_id=1, source_target_pairs={{0,7},{1,6},{2,5},{3,4},{4,3},{5,2},{6,1},{7,0},{8,15},{9,14},{10,... | collective-permute-start | bytes 835592 | tf_op jit(solution)/shard_map/ppermute | solution.py:425
  98.6 11.2 %collective-permute-start.16 = (f32[432,128]{1,0:T(8,128)}, f32[432,128]{1,0:T(8,128)S(1)}, u32[]{:S(2)}, u32[]{:S(2)}) collective-permute-start(f32[432,128]{1,0:T(8,128)} %get-tuple-element.80), channel_id=1, source_target_pairs={{0,8},{1,9},{2,10},{3,11},{4,12},{5,13},{6,14},{7,15},{8,0},{9,1},... | collective-permute-start | bytes 663560 | tf_op jit(solution)/shard_map/ppermute | solution.py:425
  109.7 11.2 %collective-permute-start.17 = (f32[432,128]{1,0:T(8,128)}, f32[432,128]{1,0:T(8,128)S(1)}, u32[]{:S(2)}, u32[]{:S(2)}) collective-permute-start(f32[432,128]{1,0:T(8,128)} %get-tuple-element.81), channel_id=1, source_target_pairs={{0,9},{1,8},{2,11},{3,10},{4,13},{5,12},{6,15},{7,14},{8,1},{9,0},... | collective-permute-start | bytes 663560 | tf_op jit(solution)/shard_map/ppermute | solution.py:425
  122.3 3.4 shard_map.89.own_ref
  127.3 3.6 collective-permute-start.20
  130.8 9.8 %collective-permute-done.17.refs_2_ = f32[432,128]{1,0:T(8,128)S(1)} collective-permute-done((f32[432,128]{1,0:T(8,128)}, f32[432,128]{1,0:T(8,128)S(1)}, u32[]{:S(2)}, u32[]{:S(2)}) %collective-permute-start.17) | collective-permute-done | bytes 221216 | tf_op jit(solution)/shard_map/ppermute | solution.py:425
  141.6 9.6 %collective-permute-done.18.refs_3_ = f32[432,128]{1,0:T(8,128)S(1)} collective-permute-done((f32[432,128]{1,0:T(8,128)}, f32[432,128]{1,0:T(8,128)S(1)}, u32[]{:S(2)}, u32[]{:S(2)}) %collective-permute-start.18) | collective-permute-done | bytes 221216 | tf_op jit(solution)/shard_map/ppermute | solution.py:425
  151.2 3.5 collective-permute-start.22
  155.3 13.0 %collective-permute-start.24 = (f32[432,128]{1,0:T(8,128)S(1)}, f32[432,128]{1,0:T(8,128)S(1)}, u32[]{:S(2)}, u32[]{:S(2)}) collective-permute-start(f32[432,128]{1,0:T(8,128)S(1)} %copy-done.53), channel_id=1, source_target_pairs={{0,13},{1,12},{2,15},{3,14},{4,9},{5,8},{6,11},{7,10},{8,5},{9,4},... | collective-permute-start | bytes 663560 | tf_op jit(solution)/shard_map/ppermute | solution.py:425
  168.5 4.1 collective-permute-start.27
  174.2 9.4 %collective-permute-done.25.refs_10_ = f32[432,128]{1,0:T(8,128)S(1)} collective-permute-done((f32[432,128]{1,0:T(8,128)S(1)}, f32[432,128]{1,0:T(8,128)S(1)}, u32[]{:S(2)}, u32[]{:S(2)}) %collective-permute-start.25) | collective-permute-done | bytes 221216 | tf_op jit(solution)/shard_map/ppermute | solution.py:425
  183.7 7.8 %collective-permute-start.30 = (f32[432,128]{1,0:T(8,128)S(1)}, f32[432,128]{1,0:T(8,128)S(1)}, u32[]{:S(2)}, u32[]{:S(2)}) collective-permute-start(f32[432,128]{1,0:T(8,128)S(1)} %copy-done.47), channel_id=1, source_target_pairs={{0,7},{1,6},{2,5},{3,4},{4,3},{5,2},{6,1},{7,0},{8,15},{9,14},{10,... | collective-permute-start | bytes 663560 | tf_op jit(solution)/shard_map/ppermute | solution.py:425
  191.5 11.9 %shard_map.88.along_ref = f32[3456,256]{1,0:T(8,128)} custom-call(s32[1]{0:T(128)} %bitcast.place_ref, f32[544,128]{1,0:T(8,128)} %get-tuple-element.52.refs_0_, f32[544,128]{1,0:T(8,128)} %copy-done.4, f32[544,128]{1,0:T(8,128)} %copy-done.5, f32[544,128]{1,0:T(8,128)} %copy-done.6, f32[544,128]{1,0:T(8,128)} %copy-done.7, f32[544,128]{1,0:T(8,128)} %copy-done.8, ...), custom_call_target="tpu_custom_call" | custom-call | flops 2038431744 | bytes 10485760 | tf_op jit(solution)/shard_map/pallas_call | solution.py:479
  204.8 9.1 %shard_map.90 = f32[6912,128]{1,0:T(8,128)} custom-call(s32[1]{0:T(128)} %bitcast.place_ref, f32[3456,256]{1,0:T(8,128)} %shard_map.88.along_ref, f32[1728,128]{1,0:T(8,128)} %shard_map.89.own_ref, f32[1728,128]{1,0:T(8,128)} %copy-done.19, f32[192,192]{1,0:T(8,128)} %constant.23.clone.kin_ref.refs_16_, f32[432,128]{1,0:T(8,128)} %get-tuple-element.79.refs_0_, ...), custom_call_target="tpu_custom_call" | custom-call | flops 1019215872 | bytes 14680064 | tf_op jit(solution)/shard_map/pallas_call | solution.py:491
  213.8 7.0 %all-to-all-start = ((f32[16,432,128]{2,1,0:T(8,128)}), f32[16,432,128]{2,1,0:T(8,128)S(1)}, u32[]{:S(2)}, u32[]{:S(2)}) async-start(f32[16,432,128]{2,1,0:T(8,128)} %bitcast.16), calls=%async_computation | async-start | bytes 7077888 | tf_op jit(solution)/shard_map/all_to_all | solution.py:431
  221.5 65.6 %all-to-all-done = f32[16,432,128]{2,1,0:T(8,128)S(1)} async-done(((f32[16,432,128]{2,1,0:T(8,128)}), f32[16,432,128]{2,1,0:T(8,128)S(1)}, u32[]{:S(2)}, u32[]{:S(2)}) %all-to-all-start) | async-done | bytes 3538976 | tf_op jit(solution)/shard_map/all_to_all | solution.py:431
  288.9 10.9 %shard_map.91 = (f32[1,2,12,192,192]{4,3,2,1,0:T(8,128)}, f32[1728,128]{1,0:T(8,128)}, f32[1728,128]{1,0:T(8,128)}, f32[3584,128]{1,0:T(8,128)}) custom-call(f32[1]{0:T(128)S(6)} %copy.12.occ_ref, f32[6912,128]{1,0:T(8,128)} %bitcast.17, f32[2,12,192,192]{3,2,1,0:T(8,128)} %get-tuple-element.95.base_ref, f32[2,192,192]{2,1,0:T(8,128)} %constant.24.clone.tables_ref), custom_call_target="tpu_custom_call" | custom-call | flops 2038431744 | bytes 16777216 | tf_op jit(solution)/shard_map/pallas_call | solution.py:510
  299.9 17.0 %all-to-all-start.1 = ((f32[32,112,128]{2,1,0:T(8,128)}), f32[32,112,128]{2,1,0:T(8,128)S(1)}, u32[]{:S(2)}, u32[]{:S(2)}) async-start(f32[32,112,128]{2,1,0:T(8,128)} %bitcast.19), calls=%async_computation.1 | async-start | bytes 3670016 | tf_op jit(solution)/shard_map/all_to_all | solution.py:435
  319.4 41.5 %all-to-all-done.1 = f32[32,112,128]{2,1,0:T(8,128)S(1)} async-done(((f32[32,112,128]{2,1,0:T(8,128)}), f32[32,112,128]{2,1,0:T(8,128)S(1)}, u32[]{:S(2)}, u32[]{:S(2)}) %all-to-all-start.1) | async-done | bytes 1835040 | tf_op jit(solution)/shard_map/all_to_all | solution.py:435
  368.9 37.9 %collective-permute-done.32.lower_other = f32[1728,128]{1,0:T(8,128)} collective-permute-done((f32[1728,128]{1,0:T(8,128)S(1)}, f32[1728,128]{1,0:T(8,128)}, u32[]{:S(2)}, u32[]{:S(2)}) %collective-permute-start.32) | collective-permute-done | bytes 884768 | tf_op jit(solution)/shard_map/ppermute | solution.py:531
  406.9 4.4 %all-to-all-done.2 = f32[32,112,128]{2,1,0:T(8,128)S(1)} async-done(((f32[32,112,128]{2,1,0:T(8,128)}), f32[32,112,128]{2,1,0:T(8,128)S(1)}, u32[]{:S(2)}, u32[]{:S(2)}) %all-to-all-start.2) | async-done | bytes 1835040 | tf_op jit(solution)/shard_map/all_to_all | solution.py:435
  412.5 6.8 %shard_map.93 = f32[12,192,192]{2,1,0:T(8,128)} custom-call(f32[3584,128]{1,0:T(8,128)} %bitcast.18, f32[1728,128]{1,0:T(8,128)} %get-tuple-element.98.upper_ref, f32[1728,128]{1,0:T(8,128)} %get-tuple-element.100.lower_ref, f32[1728,128]{1,0:T(8,128)} %collective-permute-done.31.upper_other, f32[1728,128]{1,0:T(8,128)} %collective-permute-done.32.lower_other, ...), custom_call_target="tpu_custom_call" | custom-call | flops 2038431744 | bytes 6291456 | tf_op jit(solution)/shard_map/pallas_call | solution.py:552
  (168 shorter events, 34.2 us)
Async XLA Ops:
  7.6 29.6 %collective-permute-start = (f32[544,128]{1,0:T(8,128)}, f32[544,128]{1,0:T(8,128)S(1)}, u32[]{:S(2)}, u32[]{:S(2)}) collective-permute-start(f32[544,128]{1,0:T(8,128)} %get-tuple-element.53), channel_id=1, source_target_pairs={{0,8},{1,9},{2,10},{3,11},{4,12},{5,13},{6,14},{7,15},{8,0},{9,1},... | collective-permute-start | bytes 835592 | tf_op jit(solution)/shard_map/ppermute | solution.py:425
  11.7 25.6 %collective-permute-start.1 = (f32[544,128]{1,0:T(8,128)}, f32[544,128]{1,0:T(8,128)S(1)}, u32[]{:S(2)}, u32[]{:S(2)}) collective-permute-start(f32[544,128]{1,0:T(8,128)} %get-tuple-element.54), channel_id=1, source_target_pairs={{0,1},{1,0},{2,3},{3,2},{4,5},{5,4},{6,7},{7,6},{8,9},{9,8},{10,11... | collective-permute-start | bytes 835592 | tf_op jit(solution)/shard_map/ppermute | solution.py:425
  11.7 29.9 %collective-permute-start.2 = (f32[544,128]{1,0:T(8,128)}, f32[544,128]{1,0:T(8,128)S(1)}, u32[]{:S(2)}, u32[]{:S(2)}) collective-permute-start(f32[544,128]{1,0:T(8,128)} %get-tuple-element.55), channel_id=1, source_target_pairs={{0,9},{1,8},{2,11},{3,10},{4,13},{5,12},{6,15},{7,14},{8,1},{9,0},... | collective-permute-start | bytes 835592 | tf_op jit(solution)/shard_map/ppermute | solution.py:425
  11.9 37.4 %collective-permute-start.3 = (f32[544,128]{1,0:T(8,128)}, f32[544,128]{1,0:T(8,128)S(1)}, u32[]{:S(2)}, u32[]{:S(2)}) collective-permute-start(f32[544,128]{1,0:T(8,128)} %get-tuple-element.56), channel_id=1, source_target_pairs={{0,2},{1,3},{2,0},{3,1},{4,6},{5,7},{6,4},{7,5},{8,10},{9,11},{10,... | collective-permute-start | bytes 835592 | tf_op jit(solution)/shard_map/ppermute | solution.py:425
  13.7 42.9 %collective-permute-start.4 = (f32[544,128]{1,0:T(8,128)}, f32[544,128]{1,0:T(8,128)S(1)}, u32[]{:S(2)}, u32[]{:S(2)}) collective-permute-start(f32[544,128]{1,0:T(8,128)} %get-tuple-element.57), channel_id=1, source_target_pairs={{0,10},{1,11},{2,8},{3,9},{4,14},{5,15},{6,12},{7,13},{8,2},{9,3},... | collective-permute-start | bytes 835592 | tf_op jit(solution)/shard_map/ppermute | solution.py:425
  37.3 21.2 %collective-permute-start.5 = (f32[544,128]{1,0:T(8,128)S(1)}, f32[544,128]{1,0:T(8,128)S(1)}, u32[]{:S(2)}, u32[]{:S(2)}) collective-permute-start(f32[544,128]{1,0:T(8,128)S(1)} %copy-done.46), channel_id=1, source_target_pairs={{0,3},{1,2},{2,1},{3,0},{4,7},{5,6},{6,5},{7,4},{8,11},{9,10},{10,... | collective-permute-start | bytes 835592 | tf_op jit(solution)/shard_map/ppermute | solution.py:425
  37.3 40.9 %collective-permute-start.6 = (f32[544,128]{1,0:T(8,128)S(1)}, f32[544,128]{1,0:T(8,128)S(1)}, u32[]{:S(2)}, u32[]{:S(2)}) collective-permute-start(f32[544,128]{1,0:T(8,128)S(1)} %copy-done.45), channel_id=1, source_target_pairs={{0,11},{1,10},{2,9},{3,8},{4,15},{5,14},{6,13},{7,12},{8,3},{9,2},... | collective-permute-start | bytes 835592 | tf_op jit(solution)/shard_map/ppermute | solution.py:425
  41.6 48.5 %collective-permute-start.7 = (f32[544,128]{1,0:T(8,128)S(1)}, f32[544,128]{1,0:T(8,128)S(1)}, u32[]{:S(2)}, u32[]{:S(2)}) collective-permute-start(f32[544,128]{1,0:T(8,128)S(1)} %copy-done.44), channel_id=1, source_target_pairs={{0,4},{1,5},{2,6},{3,7},{4,0},{5,1},{6,2},{7,3},{8,12},{9,13},{10,... | collective-permute-start | bytes 835592 | tf_op jit(solution)/shard_map/ppermute | solution.py:425
  49.3 40.8 %collective-permute-start.8 = (f32[544,128]{1,0:T(8,128)S(1)}, f32[544,128]{1,0:T(8,128)S(1)}, u32[]{:S(2)}, u32[]{:S(2)}) collective-permute-start(f32[544,128]{1,0:T(8,128)S(1)} %copy-done.43), channel_id=1, source_target_pairs={{0,12},{1,13},{2,14},{3,15},{4,8},{5,9},{6,10},{7,11},{8,4},{9,5},... | collective-permute-start | bytes 835592 | tf_op jit(solution)/shard_map/ppermute | solution.py:425
  56.6 36.3 %collective-permute-start.9 = (f32[544,128]{1,0:T(8,128)S(1)}, f32[544,128]{1,0:T(8,128)S(1)}, u32[]{:S(2)}, u32[]{:S(2)}) collective-permute-start(f32[544,128]{1,0:T(8,128)S(1)} %copy-done.42), channel_id=1, source_target_pairs={{0,13},{1,12},{2,15},{3,14},{4,9},{5,8},{6,11},{7,10},{8,5},{9,4},... | collective-permute-start | bytes 835592 | tf_op jit(solution)/shard_map/ppermute | solution.py:425
  58.5 40.1 %collective-permute-start.10 = (f32[544,128]{1,0:T(8,128)S(1)}, f32[544,128]{1,0:T(8,128)S(1)}, u32[]{:S(2)}, u32[]{:S(2)}) collective-permute-start(f32[544,128]{1,0:T(8,128)S(1)} %copy-done.41), channel_id=1, source_target_pairs={{0,14},{1,15},{2,12},{3,13},{4,10},{5,11},{6,8},{7,9},{8,6},{9,7},... | collective-permute-start | bytes 835592 | tf_op jit(solution)/shard_map/ppermute | solution.py:425
  78.2 31.6 %collective-permute-start.11 = (f32[544,128]{1,0:T(8,128)S(1)}, f32[544,128]{1,0:T(8,128)S(1)}, u32[]{:S(2)}, u32[]{:S(2)}) collective-permute-start(f32[544,128]{1,0:T(8,128)S(1)} %copy-done.40), channel_id=1, source_target_pairs={{0,15},{1,14},{2,13},{3,12},{4,11},{5,10},{6,9},{7,8},{8,7},{9,6},... | collective-permute-start | bytes 835592 | tf_op jit(solution)/shard_map/ppermute | solution.py:425
  90.1 30.9 %collective-permute-start.12 = (f32[544,128]{1,0:T(8,128)S(1)}, f32[544,128]{1,0:T(8,128)S(1)}, u32[]{:S(2)}, u32[]{:S(2)}) collective-permute-start(f32[544,128]{1,0:T(8,128)S(1)} %copy-done.39), channel_id=1, source_target_pairs={{0,5},{1,4},{2,7},{3,6},{4,1},{5,0},{6,3},{7,2},{8,13},{9,12},{10,... | collective-permute-start | bytes 835592 | tf_op jit(solution)/shard_map/ppermute | solution.py:425
  90.1 31.3 %collective-permute-start.13 = (f32[544,128]{1,0:T(8,128)S(1)}, f32[544,128]{1,0:T(8,128)S(1)}, u32[]{:S(2)}, u32[]{:S(2)}) collective-permute-start(f32[544,128]{1,0:T(8,128)S(1)} %copy-done.38), channel_id=1, source_target_pairs={{0,6},{1,7},{2,4},{3,5},{4,2},{5,3},{6,0},{7,1},{8,14},{9,15},{10,... | collective-permute-start | bytes 835592 | tf_op jit(solution)/shard_map/ppermute | solution.py:425
  92.9 28.5 %collective-permute-start.14 = (f32[544,128]{1,0:T(8,128)S(1)}, f32[544,128]{1,0:T(8,128)S(1)}, u32[]{:S(2)}, u32[]{:S(2)}) collective-permute-start(f32[544,128]{1,0:T(8,128)S(1)} %copy-done.37), channel_id=1, source_target_pairs={{0,7},{1,6},{2,5},{3,4},{4,3},{5,2},{6,1},{7,0},{8,15},{9,14},{10,... | collective-permute-start | bytes 835592 | tf_op jit(solution)/shard_map/ppermute | solution.py:425
  98.6 28.7 %collective-permute-start.16 = (f32[432,128]{1,0:T(8,128)}, f32[432,128]{1,0:T(8,128)S(1)}, u32[]{:S(2)}, u32[]{:S(2)}) collective-permute-start(f32[432,128]{1,0:T(8,128)} %get-tuple-element.80), channel_id=1, source_target_pairs={{0,8},{1,9},{2,10},{3,11},{4,12},{5,13},{6,14},{7,15},{8,0},{9,1},... | collective-permute-start | bytes 663560 | tf_op jit(solution)/shard_map/ppermute | solution.py:425
  109.7 30.9 %collective-permute-start.17 = (f32[432,128]{1,0:T(8,128)}, f32[432,128]{1,0:T(8,128)S(1)}, u32[]{:S(2)}, u32[]{:S(2)}) collective-permute-start(f32[432,128]{1,0:T(8,128)} %get-tuple-element.81), channel_id=1, source_target_pairs={{0,9},{1,8},{2,11},{3,10},{4,13},{5,12},{6,15},{7,14},{8,1},{9,0},... | collective-permute-start | bytes 663560 | tf_op jit(solution)/shard_map/ppermute | solution.py:425
  121.0 30.2 %collective-permute-start.18 = (f32[432,128]{1,0:T(8,128)}, f32[432,128]{1,0:T(8,128)S(1)}, u32[]{:S(2)}, u32[]{:S(2)}) collective-permute-start(f32[432,128]{1,0:T(8,128)} %get-tuple-element.82), channel_id=1, source_target_pairs={{0,10},{1,11},{2,8},{3,9},{4,14},{5,15},{6,12},{7,13},{8,2},{9,3},... | collective-permute-start | bytes 663560 | tf_op jit(solution)/shard_map/ppermute | solution.py:425
  125.7 77.9 %collective-permute-start.15 = (f32[1728,128]{1,0:T(8,128)}, f32[1728,128]{1,0:T(8,128)S(1)}, u32[]{:S(2)}, u32[]{:S(2)}) collective-permute-start(f32[1728,128]{1,0:T(8,128)} %shard_map.89.own_ref), channel_id=1, source_target_pairs={{0,16},{16,0},{1,17},{17,1},{2,18},{18,2},{3,19},{19,3},{4,20},{20... | collective-permute-start | bytes 2654216 | tf_op jit(solution)/shard_map/ppermute | solution.py:478
  127.3 27.5 %collective-permute-start.19 = (f32[432,128]{1,0:T(8,128)S(1)}, f32[432,128]{1,0:T(8,128)S(1)}, u32[]{:S(2)}, u32[]{:S(2)}) collective-permute-start(f32[432,128]{1,0:T(8,128)S(1)} %copy-done.58), channel_id=1, source_target_pairs={{0,1},{1,0},{2,3},{3,2},{4,5},{5,4},{6,7},{7,6},{8,9},{9,8},{10,11... | collective-permute-start | bytes 663560 | tf_op jit(solution)/shard_map/ppermute | solution.py:425
  127.3 28.0 %collective-permute-start.20 = (f32[432,128]{1,0:T(8,128)S(1)}, f32[432,128]{1,0:T(8,128)S(1)}, u32[]{:S(2)}, u32[]{:S(2)}) collective-permute-start(f32[432,128]{1,0:T(8,128)S(1)} %copy-done.57), channel_id=1, source_target_pairs={{0,11},{1,10},{2,9},{3,8},{4,15},{5,14},{6,13},{7,12},{8,3},{9,2},... | collective-permute-start | bytes 663560 | tf_op jit(solution)/shard_map/ppermute | solution.py:425
  140.7 27.6 %collective-permute-start.21 = (f32[432,128]{1,0:T(8,128)S(1)}, f32[432,128]{1,0:T(8,128)S(1)}, u32[]{:S(2)}, u32[]{:S(2)}) collective-permute-start(f32[432,128]{1,0:T(8,128)S(1)} %copy-done.56), channel_id=1, source_target_pairs={{0,2},{1,3},{2,0},{3,1},{4,6},{5,7},{6,4},{7,5},{8,10},{9,11},{10,... | collective-permute-start | bytes 663560 | tf_op jit(solution)/shard_map/ppermute | solution.py:425
  155.3 18.9 %collective-permute-start.24 = (f32[432,128]{1,0:T(8,128)S(1)}, f32[432,128]{1,0:T(8,128)S(1)}, u32[]{:S(2)}, u32[]{:S(2)}) collective-permute-start(f32[432,128]{1,0:T(8,128)S(1)} %copy-done.53), channel_id=1, source_target_pairs={{0,13},{1,12},{2,15},{3,14},{4,9},{5,8},{6,11},{7,10},{8,5},{9,4},... | collective-permute-start | bytes 663560 | tf_op jit(solution)/shard_map/ppermute | solution.py:425
  168.5 35.1 %collective-permute-start.27 = (f32[432,128]{1,0:T(8,128)S(1)}, f32[432,128]{1,0:T(8,128)S(1)}, u32[]{:S(2)}, u32[]{:S(2)}) collective-permute-start(f32[432,128]{1,0:T(8,128)S(1)} %copy-done.50), channel_id=1, source_target_pairs={{0,5},{1,4},{2,7},{3,6},{4,1},{5,0},{6,3},{7,2},{8,13},{9,12},{10,... | collective-permute-start | bytes 663560 | tf_op jit(solution)/shard_map/ppermute | solution.py:425
  174.2 29.4 %collective-permute-start.28 = (f32[432,128]{1,0:T(8,128)S(1)}, f32[432,128]{1,0:T(8,128)S(1)}, u32[]{:S(2)}, u32[]{:S(2)}) collective-permute-start(f32[432,128]{1,0:T(8,128)S(1)} %copy-done.49), channel_id=1, source_target_pairs={{0,15},{1,14},{2,13},{3,12},{4,11},{5,10},{6,9},{7,8},{8,7},{9,6},... | collective-permute-start | bytes 663560 | tf_op jit(solution)/shard_map/ppermute | solution.py:425
  183.6 20.0 %collective-permute-start.29 = (f32[432,128]{1,0:T(8,128)S(1)}, f32[432,128]{1,0:T(8,128)S(1)}, u32[]{:S(2)}, u32[]{:S(2)}) collective-permute-start(f32[432,128]{1,0:T(8,128)S(1)} %copy-done.48), channel_id=1, source_target_pairs={{0,6},{1,7},{2,4},{3,5},{4,2},{5,3},{6,0},{7,1},{8,14},{9,15},{10,... | collective-permute-start | bytes 663560 | tf_op jit(solution)/shard_map/ppermute | solution.py:425
  183.7 19.9 %collective-permute-start.30 = (f32[432,128]{1,0:T(8,128)S(1)}, f32[432,128]{1,0:T(8,128)S(1)}, u32[]{:S(2)}, u32[]{:S(2)}) collective-permute-start(f32[432,128]{1,0:T(8,128)S(1)} %copy-done.47), channel_id=1, source_target_pairs={{0,7},{1,6},{2,5},{3,4},{4,3},{5,2},{6,1},{7,0},{8,15},{9,14},{10,... | collective-permute-start | bytes 663560 | tf_op jit(solution)/shard_map/ppermute | solution.py:425
  213.8 73.2 %all-to-all-start = ((f32[16,432,128]{2,1,0:T(8,128)}), f32[16,432,128]{2,1,0:T(8,128)S(1)}, u32[]{:S(2)}, u32[]{:S(2)}) async-start(f32[16,432,128]{2,1,0:T(8,128)} %bitcast.16), calls=%async_computation | async-start | bytes 7077888 | tf_op jit(solution)/shard_map/all_to_all | solution.py:431
  299.9 61.1 %all-to-all-start.1 = ((f32[32,112,128]{2,1,0:T(8,128)}), f32[32,112,128]{2,1,0:T(8,128)S(1)}, u32[]{:S(2)}, u32[]{:S(2)}) async-start(f32[32,112,128]{2,1,0:T(8,128)} %bitcast.19), calls=%async_computation.1 | async-start | bytes 3670016 | tf_op jit(solution)/shard_map/all_to_all | solution.py:435
  316.8 47.5 %collective-permute-start.31 = (f32[1728,128]{1,0:T(8,128)S(1)}, f32[1728,128]{1,0:T(8,128)}, u32[]{:S(2)}, u32[]{:S(2)}) collective-permute-start(f32[1728,128]{1,0:T(8,128)S(1)} %copy-done.20), channel_id=1, source_target_pairs={{0,16},{16,0},{1,17},{17,1},{2,18},{18,2},{3,19},{19,3},{4,20},{20... | collective-permute-start | bytes 2654216 | tf_op jit(solution)/shard_map/ppermute | solution.py:530
  364.4 46.9 %all-to-all-start.2 = ((f32[32,112,128]{2,1,0:T(8,128)}), f32[32,112,128]{2,1,0:T(8,128)S(1)}, u32[]{:S(2)}, u32[]{:S(2)}) async-start(f32[32,112,128]{2,1,0:T(8,128)} %bitcast.14), calls=%async_computation.2 | async-start | bytes 3670016 | tf_op jit(solution)/shard_map/all_to_all | solution.py:435
  367.2 39.6 %collective-permute-start.32 = (f32[1728,128]{1,0:T(8,128)S(1)}, f32[1728,128]{1,0:T(8,128)}, u32[]{:S(2)}, u32[]{:S(2)}) collective-permute-start(f32[1728,128]{1,0:T(8,128)S(1)} %copy-done.21), channel_id=1, source_target_pairs={{0,16},{16,0},{1,17},{17,1},{2,18},{18,2},{3,19},{19,3},{4,20},{20... | collective-permute-start | bytes 2654216 | tf_op jit(solution)/shard_map/ppermute | solution.py:531
  (63 other events, 2165.1 us)

commit v7 on v6

--- a/solution.py
+++ b/solution.py
@@ -133,7 +133,7 @@
 
 def chunk_rows(sizes):
     planes, _, rows, share = sizes
-    return whole_tiles(planes * (2 * rows + share)), whole_tiles(planes * share)
+    return whole_tiles(planes * share)
 
 
 def kinetic(plane, kin):
@@ -164,26 +164,32 @@
                 out_ref[pl.ds(to * chunk + used, chunk - used), :] = jnp.zeros((chunk - used, LANES), jnp.float32)
 
 
-def pack_kernel(sizes, bunch, turns, place_ref, psi_ref, ion_ref, hxc_ref, *refs):
+def potential_kernel(sizes, bunch, place_ref, ion_ref, hxc_ref, out_ref, packed):
+    planes, grid, rows, share = sizes
+    chunk = chunk_rows(sizes)
+    band = place_ref[0] // grid
+    fill(out_ref, grid, chunk, planes * share)
+    for inner in range(bunch):
+        plane = pl.program_id(0) * bunch + inner
+        slot = packed.at[inner]
+        pack(ion_ref[inner] + hxc_ref[inner], slot)
+        for to in range(grid):
+            start = to * rows + band * share
+            out_ref[pl.ds(to * chunk + plane * share, share), :] = slot[pl.ds(start, share), :]
+
+
+def pack_kernel(sizes, bunch, turns, place_ref, psi_ref, *refs):
     planes, grid, rows, share = sizes
     *out_refs, packed = refs
-    stride = 2 * rows + share
-    band, mine = place_ref[0] // grid, place_ref[0] % grid
-    for out_ref in out_refs:
-        fill(out_ref, 1, chunk_rows(sizes)[0], planes * stride)
+    mine = place_ref[0] % grid
     for inner in range(bunch):
-        first = (pl.program_id(0) * bunch + inner) * stride
+        plane = pl.program_id(0) * bunch + inner
         for part in range(2):
-            slot = packed.at[inner * 3 + part]
+            slot = packed.at[inner * 2 + part]
             pack(psi_ref[0, part, inner], slot)
             for turn, out_ref in zip(turns, out_refs):
                 start = (mine ^ turn) * rows
-                out_ref[pl.ds(first + part * rows, rows), :] = slot[pl.ds(start, rows), :]
-        slot = packed.at[inner * 3 + 2]
-        pack(ion_ref[inner] + hxc_ref[inner], slot)
-        for turn, out_ref in zip(turns, out_refs):
-            start = (mine ^ turn) * rows + band * share
-            out_ref[pl.ds(first + 2 * rows, share), :] = slot[pl.ds(start, share), :]
+                out_ref[pl.ds((plane * 2 + part) * rows, rows), :] = slot[pl.ds(start, rows), :]
 
 
 def plane_kernel(sizes, bunch, turns, place_ref, psi_ref, ion_ref, hxc_ref, kin_ref, *refs):
@@ -214,27 +220,30 @@
             )
 
 
-def share_kernel(sizes, turns, place_ref, *refs):
-    planes, grid, rows, share = sizes
-    *moved_refs, out_ref = refs
+def share_kernel(sizes, moved_ref, out_ref):
+    planes, grid, rows, share = sizes
     length = planes * grid
-    stride = 2 * rows + share
-    for turn, moved_ref in zip(turns, moved_refs):
-        first = (place_ref[0] % grid ^ turn) * planes
+    chunk = chunk_rows(sizes)
+    for source in range(grid):
         for row in range(share):
-            out_ref[pl.ds(row * length + first, planes), :] = moved_ref[pl.ds(2 * rows + row, planes, stride=stride), :]
-
-
-def along_kernel(sizes, turns, place_ref, *refs):
+            start = source * chunk + row
+            out_ref[pl.ds(row * length + source * planes, planes), :] = moved_ref[pl.ds(start, planes, stride=share), :]
+
+
+def along_kernel(sizes, steps, turns, place_ref, *refs):
     planes, grid, rows, share = sizes
     *moved_refs, kin_ref, out_ref, lines = refs
-    stride = 2 * rows + share
-    row = pl.program_id(0)
-    for turn, moved_ref in zip(turns, moved_refs):
-        first = (place_ref[0] % grid ^ turn) * planes
-        for part in range(2):
-            lines[part, pl.ds(first, planes), :] = moved_ref[pl.ds(part * rows + row, planes, stride=stride), :]
-    out_ref[...] = product(kin_ref[...], jnp.concatenate([lines[0], lines[1]], axis=1))
+    length = planes * grid
+    kin = split(kin_ref[...])
+    for inner in range(rows // steps):
+        row = pl.program_id(0) * (rows // steps) + inner
+        slot = lines.at[inner]
+        for turn, moved_ref in zip(turns, moved_refs):
+            first = (place_ref[0] % grid ^ turn) * planes
+            for part in range(2):
+                slot[part, pl.ds(first, planes), :] = moved_ref[pl.ds(part * rows + row, planes, stride=2 * rows), :]
+        field = jnp.concatenate([slot[0], slot[1]], axis=1)
+        out_ref[inner * length : (inner + 1) * length, :] = product_of_parts(kin, split(field))
 
 
 def update_kernel(sizes, steps, turns, place_ref, along_ref, own_ref, other_ref, kin_ref, *refs):
@@ -269,7 +278,7 @@
 ):
     planes, grid, rows, share = sizes
     length = planes * grid
-    chunk = chunk_rows(sizes)[1]
+    chunk = chunk_rows(sizes)
     cell_rows = rows * grid
     half = cell_rows // 2
     fill(out_ref, 2 * grid, chunk, planes * share)
@@ -308,7 +317,7 @@
 def filter_kernel(sizes, spec_ref, cells_ref, tables_ref, out_ref, lines):
     planes, grid, rows, share = sizes
     length = planes * grid
-    chunk = chunk_rows(sizes)[1]
+    chunk = chunk_rows(sizes)
 
     def places():
         for source in range(grid):
@@ -344,7 +353,7 @@
     planes, grid, rows, share = sizes
     length = planes * grid
     half = rows * grid // 2
-    chunk = chunk_rows(sizes)[1]
+    chunk = chunk_rows(sizes)
     turn, basis = split(tables_ref[1]), split(tables_ref[0])
     lines = []
     for inner in range(bunch):
@@ -380,17 +389,11 @@
     return pl.CostEstimate(flops=flops, bytes_accessed=moved, transcendentals=0)
 
 
-def turn_orders(grid):
-    half = grid // 2
-    near, far = list(range(1, half)), list(range(half, grid))
-    first, second = [], far[:3]
-    for index in range(half):
-        first += far[index : index + 1] + (near[index : index + 1] if index < half - 4 else [])
-    first += near[half - 4 :]
-    for index in range(3, half):
-        second += near[index - 3 : index - 2] + far[index : index + 1]
-    second += near[half - 3 :]
-    return [0] + first, [0] + second
+def turn_order(grid):
+    order = [0]
+    for near in range(grid // 2):
+        order += [near, near + grid // 2] if near else [grid // 2]
+    return order
 
 
 def packed_path(orbitals, occupations, ion_potential, hxc_potential):
@@ -420,11 +423,17 @@
     def scratch(count):
         return [pltpu.VMEM((count * bunch, cell_rows, LANES), jnp.float32)]
 
-    def swap_pieces(turns, pieces):
-        return [
-            lax.ppermute(piece, "grid", [(place, place ^ turn) for place in range(grid)]) if turn else piece
-            for turn, piece in zip(turns, pieces)
-        ]
+    line = []
+
+    def send(turn, piece, *gates):
+        if not turn:
+            return piece
+        if len(line) >= 5:
+            gates += (line[-5],)
+        if gates:
+            piece = lax.optimization_barrier((piece, *gates))[0]
+        line.append(lax.ppermute(piece, "grid", [(spot, spot ^ turn) for spot in range(grid)]))
+        return line[-1]
 
     def swap(array):
         flat = array.reshape(grid, -1, LANES)
@@ -434,21 +443,34 @@
         flat = array.reshape(2 * grid, -1, LANES)
         return lax.all_to_all(flat, ("band", "grid"), split_axis=0, concat_axis=0).reshape(array.shape)
 
-    first_turns, turns = turn_orders(grid)
-    moved_rows, spec_rows = chunk_rows(sizes)
-    spec_rows = 2 * grid * spec_rows
+    turns = turn_order(grid)
+    spec_rows = 2 * grid * chunk_rows(sizes)
     mixed_rows = 2 * planes * rows
     steps = 6 if rows % 6 == 0 and share % (rows // 6) == 0 else 2
+    shared = pl.pallas_call(
+        functools.partial(potential_kernel, sizes, bunch),
+        grid=(planes // bunch,),
+        in_specs=[smem, plane_spec, plane_spec],
+        out_specs=whole(spec_rows // 2, LANES),
+        out_shape=shape(spec_rows // 2, LANES),
+        scratch_shapes=scratch(1),
+        compiler_params=PARAMS,
+        cost_estimate=cost(0, 6 << 20),
+    )(place, ion_potential, hxc_potential)
+    place, shared = lax.optimization_barrier((place, shared))
+    shared = swap(shared)
     moved = pl.pallas_call(
-        functools.partial(pack_kernel, sizes, bunch, first_turns),
+        functools.partial(pack_kernel, sizes, bunch, turns),
         grid=(planes // bunch,),
-        in_specs=[smem, psi_spec, plane_spec, plane_spec],
-        out_specs=[whole(moved_rows, LANES)] * grid,
-        out_shape=[shape(moved_rows, LANES)] * grid,
-        scratch_shapes=scratch(3),
-        compiler_params=PARAMS,
-        cost_estimate=cost(0, 15 << 20),
-    )(place, orbitals, ion_potential, hxc_potential)
+        in_specs=[smem, psi_spec],
+        out_specs=[whole(mixed_rows, LANES)] * grid,
+        out_shape=[shape(mixed_rows, LANES)] * grid,
+        scratch_shapes=scratch(2),
+        compiler_params=PARAMS,
+        cost_estimate=cost(0, 8 << 20),
+    )(place, orbitals)
+    moved = [send(turn, piece) for turn, piece in zip(turns[:6], moved[:6])] + list(moved[6:])
+    behind = lax.optimization_barrier((place, line[1]))[0]
     *mixed, base = pl.pallas_call(
         functools.partial(plane_kernel, sizes, bunch, turns),
         grid=(planes // bunch,),
@@ -458,35 +480,29 @@
         scratch_shapes=scratch(2),
         compiler_params=PARAMS,
         cost_estimate=cost(8 * 3 * work, 20 << 20),
-    )(place, orbitals, ion_potential, hxc_potential, kin)
-    late = range(6, grid)
-    held = lax.optimization_barrier(([moved[k] for k in late], base))
-    base = held[1]
-    moved = list(moved)
-    for k, piece in zip(late, held[0]):
-        moved[k] = piece
-    moved = swap_pieces(first_turns, moved)
-
+    )(behind, orbitals, ion_potential, hxc_potential, kin)
+    for index in range(6, grid):
+        moved[index] = send(turns[index], moved[index], *([base] if index < 11 else []))
     own = pl.pallas_call(
-        functools.partial(share_kernel, sizes, first_turns),
-        in_specs=[smem] + [vmem] * grid,
+        functools.partial(share_kernel, sizes),
+        in_specs=[vmem],
         out_specs=vmem,
         out_shape=shape(share * length, LANES),
         compiler_params=PARAMS,
-        cost_estimate=cost(0, 6 << 20),
-    )(place, *moved)
+        cost_estimate=cost(0, 2 << 20),
+    )(shared)
     other = lax.ppermute(own, "band", [(0, 1), (1, 0)])
     along = pl.pallas_call(
-        functools.partial(along_kernel, sizes, first_turns),
-        grid=(rows,),
-        in_specs=[smem] + [whole(moved_rows, LANES)] * grid + [square],
-        out_specs=pl.BlockSpec((length, 2 * LANES), lambda i: (i, 0)),
+        functools.partial(along_kernel, sizes, steps, turns),
+        grid=(steps,),
+        in_specs=[smem] + [whole(mixed_rows, LANES)] * grid + [square],
+        out_specs=pl.BlockSpec((rows // steps * length, 2 * LANES), lambda i: (i, 0)),
         out_shape=shape(rows * length, 2 * LANES),
-        scratch_shapes=[pltpu.VMEM((2, length, LANES), jnp.float32)],
-        compiler_params=PARAMS,
-        cost_estimate=cost(2 * 6 * work, 10 << 20),
+        scratch_shapes=[pltpu.VMEM((rows // steps, 2, length, LANES), jnp.float32)],
+        compiler_params=PARAMS,
+        cost_estimate=cost(2 * 3 * work, 8 << 20),
     )(place, *moved, kin)
-    mixed = swap_pieces(turns, mixed)
+    mixed = [send(turn, piece) for turn, piece in zip(turns, mixed)]
     half_spec = pl.BlockSpec((rows // steps * length, LANES), lambda i: (i % (steps // 2), 0))
     update = pl.pallas_call(
         functools.partial(update_kernel, sizes, steps, turns),

time: 420 us -> 405 us (0.964)
  starting transfers between devices: 123 us -> 108 us
    ppermute x30, starting transfers between devices: 90.9 us -> 65.6 us  [send(): lax.ppermute(piece, 'grid', [(spot, spot ^ turn) for spot in range(grid)])]
    all_to_all x1 -> x2, starting transfers between devices: 7.01 us -> 17.5 us  [swap(): lax.all_to_all(flat, 'grid', split_axis=0, concat_axis=0)]
    pallas_call x3 -> x4, Pallas kernels: 22.3 us -> 18.2 us  [the longest x1 6.53 us: packed_path(): pl.pallas_call(functools.partial(along_kernel, sizes, steps, turns), grid...]
    all_to_all x1 -> x2, waiting for transfers between devices: 65.6 us -> 65.6 us  [swap(): lax.all_to_all(flat, 'grid', split_axis=0, concat_axis=0)]
  transfers between devices with their start and end apart: 36 -> 37, of which waited for: 15 -> 19; matrix products, arithmetic and copies ran while one was open for 0% -> 0% of each run, Pallas kernels for 7% -> 7%
where the time goes in v7:
time: 405 us; the launch traced here: 404 us
  waiting for transfers between devices  225 us (56%)
  starting transfers between devices  108 us (27%)
  Pallas kernels  61.2 us (15%)
  local copies, waits for them, and re-layouts  7.75 us (2%)
    ppermute x30, waiting for transfers between devices, send(): lax.ppermute(piece, 'grid', [(spot, spot ^ turn) for spot in range(grid)])  76 us
    ppermute x30, starting transfers between devices, send(): lax.ppermute(piece, 'grid', [(spot, spot ^ turn) for spot in range(grid)])  65.6 us
    all_to_all x2, waiting for transfers between devices, swap(): lax.all_to_all(flat, 'grid', split_axis=0, concat_axis=0)  65.6 us
    all_to_all x2, waiting for transfers between devices, swap_all(): lax.all_to_all(flat, ('band', 'grid'), split_axis=0, concat_axis=0)  46 us
    ppermute x1, waiting for transfers between devices, packed_path(): lower_other = lax.ppermute(lower, 'band', [(0, 1), (1, 0)])  37.9 us
    all_to_all x2, starting transfers between devices, swap_all(): lax.all_to_all(flat, ('band', 'grid'), split_axis=0, concat_axis=0)  19.8 us
    all_to_all x2, starting transfers between devices, swap(): lax.all_to_all(flat, 'grid', split_axis=0, concat_axis=0)  17.5 us
    pallas_call x1, Pallas kernels, packed_path(): pl.pallas_call(functools.partial(plane_kernel, sizes, bunch, turns), grid...  13.9 us
  transfers between devices with their start and end apart: 37, of which 19 were waited for; matrix products, arithmetic and copies ran while one was open for 0% of the time, Pallas kernels for 7%

profile of v7, /device:TPU:0, one launch (start us, length us, event | category | flops | bytes accessed | tf_op | source)
XLA Modules:
  0.0 404.1 jit_solution(12982291039127653037)
XLA Ops:
  0.6 4.1 %shard_map.86 = f32[1792,128]{1,0:T(8,128)} custom-call(s32[1]{0:T(128)} %bitcast.place_ref, f32[12,192,192]{2,1,0:T(8,128)} %ion_ref.3, f32[12,192,192]{2,1,0:T(8,128)} %hxc_ref.3), custom_call_target="tpu_custom_call" | custom-call | bytes 6291456 | tf_op jit(solution)/shard_map/pallas_call | solution.py:450
  4.8 7.4 %all-to-all-start = ((f32[16,112,128]{2,1,0:T(8,128)}), f32[16,112,128]{2,1,0:T(8,128)S(1)}, u32[]{:S(2)}, u32[]{:S(2)}) async-start(f32[16,112,128]{2,1,0:T(8,128)} %bitcast.22), calls=%async_computation | async-start | bytes 1835008 | tf_op jit(solution)/shard_map/all_to_all | solution.py:440
  12.1 5.3 %shard_map.87 = (f32[432,128]{1,0:T(8,128)}, f32[432,128]{1,0:T(8,128)}, f32[432,128]{1,0:T(8,128)}, f32[432,128]{1,0:T(8,128)}, f32[432,128]{1,0:T(8,128)}, /*i...) custom-call(s32[1]{0:T(128)} %bitcast.place_ref, ...), custom_call_target="tpu_custom_call" | custom-call | bytes 8388608 | tf_op jit(solution)/shard_map/pallas_call | solution.py:462
  17.9 3.5 collective-permute-start.4
  24.4 13.9 %shard_map.88 = (f32[432,128]{1,0:T(8,128)}, f32[432,128]{1,0:T(8,128)}, f32[432,128]{1,0:T(8,128)}, f32[432,128]{1,0:T(8,128)}, f32[432,128]{1,0:T(8,128)}, /*i...) custom-call(s32[1]{0:T(128)} %bitcast.place_ref, ...), custom_call_target="tpu_custom_call" | custom-call | flops 4076863488 | bytes 20971520 | tf_op jit(solution)/shard_map/pallas_call | solution.py:474
  38.3 17.9 %collective-permute-done.4.refs_5_ = f32[432,128]{1,0:T(8,128)S(1)} collective-permute-done((f32[432,128]{1,0:T(8,128)}, f32[432,128]{1,0:T(8,128)S(1)}, u32[]{:S(2)}, u32[]{:S(2)}) %collective-permute-start.4) | collective-permute-done | bytes 221216 | tf_op jit(solution)/shard_map/ppermute | solution.py:435
  59.2 3.0 collective-permute-start.6
  62.2 7.4 %collective-permute-done.refs_1_ = f32[432,128]{1,0:T(8,128)S(1)} collective-permute-done((f32[432,128]{1,0:T(8,128)}, f32[432,128]{1,0:T(8,128)S(1)}, u32[]{:S(2)}, u32[]{:S(2)}) %collective-permute-start) | collective-permute-done | bytes 221216 | tf_op jit(solution)/shard_map/ppermute | solution.py:435
  69.8 4.0 collective-permute-done.9.refs_10_
  75.8 3.5 collective-permute-start.13
  79.3 6.5 %collective-permute-start.12 = (f32[432,128]{1,0:T(8,128)S(1)}, f32[432,128]{1,0:T(8,128)S(1)}, u32[]{:S(2)}, u32[]{:S(2)}) collective-permute-start(f32[432,128]{1,0:T(8,128)S(1)} %copy-done.33), channel_id=1, source_target_pairs={{0,14},{1,15},{2,12},{3,13},{4,10},{5,11},{6,8},{7,9},{8,6},{9,7},... | collective-permute-start | bytes 663560 | tf_op jit(solution)/shard_map/ppermute | solution.py:435
  88.5 6.6 %collective-permute-start.10 = (f32[432,128]{1,0:T(8,128)}, f32[432,128]{1,0:T(8,128)}, u32[]{:S(2)}, u32[]{:S(2)}) collective-permute-start(f32[432,128]{1,0:T(8,128)} %get-tuple-element.89), channel_id=1, source_target_pairs={{0,13},{1,12},{2,15},{3,14},{4,9},{5,8},{6,11},{7,10},{8,5},{9,4},... | collective-permute-start | bytes 663560 | tf_op jit(solution)/shard_map/ppermute | solution.py:435
  95.1 6.7 %collective-permute-start.20 = (f32[432,128]{1,0:T(8,128)}, f32[432,128]{1,0:T(8,128)}, u32[]{:S(2)}, u32[]{:S(2)}) collective-permute-start(f32[432,128]{1,0:T(8,128)} %get-tuple-element.109), channel_id=1, source_target_pairs={{0,10},{1,11},{2,8},{3,9},{4,14},{5,15},{6,12},{7,13},{8,2},{9,3},... | collective-permute-start | bytes 663560 | tf_op jit(solution)/shard_map/ppermute | solution.py:435
  104.6 11.9 %collective-permute-start.18 = (f32[432,128]{1,0:T(8,128)}, f32[432,128]{1,0:T(8,128)}, u32[]{:S(2)}, u32[]{:S(2)}) collective-permute-start(f32[432,128]{1,0:T(8,128)} %get-tuple-element.105), channel_id=1, source_target_pairs={{0,9},{1,8},{2,11},{3,10},{4,13},{5,12},{6,15},{7,14},{8,1},{9,0},... | collective-permute-start | bytes 663560 | tf_op jit(solution)/shard_map/ppermute | solution.py:435
  122.3 8.1 %collective-permute-done.20.refs_5_ = f32[432,128]{1,0:T(8,128)} collective-permute-done((f32[432,128]{1,0:T(8,128)}, f32[432,128]{1,0:T(8,128)}, u32[]{:S(2)}, u32[]{:S(2)}) %collective-permute-start.20) | collective-permute-done | bytes 221216 | tf_op jit(solution)/shard_map/ppermute | solution.py:435
  134.0 9.4 %collective-permute-done.16.refs_1_ = f32[432,128]{1,0:T(8,128)S(1)} collective-permute-done((f32[432,128]{1,0:T(8,128)}, f32[432,128]{1,0:T(8,128)S(1)}, u32[]{:S(2)}, u32[]{:S(2)}) %collective-permute-start.16) | collective-permute-done | bytes 221216 | tf_op jit(solution)/shard_map/ppermute | solution.py:435
  144.0 4.1 %collective-permute-done.24.refs_9_ = f32[432,128]{1,0:T(8,128)S(1)} collective-permute-done((f32[432,128]{1,0:T(8,128)}, f32[432,128]{1,0:T(8,128)S(1)}, u32[]{:S(2)}, u32[]{:S(2)}) %collective-permute-start.24) | collective-permute-done | bytes 221216 | tf_op jit(solution)/shard_map/ppermute | solution.py:435
  148.1 3.0 collective-permute-start.30
  155.0 12.4 %collective-permute-done.22.refs_7_ = f32[432,128]{1,0:T(8,128)S(1)} collective-permute-done((f32[432,128]{1,0:T(8,128)}, f32[432,128]{1,0:T(8,128)S(1)}, u32[]{:S(2)}, u32[]{:S(2)}) %collective-permute-start.22) | collective-permute-done | bytes 221216 | tf_op jit(solution)/shard_map/ppermute | solution.py:435
  171.8 6.5 %shard_map.89.along_ref = f32[3456,256]{1,0:T(8,128)} custom-call(s32[1]{0:T(128)} %bitcast.place_ref, f32[432,128]{1,0:T(8,128)} %get-tuple-element.70.refs_0_, f32[432,128]{1,0:T(8,128)} %copy-done.12, f32[432,128]{1,0:T(8,128)} %copy-done.8, f32[432,128]{1,0:T(8,128)} %copy-done.11, f32[432,128]{1,0:T(8,128)} %copy-done.10, f32[432,128]{1,0:T(8,128)} %copy-done.9, ...), custom_call_target="tpu_custom_call" | custom-call | flops 1019215872 | bytes 8388608 | tf_op jit(solution)/shard_map/pallas_call | solution.py:495
  178.7 2.8 collective-permute-done.27.refs_12_
  181.5 3.9 collective-permute-done.26.refs_11_
  186.3 9.0 %shard_map.91 = f32[6912,128]{1,0:T(8,128)} custom-call(s32[1]{0:T(128)} %bitcast.place_ref, f32[3456,256]{1,0:T(8,128)} %shard_map.89.along_ref, f32[1728,128]{1,0:T(8,128)} %shard_map.90.own_ref, f32[1728,128]{1,0:T(8,128)} %copy-done.5, f32[192,192]{1,0:T(8,128)} %constant.23.clone.kin_ref.refs_16_, f32[432,128]{1,0:T(8,128)} %get-tuple-element.99.refs_0_, ...), custom_call_target="tpu_custom_call" | custom-call | flops 1019215872 | bytes 14680064 | tf_op jit(solution)/shard_map/pallas_call | solution.py:507
  195.3 10.2 %all-to-all-start.1 = ((f32[16,432,128]{2,1,0:T(8,128)}), f32[16,432,128]{2,1,0:T(8,128)S(1)}, u32[]{:S(2)}, u32[]{:S(2)}) async-start(f32[16,432,128]{2,1,0:T(8,128)} %bitcast.18), calls=%async_computation.1 | async-start | bytes 7077888 | tf_op jit(solution)/shard_map/all_to_all | solution.py:440
  206.2 65.6 %all-to-all-done.1 = f32[16,432,128]{2,1,0:T(8,128)S(1)} async-done(((f32[16,432,128]{2,1,0:T(8,128)}), f32[16,432,128]{2,1,0:T(8,128)S(1)}, u32[]{:S(2)}, u32[]{:S(2)}) %all-to-all-start.1) | async-done | bytes 3538976 | tf_op jit(solution)/shard_map/all_to_all | solution.py:440
  273.6 11.0 %shard_map.92 = (f32[1,2,12,192,192]{4,3,2,1,0:T(8,128)}, f32[1728,128]{1,0:T(8,128)}, f32[1728,128]{1,0:T(8,128)}, f32[3584,128]{1,0:T(8,128)}) custom-call(f32[1]{0:T(128)S(6)} %copy.12.occ_ref, f32[6912,128]{1,0:T(8,128)} %bitcast.19, f32[2,12,192,192]{3,2,1,0:T(8,128)} %get-tuple-element.78.base_ref, f32[2,192,192]{2,1,0:T(8,128)} %constant.24.clone.tables_ref), custom_call_target="tpu_custom_call" | custom-call | flops 2038431744 | bytes 16777216 | tf_op jit(solution)/shard_map/pallas_call | solution.py:526
  284.6 17.0 %all-to-all-start.2 = ((f32[32,112,128]{2,1,0:T(8,128)}), f32[32,112,128]{2,1,0:T(8,128)S(1)}, u32[]{:S(2)}, u32[]{:S(2)}) async-start(f32[32,112,128]{2,1,0:T(8,128)} %bitcast.23), calls=%async_computation.2 | async-start | bytes 3670016 | tf_op jit(solution)/shard_map/all_to_all | solution.py:444
  304.2 41.5 %all-to-all-done.2 = f32[32,112,128]{2,1,0:T(8,128)S(1)} async-done(((f32[32,112,128]{2,1,0:T(8,128)}), f32[32,112,128]{2,1,0:T(8,128)S(1)}, u32[]{:S(2)}, u32[]{:S(2)}) %all-to-all-start.2) | async-done | bytes 1835040 | tf_op jit(solution)/shard_map/all_to_all | solution.py:444
  349.1 2.8 all-to-all-start.3
  353.7 37.9 %collective-permute-done.32.lower_other = f32[1728,128]{1,0:T(8,128)} collective-permute-done((f32[1728,128]{1,0:T(8,128)S(1)}, f32[1728,128]{1,0:T(8,128)}, u32[]{:S(2)}, u32[]{:S(2)}) %collective-permute-start.32) | collective-permute-done | bytes 884768 | tf_op jit(solution)/shard_map/ppermute | solution.py:547
  391.6 4.4 %all-to-all-done.3 = f32[32,112,128]{2,1,0:T(8,128)S(1)} async-done(((f32[32,112,128]{2,1,0:T(8,128)}), f32[32,112,128]{2,1,0:T(8,128)S(1)}, u32[]{:S(2)}, u32[]{:S(2)}) %all-to-all-start.3) | async-done | bytes 1835040 | tf_op jit(solution)/shard_map/all_to_all | solution.py:444
  397.3 6.8 %shard_map.94 = f32[12,192,192]{2,1,0:T(8,128)} custom-call(f32[3584,128]{1,0:T(8,128)} %bitcast.20, f32[1728,128]{1,0:T(8,128)} %get-tuple-element.132.upper_ref, f32[1728,128]{1,0:T(8,128)} %get-tuple-element.134.lower_ref, f32[1728,128]{1,0:T(8,128)} %collective-permute-done.31.upper_other, f32[1728,128]{1,0:T(8,128)} %collective-permute-done.32.lower_other, ...), custom_call_target="tpu_custom_call" | custom-call | flops 2038431744 | bytes 6291456 | tf_op jit(solution)/shard_map/pallas_call | solution.py:568
  (135 shorter events, 44.2 us)
Async XLA Ops:
  4.8 111.8 %all-to-all-start = ((f32[16,112,128]{2,1,0:T(8,128)}), f32[16,112,128]{2,1,0:T(8,128)S(1)}, u32[]{:S(2)}, u32[]{:S(2)}) async-start(f32[16,112,128]{2,1,0:T(8,128)} %bitcast.22), calls=%async_computation | async-start | bytes 1835008 | tf_op jit(solution)/shard_map/all_to_all | solution.py:440
  17.9 38.3 %collective-permute-start.4 = (f32[432,128]{1,0:T(8,128)}, f32[432,128]{1,0:T(8,128)S(1)}, u32[]{:S(2)}, u32[]{:S(2)}) collective-permute-start(f32[432,128]{1,0:T(8,128)} %get-tuple-element.75), channel_id=1, source_target_pairs={{0,10},{1,11},{2,8},{3,9},{4,14},{5,15},{6,12},{7,13},{8,2},{9,3},... | collective-permute-start | bytes 663560 | tf_op jit(solution)/shard_map/ppermute | solution.py:435
  21.4 34.8 %collective-permute-start.3 = (f32[432,128]{1,0:T(8,128)}, f32[432,128]{1,0:T(8,128)S(1)}, u32[]{:S(2)}, u32[]{:S(2)}) collective-permute-start(f32[432,128]{1,0:T(8,128)} %get-tuple-element.74), channel_id=1, source_target_pairs={{0,2},{1,3},{2,0},{3,1},{4,6},{5,7},{6,4},{7,5},{8,10},{9,11},{10,... | collective-permute-start | bytes 663560 | tf_op jit(solution)/shard_map/ppermute | solution.py:435
  21.9 37.2 %collective-permute-start.2 = (f32[432,128]{1,0:T(8,128)}, f32[432,128]{1,0:T(8,128)S(1)}, u32[]{:S(2)}, u32[]{:S(2)}) collective-permute-start(f32[432,128]{1,0:T(8,128)} %get-tuple-element.73), channel_id=1, source_target_pairs={{0,9},{1,8},{2,11},{3,10},{4,13},{5,12},{6,15},{7,14},{8,1},{9,0},... | collective-permute-start | bytes 663560 | tf_op jit(solution)/shard_map/ppermute | solution.py:435
  22.0 47.6 %collective-permute-start = (f32[432,128]{1,0:T(8,128)}, f32[432,128]{1,0:T(8,128)S(1)}, u32[]{:S(2)}, u32[]{:S(2)}) collective-permute-start(f32[432,128]{1,0:T(8,128)} %get-tuple-element.71), channel_id=1, source_target_pairs={{0,8},{1,9},{2,10},{3,11},{4,12},{5,13},{6,14},{7,15},{8,0},{9,1},... | collective-permute-start | bytes 663560 | tf_op jit(solution)/shard_map/ppermute | solution.py:435
  56.2 17.6 %collective-permute-start.9 = (f32[432,128]{1,0:T(8,128)S(1)}, f32[432,128]{1,0:T(8,128)S(1)}, u32[]{:S(2)}, u32[]{:S(2)}) collective-permute-start(f32[432,128]{1,0:T(8,128)S(1)} %copy-done.40), channel_id=1, source_target_pairs={{0,5},{1,4},{2,7},{3,6},{4,1},{5,0},{6,3},{7,2},{8,13},{9,12},{10,... | collective-permute-start | bytes 663560 | tf_op jit(solution)/shard_map/ppermute | solution.py:435
  56.3 19.6 %collective-permute-start.8 = (f32[432,128]{1,0:T(8,128)S(1)}, f32[432,128]{1,0:T(8,128)S(1)}, u32[]{:S(2)}, u32[]{:S(2)}) collective-permute-start(f32[432,128]{1,0:T(8,128)S(1)} %copy-done.39), channel_id=1, source_target_pairs={{0,12},{1,13},{2,14},{3,15},{4,8},{5,9},{6,10},{7,11},{8,4},{9,5},... | collective-permute-start | bytes 663560 | tf_op jit(solution)/shard_map/ppermute | solution.py:435
  59.2 20.1 %collective-permute-start.7 = (f32[432,128]{1,0:T(8,128)S(1)}, f32[432,128]{1,0:T(8,128)S(1)}, u32[]{:S(2)}, u32[]{:S(2)}) collective-permute-start(f32[432,128]{1,0:T(8,128)S(1)} %copy-done.38), channel_id=1, source_target_pairs={{0,4},{1,5},{2,6},{3,7},{4,0},{5,1},{6,2},{7,3},{8,12},{9,13},{10,... | collective-permute-start | bytes 663560 | tf_op jit(solution)/shard_map/ppermute | solution.py:435
  59.2 29.3 %collective-permute-start.6 = (f32[432,128]{1,0:T(8,128)S(1)}, f32[432,128]{1,0:T(8,128)S(1)}, u32[]{:S(2)}, u32[]{:S(2)}) collective-permute-start(f32[432,128]{1,0:T(8,128)S(1)} %copy-done.37), channel_id=1, source_target_pairs={{0,11},{1,10},{2,9},{3,8},{4,15},{5,14},{6,13},{7,12},{8,3},{9,2},... | collective-permute-start | bytes 663560 | tf_op jit(solution)/shard_map/ppermute | solution.py:435
  69.6 18.9 %collective-permute-start.5 = (f32[432,128]{1,0:T(8,128)S(1)}, f32[432,128]{1,0:T(8,128)S(1)}, u32[]{:S(2)}, u32[]{:S(2)}) collective-permute-start(f32[432,128]{1,0:T(8,128)S(1)} %copy-done.36), channel_id=1, source_target_pairs={{0,3},{1,2},{2,1},{3,0},{4,7},{5,6},{6,5},{7,4},{8,11},{9,10},{10,... | collective-permute-start | bytes 663560 | tf_op jit(solution)/shard_map/ppermute | solution.py:435
  73.9 21.3 %collective-permute-start.14 = (f32[432,128]{1,0:T(8,128)S(1)}, f32[432,128]{1,0:T(8,128)S(1)}, u32[]{:S(2)}, u32[]{:S(2)}) collective-permute-start(f32[432,128]{1,0:T(8,128)S(1)} %copy-done.35), channel_id=1, source_target_pairs={{0,15},{1,14},{2,13},{3,12},{4,11},{5,10},{6,9},{7,8},{8,7},{9,6},... | collective-permute-start | bytes 663560 | tf_op jit(solution)/shard_map/ppermute | solution.py:435
  75.8 26.0 %collective-permute-start.13 = (f32[432,128]{1,0:T(8,128)S(1)}, f32[432,128]{1,0:T(8,128)S(1)}, u32[]{:S(2)}, u32[]{:S(2)}) collective-permute-start(f32[432,128]{1,0:T(8,128)S(1)} %copy-done.34), channel_id=1, source_target_pairs={{0,7},{1,6},{2,5},{3,4},{4,3},{5,2},{6,1},{7,0},{8,15},{9,14},{10,... | collective-permute-start | bytes 663560 | tf_op jit(solution)/shard_map/ppermute | solution.py:435
  79.3 24.6 %collective-permute-start.12 = (f32[432,128]{1,0:T(8,128)S(1)}, f32[432,128]{1,0:T(8,128)S(1)}, u32[]{:S(2)}, u32[]{:S(2)}) collective-permute-start(f32[432,128]{1,0:T(8,128)S(1)} %copy-done.33), channel_id=1, source_target_pairs={{0,14},{1,15},{2,12},{3,13},{4,10},{5,11},{6,8},{7,9},{8,6},{9,7},... | collective-permute-start | bytes 663560 | tf_op jit(solution)/shard_map/ppermute | solution.py:435
  88.5 31.2 %collective-permute-start.11 = (f32[432,128]{1,0:T(8,128)}, f32[432,128]{1,0:T(8,128)}, u32[]{:S(2)}, u32[]{:S(2)}) collective-permute-start(f32[432,128]{1,0:T(8,128)} %get-tuple-element.91), channel_id=1, source_target_pairs={{0,6},{1,7},{2,4},{3,5},{4,2},{5,3},{6,0},{7,1},{8,14},{9,15},{10,... | collective-permute-start | bytes 663560 | tf_op jit(solution)/shard_map/ppermute | solution.py:435
  88.5 32.7 %collective-permute-start.10 = (f32[432,128]{1,0:T(8,128)}, f32[432,128]{1,0:T(8,128)}, u32[]{:S(2)}, u32[]{:S(2)}) collective-permute-start(f32[432,128]{1,0:T(8,128)} %get-tuple-element.89), channel_id=1, source_target_pairs={{0,13},{1,12},{2,15},{3,14},{4,9},{5,8},{6,11},{7,10},{8,5},{9,4},... | collective-permute-start | bytes 663560 | tf_op jit(solution)/shard_map/ppermute | solution.py:435
  95.1 35.2 %collective-permute-start.20 = (f32[432,128]{1,0:T(8,128)}, f32[432,128]{1,0:T(8,128)}, u32[]{:S(2)}, u32[]{:S(2)}) collective-permute-start(f32[432,128]{1,0:T(8,128)} %get-tuple-element.109), channel_id=1, source_target_pairs={{0,10},{1,11},{2,8},{3,9},{4,14},{5,15},{6,12},{7,13},{8,2},{9,3},... | collective-permute-start | bytes 663560 | tf_op jit(solution)/shard_map/ppermute | solution.py:435
  101.8 28.6 %collective-permute-start.19 = (f32[432,128]{1,0:T(8,128)}, f32[432,128]{1,0:T(8,128)}, u32[]{:S(2)}, u32[]{:S(2)}) collective-permute-start(f32[432,128]{1,0:T(8,128)} %get-tuple-element.107), channel_id=1, source_target_pairs={{0,2},{1,3},{2,0},{3,1},{4,6},{5,7},{6,4},{7,5},{8,10},{9,11},{10,... | collective-permute-start | bytes 663560 | tf_op jit(solution)/shard_map/ppermute | solution.py:435
  104.6 26.9 %collective-permute-start.18 = (f32[432,128]{1,0:T(8,128)}, f32[432,128]{1,0:T(8,128)}, u32[]{:S(2)}, u32[]{:S(2)}) collective-permute-start(f32[432,128]{1,0:T(8,128)} %get-tuple-element.105), channel_id=1, source_target_pairs={{0,9},{1,8},{2,11},{3,10},{4,13},{5,12},{6,15},{7,14},{8,1},{9,0},... | collective-permute-start | bytes 663560 | tf_op jit(solution)/shard_map/ppermute | solution.py:435
  119.7 65.7 %collective-permute-start.15 = (f32[1728,128]{1,0:T(8,128)}, f32[1728,128]{1,0:T(8,128)S(1)}, u32[]{:S(2)}, u32[]{:S(2)}) collective-permute-start(f32[1728,128]{1,0:T(8,128)} %shard_map.90.own_ref), channel_id=1, source_target_pairs={{0,16},{16,0},{1,17},{17,1},{2,18},{18,2},{3,19},{19,3},{4,20},{20... | collective-permute-start | bytes 2654216 | tf_op jit(solution)/shard_map/ppermute | solution.py:494
  130.4 13.0 %collective-permute-start.25 = (f32[432,128]{1,0:T(8,128)}, f32[432,128]{1,0:T(8,128)S(1)}, u32[]{:S(2)}, u32[]{:S(2)}) collective-permute-start(f32[432,128]{1,0:T(8,128)} %get-tuple-element.119), channel_id=1, source_target_pairs={{0,5},{1,4},{2,7},{3,6},{4,1},{5,0},{6,3},{7,2},{8,13},{9,12},{10,... | collective-permute-start | bytes 663560 | tf_op jit(solution)/shard_map/ppermute | solution.py:435
  131.5 16.6 %collective-permute-start.24 = (f32[432,128]{1,0:T(8,128)}, f32[432,128]{1,0:T(8,128)S(1)}, u32[]{:S(2)}, u32[]{:S(2)}) collective-permute-start(f32[432,128]{1,0:T(8,128)} %get-tuple-element.117), channel_id=1, source_target_pairs={{0,12},{1,13},{2,14},{3,15},{4,8},{5,9},{6,10},{7,11},{8,4},{9,5},... | collective-permute-start | bytes 663560 | tf_op jit(solution)/shard_map/ppermute | solution.py:435
  133.3 19.2 %collective-permute-start.23 = (f32[432,128]{1,0:T(8,128)}, f32[432,128]{1,0:T(8,128)S(1)}, u32[]{:S(2)}, u32[]{:S(2)}) collective-permute-start(f32[432,128]{1,0:T(8,128)} %get-tuple-element.115), channel_id=1, source_target_pairs={{0,4},{1,5},{2,6},{3,7},{4,0},{5,1},{6,2},{7,3},{8,12},{9,13},{10,... | collective-permute-start | bytes 663560 | tf_op jit(solution)/shard_map/ppermute | solution.py:435
  143.4 24.0 %collective-permute-start.22 = (f32[432,128]{1,0:T(8,128)}, f32[432,128]{1,0:T(8,128)S(1)}, u32[]{:S(2)}, u32[]{:S(2)}) collective-permute-start(f32[432,128]{1,0:T(8,128)} %get-tuple-element.113), channel_id=1, source_target_pairs={{0,11},{1,10},{2,9},{3,8},{4,15},{5,14},{6,13},{7,12},{8,3},{9,2},... | collective-permute-start | bytes 663560 | tf_op jit(solution)/shard_map/ppermute | solution.py:435
  143.4 25.5 %collective-permute-start.21 = (f32[432,128]{1,0:T(8,128)}, f32[432,128]{1,0:T(8,128)S(1)}, u32[]{:S(2)}, u32[]{:S(2)}) collective-permute-start(f32[432,128]{1,0:T(8,128)} %get-tuple-element.111), channel_id=1, source_target_pairs={{0,3},{1,2},{2,1},{3,0},{4,7},{5,6},{6,5},{7,4},{8,11},{9,10},{10,... | collective-permute-start | bytes 663560 | tf_op jit(solution)/shard_map/ppermute | solution.py:435
  148.1 20.9 %collective-permute-start.30 = (f32[432,128]{1,0:T(8,128)}, f32[432,128]{1,0:T(8,128)S(1)}, u32[]{:S(2)}, u32[]{:S(2)}) collective-permute-start(f32[432,128]{1,0:T(8,128)} %get-tuple-element.129), channel_id=1, source_target_pairs={{0,15},{1,14},{2,13},{3,12},{4,11},{5,10},{6,9},{7,8},{8,7},{9,6},... | collective-permute-start | bytes 663560 | tf_op jit(solution)/shard_map/ppermute | solution.py:435
  152.5 25.9 %collective-permute-start.29 = (f32[432,128]{1,0:T(8,128)}, f32[432,128]{1,0:T(8,128)S(1)}, u32[]{:S(2)}, u32[]{:S(2)}) collective-permute-start(f32[432,128]{1,0:T(8,128)} %get-tuple-element.127), channel_id=1, source_target_pairs={{0,7},{1,6},{2,5},{3,4},{4,3},{5,2},{6,1},{7,0},{8,15},{9,14},{10,... | collective-permute-start | bytes 663560 | tf_op jit(solution)/shard_map/ppermute | solution.py:435
  168.9 16.4 %collective-permute-start.26 = (f32[432,128]{1,0:T(8,128)}, f32[432,128]{1,0:T(8,128)S(1)}, u32[]{:S(2)}, u32[]{:S(2)}) collective-permute-start(f32[432,128]{1,0:T(8,128)} %get-tuple-element.121), channel_id=1, source_target_pairs={{0,13},{1,12},{2,15},{3,14},{4,9},{5,8},{6,11},{7,10},{8,5},{9,4},... | collective-permute-start | bytes 663560 | tf_op jit(solution)/shard_map/ppermute | solution.py:435
  195.3 76.4 %all-to-all-start.1 = ((f32[16,432,128]{2,1,0:T(8,128)}), f32[16,432,128]{2,1,0:T(8,128)S(1)}, u32[]{:S(2)}, u32[]{:S(2)}) async-start(f32[16,432,128]{2,1,0:T(8,128)} %bitcast.18), calls=%async_computation.1 | async-start | bytes 7077888 | tf_op jit(solution)/shard_map/all_to_all | solution.py:440
  284.6 61.1 %all-to-all-start.2 = ((f32[32,112,128]{2,1,0:T(8,128)}), f32[32,112,128]{2,1,0:T(8,128)S(1)}, u32[]{:S(2)}, u32[]{:S(2)}) async-start(f32[32,112,128]{2,1,0:T(8,128)} %bitcast.23), calls=%async_computation.2 | async-start | bytes 3670016 | tf_op jit(solution)/shard_map/all_to_all | solution.py:444
  301.6 47.5 %collective-permute-start.31 = (f32[1728,128]{1,0:T(8,128)S(1)}, f32[1728,128]{1,0:T(8,128)}, u32[]{:S(2)}, u32[]{:S(2)}) collective-permute-start(f32[1728,128]{1,0:T(8,128)S(1)} %copy-done.6), channel_id=1, source_target_pairs={{0,16},{16,0},{1,17},{17,1},{2,18},{18,2},{3,19},{19,3},{4,20},{20... | collective-permute-start | bytes 2654216 | tf_op jit(solution)/shard_map/ppermute | solution.py:546
  349.1 46.9 %all-to-all-start.3 = ((f32[32,112,128]{2,1,0:T(8,128)}), f32[32,112,128]{2,1,0:T(8,128)S(1)}, u32[]{:S(2)}, u32[]{:S(2)}) async-start(f32[32,112,128]{2,1,0:T(8,128)} %bitcast.16), calls=%async_computation.3 | async-start | bytes 3670016 | tf_op jit(solution)/shard_map/all_to_all | solution.py:444
  352.0 39.6 %collective-permute-start.32 = (f32[1728,128]{1,0:T(8,128)S(1)}, f32[1728,128]{1,0:T(8,128)}, u32[]{:S(2)}, u32[]{:S(2)}) collective-permute-start(f32[1728,128]{1,0:T(8,128)S(1)} %copy-done.7), channel_id=1, source_target_pairs={{0,16},{16,0},{1,17},{17,1},{2,18},{18,2},{3,19},{19,3},{4,20},{20... | collective-permute-start | bytes 2654216 | tf_op jit(solution)/shard_map/ppermute | solution.py:547
  (46 other events, 1775.8 us)

commit v8 on v7

--- a/solution.py
+++ b/solution.py
@@ -314,7 +314,7 @@
             out_ref[pl.ds(to * chunk + plane * share, share), :] = slot[pl.ds(to * share, share), :]
 
 
-def filter_kernel(sizes, spec_ref, cells_ref, tables_ref, out_ref, lines):
+def filter_kernel(sizes, spec_ref, cells_ref, tables_ref, upper_ref, lower_ref, lines):
     planes, grid, rows, share = sizes
     length = planes * grid
     chunk = chunk_rows(sizes)
@@ -337,31 +337,37 @@
     kernel = jnp.where(total > 0.0, scale / (total + 1.0), 0.0)
     field = kernel * product(tables_ref[0], lines[...])
     lines[...] = product_of_parts(split(tables_ref[1]), split(field))
-    for first, second, here in places():
-        piece = lines[here]
-        out_ref[first, :] = piece
-        out_ref[second, :] = piece
-    used = planes * share
-    if used < chunk:
-        for to in range(2 * grid):
-            out_ref[pl.ds(to * chunk + used, chunk - used), :] = jnp.zeros((chunk - used, LANES), jnp.float32)
+    some = planes // 2
+    chunk = whole_tiles(some * share)
+    for part, out_ref in enumerate((upper_ref, lower_ref)):
+        for source in range(grid):
+            for row in range(share):
+                piece = lines[pl.ds(source * planes + part * some, some), row * LANES : (row + 1) * LANES]
+                out_ref[pl.ds(source * chunk + row, some, stride=share), :] = piece
+            if some * share < chunk:
+                rest = chunk - some * share
+                out_ref[pl.ds(source * chunk + some * share, rest), :] = jnp.zeros((rest, LANES), jnp.float32)
 
 
 def last_kernel(
-    sizes, bunch, spec_ref, upper_ref, lower_ref, upper_other, lower_other, tables_ref, out_ref, packed
+    sizes, bunch, place_ref, near_ref, far_ref, upper_ref, lower_ref, upper_other, lower_other, tables_ref, *refs
 ):
     planes, grid, rows, share = sizes
+    out_ref, packed = refs[-2:]
     length = planes * grid
     half = rows * grid // 2
-    chunk = chunk_rows(sizes)
+    chunk = whole_tiles(planes // 2 * share)
     turn, basis = split(tables_ref[1]), split(tables_ref[0])
+    band = place_ref[0] // grid
     lines = []
     for inner in range(bunch):
         plane = pl.program_id(0) * bunch + inner
         slot = packed.at[inner * 2]
-        for source in range(2 * grid):
-            start = source * chunk + plane * share
-            slot[pl.ds(source * share, share), :] = spec_ref[pl.ds(start, share), :]
+        for part, spec_ref in ((band, near_ref), (1 - band, far_ref)):
+            side = slot.at[pl.ds(pl.multiple_of(part * half, 8), half), :]
+            for source in range(grid):
+                start = source * chunk + plane * share
+                side[pl.ds(source * share, share), :] = spec_ref[pl.ds(start, share), :]
         lines.append(product_of_parts(turn, split(unpack(slot, length))))
     hartree = product_of_parts(split(jnp.concatenate(lines, axis=0)), basis)
     for inner in range(bunch):
@@ -412,11 +418,14 @@
     tables = jnp.asarray(np.stack([basis_np, basis_np.T]))
     smem = pl.BlockSpec(memory_space=pltpu.SMEM)
     vmem = pl.BlockSpec(memory_space=pltpu.VMEM)
-    bunch = next(count for count in (3, 2, 1) if planes % count == 0)
+    some = planes // 2
+    bunch = next(count for count in (3, 2, 1) if some % count == 0)
+    groups = some // bunch
     psi_spec = pl.BlockSpec((1, 2, bunch, length, length), lambda i: (0, 0, i, 0, 0))
     plane_spec = pl.BlockSpec((bunch, length, length), lambda i: (i, 0, 0))
     pair_spec = pl.BlockSpec((2, bunch, length, length), lambda i: (0, i, 0, 0))
     half_rows = pl.BlockSpec((bunch * cell_rows // 2, LANES), lambda i: (i, 0))
+    part_rows = grid * whole_tiles(some * share)
     square = whole(length, length)
     table_spec = whole(2, length, length)
 
@@ -554,34 +563,41 @@
     )
     device = lax.axis_index("band") * grid + lax.axis_index("grid")
     cells = lax.dynamic_slice_in_dim(jnp.asarray(cells_np), device * share, share, axis=0)
-    spectrum = pl.pallas_call(
+    first, second = pl.pallas_call(
         functools.partial(filter_kernel, sizes),
         in_specs=[vmem] * 3,
-        out_specs=vmem,
-        out_shape=shape(spec_rows, LANES),
+        out_specs=[vmem] * 2,
+        out_shape=[shape(part_rows, LANES)] * 2,
         scratch_shapes=[pltpu.VMEM((length, share * LANES), jnp.float32)],
         compiler_params=SMALL,
         cost_estimate=cost(6 * work, 5 << 20),
     )(spectrum, cells.reshape(1, share * LANES), tables)
-    spectrum, upper_other = lax.optimization_barrier((spectrum, upper_other))
-    spectrum = swap_all(spectrum)
-    potential = pl.pallas_call(
-        functools.partial(last_kernel, sizes, bunch),
-        grid=(planes // bunch,),
-        in_specs=[
-            vmem,
-            half_rows,
-            half_rows,
-            half_rows,
-            half_rows,
-            table_spec,
-        ],
-        out_specs=plane_spec,
-        out_shape=shape(planes, length, length),
-        scratch_shapes=scratch(2),
-        compiler_params=PARAMS,
-        cost_estimate=cost(2 * 6 * work, 6 << 20),
-    )(spectrum, upper, lower, upper_other, lower_other, tables)
+
+    def last_part(part, near, far, made):
+        cells_spec = pl.BlockSpec((bunch * cell_rows // 2, LANES), lambda i: (i + part * groups, 0))
+        return pl.pallas_call(
+            functools.partial(last_kernel, sizes, bunch),
+            grid=(groups,),
+            in_specs=[smem, vmem, vmem]
+            + [cells_spec] * 4
+            + [table_spec]
+            + [pl.BlockSpec(memory_space=pl.ANY)] * len(made),
+            out_specs=pl.BlockSpec((bunch, length, length), lambda i: (i + part * groups, 0, 0)),
+            out_shape=shape(planes, length, length),
+            scratch_shapes=scratch(2),
+            input_output_aliases={8: 0} if made else {},
+            compiler_params=PARAMS,
+            cost_estimate=cost(3 * work, 4 << 20),
+        )(place, near, far, upper, lower, upper_other, lower_other, tables, *made)
+
+    first, upper_other = lax.optimization_barrier((first, upper_other))
+    near = swap(first)
+    far = lax.ppermute(near, "band", [(0, 1), (1, 0)])
+    second, lower_other = lax.optimization_barrier((second, lower_other))
+    near_second = swap(second)
+    far_second = lax.ppermute(near_second, "band", [(0, 1), (1, 0)])
+    potential = last_part(0, near, far, [])
+    potential = last_part(1, near_second, far_second, [potential])
     return (fresh, potential)
 
 
@@ -589,7 +605,7 @@
     length = orbitals.shape[-1]
     parts = 2 * lax.axis_size("grid") * LANES
     fits = lax.axis_size("grid") & (lax.axis_size("grid") - 1) == 0
-    fits = fits and length == LANES + LANES // 2 and lax.axis_size("band") == 2 and length * length % parts == 0
+    fits = fits and orbitals.shape[2] % 2 == 0 and length == LANES + LANES // 2 and lax.axis_size("band") == 2 and length * length % parts == 0
     path = packed_path if fits else general
     return path(orbitals, occupations, ion_potential, hxc_potential)
 

time: 405 us -> 401 us (level)
  waiting for transfers between devices: 225 us -> 215 us
  starting transfers between devices: 108 us -> 113 us
    ppermute x1, waiting for transfers between devices: 37.9 us -> 9.64 us  [packed_path(): lower_other = lax.ppermute(lower, 'band', [(0, 1), (1, 0)])]
    all_to_all x2 -> x4, waiting for transfers between devices: 65.6 us -> 81.4 us  [swap(): lax.all_to_all(flat, 'grid', split_axis=0, concat_axis=0)]
    all_to_all x2 -> x4, starting transfers between devices: 17.5 us -> 24.9 us  [swap(): lax.all_to_all(flat, 'grid', split_axis=0, concat_axis=0)]
    ppermute x0 -> x2, waiting for transfers between devices: none -> 6.61 us  [the longest x1 6.61 us: packed_path(): far_second = lax.ppermute(near_second, 'band', [(0, 1), (1, 0)])]
    all_to_all x2 -> x1, waiting for transfers between devices: 46 us -> 41.3 us  [swap_all(): lax.all_to_all(flat, ('band', 'grid'), split_axis=0, concat_axis=0)]
    all_to_all x2 -> x1, starting transfers between devices: 19.8 us -> 17 us  [swap_all(): lax.all_to_all(flat, ('band', 'grid'), split_axis=0, concat_axis=0)]
    pallas_call x1 -> x2, Pallas kernels: 6.82 us -> 8.57 us  [last_part(): pl.pallas_call(functools.partial(last_kernel, sizes, bunch), grid=(groups...]
  transfers between devices with their start and end apart: 37 -> 40, of which waited for: 19 -> 21; matrix products, arithmetic and copies ran while one was open for 0% -> 0% of each run, Pallas kernels for 7% -> 9%
where the time goes in v8:
time: 401 us; the launch traced here: 400 us
  waiting for transfers between devices  215 us (54%)
  starting transfers between devices  113 us (28%)
  Pallas kernels  63.9 us (16%)
  local copies, waits for them, and re-layouts  6.87 us (2%)
    all_to_all x4, waiting for transfers between devices, swap(): lax.all_to_all(flat, 'grid', split_axis=0, concat_axis=0)  81.4 us
    ppermute x30, waiting for transfers between devices, send(): lax.ppermute(piece, 'grid', [(spot, spot ^ turn) for spot in range(grid)])  76 us
    ppermute x30, starting transfers between devices, send(): lax.ppermute(piece, 'grid', [(spot, spot ^ turn) for spot in range(grid)])  65.6 us
    all_to_all x1, waiting for transfers between devices, swap_all(): lax.all_to_all(flat, ('band', 'grid'), split_axis=0, concat_axis=0)  41.3 us
    all_to_all x4, starting transfers between devices, swap(): lax.all_to_all(flat, 'grid', split_axis=0, concat_axis=0)  24.9 us
    all_to_all x1, starting transfers between devices, swap_all(): lax.all_to_all(flat, ('band', 'grid'), split_axis=0, concat_axis=0)  17 us
    pallas_call x1, Pallas kernels, packed_path(): pl.pallas_call(functools.partial(plane_kernel, sizes, bunch, turns), grid...  13.9 us
    pallas_call x1, Pallas kernels, packed_path(): pl.pallas_call(functools.partial(fresh_kernel, sizes, bunch), grid=(plane...  10.9 us
  transfers between devices with their start and end apart: 40, of which 21 were waited for; matrix products, arithmetic and copies ran while one was open for 0% of the time, Pallas kernels for 9%

profile of v8, /device:TPU:0, one launch (start us, length us, event | category | flops | bytes accessed | tf_op | source)
XLA Modules:
  0.0 400.4 jit_solution(13807793881040598002)
XLA Ops:
  0.6 4.1 %shard_map.86 = f32[1792,128]{1,0:T(8,128)} custom-call(s32[1]{0:T(128)} %bitcast.place_ref, f32[12,192,192]{2,1,0:T(8,128)} %ion_ref.3, f32[12,192,192]{2,1,0:T(8,128)} %hxc_ref.3), custom_call_target="tpu_custom_call" | custom-call | bytes 6291456 | tf_op jit(solution)/shard_map/pallas_call | solution.py:459
  4.8 7.4 %all-to-all-start = ((f32[16,112,128]{2,1,0:T(8,128)}), f32[16,112,128]{2,1,0:T(8,128)S(1)}, u32[]{:S(2)}, u32[]{:S(2)}) async-start(f32[16,112,128]{2,1,0:T(8,128)} %bitcast.22), calls=%async_computation | async-start | bytes 1835008 | tf_op jit(solution)/shard_map/all_to_all | solution.py:449
  12.1 5.4 %shard_map.87 = (f32[432,128]{1,0:T(8,128)}, f32[432,128]{1,0:T(8,128)}, f32[432,128]{1,0:T(8,128)}, f32[432,128]{1,0:T(8,128)}, f32[432,128]{1,0:T(8,128)}, /*i...) custom-call(s32[1]{0:T(128)} %bitcast.place_ref, ...), custom_call_target="tpu_custom_call" | custom-call | bytes 8388608 | tf_op jit(solution)/shard_map/pallas_call | solution.py:471
  17.9 3.5 collective-permute-start.4
  24.4 13.9 %shard_map.88 = (f32[432,128]{1,0:T(8,128)}, f32[432,128]{1,0:T(8,128)}, f32[432,128]{1,0:T(8,128)}, f32[432,128]{1,0:T(8,128)}, f32[432,128]{1,0:T(8,128)}, /*i...) custom-call(s32[1]{0:T(128)} %bitcast.place_ref, ...), custom_call_target="tpu_custom_call" | custom-call | flops 4076863488 | bytes 20971520 | tf_op jit(solution)/shard_map/pallas_call | solution.py:483
  38.3 17.9 %collective-permute-done.4.refs_5_ = f32[432,128]{1,0:T(8,128)S(1)} collective-permute-done((f32[432,128]{1,0:T(8,128)}, f32[432,128]{1,0:T(8,128)S(1)}, u32[]{:S(2)}, u32[]{:S(2)}) %collective-permute-start.4) | collective-permute-done | bytes 221216 | tf_op jit(solution)/shard_map/ppermute | solution.py:444
  62.2 7.4 %collective-permute-done.refs_1_ = f32[432,128]{1,0:T(8,128)S(1)} collective-permute-done((f32[432,128]{1,0:T(8,128)}, f32[432,128]{1,0:T(8,128)S(1)}, u32[]{:S(2)}, u32[]{:S(2)}) %collective-permute-start) | collective-permute-done | bytes 221216 | tf_op jit(solution)/shard_map/ppermute | solution.py:444
  69.8 4.0 %collective-permute-done.9.refs_10_ = f32[432,128]{1,0:T(8,128)S(1)} collective-permute-done((f32[432,128]{1,0:T(8,128)S(1)}, f32[432,128]{1,0:T(8,128)S(1)}, u32[]{:S(2)}, u32[]{:S(2)}) %collective-permute-start.9) | collective-permute-done | bytes 221216 | tf_op jit(solution)/shard_map/ppermute | solution.py:444
  79.3 6.5 %collective-permute-start.12 = (f32[432,128]{1,0:T(8,128)S(1)}, f32[432,128]{1,0:T(8,128)S(1)}, u32[]{:S(2)}, u32[]{:S(2)}) collective-permute-start(f32[432,128]{1,0:T(8,128)S(1)} %copy-done.34), channel_id=1, source_target_pairs={{0,14},{1,15},{2,12},{3,13},{4,10},{5,11},{6,8},{7,9},{8,6},{9,7},... | collective-permute-start | bytes 663560 | tf_op jit(solution)/shard_map/ppermute | solution.py:444
  88.5 6.6 %collective-permute-start.10 = (f32[432,128]{1,0:T(8,128)}, f32[432,128]{1,0:T(8,128)}, u32[]{:S(2)}, u32[]{:S(2)}) collective-permute-start(f32[432,128]{1,0:T(8,128)} %get-tuple-element.93), channel_id=1, source_target_pairs={{0,13},{1,12},{2,15},{3,14},{4,9},{5,8},{6,11},{7,10},{8,5},{9,4},... | collective-permute-start | bytes 663560 | tf_op jit(solution)/shard_map/ppermute | solution.py:444
  95.1 6.7 %collective-permute-start.20 = (f32[432,128]{1,0:T(8,128)}, f32[432,128]{1,0:T(8,128)}, u32[]{:S(2)}, u32[]{:S(2)}) collective-permute-start(f32[432,128]{1,0:T(8,128)} %get-tuple-element.113), channel_id=1, source_target_pairs={{0,10},{1,11},{2,8},{3,9},{4,14},{5,15},{6,12},{7,13},{8,2},{9,3},... | collective-permute-start | bytes 663560 | tf_op jit(solution)/shard_map/ppermute | solution.py:444
  104.6 11.9 %collective-permute-start.18 = (f32[432,128]{1,0:T(8,128)}, f32[432,128]{1,0:T(8,128)}, u32[]{:S(2)}, u32[]{:S(2)}) collective-permute-start(f32[432,128]{1,0:T(8,128)} %get-tuple-element.109), channel_id=1, source_target_pairs={{0,9},{1,8},{2,11},{3,10},{4,13},{5,12},{6,15},{7,14},{8,1},{9,0},... | collective-permute-start | bytes 663560 | tf_op jit(solution)/shard_map/ppermute | solution.py:444
  122.2 8.2 %collective-permute-done.20.refs_5_ = f32[432,128]{1,0:T(8,128)} collective-permute-done((f32[432,128]{1,0:T(8,128)}, f32[432,128]{1,0:T(8,128)}, u32[]{:S(2)}, u32[]{:S(2)}) %collective-permute-start.20) | collective-permute-done | bytes 221216 | tf_op jit(solution)/shard_map/ppermute | solution.py:444
  134.0 9.4 %collective-permute-done.16.refs_1_ = f32[432,128]{1,0:T(8,128)S(1)} collective-permute-done((f32[432,128]{1,0:T(8,128)}, f32[432,128]{1,0:T(8,128)S(1)}, u32[]{:S(2)}, u32[]{:S(2)}) %collective-permute-start.16) | collective-permute-done | bytes 221216 | tf_op jit(solution)/shard_map/ppermute | solution.py:444
  144.0 4.1 %collective-permute-done.24.refs_9_ = f32[432,128]{1,0:T(8,128)S(1)} collective-permute-done((f32[432,128]{1,0:T(8,128)}, f32[432,128]{1,0:T(8,128)S(1)}, u32[]{:S(2)}, u32[]{:S(2)}) %collective-permute-start.24) | collective-permute-done | bytes 221216 | tf_op jit(solution)/shard_map/ppermute | solution.py:444
  155.0 12.4 %collective-permute-done.22.refs_7_ = f32[432,128]{1,0:T(8,128)S(1)} collective-permute-done((f32[432,128]{1,0:T(8,128)}, f32[432,128]{1,0:T(8,128)S(1)}, u32[]{:S(2)}, u32[]{:S(2)}) %collective-permute-start.22) | collective-permute-done | bytes 221216 | tf_op jit(solution)/shard_map/ppermute | solution.py:444
  171.8 6.5 %shard_map.89.along_ref = f32[3456,256]{1,0:T(8,128)} custom-call(s32[1]{0:T(128)} %bitcast.place_ref, f32[432,128]{1,0:T(8,128)} %get-tuple-element.74.refs_0_, f32[432,128]{1,0:T(8,128)} %copy-done.13, f32[432,128]{1,0:T(8,128)} %copy-done.9, f32[432,128]{1,0:T(8,128)} %copy-done.12, f32[432,128]{1,0:T(8,128)} %copy-done.11, f32[432,128]{1,0:T(8,128)} %copy-done.10, ...), custom_call_target="tpu_custom_call" | custom-call | flops 1019215872 | bytes 8388608 | tf_op jit(solution)/shard_map/pallas_call | solution.py:504
  181.5 3.9 collective-permute-done.26.refs_11_
  186.3 9.1 %shard_map.91 = f32[6912,128]{1,0:T(8,128)} custom-call(s32[1]{0:T(128)} %bitcast.place_ref, f32[3456,256]{1,0:T(8,128)} %shard_map.89.along_ref, f32[1728,128]{1,0:T(8,128)} %shard_map.90.own_ref, f32[1728,128]{1,0:T(8,128)} %copy-done.6, f32[192,192]{1,0:T(8,128)} %constant.23.clone.kin_ref.refs_16_, f32[432,128]{1,0:T(8,128)} %get-tuple-element.103.refs_0_, ...), custom_call_target="tpu_custom_call" | custom-call | flops 1019215872 | bytes 14680064 | tf_op jit(solution)/shard_map/pallas_call | solution.py:516
  195.4 10.2 %all-to-all-start.1 = ((f32[16,432,128]{2,1,0:T(8,128)}), f32[16,432,128]{2,1,0:T(8,128)S(1)}, u32[]{:S(2)}, u32[]{:S(2)}) async-start(f32[16,432,128]{2,1,0:T(8,128)} %bitcast.19), calls=%async_computation.1 | async-start | bytes 7077888 | tf_op jit(solution)/shard_map/all_to_all | solution.py:449
  206.2 65.6 %all-to-all-done.1 = f32[16,432,128]{2,1,0:T(8,128)S(1)} async-done(((f32[16,432,128]{2,1,0:T(8,128)}), f32[16,432,128]{2,1,0:T(8,128)S(1)}, u32[]{:S(2)}, u32[]{:S(2)}) %all-to-all-start.1) | async-done | bytes 3538976 | tf_op jit(solution)/shard_map/all_to_all | solution.py:449
  273.7 10.9 %shard_map.92 = (f32[1,2,12,192,192]{4,3,2,1,0:T(8,128)}, f32[1728,128]{1,0:T(8,128)}, f32[1728,128]{1,0:T(8,128)}, f32[3584,128]{1,0:T(8,128)}) custom-call(f32[1]{0:T(128)S(6)} %copy.14.occ_ref, f32[6912,128]{1,0:T(8,128)} %bitcast.20, f32[2,12,192,192]{3,2,1,0:T(8,128)} %get-tuple-element.82.base_ref, f32[2,192,192]{2,1,0:T(8,128)} %constant.24.clone.tables_ref), custom_call_target="tpu_custom_call" | custom-call | flops 2038431744 | bytes 16777216 | tf_op jit(solution)/shard_map/pallas_call | solution.py:535
  284.6 17.0 %all-to-all-start.2 = ((f32[32,112,128]{2,1,0:T(8,128)}), f32[32,112,128]{2,1,0:T(8,128)S(1)}, u32[]{:S(2)}, u32[]{:S(2)}) async-start(f32[32,112,128]{2,1,0:T(8,128)} %bitcast.25), calls=%async_computation.2 | async-start | bytes 3670016 | tf_op jit(solution)/shard_map/all_to_all | solution.py:453
  304.5 41.3 %all-to-all-done.2 = f32[32,112,128]{2,1,0:T(8,128)S(1)} async-done(((f32[32,112,128]{2,1,0:T(8,128)}), f32[32,112,128]{2,1,0:T(8,128)S(1)}, u32[]{:S(2)}, u32[]{:S(2)}) %all-to-all-start.2) | async-done | bytes 1835040 | tf_op jit(solution)/shard_map/all_to_all | solution.py:453
  348.9 3.6 all-to-all-start.4
  352.5 9.6 %collective-permute-done.31.lower_other = f32[1728,128]{1,0:T(8,128)} collective-permute-done((f32[1728,128]{1,0:T(8,128)}, f32[1728,128]{1,0:T(8,128)}, u32[]{:S(2)}, u32[]{:S(2)}) %collective-permute-start.31) | collective-permute-done | bytes 884768 | tf_op jit(solution)/shard_map/ppermute | solution.py:556
  362.2 3.6 all-to-all-done.4
  365.7 3.8 all-to-all-start.3
  370.5 12.3 %all-to-all-done.3 = f32[16,56,128]{2,1,0:T(8,128)S(1)} async-done(((f32[16,56,128]{2,1,0:T(8,128)}), f32[16,56,128]{2,1,0:T(8,128)S(1)}, u32[]{:S(2)}, u32[]{:S(2)}) %all-to-all-start.3) | async-done | bytes 458784 | tf_op jit(solution)/shard_map/all_to_all | solution.py:449
  384.4 4.3 %shard_map.94.refs_0_ = f32[12,192,192]{2,1,0:T(8,128)} custom-call(s32[1]{0:T(128)} %bitcast.place_ref, f32[896,128]{1,0:T(8,128)} %bitcast.24, f32[896,128]{1,0:T(8,128)} %copy-done.7, f32[1728,128]{1,0:T(8,128)} %get-tuple-element.139.upper_ref, f32[1728,128]{1,0:T(8,128)} %get-tuple-element.137.lower_ref, ...), custom_call_target="tpu_custom_call" | custom-call | flops 509607936 | bytes 4194304 | tf_op jit(solution)/shard_map/pallas_call | solution.py:578
  388.7 6.6 %collective-permute-done.32.far_ref = f32[896,128]{1,0:T(8,128)S(1)} collective-permute-done((f32[896,128]{1,0:T(8,128)S(1)}, f32[896,128]{1,0:T(8,128)S(1)}, u32[]{:S(2)}, u32[]{:S(2)}) %collective-permute-start.32) | collective-permute-done | bytes 458784 | tf_op jit(solution)/shard_map/ppermute | solution.py:598
  396.1 4.3 %shard_map.95 = f32[12,192,192]{2,1,0:T(8,128)} custom-call(s32[1]{0:T(128)} %bitcast.place_ref, f32[896,128]{1,0:T(8,128)} %bitcast.27, f32[896,128]{1,0:T(8,128)} %copy-done.8, f32[1728,128]{1,0:T(8,128)} %get-tuple-element.139.upper_ref, f32[1728,128]{1,0:T(8,128)} %get-tuple-element.137.lower_ref, ...), custom_call_target="tpu_custom_call", output_to_operand_aliasing={{}: (8, {})} | custom-call | flops 509607936 | bytes 4194304 | tf_op jit(solution)/shard_map/pallas_call | solution.py:578
  (144 shorter events, 56.9 us)
Async XLA Ops:
  4.8 111.7 %all-to-all-start = ((f32[16,112,128]{2,1,0:T(8,128)}), f32[16,112,128]{2,1,0:T(8,128)S(1)}, u32[]{:S(2)}, u32[]{:S(2)}) async-start(f32[16,112,128]{2,1,0:T(8,128)} %bitcast.22), calls=%async_computation | async-start | bytes 1835008 | tf_op jit(solution)/shard_map/all_to_all | solution.py:449
  17.9 38.3 %collective-permute-start.4 = (f32[432,128]{1,0:T(8,128)}, f32[432,128]{1,0:T(8,128)S(1)}, u32[]{:S(2)}, u32[]{:S(2)}) collective-permute-start(f32[432,128]{1,0:T(8,128)} %get-tuple-element.79), channel_id=1, source_target_pairs={{0,10},{1,11},{2,8},{3,9},{4,14},{5,15},{6,12},{7,13},{8,2},{9,3},... | collective-permute-start | bytes 663560 | tf_op jit(solution)/shard_map/ppermute | solution.py:444
  21.4 34.8 %collective-permute-start.3 = (f32[432,128]{1,0:T(8,128)}, f32[432,128]{1,0:T(8,128)S(1)}, u32[]{:S(2)}, u32[]{:S(2)}) collective-permute-start(f32[432,128]{1,0:T(8,128)} %get-tuple-element.78), channel_id=1, source_target_pairs={{0,2},{1,3},{2,0},{3,1},{4,6},{5,7},{6,4},{7,5},{8,10},{9,11},{10,... | collective-permute-start | bytes 663560 | tf_op jit(solution)/shard_map/ppermute | solution.py:444
  21.9 37.2 %collective-permute-start.2 = (f32[432,128]{1,0:T(8,128)}, f32[432,128]{1,0:T(8,128)S(1)}, u32[]{:S(2)}, u32[]{:S(2)}) collective-permute-start(f32[432,128]{1,0:T(8,128)} %get-tuple-element.77), channel_id=1, source_target_pairs={{0,9},{1,8},{2,11},{3,10},{4,13},{5,12},{6,15},{7,14},{8,1},{9,0},... | collective-permute-start | bytes 663560 | tf_op jit(solution)/shard_map/ppermute | solution.py:444
  22.0 47.6 %collective-permute-start = (f32[432,128]{1,0:T(8,128)}, f32[432,128]{1,0:T(8,128)S(1)}, u32[]{:S(2)}, u32[]{:S(2)}) collective-permute-start(f32[432,128]{1,0:T(8,128)} %get-tuple-element.75), channel_id=1, source_target_pairs={{0,8},{1,9},{2,10},{3,11},{4,12},{5,13},{6,14},{7,15},{8,0},{9,1},... | collective-permute-start | bytes 663560 | tf_op jit(solution)/shard_map/ppermute | solution.py:444
  56.2 17.6 %collective-permute-start.9 = (f32[432,128]{1,0:T(8,128)S(1)}, f32[432,128]{1,0:T(8,128)S(1)}, u32[]{:S(2)}, u32[]{:S(2)}) collective-permute-start(f32[432,128]{1,0:T(8,128)S(1)} %copy-done.41), channel_id=1, source_target_pairs={{0,5},{1,4},{2,7},{3,6},{4,1},{5,0},{6,3},{7,2},{8,13},{9,12},{10,... | collective-permute-start | bytes 663560 | tf_op jit(solution)/shard_map/ppermute | solution.py:444
  56.3 19.6 %collective-permute-start.8 = (f32[432,128]{1,0:T(8,128)S(1)}, f32[432,128]{1,0:T(8,128)S(1)}, u32[]{:S(2)}, u32[]{:S(2)}) collective-permute-start(f32[432,128]{1,0:T(8,128)S(1)} %copy-done.40), channel_id=1, source_target_pairs={{0,12},{1,13},{2,14},{3,15},{4,8},{5,9},{6,10},{7,11},{8,4},{9,5},... | collective-permute-start | bytes 663560 | tf_op jit(solution)/shard_map/ppermute | solution.py:444
  59.2 20.1 %collective-permute-start.7 = (f32[432,128]{1,0:T(8,128)S(1)}, f32[432,128]{1,0:T(8,128)S(1)}, u32[]{:S(2)}, u32[]{:S(2)}) collective-permute-start(f32[432,128]{1,0:T(8,128)S(1)} %copy-done.39), channel_id=1, source_target_pairs={{0,4},{1,5},{2,6},{3,7},{4,0},{5,1},{6,2},{7,3},{8,12},{9,13},{10,... | collective-permute-start | bytes 663560 | tf_op jit(solution)/shard_map/ppermute | solution.py:444
  59.2 29.3 %collective-permute-start.6 = (f32[432,128]{1,0:T(8,128)S(1)}, f32[432,128]{1,0:T(8,128)S(1)}, u32[]{:S(2)}, u32[]{:S(2)}) collective-permute-start(f32[432,128]{1,0:T(8,128)S(1)} %copy-done.38), channel_id=1, source_target_pairs={{0,11},{1,10},{2,9},{3,8},{4,15},{5,14},{6,13},{7,12},{8,3},{9,2},... | collective-permute-start | bytes 663560 | tf_op jit(solution)/shard_map/ppermute | solution.py:444
  69.6 18.9 %collective-permute-start.5 = (f32[432,128]{1,0:T(8,128)S(1)}, f32[432,128]{1,0:T(8,128)S(1)}, u32[]{:S(2)}, u32[]{:S(2)}) collective-permute-start(f32[432,128]{1,0:T(8,128)S(1)} %copy-done.37), channel_id=1, source_target_pairs={{0,3},{1,2},{2,1},{3,0},{4,7},{5,6},{6,5},{7,4},{8,11},{9,10},{10,... | collective-permute-start | bytes 663560 | tf_op jit(solution)/shard_map/ppermute | solution.py:444
  73.9 21.3 %collective-permute-start.14 = (f32[432,128]{1,0:T(8,128)S(1)}, f32[432,128]{1,0:T(8,128)S(1)}, u32[]{:S(2)}, u32[]{:S(2)}) collective-permute-start(f32[432,128]{1,0:T(8,128)S(1)} %copy-done.36), channel_id=1, source_target_pairs={{0,15},{1,14},{2,13},{3,12},{4,11},{5,10},{6,9},{7,8},{8,7},{9,6},... | collective-permute-start | bytes 663560 | tf_op jit(solution)/shard_map/ppermute | solution.py:444
  75.8 26.0 %collective-permute-start.13 = (f32[432,128]{1,0:T(8,128)S(1)}, f32[432,128]{1,0:T(8,128)S(1)}, u32[]{:S(2)}, u32[]{:S(2)}) collective-permute-start(f32[432,128]{1,0:T(8,128)S(1)} %copy-done.35), channel_id=1, source_target_pairs={{0,7},{1,6},{2,5},{3,4},{4,3},{5,2},{6,1},{7,0},{8,15},{9,14},{10,... | collective-permute-start | bytes 663560 | tf_op jit(solution)/shard_map/ppermute | solution.py:444
  79.3 24.6 %collective-permute-start.12 = (f32[432,128]{1,0:T(8,128)S(1)}, f32[432,128]{1,0:T(8,128)S(1)}, u32[]{:S(2)}, u32[]{:S(2)}) collective-permute-start(f32[432,128]{1,0:T(8,128)S(1)} %copy-done.34), channel_id=1, source_target_pairs={{0,14},{1,15},{2,12},{3,13},{4,10},{5,11},{6,8},{7,9},{8,6},{9,7},... | collective-permute-start | bytes 663560 | tf_op jit(solution)/shard_map/ppermute | solution.py:444
  88.5 31.1 %collective-permute-start.11 = (f32[432,128]{1,0:T(8,128)}, f32[432,128]{1,0:T(8,128)}, u32[]{:S(2)}, u32[]{:S(2)}) collective-permute-start(f32[432,128]{1,0:T(8,128)} %get-tuple-element.95), channel_id=1, source_target_pairs={{0,6},{1,7},{2,4},{3,5},{4,2},{5,3},{6,0},{7,1},{8,14},{9,15},{10,... | collective-permute-start | bytes 663560 | tf_op jit(solution)/shard_map/ppermute | solution.py:444
  88.5 32.7 %collective-permute-start.10 = (f32[432,128]{1,0:T(8,128)}, f32[432,128]{1,0:T(8,128)}, u32[]{:S(2)}, u32[]{:S(2)}) collective-permute-start(f32[432,128]{1,0:T(8,128)} %get-tuple-element.93), channel_id=1, source_target_pairs={{0,13},{1,12},{2,15},{3,14},{4,9},{5,8},{6,11},{7,10},{8,5},{9,4},... | collective-permute-start | bytes 663560 | tf_op jit(solution)/shard_map/ppermute | solution.py:444
  95.1 35.2 %collective-permute-start.20 = (f32[432,128]{1,0:T(8,128)}, f32[432,128]{1,0:T(8,128)}, u32[]{:S(2)}, u32[]{:S(2)}) collective-permute-start(f32[432,128]{1,0:T(8,128)} %get-tuple-element.113), channel_id=1, source_target_pairs={{0,10},{1,11},{2,8},{3,9},{4,14},{5,15},{6,12},{7,13},{8,2},{9,3},... | collective-permute-start | bytes 663560 | tf_op jit(solution)/shard_map/ppermute | solution.py:444
  101.8 28.6 %collective-permute-start.19 = (f32[432,128]{1,0:T(8,128)}, f32[432,128]{1,0:T(8,128)}, u32[]{:S(2)}, u32[]{:S(2)}) collective-permute-start(f32[432,128]{1,0:T(8,128)} %get-tuple-element.111), channel_id=1, source_target_pairs={{0,2},{1,3},{2,0},{3,1},{4,6},{5,7},{6,4},{7,5},{8,10},{9,11},{10,... | collective-permute-start | bytes 663560 | tf_op jit(solution)/shard_map/ppermute | solution.py:444
  104.6 26.9 %collective-permute-start.18 = (f32[432,128]{1,0:T(8,128)}, f32[432,128]{1,0:T(8,128)}, u32[]{:S(2)}, u32[]{:S(2)}) collective-permute-start(f32[432,128]{1,0:T(8,128)} %get-tuple-element.109), channel_id=1, source_target_pairs={{0,9},{1,8},{2,11},{3,10},{4,13},{5,12},{6,15},{7,14},{8,1},{9,0},... | collective-permute-start | bytes 663560 | tf_op jit(solution)/shard_map/ppermute | solution.py:444
  119.6 65.7 %collective-permute-start.15 = (f32[1728,128]{1,0:T(8,128)}, f32[1728,128]{1,0:T(8,128)S(1)}, u32[]{:S(2)}, u32[]{:S(2)}) collective-permute-start(f32[1728,128]{1,0:T(8,128)} %shard_map.90.own_ref), channel_id=1, source_target_pairs={{0,16},{16,0},{1,17},{17,1},{2,18},{18,2},{3,19},{19,3},{4,20},{20... | collective-permute-start | bytes 2654216 | tf_op jit(solution)/shard_map/ppermute | solution.py:503
  131.5 16.6 %collective-permute-start.24 = (f32[432,128]{1,0:T(8,128)}, f32[432,128]{1,0:T(8,128)S(1)}, u32[]{:S(2)}, u32[]{:S(2)}) collective-permute-start(f32[432,128]{1,0:T(8,128)} %get-tuple-element.121), channel_id=1, source_target_pairs={{0,12},{1,13},{2,14},{3,15},{4,8},{5,9},{6,10},{7,11},{8,4},{9,5},... | collective-permute-start | bytes 663560 | tf_op jit(solution)/shard_map/ppermute | solution.py:444
  133.3 19.2 %collective-permute-start.23 = (f32[432,128]{1,0:T(8,128)}, f32[432,128]{1,0:T(8,128)S(1)}, u32[]{:S(2)}, u32[]{:S(2)}) collective-permute-start(f32[432,128]{1,0:T(8,128)} %get-tuple-element.119), channel_id=1, source_target_pairs={{0,4},{1,5},{2,6},{3,7},{4,0},{5,1},{6,2},{7,3},{8,12},{9,13},{10,... | collective-permute-start | bytes 663560 | tf_op jit(solution)/shard_map/ppermute | solution.py:444
  143.4 24.0 %collective-permute-start.22 = (f32[432,128]{1,0:T(8,128)}, f32[432,128]{1,0:T(8,128)S(1)}, u32[]{:S(2)}, u32[]{:S(2)}) collective-permute-start(f32[432,128]{1,0:T(8,128)} %get-tuple-element.117), channel_id=1, source_target_pairs={{0,11},{1,10},{2,9},{3,8},{4,15},{5,14},{6,13},{7,12},{8,3},{9,2},... | collective-permute-start | bytes 663560 | tf_op jit(solution)/shard_map/ppermute | solution.py:444
  143.4 25.5 %collective-permute-start.21 = (f32[432,128]{1,0:T(8,128)}, f32[432,128]{1,0:T(8,128)S(1)}, u32[]{:S(2)}, u32[]{:S(2)}) collective-permute-start(f32[432,128]{1,0:T(8,128)} %get-tuple-element.115), channel_id=1, source_target_pairs={{0,3},{1,2},{2,1},{3,0},{4,7},{5,6},{6,5},{7,4},{8,11},{9,10},{10,... | collective-permute-start | bytes 663560 | tf_op jit(solution)/shard_map/ppermute | solution.py:444
  148.1 20.9 %collective-permute-start.30 = (f32[432,128]{1,0:T(8,128)}, f32[432,128]{1,0:T(8,128)S(1)}, u32[]{:S(2)}, u32[]{:S(2)}) collective-permute-start(f32[432,128]{1,0:T(8,128)} %get-tuple-element.133), channel_id=1, source_target_pairs={{0,15},{1,14},{2,13},{3,12},{4,11},{5,10},{6,9},{7,8},{8,7},{9,6},... | collective-permute-start | bytes 663560 | tf_op jit(solution)/shard_map/ppermute | solution.py:444
  152.5 25.9 %collective-permute-start.29 = (f32[432,128]{1,0:T(8,128)}, f32[432,128]{1,0:T(8,128)S(1)}, u32[]{:S(2)}, u32[]{:S(2)}) collective-permute-start(f32[432,128]{1,0:T(8,128)} %get-tuple-element.131), channel_id=1, source_target_pairs={{0,7},{1,6},{2,5},{3,4},{4,3},{5,2},{6,1},{7,0},{8,15},{9,14},{10,... | collective-permute-start | bytes 663560 | tf_op jit(solution)/shard_map/ppermute | solution.py:444
  168.9 16.4 %collective-permute-start.26 = (f32[432,128]{1,0:T(8,128)}, f32[432,128]{1,0:T(8,128)S(1)}, u32[]{:S(2)}, u32[]{:S(2)}) collective-permute-start(f32[432,128]{1,0:T(8,128)} %get-tuple-element.125), channel_id=1, source_target_pairs={{0,13},{1,12},{2,15},{3,14},{4,9},{5,8},{6,11},{7,10},{8,5},{9,4},... | collective-permute-start | bytes 663560 | tf_op jit(solution)/shard_map/ppermute | solution.py:444
  195.4 76.4 %all-to-all-start.1 = ((f32[16,432,128]{2,1,0:T(8,128)}), f32[16,432,128]{2,1,0:T(8,128)S(1)}, u32[]{:S(2)}, u32[]{:S(2)}) async-start(f32[16,432,128]{2,1,0:T(8,128)} %bitcast.19), calls=%async_computation.1 | async-start | bytes 7077888 | tf_op jit(solution)/shard_map/all_to_all | solution.py:449
  284.6 61.2 %all-to-all-start.2 = ((f32[32,112,128]{2,1,0:T(8,128)}), f32[32,112,128]{2,1,0:T(8,128)S(1)}, u32[]{:S(2)}, u32[]{:S(2)}) async-start(f32[32,112,128]{2,1,0:T(8,128)} %bitcast.25), calls=%async_computation.2 | async-start | bytes 3670016 | tf_op jit(solution)/shard_map/all_to_all | solution.py:453
  301.6 47.3 %collective-permute-start.33 = (f32[1728,128]{1,0:T(8,128)S(1)}, f32[1728,128]{1,0:T(8,128)}, u32[]{:S(2)}, u32[]{:S(2)}) collective-permute-start(f32[1728,128]{1,0:T(8,128)S(1)} %copy-done.3), channel_id=1, source_target_pairs={{0,16},{16,0},{1,17},{17,1},{2,18},{18,2},{3,19},{19,3},{4,20},{20... | collective-permute-start | bytes 2654216 | tf_op jit(solution)/shard_map/ppermute | solution.py:555
  304.2 58.0 %collective-permute-start.31 = (f32[1728,128]{1,0:T(8,128)}, f32[1728,128]{1,0:T(8,128)}, u32[]{:S(2)}, u32[]{:S(2)}) collective-permute-start(f32[1728,128]{1,0:T(8,128)} %get-tuple-element.137.lower_ref), channel_id=1, source_target_pairs={{0,16},{16,0},{1,17},{17,1},{2,18},{18,2},{3,19},{19,3},{4,20},{20... | collective-permute-start | bytes 2654216 | tf_op jit(solution)/shard_map/ppermute | solution.py:556
  348.9 16.8 %all-to-all-start.4 = ((f32[16,56,128]{2,1,0:T(8,128)}), f32[16,56,128]{2,1,0:T(8,128)S(1)}, u32[]{:S(2)}, u32[]{:S(2)}) async-start(f32[16,56,128]{2,1,0:T(8,128)} %bitcast.9), calls=%async_computation.4 | async-start | bytes 917504 | tf_op jit(solution)/shard_map/all_to_all | solution.py:449
  365.7 17.1 %all-to-all-start.3 = ((f32[16,56,128]{2,1,0:T(8,128)}), f32[16,56,128]{2,1,0:T(8,128)S(1)}, u32[]{:S(2)}, u32[]{:S(2)}) async-start(f32[16,56,128]{2,1,0:T(8,128)} %bitcast.7), calls=%async_computation.3 | async-start | bytes 917504 | tf_op jit(solution)/shard_map/all_to_all | solution.py:449
  (50 other events, 1835.7 us)

commit v9 on v8

--- a/solution.py
+++ b/solution.py
@@ -189,7 +189,8 @@
             pack(psi_ref[0, part, inner], slot)
             for turn, out_ref in zip(turns, out_refs):
                 start = (mine ^ turn) * rows
-                out_ref[pl.ds((plane * 2 + part) * rows, rows), :] = slot[pl.ds(start, rows), :]
+                where = pl.ds(part * planes + plane, rows, stride=2 * planes)
+                out_ref[where, :] = slot[pl.ds(start, rows), :]
 
 
 def plane_kernel(sizes, bunch, turns, place_ref, psi_ref, ion_ref, hxc_ref, kin_ref, *refs):
@@ -209,7 +210,8 @@
             pack(bare + applied[part], slot)
             for turn, out_ref in zip(turns, out_refs):
                 start = (mine ^ turn) * rows
-                out_ref[pl.ds((plane * 2 + part) * rows, rows), :] = slot[pl.ds(start, rows), :]
+                where = pl.ds(part * planes + plane, rows, stride=2 * planes)
+                out_ref[where, :] = slot[pl.ds(start, rows), :]
         for part in range(2):
             twice = kinetic(applied[part], kin) + (potential - 1.0) * applied[part]
             turned = applied[1] if part == 0 else -applied[0]
@@ -236,12 +238,12 @@
     length = planes * grid
     kin = split(kin_ref[...])
     for inner in range(rows // steps):
-        row = pl.program_id(0) * (rows // steps) + inner
         slot = lines.at[inner]
         for turn, moved_ref in zip(turns, moved_refs):
             first = (place_ref[0] % grid ^ turn) * planes
             for part in range(2):
-                slot[part, pl.ds(first, planes), :] = moved_ref[pl.ds(part * rows + row, planes, stride=2 * rows), :]
+                start = (inner * 2 + part) * planes
+                slot[part, pl.ds(first, planes), :] = moved_ref[start : start + planes, :]
         field = jnp.concatenate([slot[0], slot[1]], axis=1)
         out_ref[inner * length : (inner + 1) * length, :] = product_of_parts(kin, split(field))
 
@@ -254,13 +256,13 @@
     step = pl.program_id(0)
     mine_here = place_ref[0] // grid == step // (steps // 2)
     for inner in range(rows // steps):
-        row = step * (rows // steps) + inner
         here = slice(inner * length, (inner + 1) * length)
         slot = lines.at[inner]
         for turn, mixed_ref in zip(turns, mixed_refs):
             first = (place_ref[0] % grid ^ turn) * planes
             for part in range(2):
-                slot[part, pl.ds(first, planes), :] = mixed_ref[pl.ds(part * rows + row, planes, stride=2 * rows), :]
+                start = (inner * 2 + part) * planes
+                slot[part, pl.ds(first, planes), :] = mixed_ref[start : start + planes, :]
         along = along_ref[here, :]
         again = product_of_parts(kin, split(jnp.concatenate([slot[0], slot[1]], axis=1) + along))
         potential = jnp.where(mine_here, own_ref[here, :], other_ref[here, :])
@@ -268,9 +270,10 @@
             mine = along[:, part * LANES : (part + 1) * LANES]
             turned = along[:, LANES:] if part == 0 else -along[:, :LANES]
             twice = again[:, part * LANES : (part + 1) * LANES] + potential * mine
-            out_ref[pl.ds(part * rows + row, length, stride=2 * rows), :] = (
-                2.0 * BESSEL_ONE * turned - 4.0 * BESSEL_TWO * twice
-            )
+            slot[part] = 2.0 * BESSEL_ONE * turned - 4.0 * BESSEL_TWO * twice
+            start = (inner * 2 + part) * planes
+            for to in range(grid):
+                out_ref[to, start : start + planes, :] = slot[part, to * planes : (to + 1) * planes, :]
 
 
 def fresh_kernel(
@@ -289,8 +292,9 @@
         for part in range(2):
             slot = packed.at[inner * 4 + part]
             for source in range(grid):
-                start = ((source * planes + plane) * 2 + part) * rows
-                slot[pl.ds(source * rows, rows), :] = update_ref[pl.ds(start, rows), :]
+                start = (source * rows * 2 + part) * planes + plane
+                piece = update_ref[pl.ds(start, rows, stride=2 * planes), :]
+                slot[pl.ds(source * rows, rows), :] = piece
             fresh = base_ref[part, inner] + unpack(slot, length)
             fresh_ref[0, part, inner] = fresh
             part_sum = fresh * fresh if part_sum is None else part_sum + fresh * fresh
@@ -456,6 +460,7 @@
     spec_rows = 2 * grid * chunk_rows(sizes)
     mixed_rows = 2 * planes * rows
     steps = 6 if rows % 6 == 0 and share % (rows // 6) == 0 else 2
+    step_spec = pl.BlockSpec((mixed_rows // steps, LANES), lambda i: (i, 0))
     shared = pl.pallas_call(
         functools.partial(potential_kernel, sizes, bunch),
         grid=(planes // bunch,),
@@ -504,7 +509,7 @@
     along = pl.pallas_call(
         functools.partial(along_kernel, sizes, steps, turns),
         grid=(steps,),
-        in_specs=[smem] + [whole(mixed_rows, LANES)] * grid + [square],
+        in_specs=[smem] + [step_spec] * grid + [square],
         out_specs=pl.BlockSpec((rows // steps * length, 2 * LANES), lambda i: (i, 0)),
         out_shape=shape(rows * length, 2 * LANES),
         scratch_shapes=[pltpu.VMEM((rows // steps, 2, length, LANES), jnp.float32)],
@@ -523,14 +528,14 @@
             half_spec,
             square,
         ]
-        + [whole(mixed_rows, LANES)] * grid,
-        out_specs=whole(2 * field, LANES),
-        out_shape=shape(2 * field, LANES),
+        + [step_spec] * grid,
+        out_specs=pl.BlockSpec((grid, mixed_rows // steps, LANES), lambda i: (0, i, 0)),
+        out_shape=shape(grid, mixed_rows, LANES),
         scratch_shapes=[pltpu.VMEM((rows // steps, 2, length, LANES), jnp.float32)],
         compiler_params=PARAMS,
         cost_estimate=cost(2 * 3 * work, 14 << 20),
     )(place, along, own, other, kin, *mixed)
-    update = swap(update)
+    update = swap(update).reshape(2 * field, LANES)
 
     fresh, upper, lower, spectrum = pl.pallas_call(
         functools.partial(fresh_kernel, sizes, bunch),

time: 401 us -> 407 us (1.015)
  waiting for transfers between devices: 215 us -> 221 us
    ppermute x30, starting transfers between devices: 65.6 us -> 58.9 us  [send(): lax.ppermute(piece, 'grid', [(spot, spot ^ turn) for spot in range(grid)])]
    ppermute x30, waiting for transfers between devices: 76 us -> 82.3 us  [send(): lax.ppermute(piece, 'grid', [(spot, spot ^ turn) for spot in range(grid)])]
  transfers between devices with their start and end apart: 40 -> 40, of which waited for: 21 -> 20; matrix products, arithmetic and copies ran while one was open for 0% -> 0% of each run, Pallas kernels for 9% -> 9%
where the time goes in v9:
time: 407 us; the launch traced here: 405 us
  waiting for transfers between devices  221 us (54%)
  starting transfers between devices  109 us (27%)
  Pallas kernels  65.8 us (16%)
  local copies, waits for them, and re-layouts  6.87 us (2%)
    ppermute x30, waiting for transfers between devices, send(): lax.ppermute(piece, 'grid', [(spot, spot ^ turn) for spot in range(grid)])  82.3 us
    all_to_all x4, waiting for transfers between devices, swap(): lax.all_to_all(flat, 'grid', split_axis=0, concat_axis=0)  81.4 us
    ppermute x30, starting transfers between devices, send(): lax.ppermute(piece, 'grid', [(spot, spot ^ turn) for spot in range(grid)])  58.9 us
    all_to_all x1, waiting for transfers between devices, swap_all(): lax.all_to_all(flat, ('band', 'grid'), split_axis=0, concat_axis=0)  41.3 us
    all_to_all x4, starting transfers between devices, swap(): lax.all_to_all(flat, 'grid', split_axis=0, concat_axis=0)  28 us
    all_to_all x1, starting transfers between devices, swap_all(): lax.all_to_all(flat, ('band', 'grid'), split_axis=0, concat_axis=0)  17 us
    pallas_call x1, Pallas kernels, packed_path(): pl.pallas_call(functools.partial(plane_kernel, sizes, bunch, turns), grid...  14.5 us
    pallas_call x1, Pallas kernels, packed_path(): pl.pallas_call(functools.partial(fresh_kernel, sizes, bunch), grid=(plane...  11.1 us
  transfers between devices with their start and end apart: 40, of which 20 were waited for; matrix products, arithmetic and copies ran while one was open for 0% of the time, Pallas kernels for 9%

profile of v9, /device:TPU:0, one launch (start us, length us, event | category | flops | bytes accessed | tf_op | source)
XLA Modules:
  0.0 405.1 jit_solution(4696080212626675010)
XLA Ops:
  0.6 4.1 %shard_map.86 = f32[1792,128]{1,0:T(8,128)} custom-call(s32[1]{0:T(128)} %bitcast.place_ref, f32[12,192,192]{2,1,0:T(8,128)} %ion_ref.3, f32[12,192,192]{2,1,0:T(8,128)} %hxc_ref.3), custom_call_target="tpu_custom_call" | custom-call | bytes 6291456 | tf_op jit(solution)/shard_map/pallas_call | solution.py:464
  4.8 7.4 %all-to-all-start = ((f32[16,112,128]{2,1,0:T(8,128)}), f32[16,112,128]{2,1,0:T(8,128)S(1)}, u32[]{:S(2)}, u32[]{:S(2)}) async-start(f32[16,112,128]{2,1,0:T(8,128)} %bitcast.20), calls=%async_computation | async-start | bytes 1835008 | tf_op jit(solution)/shard_map/all_to_all | solution.py:453
  12.1 5.7 %shard_map.87 = (f32[432,128]{1,0:T(8,128)}, f32[432,128]{1,0:T(8,128)}, f32[432,128]{1,0:T(8,128)}, f32[432,128]{1,0:T(8,128)}, f32[432,128]{1,0:T(8,128)}, /*i...) custom-call(s32[1]{0:T(128)} %bitcast.place_ref, ...), custom_call_target="tpu_custom_call" | custom-call | bytes 8388608 | tf_op jit(solution)/shard_map/pallas_call | solution.py:476
  18.2 3.5 collective-permute-start.4
  24.7 14.5 %shard_map.88 = (f32[432,128]{1,0:T(8,128)}, f32[432,128]{1,0:T(8,128)}, f32[432,128]{1,0:T(8,128)}, f32[432,128]{1,0:T(8,128)}, f32[432,128]{1,0:T(8,128)}, /*i...) custom-call(s32[1]{0:T(128)} %bitcast.place_ref, ...), custom_call_target="tpu_custom_call" | custom-call | flops 4076863488 | bytes 20971520 | tf_op jit(solution)/shard_map/pallas_call | solution.py:488
  39.2 17.0 %collective-permute-done.4.refs_5_ = f32[432,128]{1,0:T(8,128)S(1)} collective-permute-done((f32[432,128]{1,0:T(8,128)}, f32[432,128]{1,0:T(8,128)S(1)}, u32[]{:S(2)}, u32[]{:S(2)}) %collective-permute-start.4) | collective-permute-done | bytes 221216 | tf_op jit(solution)/shard_map/ppermute | solution.py:448
  62.2 7.4 %collective-permute-done.refs_1_ = f32[432,128]{1,0:T(8,128)S(1)} collective-permute-done((f32[432,128]{1,0:T(8,128)}, f32[432,128]{1,0:T(8,128)S(1)}, u32[]{:S(2)}, u32[]{:S(2)}) %collective-permute-start) | collective-permute-done | bytes 221216 | tf_op jit(solution)/shard_map/ppermute | solution.py:448
  69.8 4.0 collective-permute-done.9.refs_10_
  81.1 7.3 %collective-permute-done.6.refs_7_ = f32[432,128]{1,0:T(8,128)S(1)} collective-permute-done((f32[432,128]{1,0:T(8,128)S(1)}, f32[432,128]{1,0:T(8,128)S(1)}, u32[]{:S(2)}, u32[]{:S(2)}) %collective-permute-start.6) | collective-permute-done | bytes 221216 | tf_op jit(solution)/shard_map/ppermute | solution.py:448
  88.5 6.6 %collective-permute-start.10 = (f32[432,128]{1,0:T(8,128)}, f32[432,128]{1,0:T(8,128)}, u32[]{:S(2)}, u32[]{:S(2)}) collective-permute-start(f32[432,128]{1,0:T(8,128)} %get-tuple-element.93), channel_id=1, source_target_pairs={{0,13},{1,12},{2,15},{3,14},{4,9},{5,8},{6,11},{7,10},{8,5},{9,4},... | collective-permute-start | bytes 663560 | tf_op jit(solution)/shard_map/ppermute | solution.py:448
  95.1 6.8 %collective-permute-start.20 = (f32[432,128]{1,0:T(8,128)}, f32[432,128]{1,0:T(8,128)}, u32[]{:S(2)}, u32[]{:S(2)}) collective-permute-start(f32[432,128]{1,0:T(8,128)} %get-tuple-element.113), channel_id=1, source_target_pairs={{0,10},{1,11},{2,8},{3,9},{4,14},{5,15},{6,12},{7,13},{8,2},{9,3},... | collective-permute-start | bytes 663560 | tf_op jit(solution)/shard_map/ppermute | solution.py:448
  104.4 12.2 %collective-permute-start.18 = (f32[432,128]{1,0:T(8,128)}, f32[432,128]{1,0:T(8,128)}, u32[]{:S(2)}, u32[]{:S(2)}) collective-permute-start(f32[432,128]{1,0:T(8,128)} %get-tuple-element.109), channel_id=1, source_target_pairs={{0,9},{1,8},{2,11},{3,10},{4,13},{5,12},{6,15},{7,14},{8,1},{9,0},... | collective-permute-start | bytes 663560 | tf_op jit(solution)/shard_map/ppermute | solution.py:448
  122.3 8.8 %collective-permute-done.20.refs_5_ = f32[432,128]{1,0:T(8,128)} collective-permute-done((f32[432,128]{1,0:T(8,128)}, f32[432,128]{1,0:T(8,128)}, u32[]{:S(2)}, u32[]{:S(2)}) %collective-permute-start.20) | collective-permute-done | bytes 221216 | tf_op jit(solution)/shard_map/ppermute | solution.py:448
  134.7 8.2 %collective-permute-done.16.refs_1_ = f32[432,128]{1,0:T(8,128)S(1)} collective-permute-done((f32[432,128]{1,0:T(8,128)}, f32[432,128]{1,0:T(8,128)S(1)}, u32[]{:S(2)}, u32[]{:S(2)}) %collective-permute-start.16) | collective-permute-done | bytes 221216 | tf_op jit(solution)/shard_map/ppermute | solution.py:448
  143.9 4.3 %collective-permute-done.25.refs_10_ = f32[432,128]{1,0:T(8,128)S(1)} collective-permute-done((f32[432,128]{1,0:T(8,128)}, f32[432,128]{1,0:T(8,128)S(1)}, u32[]{:S(2)}, u32[]{:S(2)}) %collective-permute-start.25) | collective-permute-done | bytes 221216 | tf_op jit(solution)/shard_map/ppermute | solution.py:448
  156.1 12.0 %collective-permute-done.22.refs_7_ = f32[432,128]{1,0:T(8,128)S(1)} collective-permute-done((f32[432,128]{1,0:T(8,128)}, f32[432,128]{1,0:T(8,128)S(1)}, u32[]{:S(2)}, u32[]{:S(2)}) %collective-permute-start.22) | collective-permute-done | bytes 221216 | tf_op jit(solution)/shard_map/ppermute | solution.py:448
  170.0 6.6 %shard_map.89.along_ref = f32[3456,256]{1,0:T(8,128)} custom-call(s32[1]{0:T(128)} %bitcast.place_ref, f32[432,128]{1,0:T(8,128)} %get-tuple-element.74.refs_0_, f32[432,128]{1,0:T(8,128)} %copy-done.13, f32[432,128]{1,0:T(8,128)} %copy-done.9, f32[432,128]{1,0:T(8,128)} %copy-done.12, f32[432,128]{1,0:T(8,128)} %copy-done.11, f32[432,128]{1,0:T(8,128)} %copy-done.10, ...), custom_call_target="tpu_custom_call" | custom-call | flops 1019215872 | bytes 8388608 | tf_op jit(solution)/shard_map/pallas_call | solution.py:509
  182.2 3.7 collective-permute-done.26.refs_11_
  186.9 9.8 %shard_map.91 = f32[16,432,128]{2,1,0:T(8,128)} custom-call(s32[1]{0:T(128)} %bitcast.place_ref, f32[3456,256]{1,0:T(8,128)} %shard_map.89.along_ref, f32[1728,128]{1,0:T(8,128)} %shard_map.90.own_ref, f32[1728,128]{1,0:T(8,128)} %copy-done.6, f32[192,192]{1,0:T(8,128)} %constant.23.clone.kin_ref.refs_16_, f32[432,128]{1,0:T(8,128)} %get-tuple-element.103.refs_0_, ...), custom_call_target="tpu_custom_call" | custom-call | flops 1019215872 | bytes 14680064 | tf_op jit(solution)/shard_map/pallas_call | solution.py:521
  196.8 13.3 %all-to-all-start.1 = ((f32[16,432,128]{2,1,0:T(8,128)}), f32[16,432,128]{2,1,0:T(8,128)S(1)}, u32[]{:S(2)}, u32[]{:S(2)}) async-start(f32[16,432,128]{2,1,0:T(8,128)} %shard_map.91), calls=%async_computation.1 | async-start | bytes 7077888 | tf_op jit(solution)/shard_map/all_to_all | solution.py:453
  210.7 65.6 %all-to-all-done.1 = f32[16,432,128]{2,1,0:T(8,128)S(1)} async-done(((f32[16,432,128]{2,1,0:T(8,128)}), f32[16,432,128]{2,1,0:T(8,128)S(1)}, u32[]{:S(2)}, u32[]{:S(2)}) %all-to-all-start.1) | async-done | bytes 3538976 | tf_op jit(solution)/shard_map/all_to_all | solution.py:453
  278.2 11.1 %shard_map.92 = (f32[1,2,12,192,192]{4,3,2,1,0:T(8,128)}, f32[1728,128]{1,0:T(8,128)}, f32[1728,128]{1,0:T(8,128)}, f32[3584,128]{1,0:T(8,128)}) custom-call(f32[1]{0:T(128)S(6)} %copy.14.occ_ref, f32[6912,128]{1,0:T(8,128)} %bitcast.18, f32[2,12,192,192]{3,2,1,0:T(8,128)} %get-tuple-element.82.base_ref, f32[2,192,192]{2,1,0:T(8,128)} %constant.24.clone.tables_ref), custom_call_target="tpu_custom_call" | custom-call | flops 2038431744 | bytes 16777216 | tf_op jit(solution)/shard_map/pallas_call | solution.py:540
  289.3 17.0 %all-to-all-start.2 = ((f32[32,112,128]{2,1,0:T(8,128)}), f32[32,112,128]{2,1,0:T(8,128)S(1)}, u32[]{:S(2)}, u32[]{:S(2)}) async-start(f32[32,112,128]{2,1,0:T(8,128)} %bitcast.23), calls=%async_computation.2 | async-start | bytes 3670016 | tf_op jit(solution)/shard_map/all_to_all | solution.py:457
  309.2 41.3 %all-to-all-done.2 = f32[32,112,128]{2,1,0:T(8,128)S(1)} async-done(((f32[32,112,128]{2,1,0:T(8,128)}), f32[32,112,128]{2,1,0:T(8,128)S(1)}, u32[]{:S(2)}, u32[]{:S(2)}) %all-to-all-start.2) | async-done | bytes 1835040 | tf_op jit(solution)/shard_map/all_to_all | solution.py:457
  353.6 3.6 all-to-all-start.4
  357.2 9.6 %collective-permute-done.31.lower_other = f32[1728,128]{1,0:T(8,128)} collective-permute-done((f32[1728,128]{1,0:T(8,128)}, f32[1728,128]{1,0:T(8,128)}, u32[]{:S(2)}, u32[]{:S(2)}) %collective-permute-start.31) | collective-permute-done | bytes 884768 | tf_op jit(solution)/shard_map/ppermute | solution.py:561
  366.8 3.6 all-to-all-done.4
  370.4 3.8 all-to-all-start.3
  375.2 12.3 %all-to-all-done.3 = f32[16,56,128]{2,1,0:T(8,128)S(1)} async-done(((f32[16,56,128]{2,1,0:T(8,128)}), f32[16,56,128]{2,1,0:T(8,128)S(1)}, u32[]{:S(2)}, u32[]{:S(2)}) %all-to-all-start.3) | async-done | bytes 458784 | tf_op jit(solution)/shard_map/all_to_all | solution.py:453
  389.1 4.3 %shard_map.94.refs_0_ = f32[12,192,192]{2,1,0:T(8,128)} custom-call(s32[1]{0:T(128)} %bitcast.place_ref, f32[896,128]{1,0:T(8,128)} %bitcast.22, f32[896,128]{1,0:T(8,128)} %copy-done.7, f32[1728,128]{1,0:T(8,128)} %get-tuple-element.139.upper_ref, f32[1728,128]{1,0:T(8,128)} %get-tuple-element.137.lower_ref, ...), custom_call_target="tpu_custom_call" | custom-call | flops 509607936 | bytes 4194304 | tf_op jit(solution)/shard_map/pallas_call | solution.py:583
  393.4 6.6 %collective-permute-done.32.far_ref = f32[896,128]{1,0:T(8,128)S(1)} collective-permute-done((f32[896,128]{1,0:T(8,128)S(1)}, f32[896,128]{1,0:T(8,128)S(1)}, u32[]{:S(2)}, u32[]{:S(2)}) %collective-permute-start.32) | collective-permute-done | bytes 458784 | tf_op jit(solution)/shard_map/ppermute | solution.py:603
  400.8 4.3 %shard_map.95 = f32[12,192,192]{2,1,0:T(8,128)} custom-call(s32[1]{0:T(128)} %bitcast.place_ref, f32[896,128]{1,0:T(8,128)} %bitcast.25, f32[896,128]{1,0:T(8,128)} %copy-done.8, f32[1728,128]{1,0:T(8,128)} %get-tuple-element.139.upper_ref, f32[1728,128]{1,0:T(8,128)} %get-tuple-element.137.lower_ref, ...), custom_call_target="tpu_custom_call", output_to_operand_aliasing={{}: (8, {})} | custom-call | flops 509607936 | bytes 4194304 | tf_op jit(solution)/shard_map/pallas_call | solution.py:583
  (144 shorter events, 57.2 us)
Async XLA Ops:
  4.8 111.8 %all-to-all-start = ((f32[16,112,128]{2,1,0:T(8,128)}), f32[16,112,128]{2,1,0:T(8,128)S(1)}, u32[]{:S(2)}, u32[]{:S(2)}) async-start(f32[16,112,128]{2,1,0:T(8,128)} %bitcast.20), calls=%async_computation | async-start | bytes 1835008 | tf_op jit(solution)/shard_map/all_to_all | solution.py:453
  18.2 38.0 %collective-permute-start.4 = (f32[432,128]{1,0:T(8,128)}, f32[432,128]{1,0:T(8,128)S(1)}, u32[]{:S(2)}, u32[]{:S(2)}) collective-permute-start(f32[432,128]{1,0:T(8,128)} %get-tuple-element.79), channel_id=1, source_target_pairs={{0,10},{1,11},{2,8},{3,9},{4,14},{5,15},{6,12},{7,13},{8,2},{9,3},... | collective-permute-start | bytes 663560 | tf_op jit(solution)/shard_map/ppermute | solution.py:448
  21.7 34.5 %collective-permute-start.3 = (f32[432,128]{1,0:T(8,128)}, f32[432,128]{1,0:T(8,128)S(1)}, u32[]{:S(2)}, u32[]{:S(2)}) collective-permute-start(f32[432,128]{1,0:T(8,128)} %get-tuple-element.78), channel_id=1, source_target_pairs={{0,2},{1,3},{2,0},{3,1},{4,6},{5,7},{6,4},{7,5},{8,10},{9,11},{10,... | collective-permute-start | bytes 663560 | tf_op jit(solution)/shard_map/ppermute | solution.py:448
  22.3 36.9 %collective-permute-start.2 = (f32[432,128]{1,0:T(8,128)}, f32[432,128]{1,0:T(8,128)S(1)}, u32[]{:S(2)}, u32[]{:S(2)}) collective-permute-start(f32[432,128]{1,0:T(8,128)} %get-tuple-element.77), channel_id=1, source_target_pairs={{0,9},{1,8},{2,11},{3,10},{4,13},{5,12},{6,15},{7,14},{8,1},{9,0},... | collective-permute-start | bytes 663560 | tf_op jit(solution)/shard_map/ppermute | solution.py:448
  22.3 47.2 %collective-permute-start = (f32[432,128]{1,0:T(8,128)}, f32[432,128]{1,0:T(8,128)S(1)}, u32[]{:S(2)}, u32[]{:S(2)}) collective-permute-start(f32[432,128]{1,0:T(8,128)} %get-tuple-element.75), channel_id=1, source_target_pairs={{0,8},{1,9},{2,10},{3,11},{4,12},{5,13},{6,14},{7,15},{8,0},{9,1},... | collective-permute-start | bytes 663560 | tf_op jit(solution)/shard_map/ppermute | solution.py:448
  56.2 17.6 %collective-permute-start.9 = (f32[432,128]{1,0:T(8,128)S(1)}, f32[432,128]{1,0:T(8,128)S(1)}, u32[]{:S(2)}, u32[]{:S(2)}) collective-permute-start(f32[432,128]{1,0:T(8,128)S(1)} %copy-done.41), channel_id=1, source_target_pairs={{0,5},{1,4},{2,7},{3,6},{4,1},{5,0},{6,3},{7,2},{8,13},{9,12},{10,... | collective-permute-start | bytes 663560 | tf_op jit(solution)/shard_map/ppermute | solution.py:448
  56.3 19.6 %collective-permute-start.8 = (f32[432,128]{1,0:T(8,128)S(1)}, f32[432,128]{1,0:T(8,128)S(1)}, u32[]{:S(2)}, u32[]{:S(2)}) collective-permute-start(f32[432,128]{1,0:T(8,128)S(1)} %copy-done.40), channel_id=1, source_target_pairs={{0,12},{1,13},{2,14},{3,15},{4,8},{5,9},{6,10},{7,11},{8,4},{9,5},... | collective-permute-start | bytes 663560 | tf_op jit(solution)/shard_map/ppermute | solution.py:448
  59.2 20.1 %collective-permute-start.7 = (f32[432,128]{1,0:T(8,128)S(1)}, f32[432,128]{1,0:T(8,128)S(1)}, u32[]{:S(2)}, u32[]{:S(2)}) collective-permute-start(f32[432,128]{1,0:T(8,128)S(1)} %copy-done.39), channel_id=1, source_target_pairs={{0,4},{1,5},{2,6},{3,7},{4,0},{5,1},{6,2},{7,3},{8,12},{9,13},{10,... | collective-permute-start | bytes 663560 | tf_op jit(solution)/shard_map/ppermute | solution.py:448
  59.2 29.3 %collective-permute-start.6 = (f32[432,128]{1,0:T(8,128)S(1)}, f32[432,128]{1,0:T(8,128)S(1)}, u32[]{:S(2)}, u32[]{:S(2)}) collective-permute-start(f32[432,128]{1,0:T(8,128)S(1)} %copy-done.38), channel_id=1, source_target_pairs={{0,11},{1,10},{2,9},{3,8},{4,15},{5,14},{6,13},{7,12},{8,3},{9,2},... | collective-permute-start | bytes 663560 | tf_op jit(solution)/shard_map/ppermute | solution.py:448
  69.6 18.9 %collective-permute-start.5 = (f32[432,128]{1,0:T(8,128)S(1)}, f32[432,128]{1,0:T(8,128)S(1)}, u32[]{:S(2)}, u32[]{:S(2)}) collective-permute-start(f32[432,128]{1,0:T(8,128)S(1)} %copy-done.37), channel_id=1, source_target_pairs={{0,3},{1,2},{2,1},{3,0},{4,7},{5,6},{6,5},{7,4},{8,11},{9,10},{10,... | collective-permute-start | bytes 663560 | tf_op jit(solution)/shard_map/ppermute | solution.py:448
  73.9 21.3 %collective-permute-start.14 = (f32[432,128]{1,0:T(8,128)S(1)}, f32[432,128]{1,0:T(8,128)S(1)}, u32[]{:S(2)}, u32[]{:S(2)}) collective-permute-start(f32[432,128]{1,0:T(8,128)S(1)} %copy-done.36), channel_id=1, source_target_pairs={{0,15},{1,14},{2,13},{3,12},{4,11},{5,10},{6,9},{7,8},{8,7},{9,6},... | collective-permute-start | bytes 663560 | tf_op jit(solution)/shard_map/ppermute | solution.py:448
  75.8 26.2 %collective-permute-start.13 = (f32[432,128]{1,0:T(8,128)S(1)}, f32[432,128]{1,0:T(8,128)S(1)}, u32[]{:S(2)}, u32[]{:S(2)}) collective-permute-start(f32[432,128]{1,0:T(8,128)S(1)} %copy-done.35), channel_id=1, source_target_pairs={{0,7},{1,6},{2,5},{3,4},{4,3},{5,2},{6,1},{7,0},{8,15},{9,14},{10,... | collective-permute-start | bytes 663560 | tf_op jit(solution)/shard_map/ppermute | solution.py:448
  79.3 24.4 %collective-permute-start.12 = (f32[432,128]{1,0:T(8,128)S(1)}, f32[432,128]{1,0:T(8,128)S(1)}, u32[]{:S(2)}, u32[]{:S(2)}) collective-permute-start(f32[432,128]{1,0:T(8,128)S(1)} %copy-done.34), channel_id=1, source_target_pairs={{0,14},{1,15},{2,12},{3,13},{4,10},{5,11},{6,8},{7,9},{8,6},{9,7},... | collective-permute-start | bytes 663560 | tf_op jit(solution)/shard_map/ppermute | solution.py:448
  88.5 31.2 %collective-permute-start.11 = (f32[432,128]{1,0:T(8,128)}, f32[432,128]{1,0:T(8,128)}, u32[]{:S(2)}, u32[]{:S(2)}) collective-permute-start(f32[432,128]{1,0:T(8,128)} %get-tuple-element.95), channel_id=1, source_target_pairs={{0,6},{1,7},{2,4},{3,5},{4,2},{5,3},{6,0},{7,1},{8,14},{9,15},{10,... | collective-permute-start | bytes 663560 | tf_op jit(solution)/shard_map/ppermute | solution.py:448
  88.5 32.7 %collective-permute-start.10 = (f32[432,128]{1,0:T(8,128)}, f32[432,128]{1,0:T(8,128)}, u32[]{:S(2)}, u32[]{:S(2)}) collective-permute-start(f32[432,128]{1,0:T(8,128)} %get-tuple-element.93), channel_id=1, source_target_pairs={{0,13},{1,12},{2,15},{3,14},{4,9},{5,8},{6,11},{7,10},{8,5},{9,4},... | collective-permute-start | bytes 663560 | tf_op jit(solution)/shard_map/ppermute | solution.py:448
  95.1 35.9 %collective-permute-start.20 = (f32[432,128]{1,0:T(8,128)}, f32[432,128]{1,0:T(8,128)}, u32[]{:S(2)}, u32[]{:S(2)}) collective-permute-start(f32[432,128]{1,0:T(8,128)} %get-tuple-element.113), channel_id=1, source_target_pairs={{0,10},{1,11},{2,8},{3,9},{4,14},{5,15},{6,12},{7,13},{8,2},{9,3},... | collective-permute-start | bytes 663560 | tf_op jit(solution)/shard_map/ppermute | solution.py:448
  102.0 29.1 %collective-permute-start.19 = (f32[432,128]{1,0:T(8,128)}, f32[432,128]{1,0:T(8,128)}, u32[]{:S(2)}, u32[]{:S(2)}) collective-permute-start(f32[432,128]{1,0:T(8,128)} %get-tuple-element.111), channel_id=1, source_target_pairs={{0,2},{1,3},{2,0},{3,1},{4,6},{5,7},{6,4},{7,5},{8,10},{9,11},{10,... | collective-permute-start | bytes 663560 | tf_op jit(solution)/shard_map/ppermute | solution.py:448
  104.4 27.4 %collective-permute-start.18 = (f32[432,128]{1,0:T(8,128)}, f32[432,128]{1,0:T(8,128)}, u32[]{:S(2)}, u32[]{:S(2)}) collective-permute-start(f32[432,128]{1,0:T(8,128)} %get-tuple-element.109), channel_id=1, source_target_pairs={{0,9},{1,8},{2,11},{3,10},{4,13},{5,12},{6,15},{7,14},{8,1},{9,0},... | collective-permute-start | bytes 663560 | tf_op jit(solution)/shard_map/ppermute | solution.py:448
  119.7 66.2 %collective-permute-start.15 = (f32[1728,128]{1,0:T(8,128)}, f32[1728,128]{1,0:T(8,128)S(1)}, u32[]{:S(2)}, u32[]{:S(2)}) collective-permute-start(f32[1728,128]{1,0:T(8,128)} %shard_map.90.own_ref), channel_id=1, source_target_pairs={{0,16},{16,0},{1,17},{17,1},{2,18},{18,2},{3,19},{19,3},{4,20},{20... | collective-permute-start | bytes 2654216 | tf_op jit(solution)/shard_map/ppermute | solution.py:508
  131.1 17.1 %collective-permute-start.25 = (f32[432,128]{1,0:T(8,128)}, f32[432,128]{1,0:T(8,128)S(1)}, u32[]{:S(2)}, u32[]{:S(2)}) collective-permute-start(f32[432,128]{1,0:T(8,128)} %get-tuple-element.123), channel_id=1, source_target_pairs={{0,5},{1,4},{2,7},{3,6},{4,1},{5,0},{6,3},{7,2},{8,13},{9,12},{10,... | collective-permute-start | bytes 663560 | tf_op jit(solution)/shard_map/ppermute | solution.py:448
  134.0 19.4 %collective-permute-start.23 = (f32[432,128]{1,0:T(8,128)}, f32[432,128]{1,0:T(8,128)S(1)}, u32[]{:S(2)}, u32[]{:S(2)}) collective-permute-start(f32[432,128]{1,0:T(8,128)} %get-tuple-element.119), channel_id=1, source_target_pairs={{0,4},{1,5},{2,6},{3,7},{4,0},{5,1},{6,2},{7,3},{8,12},{9,13},{10,... | collective-permute-start | bytes 663560 | tf_op jit(solution)/shard_map/ppermute | solution.py:448
  142.9 25.2 %collective-permute-start.22 = (f32[432,128]{1,0:T(8,128)}, f32[432,128]{1,0:T(8,128)S(1)}, u32[]{:S(2)}, u32[]{:S(2)}) collective-permute-start(f32[432,128]{1,0:T(8,128)} %get-tuple-element.117), channel_id=1, source_target_pairs={{0,11},{1,10},{2,9},{3,8},{4,15},{5,14},{6,13},{7,12},{8,3},{9,2},... | collective-permute-start | bytes 663560 | tf_op jit(solution)/shard_map/ppermute | solution.py:448
  148.2 21.0 %collective-permute-start.21 = (f32[432,128]{1,0:T(8,128)}, f32[432,128]{1,0:T(8,128)S(1)}, u32[]{:S(2)}, u32[]{:S(2)}) collective-permute-start(f32[432,128]{1,0:T(8,128)} %get-tuple-element.115), channel_id=1, source_target_pairs={{0,3},{1,2},{2,1},{3,0},{4,7},{5,6},{6,5},{7,4},{8,11},{9,10},{10,... | collective-permute-start | bytes 663560 | tf_op jit(solution)/shard_map/ppermute | solution.py:448
  148.2 21.0 %collective-permute-start.30 = (f32[432,128]{1,0:T(8,128)}, f32[432,128]{1,0:T(8,128)S(1)}, u32[]{:S(2)}, u32[]{:S(2)}) collective-permute-start(f32[432,128]{1,0:T(8,128)} %get-tuple-element.133), channel_id=1, source_target_pairs={{0,15},{1,14},{2,13},{3,12},{4,11},{5,10},{6,9},{7,8},{8,7},{9,6},... | collective-permute-start | bytes 663560 | tf_op jit(solution)/shard_map/ppermute | solution.py:448
  153.4 23.3 %collective-permute-start.29 = (f32[432,128]{1,0:T(8,128)}, f32[432,128]{1,0:T(8,128)S(1)}, u32[]{:S(2)}, u32[]{:S(2)}) collective-permute-start(f32[432,128]{1,0:T(8,128)} %get-tuple-element.131), channel_id=1, source_target_pairs={{0,7},{1,6},{2,5},{3,4},{4,3},{5,2},{6,1},{7,0},{8,15},{9,14},{10,... | collective-permute-start | bytes 663560 | tf_op jit(solution)/shard_map/ppermute | solution.py:448
  169.3 16.6 %collective-permute-start.26 = (f32[432,128]{1,0:T(8,128)}, f32[432,128]{1,0:T(8,128)S(1)}, u32[]{:S(2)}, u32[]{:S(2)}) collective-permute-start(f32[432,128]{1,0:T(8,128)} %get-tuple-element.125), channel_id=1, source_target_pairs={{0,13},{1,12},{2,15},{3,14},{4,9},{5,8},{6,11},{7,10},{8,5},{9,4},... | collective-permute-start | bytes 663560 | tf_op jit(solution)/shard_map/ppermute | solution.py:448
  196.8 79.5 %all-to-all-start.1 = ((f32[16,432,128]{2,1,0:T(8,128)}), f32[16,432,128]{2,1,0:T(8,128)S(1)}, u32[]{:S(2)}, u32[]{:S(2)}) async-start(f32[16,432,128]{2,1,0:T(8,128)} %shard_map.91), calls=%async_computation.1 | async-start | bytes 7077888 | tf_op jit(solution)/shard_map/all_to_all | solution.py:453
  289.3 61.2 %all-to-all-start.2 = ((f32[32,112,128]{2,1,0:T(8,128)}), f32[32,112,128]{2,1,0:T(8,128)S(1)}, u32[]{:S(2)}, u32[]{:S(2)}) async-start(f32[32,112,128]{2,1,0:T(8,128)} %bitcast.23), calls=%async_computation.2 | async-start | bytes 3670016 | tf_op jit(solution)/shard_map/all_to_all | solution.py:457
  306.3 47.3 %collective-permute-start.33 = (f32[1728,128]{1,0:T(8,128)S(1)}, f32[1728,128]{1,0:T(8,128)}, u32[]{:S(2)}, u32[]{:S(2)}) collective-permute-start(f32[1728,128]{1,0:T(8,128)S(1)} %copy-done.3), channel_id=1, source_target_pairs={{0,16},{16,0},{1,17},{17,1},{2,18},{18,2},{3,19},{19,3},{4,20},{20... | collective-permute-start | bytes 2654216 | tf_op jit(solution)/shard_map/ppermute | solution.py:560
  308.8 58.0 %collective-permute-start.31 = (f32[1728,128]{1,0:T(8,128)}, f32[1728,128]{1,0:T(8,128)}, u32[]{:S(2)}, u32[]{:S(2)}) collective-permute-start(f32[1728,128]{1,0:T(8,128)} %get-tuple-element.137.lower_ref), channel_id=1, source_target_pairs={{0,16},{16,0},{1,17},{17,1},{2,18},{18,2},{3,19},{19,3},{4,20},{20... | collective-permute-start | bytes 2654216 | tf_op jit(solution)/shard_map/ppermute | solution.py:561
  353.6 16.8 %all-to-all-start.4 = ((f32[16,56,128]{2,1,0:T(8,128)}), f32[16,56,128]{2,1,0:T(8,128)S(1)}, u32[]{:S(2)}, u32[]{:S(2)}) async-start(f32[16,56,128]{2,1,0:T(8,128)} %bitcast.8), calls=%async_computation.4 | async-start | bytes 917504 | tf_op jit(solution)/shard_map/all_to_all | solution.py:453
  370.4 17.1 %all-to-all-start.3 = ((f32[16,56,128]{2,1,0:T(8,128)}), f32[16,56,128]{2,1,0:T(8,128)S(1)}, u32[]{:S(2)}, u32[]{:S(2)}) async-start(f32[16,56,128]{2,1,0:T(8,128)} %bitcast.6), calls=%async_computation.3 | async-start | bytes 917504 | tf_op jit(solution)/shard_map/all_to_all | solution.py:453
  (50 other events, 1797.1 us)

commit v10 on v8

--- a/solution.py
+++ b/solution.py
@@ -220,17 +220,18 @@
             )
 
 
-def share_kernel(sizes, moved_ref, out_ref):
+def share_kernel(sizes, place_ref, moved_ref, out_ref):
     planes, grid, rows, share = sizes
     length = planes * grid
     chunk = chunk_rows(sizes)
     for source in range(grid):
         for row in range(share):
             start = source * chunk + row
-            out_ref[pl.ds(row * length + source * planes, planes), :] = moved_ref[pl.ds(start, planes, stride=share), :]
-
-
-def along_kernel(sizes, steps, turns, place_ref, *refs):
+            first = row * length + (place_ref[0] % grid ^ source) * planes
+            out_ref[pl.ds(first, planes), :] = moved_ref[pl.ds(start, planes, stride=share), :]
+
+
+def along_kernel(sizes, steps, turns, *refs):
     planes, grid, rows, share = sizes
     *moved_refs, kin_ref, out_ref, lines = refs
     length = planes * grid
@@ -239,9 +240,9 @@
         row = pl.program_id(0) * (rows // steps) + inner
         slot = lines.at[inner]
         for turn, moved_ref in zip(turns, moved_refs):
-            first = (place_ref[0] % grid ^ turn) * planes
+            here = slice(turn * planes, (turn + 1) * planes)
             for part in range(2):
-                slot[part, pl.ds(first, planes), :] = moved_ref[pl.ds(part * rows + row, planes, stride=2 * rows), :]
+                slot[part, here, :] = moved_ref[pl.ds(part * rows + row, planes, stride=2 * rows), :]
         field = jnp.concatenate([slot[0], slot[1]], axis=1)
         out_ref[inner * length : (inner + 1) * length, :] = product_of_parts(kin, split(field))
 
@@ -258,9 +259,9 @@
         here = slice(inner * length, (inner + 1) * length)
         slot = lines.at[inner]
         for turn, mixed_ref in zip(turns, mixed_refs):
-            first = (place_ref[0] % grid ^ turn) * planes
+            rest = slice(turn * planes, (turn + 1) * planes)
             for part in range(2):
-                slot[part, pl.ds(first, planes), :] = mixed_ref[pl.ds(part * rows + row, planes, stride=2 * rows), :]
+                slot[part, rest, :] = mixed_ref[pl.ds(part * rows + row, planes, stride=2 * rows), :]
         along = along_ref[here, :]
         again = product_of_parts(kin, split(jnp.concatenate([slot[0], slot[1]], axis=1) + along))
         potential = jnp.where(mine_here, own_ref[here, :], other_ref[here, :])
@@ -268,9 +269,11 @@
             mine = along[:, part * LANES : (part + 1) * LANES]
             turned = along[:, LANES:] if part == 0 else -along[:, :LANES]
             twice = again[:, part * LANES : (part + 1) * LANES] + potential * mine
-            out_ref[pl.ds(part * rows + row, length, stride=2 * rows), :] = (
-                2.0 * BESSEL_ONE * turned - 4.0 * BESSEL_TWO * twice
-            )
+            slot[part] = 2.0 * BESSEL_ONE * turned - 4.0 * BESSEL_TWO * twice
+            for turn in range(grid):
+                start = (place_ref[0] % grid ^ turn) * planes * 2 * rows + part * rows + row
+                piece = slot[part, turn * planes : (turn + 1) * planes, :]
+                out_ref[pl.ds(start, planes, stride=2 * rows), :] = piece
 
 
 def fresh_kernel(
@@ -413,7 +416,12 @@
     field = planes * cell_rows
     work = 2 * planes * length**3
     place = lax.axis_index(("band", "grid")).astype(jnp.int32).reshape(1)
-    kin = jnp.asarray(kinetic_matrix(length))
+    kin_np = kinetic_matrix(length)
+    kin = jnp.asarray(kin_np)
+    blocks = kin_np.reshape(grid, planes, grid, planes)
+    orders = [[spot ^ turn for turn in range(grid)] for spot in range(grid)]
+    turned = np.stack([blocks[order][:, :, order].reshape(length, length) for order in orders])
+    turned_kin = lax.dynamic_index_in_dim(jnp.asarray(turned), lax.axis_index("grid"), keepdims=False)
     basis_np, squares_np = real_basis(length)
     tables = jnp.asarray(np.stack([basis_np, basis_np.T]))
     smem = pl.BlockSpec(memory_space=pltpu.SMEM)
@@ -432,17 +440,14 @@
     def scratch(count):
         return [pltpu.VMEM((count * bunch, cell_rows, LANES), jnp.float32)]
 
-    line = []
-
-    def send(turn, piece, *gates):
+    def send(turn, piece):
         if not turn:
             return piece
-        if len(line) >= 5:
-            gates += (line[-5],)
-        if gates:
-            piece = lax.optimization_barrier((piece, *gates))[0]
-        line.append(lax.ppermute(piece, "grid", [(spot, spot ^ turn) for spot in range(grid)]))
-        return line[-1]
+        return lax.ppermute(piece, "grid", [(spot, spot ^ turn) for spot in range(grid)])
+
+    def hold(pieces, gates):
+        late = lax.optimization_barrier((list(pieces[6:]), gates))[0]
+        return list(pieces[:6]) + list(late)
 
     def swap(array):
         flat = array.reshape(grid, -1, LANES)
@@ -453,6 +458,9 @@
         return lax.all_to_all(flat, ("band", "grid"), split_axis=0, concat_axis=0).reshape(array.shape)
 
     turns = turn_order(grid)
+    first_turns = [0] * grid
+    for rank, name in enumerate(sorted(range(grid - 1), key=str)):
+        first_turns[name + 1] = turns[rank + 1]
     spec_rows = 2 * grid * chunk_rows(sizes)
     mixed_rows = 2 * planes * rows
     steps = 6 if rows % 6 == 0 and share % (rows // 6) == 0 else 2
@@ -469,7 +477,7 @@
     place, shared = lax.optimization_barrier((place, shared))
     shared = swap(shared)
     moved = pl.pallas_call(
-        functools.partial(pack_kernel, sizes, bunch, turns),
+        functools.partial(pack_kernel, sizes, bunch, first_turns),
         grid=(planes // bunch,),
         in_specs=[smem, psi_spec],
         out_specs=[whole(mixed_rows, LANES)] * grid,
@@ -478,8 +486,6 @@
         compiler_params=PARAMS,
         cost_estimate=cost(0, 8 << 20),
     )(place, orbitals)
-    moved = [send(turn, piece) for turn, piece in zip(turns[:6], moved[:6])] + list(moved[6:])
-    behind = lax.optimization_barrier((place, line[1]))[0]
     *mixed, base = pl.pallas_call(
         functools.partial(plane_kernel, sizes, bunch, turns),
         grid=(planes // bunch,),
@@ -489,28 +495,27 @@
         scratch_shapes=scratch(2),
         compiler_params=PARAMS,
         cost_estimate=cost(8 * 3 * work, 20 << 20),
-    )(behind, orbitals, ion_potential, hxc_potential, kin)
-    for index in range(6, grid):
-        moved[index] = send(turns[index], moved[index], *([base] if index < 11 else []))
+    )(place, orbitals, ion_potential, hxc_potential, kin)
+    moved = [send(turn, piece) for turn, piece in zip(first_turns, moved)]
     own = pl.pallas_call(
         functools.partial(share_kernel, sizes),
-        in_specs=[vmem],
+        in_specs=[smem, vmem],
         out_specs=vmem,
         out_shape=shape(share * length, LANES),
         compiler_params=PARAMS,
         cost_estimate=cost(0, 2 << 20),
-    )(shared)
+    )(place, shared)
     other = lax.ppermute(own, "band", [(0, 1), (1, 0)])
     along = pl.pallas_call(
-        functools.partial(along_kernel, sizes, steps, turns),
+        functools.partial(along_kernel, sizes, steps, first_turns),
         grid=(steps,),
-        in_specs=[smem] + [whole(mixed_rows, LANES)] * grid + [square],
+        in_specs=[whole(mixed_rows, LANES)] * grid + [square],
         out_specs=pl.BlockSpec((rows // steps * length, 2 * LANES), lambda i: (i, 0)),
         out_shape=shape(rows * length, 2 * LANES),
         scratch_shapes=[pltpu.VMEM((rows // steps, 2, length, LANES), jnp.float32)],
         compiler_params=PARAMS,
         cost_estimate=cost(2 * 3 * work, 8 << 20),
-    )(place, *moved, kin)
+    )(*moved, turned_kin)
     mixed = [send(turn, piece) for turn, piece in zip(turns, mixed)]
     half_spec = pl.BlockSpec((rows // steps * length, LANES), lambda i: (i % (steps // 2), 0))
     update = pl.pallas_call(
@@ -529,7 +534,7 @@
         scratch_shapes=[pltpu.VMEM((rows // steps, 2, length, LANES), jnp.float32)],
         compiler_params=PARAMS,
         cost_estimate=cost(2 * 3 * work, 14 << 20),
-    )(place, along, own, other, kin, *mixed)
+    )(place, along, own, other, turned_kin, *mixed)
     update = swap(update)
 
     fresh, upper, lower, spectrum = pl.pallas_call(

time: 401 us -> 406 us (1.012)
  waiting for transfers between devices: 215 us -> 252 us
  starting transfers between devices: 113 us -> 78.9 us
    ppermute x30, waiting for transfers between devices: 76 us -> 113 us  [send(): lax.ppermute(piece, 'grid', [(spot, spot ^ turn) for spot in range(grid)])]
    ppermute x30, starting transfers between devices: 65.6 us -> 32.9 us  [send(): lax.ppermute(piece, 'grid', [(spot, spot ^ turn) for spot in range(grid)])]
  transfers between devices with their start and end apart: 40 -> 40, of which waited for: 21 -> 22; matrix products, arithmetic and copies ran while one was open for 0% -> 1% of each run, Pallas kernels for 9% -> 9%
where the time goes in v10:
time: 406 us; the launch traced here: 405 us
  waiting for transfers between devices  252 us (62%)
  starting transfers between devices  78.9 us (19%)
  Pallas kernels  64 us (16%)
  local copies, waits for them, and re-layouts  8.37 us (2%)
    ppermute x30, waiting for transfers between devices, send(): lax.ppermute(piece, 'grid', [(spot, spot ^ turn) for spot in range(grid)])  113 us
    all_to_all x4, waiting for transfers between devices, swap(): lax.all_to_all(flat, 'grid', split_axis=0, concat_axis=0)  81.5 us
    all_to_all x1, waiting for transfers between devices, swap_all(): lax.all_to_all(flat, ('band', 'grid'), split_axis=0, concat_axis=0)  41.3 us
    ppermute x30, starting transfers between devices, send(): lax.ppermute(piece, 'grid', [(spot, spot ^ turn) for spot in range(grid)])  32.9 us
    all_to_all x4, starting transfers between devices, swap(): lax.all_to_all(flat, 'grid', split_axis=0, concat_axis=0)  23.6 us
    all_to_all x1, starting transfers between devices, swap_all(): lax.all_to_all(flat, ('band', 'grid'), split_axis=0, concat_axis=0)  16.9 us
    pallas_call x1, Pallas kernels, packed_path(): pl.pallas_call(functools.partial(plane_kernel, sizes, bunch, turns), grid...  13.9 us
    pallas_call x1, Pallas kernels, packed_path(): pl.pallas_call(functools.partial(fresh_kernel, sizes, bunch), grid=(plane...  10.9 us
  transfers between devices with their start and end apart: 40, of which 22 were waited for; matrix products, arithmetic and copies ran while one was open for 1% of the time, Pallas kernels for 9%

profile of v10, /device:TPU:0, one launch (start us, length us, event | category | flops | bytes accessed | tf_op | source)
XLA Modules:
  0.0 405.1 jit_solution(3808670201658820219)
XLA Ops:
  0.6 4.1 %shard_map.95 = f32[1792,128]{1,0:T(8,128)} custom-call(s32[1]{0:T(128)} %bitcast.place_ref, f32[12,192,192]{2,1,0:T(8,128)} %ion_ref.3, f32[12,192,192]{2,1,0:T(8,128)} %hxc_ref.3), custom_call_target="tpu_custom_call" | custom-call | bytes 6291456 | tf_op jit(solution)/shard_map/pallas_call | solution.py:467
  4.8 7.4 %all-to-all-start = ((f32[16,112,128]{2,1,0:T(8,128)}), f32[16,112,128]{2,1,0:T(8,128)S(1)}, u32[]{:S(2)}, u32[]{:S(2)}) async-start(f32[16,112,128]{2,1,0:T(8,128)} %bitcast.24), calls=%async_computation | async-start | bytes 1835008 | tf_op jit(solution)/shard_map/all_to_all | solution.py:454
  12.1 5.3 %shard_map.96 = (f32[432,128]{1,0:T(8,128)}, f32[432,128]{1,0:T(8,128)}, f32[432,128]{1,0:T(8,128)}, f32[432,128]{1,0:T(8,128)}, f32[432,128]{1,0:T(8,128)}, /*i...) custom-call(s32[1]{0:T(128)} %bitcast.place_ref, ...), custom_call_target="tpu_custom_call" | custom-call | bytes 8388608 | tf_op jit(solution)/shard_map/pallas_call | solution.py:479
  24.8 30.5 %collective-permute-done.refs_1_ = f32[432,128]{1,0:T(8,128)S(1)} collective-permute-done((f32[432,128]{1,0:T(8,128)}, f32[432,128]{1,0:T(8,128)S(1)}, u32[]{:S(2)}, u32[]{:S(2)}) %collective-permute-start) | collective-permute-done | bytes 221216 | tf_op jit(solution)/shard_map/ppermute | solution.py:446
  59.1 6.6 %collective-permute-start.3 = (f32[432,128]{1,0:T(8,128)}, f32[432,128]{1,0:T(8,128)S(1)}, u32[]{:S(2)}, u32[]{:S(2)}) collective-permute-start(f32[432,128]{1,0:T(8,128)} %get-tuple-element.52), channel_id=1, source_target_pairs={{0,12},{1,13},{2,14},{3,15},{4,8},{5,9},{6,10},{7,11},{8,4},{9,5},... | collective-permute-start | bytes 663560 | tf_op jit(solution)/shard_map/ppermute | solution.py:446
  65.8 4.8 %collective-permute-done.12.refs_13_ = f32[432,128]{1,0:T(8,128)S(1)} collective-permute-done((f32[432,128]{1,0:T(8,128)}, f32[432,128]{1,0:T(8,128)S(1)}, u32[]{:S(2)}, u32[]{:S(2)}) %collective-permute-start.12) | collective-permute-done | bytes 221216 | tf_op jit(solution)/shard_map/ppermute | solution.py:446
  70.8 8.3 %collective-permute-done.14.refs_15_ = f32[432,128]{1,0:T(8,128)S(1)} collective-permute-done((f32[432,128]{1,0:T(8,128)}, f32[432,128]{1,0:T(8,128)S(1)}, u32[]{:S(2)}, u32[]{:S(2)}) %collective-permute-start.14) | collective-permute-done | bytes 221216 | tf_op jit(solution)/shard_map/ppermute | solution.py:446
  79.1 6.2 %collective-permute-done.2.refs_3_ = f32[432,128]{1,0:T(8,128)S(1)} collective-permute-done((f32[432,128]{1,0:T(8,128)}, f32[432,128]{1,0:T(8,128)S(1)}, u32[]{:S(2)}, u32[]{:S(2)}) %collective-permute-start.2) | collective-permute-done | bytes 221216 | tf_op jit(solution)/shard_map/ppermute | solution.py:446
  85.2 5.1 %collective-permute-start.7 = (f32[432,128]{1,0:T(8,128)}, f32[432,128]{1,0:T(8,128)S(1)}, u32[]{:S(2)}, u32[]{:S(2)}) collective-permute-start(f32[432,128]{1,0:T(8,128)} %get-tuple-element.56), channel_id=1, source_target_pairs={{0,14},{1,15},{2,12},{3,13},{4,10},{5,11},{6,8},{7,9},{8,6},{9,7},... | collective-permute-start | bytes 663560 | tf_op jit(solution)/shard_map/ppermute | solution.py:446
  90.3 13.9 %shard_map.99 = (f32[432,128]{1,0:T(8,128)}, f32[432,128]{1,0:T(8,128)}, f32[432,128]{1,0:T(8,128)}, f32[432,128]{1,0:T(8,128)}, f32[432,128]{1,0:T(8,128)}, /*i...) custom-call(s32[1]{0:T(128)} %bitcast.place_ref, ...), custom_call_target="tpu_custom_call" | custom-call | flops 4076863488 | bytes 20971520 | tf_op jit(solution)/shard_map/pallas_call | solution.py:489
  116.2 17.0 %collective-permute-done.16.refs_1_ = f32[432,128]{1,0:T(8,128)S(1)} collective-permute-done((f32[432,128]{1,0:T(8,128)}, f32[432,128]{1,0:T(8,128)S(1)}, u32[]{:S(2)}, u32[]{:S(2)}) %collective-permute-start.16) | collective-permute-done | bytes 221216 | tf_op jit(solution)/shard_map/ppermute | solution.py:446
  133.5 8.9 %collective-permute-done.18.refs_3_ = f32[432,128]{1,0:T(8,128)S(1)} collective-permute-done((f32[432,128]{1,0:T(8,128)}, f32[432,128]{1,0:T(8,128)S(1)}, u32[]{:S(2)}, u32[]{:S(2)}) %collective-permute-start.18) | collective-permute-done | bytes 221216 | tf_op jit(solution)/shard_map/ppermute | solution.py:446
  143.5 9.4 %collective-permute-done.20.refs_5_ = f32[432,128]{1,0:T(8,128)S(1)} collective-permute-done((f32[432,128]{1,0:T(8,128)}, f32[432,128]{1,0:T(8,128)S(1)}, u32[]{:S(2)}, u32[]{:S(2)}) %collective-permute-start.20) | collective-permute-done | bytes 221216 | tf_op jit(solution)/shard_map/ppermute | solution.py:446
  153.0 3.2 collective-permute-done.22.refs_7_
  165.0 6.5 %collective-permute-done.25.refs_10_ = f32[432,128]{1,0:T(8,128)} collective-permute-done((f32[432,128]{1,0:T(8,128)}, f32[432,128]{1,0:T(8,128)}, u32[]{:S(2)}, u32[]{:S(2)}) %collective-permute-start.25) | collective-permute-done | bytes 221216 | tf_op jit(solution)/shard_map/ppermute | solution.py:446
  175.6 6.4 %shard_map.97.along_ref = f32[3456,256]{1,0:T(8,128)} custom-call(f32[432,128]{1,0:T(8,128)} %get-tuple-element.48.refs_0_, f32[432,128]{1,0:T(8,128)} %copy-done.9, f32[432,128]{1,0:T(8,128)} %copy-done.10, f32[432,128]{1,0:T(8,128)} %copy-done.16, f32[432,128]{1,0:T(8,128)} %copy-done.17, f32[432,128]{1,0:T(8,128)} %copy-done.18, f32[432,128]{1,0:T(8,128)} %copy-done.19, ...), custom_call_target="tpu_custom_call" | custom-call | flops 1019215872 | bytes 8388608 | tf_op jit(solution)/shard_map/pallas_call | solution.py:509
  182.6 3.5 collective-permute-done.29.refs_14_
  186.1 5.2 %collective-permute-done.30.refs_15_ = f32[432,128]{1,0:T(8,128)} collective-permute-done((f32[432,128]{1,0:T(8,128)}, f32[432,128]{1,0:T(8,128)}, u32[]{:S(2)}, u32[]{:S(2)}) %collective-permute-start.30) | collective-permute-done | bytes 221216 | tf_op jit(solution)/shard_map/ppermute | solution.py:446
  192.2 9.3 %shard_map.100 = f32[6912,128]{1,0:T(8,128)} custom-call(s32[1]{0:T(128)} %bitcast.place_ref, f32[3456,256]{1,0:T(8,128)} %shard_map.97.along_ref, f32[1728,128]{1,0:T(8,128)} %shard_map.98.own_ref, f32[1728,128]{1,0:T(8,128)} %copy-done.6, f32[192,192]{1,0:T(8,128)} %dynamic-slice_bitcast_fusion.refs_16_.kin_ref, f32[432,128]{1,0:T(8,128)} %get-tuple-element.65.refs_0_, ...), custom_call_target="tpu_custom_call" | custom-call | flops 1019215872 | bytes 14680064 | tf_op jit(solution)/shard_map/pallas_call | solution.py:521
  201.5 8.9 %all-to-all-start.1 = ((f32[16,432,128]{2,1,0:T(8,128)}), f32[16,432,128]{2,1,0:T(8,128)S(1)}, u32[]{:S(2)}, u32[]{:S(2)}) async-start(f32[16,432,128]{2,1,0:T(8,128)} %bitcast.21), calls=%async_computation.1 | async-start | bytes 7077888 | tf_op jit(solution)/shard_map/all_to_all | solution.py:454
  211.1 65.6 %all-to-all-done.1 = f32[16,432,128]{2,1,0:T(8,128)S(1)} async-done(((f32[16,432,128]{2,1,0:T(8,128)}), f32[16,432,128]{2,1,0:T(8,128)S(1)}, u32[]{:S(2)}, u32[]{:S(2)}) %all-to-all-start.1) | async-done | bytes 3538976 | tf_op jit(solution)/shard_map/all_to_all | solution.py:454
  278.4 10.9 %shard_map.101 = (f32[1,2,12,192,192]{4,3,2,1,0:T(8,128)}, f32[1728,128]{1,0:T(8,128)}, f32[1728,128]{1,0:T(8,128)}, f32[3584,128]{1,0:T(8,128)}) custom-call(f32[1]{0:T(128)S(6)} %copy.15.occ_ref, f32[6912,128]{1,0:T(8,128)} %bitcast.22, f32[2,12,192,192]{3,2,1,0:T(8,128)} %get-tuple-element.81.base_ref, f32[2,192,192]{2,1,0:T(8,128)} %constant.31.clone.tables_ref), custom_call_target="tpu_custom_call" | custom-call | flops 2038431744 | bytes 16777216 | tf_op jit(solution)/shard_map/pallas_call | solution.py:540
  289.4 16.9 %all-to-all-start.2 = ((f32[32,112,128]{2,1,0:T(8,128)}), f32[32,112,128]{2,1,0:T(8,128)S(1)}, u32[]{:S(2)}, u32[]{:S(2)}) async-start(f32[32,112,128]{2,1,0:T(8,128)} %bitcast.27), calls=%async_computation.2 | async-start | bytes 3670016 | tf_op jit(solution)/shard_map/all_to_all | solution.py:458
  309.2 41.3 %all-to-all-done.2 = f32[32,112,128]{2,1,0:T(8,128)S(1)} async-done(((f32[32,112,128]{2,1,0:T(8,128)}), f32[32,112,128]{2,1,0:T(8,128)S(1)}, u32[]{:S(2)}, u32[]{:S(2)}) %all-to-all-start.2) | async-done | bytes 1835040 | tf_op jit(solution)/shard_map/all_to_all | solution.py:458
  353.7 3.6 all-to-all-start.4
  357.3 9.6 %collective-permute-done.31.lower_other = f32[1728,128]{1,0:T(8,128)} collective-permute-done((f32[1728,128]{1,0:T(8,128)}, f32[1728,128]{1,0:T(8,128)}, u32[]{:S(2)}, u32[]{:S(2)}) %collective-permute-start.31) | collective-permute-done | bytes 884768 | tf_op jit(solution)/shard_map/ppermute | solution.py:561
  366.9 3.6 all-to-all-done.4
  370.5 3.8 all-to-all-start.3
  375.2 12.3 %all-to-all-done.3 = f32[16,56,128]{2,1,0:T(8,128)S(1)} async-done(((f32[16,56,128]{2,1,0:T(8,128)}), f32[16,56,128]{2,1,0:T(8,128)S(1)}, u32[]{:S(2)}, u32[]{:S(2)}) %all-to-all-start.3) | async-done | bytes 458784 | tf_op jit(solution)/shard_map/all_to_all | solution.py:454
  389.2 4.3 %shard_map.103.refs_0_ = f32[12,192,192]{2,1,0:T(8,128)} custom-call(s32[1]{0:T(128)} %bitcast.place_ref, f32[896,128]{1,0:T(8,128)} %bitcast.26, f32[896,128]{1,0:T(8,128)} %copy-done.7, f32[1728,128]{1,0:T(8,128)} %get-tuple-element.87.upper_ref, f32[1728,128]{1,0:T(8,128)} %get-tuple-element.85.lower_ref, ...), custom_call_target="tpu_custom_call" | custom-call | flops 509607936 | bytes 4194304 | tf_op jit(solution)/shard_map/pallas_call | solution.py:583
  393.5 6.6 %collective-permute-done.32.far_ref = f32[896,128]{1,0:T(8,128)S(1)} collective-permute-done((f32[896,128]{1,0:T(8,128)S(1)}, f32[896,128]{1,0:T(8,128)S(1)}, u32[]{:S(2)}, u32[]{:S(2)}) %collective-permute-start.32) | collective-permute-done | bytes 458784 | tf_op jit(solution)/shard_map/ppermute | solution.py:603
  400.8 4.3 %shard_map.104 = f32[12,192,192]{2,1,0:T(8,128)} custom-call(s32[1]{0:T(128)} %bitcast.place_ref, f32[896,128]{1,0:T(8,128)} %bitcast.29, f32[896,128]{1,0:T(8,128)} %copy-done.8, f32[1728,128]{1,0:T(8,128)} %get-tuple-element.87.upper_ref, f32[1728,128]{1,0:T(8,128)} %get-tuple-element.85.lower_ref, ...), custom_call_target="tpu_custom_call", output_to_operand_aliasing={{}: (8, {})} | custom-call | flops 509607936 | bytes 4194304 | tf_op jit(solution)/shard_map/pallas_call | solution.py:583
  (123 shorter events, 50.2 us)
Async XLA Ops:
  4.8 105.2 %all-to-all-start = ((f32[16,112,128]{2,1,0:T(8,128)}), f32[16,112,128]{2,1,0:T(8,128)S(1)}, u32[]{:S(2)}, u32[]{:S(2)}) async-start(f32[16,112,128]{2,1,0:T(8,128)} %bitcast.24), calls=%async_computation | async-start | bytes 1835008 | tf_op jit(solution)/shard_map/all_to_all | solution.py:454
  17.5 37.8 %collective-permute-start = (f32[432,128]{1,0:T(8,128)}, f32[432,128]{1,0:T(8,128)S(1)}, u32[]{:S(2)}, u32[]{:S(2)}) collective-permute-start(f32[432,128]{1,0:T(8,128)} %get-tuple-element.49), channel_id=1, source_target_pairs={{0,8},{1,9},{2,10},{3,11},{4,12},{5,13},{6,14},{7,15},{8,0},{9,1},... | collective-permute-start | bytes 663560 | tf_op jit(solution)/shard_map/ppermute | solution.py:446
  20.3 35.3 %collective-permute-start.1 = (f32[432,128]{1,0:T(8,128)}, f32[432,128]{1,0:T(8,128)S(1)}, u32[]{:S(2)}, u32[]{:S(2)}) collective-permute-start(f32[432,128]{1,0:T(8,128)} %get-tuple-element.50), channel_id=1, source_target_pairs={{0,1},{1,0},{2,3},{3,2},{4,5},{5,4},{6,7},{7,6},{8,9},{9,8},{10,11... | collective-permute-start | bytes 663560 | tf_op jit(solution)/shard_map/ppermute | solution.py:446
  20.3 38.8 %collective-permute-start.10 = (f32[432,128]{1,0:T(8,128)}, f32[432,128]{1,0:T(8,128)S(1)}, u32[]{:S(2)}, u32[]{:S(2)}) collective-permute-start(f32[432,128]{1,0:T(8,128)} %get-tuple-element.59), channel_id=1, source_target_pairs={{0,9},{1,8},{2,11},{3,10},{4,13},{5,12},{6,15},{7,14},{8,1},{9,0},... | collective-permute-start | bytes 663560 | tf_op jit(solution)/shard_map/ppermute | solution.py:446
  20.5 38.6 %collective-permute-start.11 = (f32[432,128]{1,0:T(8,128)}, f32[432,128]{1,0:T(8,128)S(1)}, u32[]{:S(2)}, u32[]{:S(2)}) collective-permute-start(f32[432,128]{1,0:T(8,128)} %get-tuple-element.60), channel_id=1, source_target_pairs={{0,2},{1,3},{2,0},{3,1},{4,6},{5,7},{6,4},{7,5},{8,10},{9,11},{10,... | collective-permute-start | bytes 663560 | tf_op jit(solution)/shard_map/ppermute | solution.py:446
  22.4 48.1 %collective-permute-start.12 = (f32[432,128]{1,0:T(8,128)}, f32[432,128]{1,0:T(8,128)S(1)}, u32[]{:S(2)}, u32[]{:S(2)}) collective-permute-start(f32[432,128]{1,0:T(8,128)} %get-tuple-element.61), channel_id=1, source_target_pairs={{0,10},{1,11},{2,8},{3,9},{4,14},{5,15},{6,12},{7,13},{8,2},{9,3},... | collective-permute-start | bytes 663560 | tf_op jit(solution)/shard_map/ppermute | solution.py:446
  55.6 23.5 %collective-permute-start.14 = (f32[432,128]{1,0:T(8,128)}, f32[432,128]{1,0:T(8,128)S(1)}, u32[]{:S(2)}, u32[]{:S(2)}) collective-permute-start(f32[432,128]{1,0:T(8,128)} %get-tuple-element.63), channel_id=1, source_target_pairs={{0,11},{1,10},{2,9},{3,8},{4,15},{5,14},{6,13},{7,12},{8,3},{9,2},... | collective-permute-start | bytes 663560 | tf_op jit(solution)/shard_map/ppermute | solution.py:446
  59.1 26.1 %collective-permute-start.2 = (f32[432,128]{1,0:T(8,128)}, f32[432,128]{1,0:T(8,128)S(1)}, u32[]{:S(2)}, u32[]{:S(2)}) collective-permute-start(f32[432,128]{1,0:T(8,128)} %get-tuple-element.51), channel_id=1, source_target_pairs={{0,4},{1,5},{2,6},{3,7},{4,0},{5,1},{6,2},{7,3},{8,12},{9,13},{10,... | collective-permute-start | bytes 663560 | tf_op jit(solution)/shard_map/ppermute | solution.py:446
  59.1 31.2 %collective-permute-start.3 = (f32[432,128]{1,0:T(8,128)}, f32[432,128]{1,0:T(8,128)S(1)}, u32[]{:S(2)}, u32[]{:S(2)}) collective-permute-start(f32[432,128]{1,0:T(8,128)} %get-tuple-element.52), channel_id=1, source_target_pairs={{0,12},{1,13},{2,14},{3,15},{4,8},{5,9},{6,10},{7,11},{8,4},{9,5},... | collective-permute-start | bytes 663560 | tf_op jit(solution)/shard_map/ppermute | solution.py:446
  70.5 33.8 %collective-permute-start.4 = (f32[432,128]{1,0:T(8,128)}, f32[432,128]{1,0:T(8,128)S(1)}, u32[]{:S(2)}, u32[]{:S(2)}) collective-permute-start(f32[432,128]{1,0:T(8,128)} %get-tuple-element.53), channel_id=1, source_target_pairs={{0,5},{1,4},{2,7},{3,6},{4,1},{5,0},{6,3},{7,2},{8,13},{9,12},{10,... | collective-permute-start | bytes 663560 | tf_op jit(solution)/shard_map/ppermute | solution.py:446
  70.6 35.7 %collective-permute-start.5 = (f32[432,128]{1,0:T(8,128)}, f32[432,128]{1,0:T(8,128)S(1)}, u32[]{:S(2)}, u32[]{:S(2)}) collective-permute-start(f32[432,128]{1,0:T(8,128)} %get-tuple-element.54), channel_id=1, source_target_pairs={{0,13},{1,12},{2,15},{3,14},{4,9},{5,8},{6,11},{7,10},{8,5},{9,4},... | collective-permute-start | bytes 663560 | tf_op jit(solution)/shard_map/ppermute | solution.py:446
  79.1 29.4 %collective-permute-start.6 = (f32[432,128]{1,0:T(8,128)}, f32[432,128]{1,0:T(8,128)S(1)}, u32[]{:S(2)}, u32[]{:S(2)}) collective-permute-start(f32[432,128]{1,0:T(8,128)} %get-tuple-element.55), channel_id=1, source_target_pairs={{0,6},{1,7},{2,4},{3,5},{4,2},{5,3},{6,0},{7,1},{8,14},{9,15},{10,... | collective-permute-start | bytes 663560 | tf_op jit(solution)/shard_map/ppermute | solution.py:446
  85.2 23.3 %collective-permute-start.7 = (f32[432,128]{1,0:T(8,128)}, f32[432,128]{1,0:T(8,128)S(1)}, u32[]{:S(2)}, u32[]{:S(2)}) collective-permute-start(f32[432,128]{1,0:T(8,128)} %get-tuple-element.56), channel_id=1, source_target_pairs={{0,14},{1,15},{2,12},{3,13},{4,10},{5,11},{6,8},{7,9},{8,6},{9,7},... | collective-permute-start | bytes 663560 | tf_op jit(solution)/shard_map/ppermute | solution.py:446
  90.3 22.8 %collective-permute-start.8 = (f32[432,128]{1,0:T(8,128)}, f32[432,128]{1,0:T(8,128)}, u32[]{:S(2)}, u32[]{:S(2)}) collective-permute-start(f32[432,128]{1,0:T(8,128)} %get-tuple-element.57), channel_id=1, source_target_pairs={{0,7},{1,6},{2,5},{3,4},{4,3},{5,2},{6,1},{7,0},{8,15},{9,14},{10,... | collective-permute-start | bytes 663560 | tf_op jit(solution)/shard_map/ppermute | solution.py:446
  106.2 26.9 %collective-permute-start.16 = (f32[432,128]{1,0:T(8,128)}, f32[432,128]{1,0:T(8,128)S(1)}, u32[]{:S(2)}, u32[]{:S(2)}) collective-permute-start(f32[432,128]{1,0:T(8,128)} %get-tuple-element.66), channel_id=1, source_target_pairs={{0,8},{1,9},{2,10},{3,11},{4,12},{5,13},{6,14},{7,15},{8,0},{9,1},... | collective-permute-start | bytes 663560 | tf_op jit(solution)/shard_map/ppermute | solution.py:446
  108.5 25.0 %collective-permute-start.17 = (f32[432,128]{1,0:T(8,128)}, f32[432,128]{1,0:T(8,128)S(1)}, u32[]{:S(2)}, u32[]{:S(2)}) collective-permute-start(f32[432,128]{1,0:T(8,128)} %get-tuple-element.67), channel_id=1, source_target_pairs={{0,1},{1,0},{2,3},{3,2},{4,5},{5,4},{6,7},{7,6},{8,9},{9,8},{10,11... | collective-permute-start | bytes 663560 | tf_op jit(solution)/shard_map/ppermute | solution.py:446
  109.3 33.1 %collective-permute-start.18 = (f32[432,128]{1,0:T(8,128)}, f32[432,128]{1,0:T(8,128)S(1)}, u32[]{:S(2)}, u32[]{:S(2)}) collective-permute-start(f32[432,128]{1,0:T(8,128)} %get-tuple-element.68), channel_id=1, source_target_pairs={{0,9},{1,8},{2,11},{3,10},{4,13},{5,12},{6,15},{7,14},{8,1},{9,0},... | collective-permute-start | bytes 663560 | tf_op jit(solution)/shard_map/ppermute | solution.py:446
  113.1 78.2 %collective-permute-start.15 = (f32[1728,128]{1,0:T(8,128)}, f32[1728,128]{1,0:T(8,128)S(1)}, u32[]{:S(2)}, u32[]{:S(2)}) collective-permute-start(f32[1728,128]{1,0:T(8,128)} %shard_map.98.own_ref), channel_id=1, source_target_pairs={{0,16},{16,0},{1,17},{17,1},{2,18},{18,2},{3,19},{19,3},{4,20},{20... | collective-permute-start | bytes 2654216 | tf_op jit(solution)/shard_map/ppermute | solution.py:508
  115.1 27.3 %collective-permute-start.19 = (f32[432,128]{1,0:T(8,128)}, f32[432,128]{1,0:T(8,128)S(1)}, u32[]{:S(2)}, u32[]{:S(2)}) collective-permute-start(f32[432,128]{1,0:T(8,128)} %get-tuple-element.69), channel_id=1, source_target_pairs={{0,2},{1,3},{2,0},{3,1},{4,6},{5,7},{6,4},{7,5},{8,10},{9,11},{10,... | collective-permute-start | bytes 663560 | tf_op jit(solution)/shard_map/ppermute | solution.py:446
  133.2 19.7 %collective-permute-start.20 = (f32[432,128]{1,0:T(8,128)}, f32[432,128]{1,0:T(8,128)S(1)}, u32[]{:S(2)}, u32[]{:S(2)}) collective-permute-start(f32[432,128]{1,0:T(8,128)} %get-tuple-element.70), channel_id=1, source_target_pairs={{0,10},{1,11},{2,8},{3,9},{4,14},{5,15},{6,12},{7,13},{8,2},{9,3},... | collective-permute-start | bytes 663560 | tf_op jit(solution)/shard_map/ppermute | solution.py:446
  133.5 19.4 %collective-permute-start.21 = (f32[432,128]{1,0:T(8,128)}, f32[432,128]{1,0:T(8,128)S(1)}, u32[]{:S(2)}, u32[]{:S(2)}) collective-permute-start(f32[432,128]{1,0:T(8,128)} %get-tuple-element.71), channel_id=1, source_target_pairs={{0,3},{1,2},{2,1},{3,0},{4,7},{5,6},{6,5},{7,4},{8,11},{9,10},{10,... | collective-permute-start | bytes 663560 | tf_op jit(solution)/shard_map/ppermute | solution.py:446
  142.4 18.3 %collective-permute-start.23 = (f32[432,128]{1,0:T(8,128)}, f32[432,128]{1,0:T(8,128)S(1)}, u32[]{:S(2)}, u32[]{:S(2)}) collective-permute-start(f32[432,128]{1,0:T(8,128)} %get-tuple-element.73), channel_id=1, source_target_pairs={{0,4},{1,5},{2,6},{3,7},{4,0},{5,1},{6,2},{7,3},{8,12},{9,13},{10,... | collective-permute-start | bytes 663560 | tf_op jit(solution)/shard_map/ppermute | solution.py:446
  152.9 18.6 %collective-permute-start.25 = (f32[432,128]{1,0:T(8,128)}, f32[432,128]{1,0:T(8,128)}, u32[]{:S(2)}, u32[]{:S(2)}) collective-permute-start(f32[432,128]{1,0:T(8,128)} %get-tuple-element.75), channel_id=1, source_target_pairs={{0,5},{1,4},{2,7},{3,6},{4,1},{5,0},{6,3},{7,2},{8,13},{9,12},{10,... | collective-permute-start | bytes 663560 | tf_op jit(solution)/shard_map/ppermute | solution.py:446
  160.7 21.3 %collective-permute-start.27 = (f32[432,128]{1,0:T(8,128)}, f32[432,128]{1,0:T(8,128)}, u32[]{:S(2)}, u32[]{:S(2)}) collective-permute-start(f32[432,128]{1,0:T(8,128)} %get-tuple-element.77), channel_id=1, source_target_pairs={{0,6},{1,7},{2,4},{3,5},{4,2},{5,3},{6,0},{7,1},{8,14},{9,15},{10,... | collective-permute-start | bytes 663560 | tf_op jit(solution)/shard_map/ppermute | solution.py:446
  163.4 19.2 %collective-permute-start.28 = (f32[432,128]{1,0:T(8,128)}, f32[432,128]{1,0:T(8,128)}, u32[]{:S(2)}, u32[]{:S(2)}) collective-permute-start(f32[432,128]{1,0:T(8,128)} %get-tuple-element.78), channel_id=1, source_target_pairs={{0,14},{1,15},{2,12},{3,13},{4,10},{5,11},{6,8},{7,9},{8,6},{9,7},... | collective-permute-start | bytes 663560 | tf_op jit(solution)/shard_map/ppermute | solution.py:446
  171.5 19.8 %collective-permute-start.30 = (f32[432,128]{1,0:T(8,128)}, f32[432,128]{1,0:T(8,128)}, u32[]{:S(2)}, u32[]{:S(2)}) collective-permute-start(f32[432,128]{1,0:T(8,128)} %get-tuple-element.80), channel_id=1, source_target_pairs={{0,15},{1,14},{2,13},{3,12},{4,11},{5,10},{6,9},{7,8},{8,7},{9,6},... | collective-permute-start | bytes 663560 | tf_op jit(solution)/shard_map/ppermute | solution.py:446
  201.5 75.1 %all-to-all-start.1 = ((f32[16,432,128]{2,1,0:T(8,128)}), f32[16,432,128]{2,1,0:T(8,128)S(1)}, u32[]{:S(2)}, u32[]{:S(2)}) async-start(f32[16,432,128]{2,1,0:T(8,128)} %bitcast.21), calls=%async_computation.1 | async-start | bytes 7077888 | tf_op jit(solution)/shard_map/all_to_all | solution.py:454
  289.4 61.1 %all-to-all-start.2 = ((f32[32,112,128]{2,1,0:T(8,128)}), f32[32,112,128]{2,1,0:T(8,128)S(1)}, u32[]{:S(2)}, u32[]{:S(2)}) async-start(f32[32,112,128]{2,1,0:T(8,128)} %bitcast.27), calls=%async_computation.2 | async-start | bytes 3670016 | tf_op jit(solution)/shard_map/all_to_all | solution.py:458
  306.4 47.3 %collective-permute-start.33 = (f32[1728,128]{1,0:T(8,128)S(1)}, f32[1728,128]{1,0:T(8,128)}, u32[]{:S(2)}, u32[]{:S(2)}) collective-permute-start(f32[1728,128]{1,0:T(8,128)S(1)} %copy-done.3), channel_id=1, source_target_pairs={{0,16},{16,0},{1,17},{17,1},{2,18},{18,2},{3,19},{19,3},{4,20},{20... | collective-permute-start | bytes 2654216 | tf_op jit(solution)/shard_map/ppermute | solution.py:560
  308.9 58.0 %collective-permute-start.31 = (f32[1728,128]{1,0:T(8,128)}, f32[1728,128]{1,0:T(8,128)}, u32[]{:S(2)}, u32[]{:S(2)}) collective-permute-start(f32[1728,128]{1,0:T(8,128)} %get-tuple-element.85.lower_ref), channel_id=1, source_target_pairs={{0,16},{16,0},{1,17},{17,1},{2,18},{18,2},{3,19},{19,3},{4,20},{20... | collective-permute-start | bytes 2654216 | tf_op jit(solution)/shard_map/ppermute | solution.py:561
  353.7 16.8 %all-to-all-start.4 = ((f32[16,56,128]{2,1,0:T(8,128)}), f32[16,56,128]{2,1,0:T(8,128)S(1)}, u32[]{:S(2)}, u32[]{:S(2)}) async-start(f32[16,56,128]{2,1,0:T(8,128)} %bitcast.10), calls=%async_computation.4 | async-start | bytes 917504 | tf_op jit(solution)/shard_map/all_to_all | solution.py:454
  370.5 17.1 %all-to-all-start.3 = ((f32[16,56,128]{2,1,0:T(8,128)}), f32[16,56,128]{2,1,0:T(8,128)S(1)}, u32[]{:S(2)}, u32[]{:S(2)}) async-start(f32[16,56,128]{2,1,0:T(8,128)} %bitcast.8), calls=%async_computation.3 | async-start | bytes 917504 | tf_op jit(solution)/shard_map/all_to_all | solution.py:454
  (39 other events, 1012.2 us)

commit v11 on v8

--- a/solution.py
+++ b/solution.py
@@ -232,45 +232,47 @@
 
 def along_kernel(sizes, steps, turns, place_ref, *refs):
     planes, grid, rows, share = sizes
-    *moved_refs, kin_ref, out_ref, lines = refs
-    length = planes * grid
-    kin = split(kin_ref[...])
-    for inner in range(rows // steps):
-        row = pl.program_id(0) * (rows // steps) + inner
-        slot = lines.at[inner]
-        for turn, moved_ref in zip(turns, moved_refs):
-            first = (place_ref[0] % grid ^ turn) * planes
-            for part in range(2):
-                slot[part, pl.ds(first, planes), :] = moved_ref[pl.ds(part * rows + row, planes, stride=2 * rows), :]
-        field = jnp.concatenate([slot[0], slot[1]], axis=1)
-        out_ref[inner * length : (inner + 1) * length, :] = product_of_parts(kin, split(field))
-
-
-def update_kernel(sizes, steps, turns, place_ref, along_ref, own_ref, other_ref, kin_ref, *refs):
-    planes, grid, rows, share = sizes
-    *mixed_refs, out_ref, lines = refs
+    moved_refs, (own_ref, other_ref, kin_ref, out_ref, lines) = refs[:grid], refs[grid:]
     length = planes * grid
     kin = split(kin_ref[...])
     step = pl.program_id(0)
     mine_here = place_ref[0] // grid == step // (steps // 2)
     for inner in range(rows // steps):
         row = step * (rows // steps) + inner
+        slot = lines.at[inner]
+        for turn, moved_ref in zip(turns, moved_refs):
+            first = (place_ref[0] % grid ^ turn) * planes
+            for part in range(2):
+                slot[part, pl.ds(first, planes), :] = moved_ref[pl.ds(part * rows + row, planes, stride=2 * rows), :]
+        along = product_of_parts(kin, split(jnp.concatenate([slot[0], slot[1]], axis=1)))
+        again = product_of_parts(kin, split(along))
         here = slice(inner * length, (inner + 1) * length)
+        potential = jnp.where(mine_here, own_ref[here, :], other_ref[here, :])
+        for part in range(2):
+            lanes = slice(part * LANES, (part + 1) * LANES)
+            turned = along[:, LANES:] if part == 0 else -along[:, :LANES]
+            twice = again[:, lanes] + potential * along[:, lanes]
+            out_ref[here, lanes] = 2.0 * BESSEL_ONE * turned - 4.0 * BESSEL_TWO * twice
+
+
+def update_kernel(sizes, steps, turns, place_ref, along_ref, kin_ref, *refs):
+    planes, grid, rows, share = sizes
+    *mixed_refs, out_ref, lines = refs
+    length = planes * grid
+    kin = split(-4.0 * BESSEL_TWO * kin_ref[...])
+    step = pl.program_id(0)
+    for inner in range(rows // steps):
+        row = step * (rows // steps) + inner
         slot = lines.at[inner]
         for turn, mixed_ref in zip(turns, mixed_refs):
             first = (place_ref[0] % grid ^ turn) * planes
             for part in range(2):
                 slot[part, pl.ds(first, planes), :] = mixed_ref[pl.ds(part * rows + row, planes, stride=2 * rows), :]
-        along = along_ref[here, :]
-        again = product_of_parts(kin, split(jnp.concatenate([slot[0], slot[1]], axis=1) + along))
-        potential = jnp.where(mine_here, own_ref[here, :], other_ref[here, :])
+        mixed = product_of_parts(kin, split(jnp.concatenate([slot[0], slot[1]], axis=1)))
+        update = along_ref[inner * length : (inner + 1) * length, :] + mixed
         for part in range(2):
-            mine = along[:, part * LANES : (part + 1) * LANES]
-            turned = along[:, LANES:] if part == 0 else -along[:, :LANES]
-            twice = again[:, part * LANES : (part + 1) * LANES] + potential * mine
-            out_ref[pl.ds(part * rows + row, length, stride=2 * rows), :] = (
-                2.0 * BESSEL_ONE * turned - 4.0 * BESSEL_TWO * twice
-            )
+            where = pl.ds(part * rows + row, length, stride=2 * rows)
+            out_ref[where, :] = update[:, part * LANES : (part + 1) * LANES]
 
 
 def fresh_kernel(
@@ -456,18 +458,6 @@
     spec_rows = 2 * grid * chunk_rows(sizes)
     mixed_rows = 2 * planes * rows
     steps = 6 if rows % 6 == 0 and share % (rows // 6) == 0 else 2
-    shared = pl.pallas_call(
-        functools.partial(potential_kernel, sizes, bunch),
-        grid=(planes // bunch,),
-        in_specs=[smem, plane_spec, plane_spec],
-        out_specs=whole(spec_rows // 2, LANES),
-        out_shape=shape(spec_rows // 2, LANES),
-        scratch_shapes=scratch(1),
-        compiler_params=PARAMS,
-        cost_estimate=cost(0, 6 << 20),
-    )(place, ion_potential, hxc_potential)
-    place, shared = lax.optimization_barrier((place, shared))
-    shared = swap(shared)
     moved = pl.pallas_call(
         functools.partial(pack_kernel, sizes, bunch, turns),
         grid=(planes // bunch,),
@@ -480,6 +470,17 @@
     )(place, orbitals)
     moved = [send(turn, piece) for turn, piece in zip(turns[:6], moved[:6])] + list(moved[6:])
     behind = lax.optimization_barrier((place, line[1]))[0]
+    shared = pl.pallas_call(
+        functools.partial(potential_kernel, sizes, bunch),
+        grid=(planes // bunch,),
+        in_specs=[smem, plane_spec, plane_spec],
+        out_specs=whole(spec_rows // 2, LANES),
+        out_shape=shape(spec_rows // 2, LANES),
+        scratch_shapes=scratch(1),
+        compiler_params=PARAMS,
+        cost_estimate=cost(0, 6 << 20),
+    )(behind, ion_potential, hxc_potential)
+    shared = swap(shared)
     *mixed, base = pl.pallas_call(
         functools.partial(plane_kernel, sizes, bunch, turns),
         grid=(planes // bunch,),
@@ -501,26 +502,24 @@
         cost_estimate=cost(0, 2 << 20),
     )(shared)
     other = lax.ppermute(own, "band", [(0, 1), (1, 0)])
+    half_spec = pl.BlockSpec((rows // steps * length, LANES), lambda i: (i % (steps // 2), 0))
     along = pl.pallas_call(
         functools.partial(along_kernel, sizes, steps, turns),
         grid=(steps,),
-        in_specs=[smem] + [whole(mixed_rows, LANES)] * grid + [square],
+        in_specs=[smem] + [whole(mixed_rows, LANES)] * grid + [half_spec, half_spec, square],
         out_specs=pl.BlockSpec((rows // steps * length, 2 * LANES), lambda i: (i, 0)),
         out_shape=shape(rows * length, 2 * LANES),
         scratch_shapes=[pltpu.VMEM((rows // steps, 2, length, LANES), jnp.float32)],
         compiler_params=PARAMS,
-        cost_estimate=cost(2 * 3 * work, 8 << 20),
-    )(place, *moved, kin)
+        cost_estimate=cost(4 * 3 * work, 10 << 20),
+    )(place, *moved, own, other, kin)
     mixed = [send(turn, piece) for turn, piece in zip(turns, mixed)]
-    half_spec = pl.BlockSpec((rows // steps * length, LANES), lambda i: (i % (steps // 2), 0))
     update = pl.pallas_call(
         functools.partial(update_kernel, sizes, steps, turns),
         grid=(steps,),
         in_specs=[
             smem,
             pl.BlockSpec((rows // steps * length, 2 * LANES), lambda i: (i, 0)),
-            half_spec,
-            half_spec,
             square,
         ]
         + [whole(mixed_rows, LANES)] * grid,
@@ -529,7 +528,7 @@
         scratch_shapes=[pltpu.VMEM((rows // steps, 2, length, LANES), jnp.float32)],
         compiler_params=PARAMS,
         cost_estimate=cost(2 * 3 * work, 14 << 20),
-    )(place, along, own, other, kin, *mixed)
+    )(place, along, kin, *mixed)
     update = swap(update)
 
     fresh, upper, lower, spectrum = pl.pallas_call(

time: 401 us -> 411 us (1.025)
  waiting for transfers between devices: 215 us -> 226 us
    ppermute x30, waiting for transfers between devices: 76 us -> 87.5 us  [send(): lax.ppermute(piece, 'grid', [(spot, spot ^ turn) for spot in range(grid)])]
    all_to_all x4, starting transfers between devices: 24.9 us -> 19.7 us  [swap(): lax.all_to_all(flat, 'grid', split_axis=0, concat_axis=0)]
  transfers between devices with their start and end apart: 40 -> 40, of which waited for: 21 -> 21; matrix products, arithmetic and copies ran while one was open for 0% -> 0% of each run, Pallas kernels for 9% -> 8%
where the time goes in v11:
time: 411 us; the launch traced here: 410 us
  waiting for transfers between devices  226 us (55%)
  starting transfers between devices  109 us (27%)
  Pallas kernels  66 us (16%)
  local copies, waits for them, and re-layouts  6.53 us (2%)
    ppermute x30, waiting for transfers between devices, send(): lax.ppermute(piece, 'grid', [(spot, spot ^ turn) for spot in range(grid)])  87.5 us
    all_to_all x4, waiting for transfers between devices, swap(): lax.all_to_all(flat, 'grid', split_axis=0, concat_axis=0)  81.5 us
    ppermute x30, starting transfers between devices, send(): lax.ppermute(piece, 'grid', [(spot, spot ^ turn) for spot in range(grid)])  67 us
    all_to_all x1, waiting for transfers between devices, swap_all(): lax.all_to_all(flat, ('band', 'grid'), split_axis=0, concat_axis=0)  41.3 us
    all_to_all x4, starting transfers between devices, swap(): lax.all_to_all(flat, 'grid', split_axis=0, concat_axis=0)  19.7 us
    all_to_all x1, starting transfers between devices, swap_all(): lax.all_to_all(flat, ('band', 'grid'), split_axis=0, concat_axis=0)  17 us
    pallas_call x1, Pallas kernels, packed_path(): pl.pallas_call(functools.partial(plane_kernel, sizes, bunch, turns), grid...  13.9 us
    pallas_call x1, Pallas kernels, packed_path(): pl.pallas_call(functools.partial(fresh_kernel, sizes, bunch), grid=(plane...  10.9 us
  transfers between devices with their start and end apart: 40, of which 21 were waited for; matrix products, arithmetic and copies ran while one was open for 0% of the time, Pallas kernels for 8%

profile of v11, /device:TPU:0, one launch (start us, length us, event | category | flops | bytes accessed | tf_op | source)
XLA Modules:
  0.0 410.0 jit_solution(14257577609543693641)
XLA Ops:
  0.6 5.4 %shard_map.86 = (f32[432,128]{1,0:T(8,128)}, f32[432,128]{1,0:T(8,128)}, f32[432,128]{1,0:T(8,128)}, f32[432,128]{1,0:T(8,128)}, f32[432,128]{1,0:T(8,128)}, /*i...) custom-call(s32[1]{0:T(128)} %bitcast.place_ref, ...), custom_call_target="tpu_custom_call" | custom-call | bytes 8388608 | tf_op jit(solution)/shard_map/pallas_call | solution.py:461
  7.9 4.2 %shard_map.88 = f32[1792,128]{1,0:T(8,128)} custom-call(s32[1]{0:T(128)} %bitcast.place_ref, f32[12,192,192]{2,1,0:T(8,128)} %ion_ref.3, f32[12,192,192]{2,1,0:T(8,128)} %hxc_ref.3), custom_call_target="tpu_custom_call" | custom-call | bytes 6291456 | tf_op jit(solution)/shard_map/pallas_call | solution.py:473
  12.1 7.3 %all-to-all-start = ((f32[16,112,128]{2,1,0:T(8,128)}), f32[16,112,128]{2,1,0:T(8,128)S(1)}, u32[]{:S(2)}, u32[]{:S(2)}) async-start(f32[16,112,128]{2,1,0:T(8,128)} %bitcast.22), calls=%async_computation | async-start | bytes 1835008 | tf_op jit(solution)/shard_map/all_to_all | solution.py:451
  19.4 3.8 collective-permute-start.4
  25.9 13.9 %shard_map.87 = (f32[432,128]{1,0:T(8,128)}, f32[432,128]{1,0:T(8,128)}, f32[432,128]{1,0:T(8,128)}, f32[432,128]{1,0:T(8,128)}, f32[432,128]{1,0:T(8,128)}, /*i...) custom-call(s32[1]{0:T(128)} %bitcast.place_ref, ...), custom_call_target="tpu_custom_call" | custom-call | flops 4076863488 | bytes 20971520 | tf_op jit(solution)/shard_map/pallas_call | solution.py:484
  39.8 23.6 %collective-permute-done.4.refs_5_ = f32[432,128]{1,0:T(8,128)S(1)} collective-permute-done((f32[432,128]{1,0:T(8,128)S(1)}, f32[432,128]{1,0:T(8,128)S(1)}, u32[]{:S(2)}, u32[]{:S(2)}) %collective-permute-start.4) | collective-permute-done | bytes 221216 | tf_op jit(solution)/shard_map/ppermute | solution.py:446
  69.5 7.4 %collective-permute-done.refs_1_ = f32[432,128]{1,0:T(8,128)S(1)} collective-permute-done((f32[432,128]{1,0:T(8,128)S(1)}, f32[432,128]{1,0:T(8,128)S(1)}, u32[]{:S(2)}, u32[]{:S(2)}) %collective-permute-start) | collective-permute-done | bytes 221216 | tf_op jit(solution)/shard_map/ppermute | solution.py:446
  77.1 4.0 collective-permute-done.9.refs_10_
  91.6 4.1 %collective-permute-done.6.refs_7_ = f32[432,128]{1,0:T(8,128)S(1)} collective-permute-done((f32[432,128]{1,0:T(8,128)}, f32[432,128]{1,0:T(8,128)S(1)}, u32[]{:S(2)}, u32[]{:S(2)}) %collective-permute-start.6) | collective-permute-done | bytes 221216 | tf_op jit(solution)/shard_map/ppermute | solution.py:446
  97.3 6.4 %collective-permute-start.10 = (f32[432,128]{1,0:T(8,128)}, f32[432,128]{1,0:T(8,128)S(1)}, u32[]{:S(2)}, u32[]{:S(2)}) collective-permute-start(f32[432,128]{1,0:T(8,128)} %get-tuple-element.90), channel_id=1, source_target_pairs={{0,13},{1,12},{2,15},{3,14},{4,9},{5,8},{6,11},{7,10},{8,5},{9,4},... | collective-permute-start | bytes 663560 | tf_op jit(solution)/shard_map/ppermute | solution.py:446
  105.6 5.3 %collective-permute-start.20 = (f32[432,128]{1,0:T(8,128)}, f32[432,128]{1,0:T(8,128)S(1)}, u32[]{:S(2)}, u32[]{:S(2)}) collective-permute-start(f32[432,128]{1,0:T(8,128)} %get-tuple-element.109), channel_id=1, source_target_pairs={{0,10},{1,11},{2,8},{3,9},{4,14},{5,15},{6,12},{7,13},{8,2},{9,3},... | collective-permute-start | bytes 663560 | tf_op jit(solution)/shard_map/ppermute | solution.py:446
  112.7 11.0 %collective-permute-start.18 = (f32[432,128]{1,0:T(8,128)}, f32[432,128]{1,0:T(8,128)S(1)}, u32[]{:S(2)}, u32[]{:S(2)}) collective-permute-start(f32[432,128]{1,0:T(8,128)} %get-tuple-element.105), channel_id=1, source_target_pairs={{0,9},{1,8},{2,11},{3,10},{4,13},{5,12},{6,15},{7,14},{8,1},{9,0},... | collective-permute-start | bytes 663560 | tf_op jit(solution)/shard_map/ppermute | solution.py:446
  125.0 12.9 %collective-permute-done.20.refs_5_ = f32[432,128]{1,0:T(8,128)S(1)} collective-permute-done((f32[432,128]{1,0:T(8,128)}, f32[432,128]{1,0:T(8,128)S(1)}, u32[]{:S(2)}, u32[]{:S(2)}) %collective-permute-start.20) | collective-permute-done | bytes 221216 | tf_op jit(solution)/shard_map/ppermute | solution.py:446
  144.3 10.5 %collective-permute-done.16.refs_1_ = f32[432,128]{1,0:T(8,128)S(1)} collective-permute-done((f32[432,128]{1,0:T(8,128)}, f32[432,128]{1,0:T(8,128)S(1)}, u32[]{:S(2)}, u32[]{:S(2)}) %collective-permute-start.16) | collective-permute-done | bytes 221216 | tf_op jit(solution)/shard_map/ppermute | solution.py:446
  160.4 10.6 %collective-permute-start.29 = (f32[432,128]{1,0:T(8,128)}, f32[432,128]{1,0:T(8,128)S(1)}, u32[]{:S(2)}, u32[]{:S(2)}) collective-permute-start(f32[432,128]{1,0:T(8,128)} %get-tuple-element.127), channel_id=1, source_target_pairs={{0,7},{1,6},{2,5},{3,4},{4,3},{5,2},{6,1},{7,0},{8,15},{9,14},{10,... | collective-permute-start | bytes 663560 | tf_op jit(solution)/shard_map/ppermute | solution.py:446
  171.0 4.0 collective-permute-done.22.refs_7_
  178.8 9.4 %shard_map.90.along_ref = f32[3456,256]{1,0:T(8,128)} custom-call(s32[1]{0:T(128)} %bitcast.place_ref, f32[432,128]{1,0:T(8,128)} %get-tuple-element.71.refs_0_, f32[432,128]{1,0:T(8,128)} %copy-done.13, f32[432,128]{1,0:T(8,128)} %copy-done.9, f32[432,128]{1,0:T(8,128)} %copy-done.12, f32[432,128]{1,0:T(8,128)} %copy-done.11, f32[432,128]{1,0:T(8,128)} %copy-done.10, ...), custom_call_target="tpu_custom_call" | custom-call | flops 2038431744 | bytes 10485760 | tf_op jit(solution)/shard_map/pallas_call | solution.py:506
  188.2 4.3 %collective-permute-done.27.refs_12_ = f32[432,128]{1,0:T(8,128)S(1)} collective-permute-done((f32[432,128]{1,0:T(8,128)}, f32[432,128]{1,0:T(8,128)S(1)}, u32[]{:S(2)}, u32[]{:S(2)}) %collective-permute-start.27) | collective-permute-done | bytes 221216 | tf_op jit(solution)/shard_map/ppermute | solution.py:446
  192.5 8.6 %collective-permute-done.26.refs_11_ = f32[432,128]{1,0:T(8,128)S(1)} collective-permute-done((f32[432,128]{1,0:T(8,128)}, f32[432,128]{1,0:T(8,128)S(1)}, u32[]{:S(2)}, u32[]{:S(2)}) %collective-permute-start.26) | collective-permute-done | bytes 221216 | tf_op jit(solution)/shard_map/ppermute | solution.py:446
  201.8 8.2 %shard_map.91 = f32[6912,128]{1,0:T(8,128)} custom-call(s32[1]{0:T(128)} %bitcast.place_ref, f32[3456,256]{1,0:T(8,128)} %shard_map.90.along_ref, f32[192,192]{1,0:T(8,128)} %constant.23.clone.kin_ref.refs_18_, f32[432,128]{1,0:T(8,128)} %get-tuple-element.99.refs_0_, f32[432,128]{1,0:T(8,128)} %copy-done.27, f32[432,128]{1,0:T(8,128)} %copy-done.26, ...), custom_call_target="tpu_custom_call" | custom-call | flops 1019215872 | bytes 14680064 | tf_op jit(solution)/shard_map/pallas_call | solution.py:517
  210.0 5.1 %all-to-all-start.1 = ((f32[16,432,128]{2,1,0:T(8,128)}), f32[16,432,128]{2,1,0:T(8,128)S(1)}, u32[]{:S(2)}, u32[]{:S(2)}) async-start(f32[16,432,128]{2,1,0:T(8,128)} %bitcast.20), calls=%async_computation.1 | async-start | bytes 7077888 | tf_op jit(solution)/shard_map/all_to_all | solution.py:451
  215.7 65.6 %all-to-all-done.1 = f32[16,432,128]{2,1,0:T(8,128)S(1)} async-done(((f32[16,432,128]{2,1,0:T(8,128)}), f32[16,432,128]{2,1,0:T(8,128)S(1)}, u32[]{:S(2)}, u32[]{:S(2)}) %all-to-all-start.1) | async-done | bytes 3538976 | tf_op jit(solution)/shard_map/all_to_all | solution.py:451
  283.2 10.9 %shard_map.92 = (f32[1,2,12,192,192]{4,3,2,1,0:T(8,128)}, f32[1728,128]{1,0:T(8,128)}, f32[1728,128]{1,0:T(8,128)}, f32[3584,128]{1,0:T(8,128)}) custom-call(f32[1]{0:T(128)S(6)} %copy.14.occ_ref, f32[6912,128]{1,0:T(8,128)} %bitcast.19, f32[2,12,192,192]{3,2,1,0:T(8,128)} %get-tuple-element.79.base_ref, f32[2,192,192]{2,1,0:T(8,128)} %constant.24.clone.tables_ref), custom_call_target="tpu_custom_call" | custom-call | flops 2038431744 | bytes 16777216 | tf_op jit(solution)/shard_map/pallas_call | solution.py:534
  294.2 17.0 %all-to-all-start.2 = ((f32[32,112,128]{2,1,0:T(8,128)}), f32[32,112,128]{2,1,0:T(8,128)S(1)}, u32[]{:S(2)}, u32[]{:S(2)}) async-start(f32[32,112,128]{2,1,0:T(8,128)} %bitcast.25), calls=%async_computation.2 | async-start | bytes 3670016 | tf_op jit(solution)/shard_map/all_to_all | solution.py:455
  314.1 41.3 %all-to-all-done.2 = f32[32,112,128]{2,1,0:T(8,128)S(1)} async-done(((f32[32,112,128]{2,1,0:T(8,128)}), f32[32,112,128]{2,1,0:T(8,128)S(1)}, u32[]{:S(2)}, u32[]{:S(2)}) %all-to-all-start.2) | async-done | bytes 1835040 | tf_op jit(solution)/shard_map/all_to_all | solution.py:455
  362.1 9.6 %collective-permute-done.31.lower_other = f32[1728,128]{1,0:T(8,128)} collective-permute-done((f32[1728,128]{1,0:T(8,128)}, f32[1728,128]{1,0:T(8,128)}, u32[]{:S(2)}, u32[]{:S(2)}) %collective-permute-start.31) | collective-permute-done | bytes 884768 | tf_op jit(solution)/shard_map/ppermute | solution.py:555
  371.7 3.6 all-to-all-done.4
  375.3 3.8 all-to-all-start.3
  380.1 12.3 %all-to-all-done.3 = f32[16,56,128]{2,1,0:T(8,128)S(1)} async-done(((f32[16,56,128]{2,1,0:T(8,128)}), f32[16,56,128]{2,1,0:T(8,128)S(1)}, u32[]{:S(2)}, u32[]{:S(2)}) %all-to-all-start.3) | async-done | bytes 458784 | tf_op jit(solution)/shard_map/all_to_all | solution.py:451
  394.0 4.3 %shard_map.94.refs_0_ = f32[12,192,192]{2,1,0:T(8,128)} custom-call(s32[1]{0:T(128)} %bitcast.place_ref, f32[896,128]{1,0:T(8,128)} %bitcast.24, f32[896,128]{1,0:T(8,128)} %copy-done.7, f32[1728,128]{1,0:T(8,128)} %get-tuple-element.135.upper_ref, f32[1728,128]{1,0:T(8,128)} %get-tuple-element.133.lower_ref, ...), custom_call_target="tpu_custom_call" | custom-call | flops 509607936 | bytes 4194304 | tf_op jit(solution)/shard_map/pallas_call | solution.py:577
  398.3 6.6 %collective-permute-done.32.far_ref = f32[896,128]{1,0:T(8,128)S(1)} collective-permute-done((f32[896,128]{1,0:T(8,128)S(1)}, f32[896,128]{1,0:T(8,128)S(1)}, u32[]{:S(2)}, u32[]{:S(2)}) %collective-permute-start.32) | collective-permute-done | bytes 458784 | tf_op jit(solution)/shard_map/ppermute | solution.py:597
  405.7 4.3 %shard_map.95 = f32[12,192,192]{2,1,0:T(8,128)} custom-call(s32[1]{0:T(128)} %bitcast.place_ref, f32[896,128]{1,0:T(8,128)} %bitcast.27, f32[896,128]{1,0:T(8,128)} %copy-done.8, f32[1728,128]{1,0:T(8,128)} %get-tuple-element.135.upper_ref, f32[1728,128]{1,0:T(8,128)} %get-tuple-element.133.lower_ref, ...), custom_call_target="tpu_custom_call", output_to_operand_aliasing={{}: (8, {})} | custom-call | flops 509607936 | bytes 4194304 | tf_op jit(solution)/shard_map/pallas_call | solution.py:577
  (150 shorter events, 58.9 us)
Async XLA Ops:
  12.1 76.4 %all-to-all-start = ((f32[16,112,128]{2,1,0:T(8,128)}), f32[16,112,128]{2,1,0:T(8,128)S(1)}, u32[]{:S(2)}, u32[]{:S(2)}) async-start(f32[16,112,128]{2,1,0:T(8,128)} %bitcast.22), calls=%async_computation | async-start | bytes 1835008 | tf_op jit(solution)/shard_map/all_to_all | solution.py:451
  19.4 44.1 %collective-permute-start.4 = (f32[432,128]{1,0:T(8,128)S(1)}, f32[432,128]{1,0:T(8,128)S(1)}, u32[]{:S(2)}, u32[]{:S(2)}) collective-permute-start(f32[432,128]{1,0:T(8,128)S(1)} %copy-done.44), channel_id=1, source_target_pairs={{0,10},{1,11},{2,8},{3,9},{4,14},{5,15},{6,12},{7,13},{8,2},{9,3},... | collective-permute-start | bytes 663560 | tf_op jit(solution)/shard_map/ppermute | solution.py:446
  23.2 40.3 %collective-permute-start.3 = (f32[432,128]{1,0:T(8,128)S(1)}, f32[432,128]{1,0:T(8,128)S(1)}, u32[]{:S(2)}, u32[]{:S(2)}) collective-permute-start(f32[432,128]{1,0:T(8,128)S(1)} %copy-done.43), channel_id=1, source_target_pairs={{0,2},{1,3},{2,0},{3,1},{4,6},{5,7},{6,4},{7,5},{8,10},{9,11},{10,... | collective-permute-start | bytes 663560 | tf_op jit(solution)/shard_map/ppermute | solution.py:446
  23.8 42.6 %collective-permute-start.2 = (f32[432,128]{1,0:T(8,128)S(1)}, f32[432,128]{1,0:T(8,128)S(1)}, u32[]{:S(2)}, u32[]{:S(2)}) collective-permute-start(f32[432,128]{1,0:T(8,128)S(1)} %copy-done.42), channel_id=1, source_target_pairs={{0,9},{1,8},{2,11},{3,10},{4,13},{5,12},{6,15},{7,14},{8,1},{9,0},... | collective-permute-start | bytes 663560 | tf_op jit(solution)/shard_map/ppermute | solution.py:446
  23.8 53.0 %collective-permute-start = (f32[432,128]{1,0:T(8,128)S(1)}, f32[432,128]{1,0:T(8,128)S(1)}, u32[]{:S(2)}, u32[]{:S(2)}) collective-permute-start(f32[432,128]{1,0:T(8,128)S(1)} %copy-done.41), channel_id=1, source_target_pairs={{0,8},{1,9},{2,10},{3,11},{4,12},{5,13},{6,14},{7,15},{8,0},{9,1},... | collective-permute-start | bytes 663560 | tf_op jit(solution)/shard_map/ppermute | solution.py:446
  63.5 17.6 %collective-permute-start.9 = (f32[432,128]{1,0:T(8,128)S(1)}, f32[432,128]{1,0:T(8,128)S(1)}, u32[]{:S(2)}, u32[]{:S(2)}) collective-permute-start(f32[432,128]{1,0:T(8,128)S(1)} %copy-done.40), channel_id=1, source_target_pairs={{0,5},{1,4},{2,7},{3,6},{4,1},{5,0},{6,3},{7,2},{8,13},{9,12},{10,... | collective-permute-start | bytes 663560 | tf_op jit(solution)/shard_map/ppermute | solution.py:446
  63.5 19.6 %collective-permute-start.8 = (f32[432,128]{1,0:T(8,128)S(1)}, f32[432,128]{1,0:T(8,128)S(1)}, u32[]{:S(2)}, u32[]{:S(2)}) collective-permute-start(f32[432,128]{1,0:T(8,128)S(1)} %copy-done.39), channel_id=1, source_target_pairs={{0,12},{1,13},{2,14},{3,15},{4,8},{5,9},{6,10},{7,11},{8,4},{9,5},... | collective-permute-start | bytes 663560 | tf_op jit(solution)/shard_map/ppermute | solution.py:446
  66.4 20.1 %collective-permute-start.7 = (f32[432,128]{1,0:T(8,128)S(1)}, f32[432,128]{1,0:T(8,128)S(1)}, u32[]{:S(2)}, u32[]{:S(2)}) collective-permute-start(f32[432,128]{1,0:T(8,128)S(1)} %copy-done.38), channel_id=1, source_target_pairs={{0,4},{1,5},{2,6},{3,7},{4,0},{5,1},{6,2},{7,3},{8,12},{9,13},{10,... | collective-permute-start | bytes 663560 | tf_op jit(solution)/shard_map/ppermute | solution.py:446
  66.4 29.3 %collective-permute-start.6 = (f32[432,128]{1,0:T(8,128)}, f32[432,128]{1,0:T(8,128)S(1)}, u32[]{:S(2)}, u32[]{:S(2)}) collective-permute-start(f32[432,128]{1,0:T(8,128)} %get-tuple-element.82), channel_id=1, source_target_pairs={{0,11},{1,10},{2,9},{3,8},{4,15},{5,14},{6,13},{7,12},{8,3},{9,2},... | collective-permute-start | bytes 663560 | tf_op jit(solution)/shard_map/ppermute | solution.py:446
  76.8 20.4 %collective-permute-start.5 = (f32[432,128]{1,0:T(8,128)}, f32[432,128]{1,0:T(8,128)S(1)}, u32[]{:S(2)}, u32[]{:S(2)}) collective-permute-start(f32[432,128]{1,0:T(8,128)} %get-tuple-element.80), channel_id=1, source_target_pairs={{0,3},{1,2},{2,1},{3,0},{4,7},{5,6},{6,5},{7,4},{8,11},{9,10},{10,... | collective-permute-start | bytes 663560 | tf_op jit(solution)/shard_map/ppermute | solution.py:446
  83.1 22.5 %collective-permute-start.13 = (f32[432,128]{1,0:T(8,128)}, f32[432,128]{1,0:T(8,128)S(1)}, u32[]{:S(2)}, u32[]{:S(2)}) collective-permute-start(f32[432,128]{1,0:T(8,128)} %get-tuple-element.96), channel_id=1, source_target_pairs={{0,7},{1,6},{2,5},{3,4},{4,3},{5,2},{6,1},{7,0},{8,15},{9,14},{10,... | collective-permute-start | bytes 663560 | tf_op jit(solution)/shard_map/ppermute | solution.py:446
  86.5 24.4 %collective-permute-start.12 = (f32[432,128]{1,0:T(8,128)}, f32[432,128]{1,0:T(8,128)}, u32[]{:S(2)}, u32[]{:S(2)}) collective-permute-start(f32[432,128]{1,0:T(8,128)} %get-tuple-element.94), channel_id=1, source_target_pairs={{0,14},{1,15},{2,12},{3,13},{4,10},{5,11},{6,8},{7,9},{8,6},{9,7},... | collective-permute-start | bytes 663560 | tf_op jit(solution)/shard_map/ppermute | solution.py:446
  95.7 82.1 %collective-permute-start.15 = (f32[1728,128]{1,0:T(8,128)}, f32[1728,128]{1,0:T(8,128)S(1)}, u32[]{:S(2)}, u32[]{:S(2)}) collective-permute-start(f32[1728,128]{1,0:T(8,128)} %shard_map.89.refs_16_), channel_id=1, source_target_pairs={{0,16},{16,0},{1,17},{17,1},{2,18},{18,2},{3,19},{19,3},{4,20},{20... | collective-permute-start | bytes 2654216 | tf_op jit(solution)/shard_map/ppermute | solution.py:504
  97.3 26.4 %collective-permute-start.10 = (f32[432,128]{1,0:T(8,128)}, f32[432,128]{1,0:T(8,128)S(1)}, u32[]{:S(2)}, u32[]{:S(2)}) collective-permute-start(f32[432,128]{1,0:T(8,128)} %get-tuple-element.90), channel_id=1, source_target_pairs={{0,13},{1,12},{2,15},{3,14},{4,9},{5,8},{6,11},{7,10},{8,5},{9,4},... | collective-permute-start | bytes 663560 | tf_op jit(solution)/shard_map/ppermute | solution.py:446
  105.6 32.3 %collective-permute-start.20 = (f32[432,128]{1,0:T(8,128)}, f32[432,128]{1,0:T(8,128)S(1)}, u32[]{:S(2)}, u32[]{:S(2)}) collective-permute-start(f32[432,128]{1,0:T(8,128)} %get-tuple-element.109), channel_id=1, source_target_pairs={{0,10},{1,11},{2,8},{3,9},{4,14},{5,15},{6,12},{7,13},{8,2},{9,3},... | collective-permute-start | bytes 663560 | tf_op jit(solution)/shard_map/ppermute | solution.py:446
  110.9 27.0 %collective-permute-start.19 = (f32[432,128]{1,0:T(8,128)}, f32[432,128]{1,0:T(8,128)S(1)}, u32[]{:S(2)}, u32[]{:S(2)}) collective-permute-start(f32[432,128]{1,0:T(8,128)} %get-tuple-element.107), channel_id=1, source_target_pairs={{0,2},{1,3},{2,0},{3,1},{4,6},{5,7},{6,4},{7,5},{8,10},{9,11},{10,... | collective-permute-start | bytes 663560 | tf_op jit(solution)/shard_map/ppermute | solution.py:446
  112.7 27.3 %collective-permute-start.18 = (f32[432,128]{1,0:T(8,128)}, f32[432,128]{1,0:T(8,128)S(1)}, u32[]{:S(2)}, u32[]{:S(2)}) collective-permute-start(f32[432,128]{1,0:T(8,128)} %get-tuple-element.105), channel_id=1, source_target_pairs={{0,9},{1,8},{2,11},{3,10},{4,13},{5,12},{6,15},{7,14},{8,1},{9,0},... | collective-permute-start | bytes 663560 | tf_op jit(solution)/shard_map/ppermute | solution.py:446
  123.7 18.0 %collective-permute-start.17 = (f32[432,128]{1,0:T(8,128)}, f32[432,128]{1,0:T(8,128)S(1)}, u32[]{:S(2)}, u32[]{:S(2)}) collective-permute-start(f32[432,128]{1,0:T(8,128)} %get-tuple-element.103), channel_id=1, source_target_pairs={{0,1},{1,0},{2,3},{3,2},{4,5},{5,4},{6,7},{7,6},{8,9},{9,8},{10,11... | collective-permute-start | bytes 663560 | tf_op jit(solution)/shard_map/ppermute | solution.py:446
  138.0 16.9 %collective-permute-start.16 = (f32[432,128]{1,0:T(8,128)}, f32[432,128]{1,0:T(8,128)S(1)}, u32[]{:S(2)}, u32[]{:S(2)}) collective-permute-start(f32[432,128]{1,0:T(8,128)} %get-tuple-element.101), channel_id=1, source_target_pairs={{0,8},{1,9},{2,10},{3,11},{4,12},{5,13},{6,14},{7,15},{8,0},{9,1},... | collective-permute-start | bytes 663560 | tf_op jit(solution)/shard_map/ppermute | solution.py:446
  138.0 16.9 %collective-permute-start.25 = (f32[432,128]{1,0:T(8,128)}, f32[432,128]{1,0:T(8,128)S(1)}, u32[]{:S(2)}, u32[]{:S(2)}) collective-permute-start(f32[432,128]{1,0:T(8,128)} %get-tuple-element.119), channel_id=1, source_target_pairs={{0,5},{1,4},{2,7},{3,6},{4,1},{5,0},{6,3},{7,2},{8,13},{9,12},{10,... | collective-permute-start | bytes 663560 | tf_op jit(solution)/shard_map/ppermute | solution.py:446
  140.0 18.0 %collective-permute-start.24 = (f32[432,128]{1,0:T(8,128)}, f32[432,128]{1,0:T(8,128)S(1)}, u32[]{:S(2)}, u32[]{:S(2)}) collective-permute-start(f32[432,128]{1,0:T(8,128)} %get-tuple-element.117), channel_id=1, source_target_pairs={{0,12},{1,13},{2,14},{3,15},{4,8},{5,9},{6,10},{7,11},{8,4},{9,5},... | collective-permute-start | bytes 663560 | tf_op jit(solution)/shard_map/ppermute | solution.py:446
  141.7 18.7 %collective-permute-start.23 = (f32[432,128]{1,0:T(8,128)}, f32[432,128]{1,0:T(8,128)S(1)}, u32[]{:S(2)}, u32[]{:S(2)}) collective-permute-start(f32[432,128]{1,0:T(8,128)} %get-tuple-element.115), channel_id=1, source_target_pairs={{0,4},{1,5},{2,6},{3,7},{4,0},{5,1},{6,2},{7,3},{8,12},{9,13},{10,... | collective-permute-start | bytes 663560 | tf_op jit(solution)/shard_map/ppermute | solution.py:446
  154.8 20.2 %collective-permute-start.22 = (f32[432,128]{1,0:T(8,128)}, f32[432,128]{1,0:T(8,128)S(1)}, u32[]{:S(2)}, u32[]{:S(2)}) collective-permute-start(f32[432,128]{1,0:T(8,128)} %get-tuple-element.113), channel_id=1, source_target_pairs={{0,11},{1,10},{2,9},{3,8},{4,15},{5,14},{6,13},{7,12},{8,3},{9,2},... | collective-permute-start | bytes 663560 | tf_op jit(solution)/shard_map/ppermute | solution.py:446
  154.9 22.9 %collective-permute-start.21 = (f32[432,128]{1,0:T(8,128)}, f32[432,128]{1,0:T(8,128)S(1)}, u32[]{:S(2)}, u32[]{:S(2)}) collective-permute-start(f32[432,128]{1,0:T(8,128)} %get-tuple-element.111), channel_id=1, source_target_pairs={{0,3},{1,2},{2,1},{3,0},{4,7},{5,6},{6,5},{7,4},{8,11},{9,10},{10,... | collective-permute-start | bytes 663560 | tf_op jit(solution)/shard_map/ppermute | solution.py:446
  157.9 30.2 %collective-permute-start.30 = (f32[432,128]{1,0:T(8,128)}, f32[432,128]{1,0:T(8,128)S(1)}, u32[]{:S(2)}, u32[]{:S(2)}) collective-permute-start(f32[432,128]{1,0:T(8,128)} %get-tuple-element.129), channel_id=1, source_target_pairs={{0,15},{1,14},{2,13},{3,12},{4,11},{5,10},{6,9},{7,8},{8,7},{9,6},... | collective-permute-start | bytes 663560 | tf_op jit(solution)/shard_map/ppermute | solution.py:446
  160.4 27.7 %collective-permute-start.29 = (f32[432,128]{1,0:T(8,128)}, f32[432,128]{1,0:T(8,128)S(1)}, u32[]{:S(2)}, u32[]{:S(2)}) collective-permute-start(f32[432,128]{1,0:T(8,128)} %get-tuple-element.127), channel_id=1, source_target_pairs={{0,7},{1,6},{2,5},{3,4},{4,3},{5,2},{6,1},{7,0},{8,15},{9,14},{10,... | collective-permute-start | bytes 663560 | tf_op jit(solution)/shard_map/ppermute | solution.py:446
  177.8 23.3 %collective-permute-start.26 = (f32[432,128]{1,0:T(8,128)}, f32[432,128]{1,0:T(8,128)S(1)}, u32[]{:S(2)}, u32[]{:S(2)}) collective-permute-start(f32[432,128]{1,0:T(8,128)} %get-tuple-element.121), channel_id=1, source_target_pairs={{0,13},{1,12},{2,15},{3,14},{4,9},{5,8},{6,11},{7,10},{8,5},{9,4},... | collective-permute-start | bytes 663560 | tf_op jit(solution)/shard_map/ppermute | solution.py:446
  210.0 71.3 %all-to-all-start.1 = ((f32[16,432,128]{2,1,0:T(8,128)}), f32[16,432,128]{2,1,0:T(8,128)S(1)}, u32[]{:S(2)}, u32[]{:S(2)}) async-start(f32[16,432,128]{2,1,0:T(8,128)} %bitcast.20), calls=%async_computation.1 | async-start | bytes 7077888 | tf_op jit(solution)/shard_map/all_to_all | solution.py:451
  294.2 61.2 %all-to-all-start.2 = ((f32[32,112,128]{2,1,0:T(8,128)}), f32[32,112,128]{2,1,0:T(8,128)S(1)}, u32[]{:S(2)}, u32[]{:S(2)}) async-start(f32[32,112,128]{2,1,0:T(8,128)} %bitcast.25), calls=%async_computation.2 | async-start | bytes 3670016 | tf_op jit(solution)/shard_map/all_to_all | solution.py:455
  311.2 47.3 %collective-permute-start.33 = (f32[1728,128]{1,0:T(8,128)S(1)}, f32[1728,128]{1,0:T(8,128)}, u32[]{:S(2)}, u32[]{:S(2)}) collective-permute-start(f32[1728,128]{1,0:T(8,128)S(1)} %copy-done.3), channel_id=1, source_target_pairs={{0,16},{16,0},{1,17},{17,1},{2,18},{18,2},{3,19},{19,3},{4,20},{20... | collective-permute-start | bytes 2654216 | tf_op jit(solution)/shard_map/ppermute | solution.py:554
  313.8 58.0 %collective-permute-start.31 = (f32[1728,128]{1,0:T(8,128)}, f32[1728,128]{1,0:T(8,128)}, u32[]{:S(2)}, u32[]{:S(2)}) collective-permute-start(f32[1728,128]{1,0:T(8,128)} %get-tuple-element.133.lower_ref), channel_id=1, source_target_pairs={{0,16},{16,0},{1,17},{17,1},{2,18},{18,2},{3,19},{19,3},{4,20},{20... | collective-permute-start | bytes 2654216 | tf_op jit(solution)/shard_map/ppermute | solution.py:555
  375.3 17.1 %all-to-all-start.3 = ((f32[16,56,128]{2,1,0:T(8,128)}), f32[16,56,128]{2,1,0:T(8,128)S(1)}, u32[]{:S(2)}, u32[]{:S(2)}) async-start(f32[16,56,128]{2,1,0:T(8,128)} %bitcast.7), calls=%async_computation.3 | async-start | bytes 917504 | tf_op jit(solution)/shard_map/all_to_all | solution.py:451
  (53 other events, 2085.9 us)

commit v12 on v11

--- a/solution.py
+++ b/solution.py
@@ -164,6 +164,14 @@
                 out_ref[pl.ds(to * chunk + used, chunk - used), :] = jnp.zeros((chunk - used, LANES), jnp.float32)
 
 
+def move(to_ref, to, from_ref, start, count, step=1):
+    if count < 8:
+        to_ref[pl.ds(to, count), :] = from_ref[pl.ds(start, count, stride=step), :]
+        return
+    for first in [*range(0, count - 7, 8)] + ([count - 8] if count % 8 else []):
+        to_ref[pl.ds(to + first, 8), :] = from_ref[pl.ds(start + first * step, 8, stride=step), :]
+
+
 def potential_kernel(sizes, bunch, place_ref, ion_ref, hxc_ref, out_ref, packed):
     planes, grid, rows, share = sizes
     chunk = chunk_rows(sizes)
@@ -175,7 +183,7 @@
         pack(ion_ref[inner] + hxc_ref[inner], slot)
         for to in range(grid):
             start = to * rows + band * share
-            out_ref[pl.ds(to * chunk + plane * share, share), :] = slot[pl.ds(start, share), :]
+            move(out_ref, to * chunk + plane * share, slot, start, share)
 
 
 def pack_kernel(sizes, bunch, turns, place_ref, psi_ref, *refs):
@@ -189,7 +197,7 @@
             pack(psi_ref[0, part, inner], slot)
             for turn, out_ref in zip(turns, out_refs):
                 start = (mine ^ turn) * rows
-                out_ref[pl.ds((plane * 2 + part) * rows, rows), :] = slot[pl.ds(start, rows), :]
+                move(out_ref, (plane * 2 + part) * rows, slot, start, rows)
 
 
 def plane_kernel(sizes, bunch, turns, place_ref, psi_ref, ion_ref, hxc_ref, kin_ref, *refs):
@@ -209,7 +217,7 @@
             pack(bare + applied[part], slot)
             for turn, out_ref in zip(turns, out_refs):
                 start = (mine ^ turn) * rows
-                out_ref[pl.ds((plane * 2 + part) * rows, rows), :] = slot[pl.ds(start, rows), :]
+                move(out_ref, (plane * 2 + part) * rows, slot, start, rows)
         for part in range(2):
             twice = kinetic(applied[part], kin) + (potential - 1.0) * applied[part]
             turned = applied[1] if part == 0 else -applied[0]
@@ -227,7 +235,7 @@
     for source in range(grid):
         for row in range(share):
             start = source * chunk + row
-            out_ref[pl.ds(row * length + source * planes, planes), :] = moved_ref[pl.ds(start, planes, stride=share), :]
+            move(out_ref, row * length + source * planes, moved_ref, start, planes, share)
 
 
 def along_kernel(sizes, steps, turns, place_ref, *refs):
@@ -243,7 +251,7 @@
         for turn, moved_ref in zip(turns, moved_refs):
             first = (place_ref[0] % grid ^ turn) * planes
             for part in range(2):
-                slot[part, pl.ds(first, planes), :] = moved_ref[pl.ds(part * rows + row, planes, stride=2 * rows), :]
+                move(slot.at[part], first, moved_ref, part * rows + row, planes, 2 * rows)
         along = product_of_parts(kin, split(jnp.concatenate([slot[0], slot[1]], axis=1)))
         again = product_of_parts(kin, split(along))
         here = slice(inner * length, (inner + 1) * length)
@@ -267,7 +275,7 @@
         for turn, mixed_ref in zip(turns, mixed_refs):
             first = (place_ref[0] % grid ^ turn) * planes
             for part in range(2):
-                slot[part, pl.ds(first, planes), :] = mixed_ref[pl.ds(part * rows + row, planes, stride=2 * rows), :]
+                move(slot.at[part], first, mixed_ref, part * rows + row, planes, 2 * rows)
         mixed = product_of_parts(kin, split(jnp.concatenate([slot[0], slot[1]], axis=1)))
         update = along_ref[inner * length : (inner + 1) * length, :] + mixed
         for part in range(2):
@@ -292,7 +300,7 @@
             slot = packed.at[inner * 4 + part]
             for source in range(grid):
                 start = ((source * planes + plane) * 2 + part) * rows
-                slot[pl.ds(source * rows, rows), :] = update_ref[pl.ds(start, rows), :]
+                move(slot, source * rows, update_ref, start, rows)
             fresh = base_ref[part, inner] + unpack(slot, length)
             fresh_ref[0, part, inner] = fresh
             part_sum = fresh * fresh if part_sum is None else part_sum + fresh * fresh
@@ -313,7 +321,7 @@
         slot = packed.at[inner * 4 + 3]
         pack(spectrum + jnp.where(first, means[inner] * length, 0.0), slot)
         for to in range(2 * grid):
-            out_ref[pl.ds(to * chunk + plane * share, share), :] = slot[pl.ds(to * share, share), :]
+            move(out_ref, to * chunk + plane * share, slot, to * share, share)
 
 
 def filter_kernel(sizes, spec_ref, cells_ref, tables_ref, upper_ref, lower_ref, lines):
@@ -369,7 +377,7 @@
             side = slot.at[pl.ds(pl.multiple_of(part * half, 8), half), :]
             for source in range(grid):
                 start = source * chunk + plane * share
-                side[pl.ds(source * share, share), :] = spec_ref[pl.ds(start, share), :]
+                move(side, source * share, spec_ref, start, share)
         lines.append(product_of_parts(turn, split(unpack(slot, length))))
     hartree = product_of_parts(split(jnp.concatenate(lines, axis=0)), basis)
     for inner in range(bunch):
@@ -458,6 +466,18 @@
     spec_rows = 2 * grid * chunk_rows(sizes)
     mixed_rows = 2 * planes * rows
     steps = 6 if rows % 6 == 0 and share % (rows // 6) == 0 else 2
+    shared = pl.pallas_call(
+        functools.partial(potential_kernel, sizes, bunch),
+        grid=(planes // bunch,),
+        in_specs=[smem, plane_spec, plane_spec],
+        out_specs=whole(spec_rows // 2, LANES),
+        out_shape=shape(spec_rows // 2, LANES),
+        scratch_shapes=scratch(1),
+        compiler_params=PARAMS,
+        cost_estimate=cost(0, 6 << 20),
+    )(place, ion_potential, hxc_potential)
+    place, shared = lax.optimization_barrier((place, shared))
+    shared = swap(shared)
     moved = pl.pallas_call(
         functools.partial(pack_kernel, sizes, bunch, turns),
         grid=(planes // bunch,),
@@ -470,17 +490,6 @@
     )(place, orbitals)
     moved = [send(turn, piece) for turn, piece in zip(turns[:6], moved[:6])] + list(moved[6:])
     behind = lax.optimization_barrier((place, line[1]))[0]
-    shared = pl.pallas_call(
-        functools.partial(potential_kernel, sizes, bunch),
-        grid=(planes // bunch,),
-        in_specs=[smem, plane_spec, plane_spec],
-        out_specs=whole(spec_rows // 2, LANES),
-        out_shape=shape(spec_rows // 2, LANES),
-        scratch_shapes=scratch(1),
-        compiler_params=PARAMS,
-        cost_estimate=cost(0, 6 << 20),
-    )(behind, ion_potential, hxc_potential)
-    shared = swap(shared)
     *mixed, base = pl.pallas_call(
         functools.partial(plane_kernel, sizes, bunch, turns),
         grid=(planes // bunch,),

time: 411 us -> 404 us (0.983)
  waiting for transfers between devices: 226 us -> 219 us
    ppermute x30, waiting for transfers between devices: 87.5 us -> 80.5 us  [send(): lax.ppermute(piece, 'grid', [(spot, spot ^ turn) for spot in range(grid)])]
  transfers between devices with their start and end apart: 40 -> 40, of which waited for: 21 -> 20; matrix products, arithmetic and copies ran while one was open for 0% -> 0% of each run, Pallas kernels for 8% -> 10%
where the time goes in v12:
time: 404 us; the launch traced here: 403 us
  waiting for transfers between devices  219 us (54%)
  starting transfers between devices  109 us (27%)
  Pallas kernels  66.1 us (16%)
  local copies, waits for them, and re-layouts  6.51 us (2%)
    all_to_all x4, waiting for transfers between devices, swap(): lax.all_to_all(flat, 'grid', split_axis=0, concat_axis=0)  81.5 us
    ppermute x30, waiting for transfers between devices, send(): lax.ppermute(piece, 'grid', [(spot, spot ^ turn) for spot in range(grid)])  80.5 us
    ppermute x30, starting transfers between devices, send(): lax.ppermute(piece, 'grid', [(spot, spot ^ turn) for spot in range(grid)])  66.7 us
    all_to_all x1, waiting for transfers between devices, swap_all(): lax.all_to_all(flat, ('band', 'grid'), split_axis=0, concat_axis=0)  41.3 us
    all_to_all x4, starting transfers between devices, swap(): lax.all_to_all(flat, 'grid', split_axis=0, concat_axis=0)  19.8 us
    all_to_all x1, starting transfers between devices, swap_all(): lax.all_to_all(flat, ('band', 'grid'), split_axis=0, concat_axis=0)  17 us
    pallas_call x1, Pallas kernels, packed_path(): pl.pallas_call(functools.partial(plane_kernel, sizes, bunch, turns), grid...  14 us
    pallas_call x1, Pallas kernels, packed_path(): pl.pallas_call(functools.partial(fresh_kernel, sizes, bunch), grid=(plane...  11 us
  transfers between devices with their start and end apart: 40, of which 20 were waited for; matrix products, arithmetic and copies ran while one was open for 0% of the time, Pallas kernels for 10%

profile of v12, /device:TPU:0, one launch (start us, length us, event | category | flops | bytes accessed | tf_op | source)
XLA Modules:
  0.0 402.8 jit_solution(3408767347838948866)
XLA Ops:
  0.6 4.1 %shard_map.86 = f32[1792,128]{1,0:T(8,128)} custom-call(s32[1]{0:T(128)} %bitcast.place_ref, f32[12,192,192]{2,1,0:T(8,128)} %ion_ref.3, f32[12,192,192]{2,1,0:T(8,128)} %hxc_ref.3), custom_call_target="tpu_custom_call" | custom-call | bytes 6291456 | tf_op jit(solution)/shard_map/pallas_call | solution.py:469
  4.8 7.4 %all-to-all-start = ((f32[16,112,128]{2,1,0:T(8,128)}), f32[16,112,128]{2,1,0:T(8,128)S(1)}, u32[]{:S(2)}, u32[]{:S(2)}) async-start(f32[16,112,128]{2,1,0:T(8,128)} %bitcast.22), calls=%async_computation | async-start | bytes 1835008 | tf_op jit(solution)/shard_map/all_to_all | solution.py:459
  12.1 5.4 %shard_map.87 = (f32[432,128]{1,0:T(8,128)}, f32[432,128]{1,0:T(8,128)}, f32[432,128]{1,0:T(8,128)}, f32[432,128]{1,0:T(8,128)}, f32[432,128]{1,0:T(8,128)}, /*i...) custom-call(s32[1]{0:T(128)} %bitcast.place_ref, ...), custom_call_target="tpu_custom_call" | custom-call | bytes 8388608 | tf_op jit(solution)/shard_map/pallas_call | solution.py:481
  24.3 14.0 %shard_map.88 = (f32[432,128]{1,0:T(8,128)}, f32[432,128]{1,0:T(8,128)}, f32[432,128]{1,0:T(8,128)}, f32[432,128]{1,0:T(8,128)}, f32[432,128]{1,0:T(8,128)}, /*i...) custom-call(s32[1]{0:T(128)} %bitcast.place_ref, ...), custom_call_target="tpu_custom_call" | custom-call | flops 4076863488 | bytes 20971520 | tf_op jit(solution)/shard_map/pallas_call | solution.py:493
  38.3 17.9 %collective-permute-done.4.refs_5_ = f32[432,128]{1,0:T(8,128)S(1)} collective-permute-done((f32[432,128]{1,0:T(8,128)}, f32[432,128]{1,0:T(8,128)S(1)}, u32[]{:S(2)}, u32[]{:S(2)}) %collective-permute-start.4) | collective-permute-done | bytes 221216 | tf_op jit(solution)/shard_map/ppermute | solution.py:454
  62.2 7.4 %collective-permute-done.refs_1_ = f32[432,128]{1,0:T(8,128)S(1)} collective-permute-done((f32[432,128]{1,0:T(8,128)}, f32[432,128]{1,0:T(8,128)S(1)}, u32[]{:S(2)}, u32[]{:S(2)}) %collective-permute-start) | collective-permute-done | bytes 221216 | tf_op jit(solution)/shard_map/ppermute | solution.py:454
  69.8 4.0 %collective-permute-done.9.refs_10_ = f32[432,128]{1,0:T(8,128)S(1)} collective-permute-done((f32[432,128]{1,0:T(8,128)S(1)}, f32[432,128]{1,0:T(8,128)S(1)}, u32[]{:S(2)}, u32[]{:S(2)}) %collective-permute-start.9) | collective-permute-done | bytes 221216 | tf_op jit(solution)/shard_map/ppermute | solution.py:454
  84.3 4.1 %collective-permute-done.6.refs_7_ = f32[432,128]{1,0:T(8,128)S(1)} collective-permute-done((f32[432,128]{1,0:T(8,128)}, f32[432,128]{1,0:T(8,128)S(1)}, u32[]{:S(2)}, u32[]{:S(2)}) %collective-permute-start.6) | collective-permute-done | bytes 221216 | tf_op jit(solution)/shard_map/ppermute | solution.py:454
  90.1 6.4 %collective-permute-start.10 = (f32[432,128]{1,0:T(8,128)}, f32[432,128]{1,0:T(8,128)S(1)}, u32[]{:S(2)}, u32[]{:S(2)}) collective-permute-start(f32[432,128]{1,0:T(8,128)} %get-tuple-element.93), channel_id=1, source_target_pairs={{0,13},{1,12},{2,15},{3,14},{4,9},{5,8},{6,11},{7,10},{8,5},{9,4},... | collective-permute-start | bytes 663560 | tf_op jit(solution)/shard_map/ppermute | solution.py:454
  98.4 5.3 %collective-permute-start.20 = (f32[432,128]{1,0:T(8,128)}, f32[432,128]{1,0:T(8,128)S(1)}, u32[]{:S(2)}, u32[]{:S(2)}) collective-permute-start(f32[432,128]{1,0:T(8,128)} %get-tuple-element.113), channel_id=1, source_target_pairs={{0,10},{1,11},{2,8},{3,9},{4,14},{5,15},{6,12},{7,13},{8,2},{9,3},... | collective-permute-start | bytes 663560 | tf_op jit(solution)/shard_map/ppermute | solution.py:454
  105.4 11.0 %collective-permute-start.18 = (f32[432,128]{1,0:T(8,128)}, f32[432,128]{1,0:T(8,128)S(1)}, u32[]{:S(2)}, u32[]{:S(2)}) collective-permute-start(f32[432,128]{1,0:T(8,128)} %get-tuple-element.109), channel_id=1, source_target_pairs={{0,9},{1,8},{2,11},{3,10},{4,13},{5,12},{6,15},{7,14},{8,1},{9,0},... | collective-permute-start | bytes 663560 | tf_op jit(solution)/shard_map/ppermute | solution.py:454
  117.8 12.9 %collective-permute-done.20.refs_5_ = f32[432,128]{1,0:T(8,128)S(1)} collective-permute-done((f32[432,128]{1,0:T(8,128)}, f32[432,128]{1,0:T(8,128)S(1)}, u32[]{:S(2)}, u32[]{:S(2)}) %collective-permute-start.20) | collective-permute-done | bytes 221216 | tf_op jit(solution)/shard_map/ppermute | solution.py:454
  137.0 10.5 %collective-permute-done.16.refs_1_ = f32[432,128]{1,0:T(8,128)S(1)} collective-permute-done((f32[432,128]{1,0:T(8,128)}, f32[432,128]{1,0:T(8,128)S(1)}, u32[]{:S(2)}, u32[]{:S(2)}) %collective-permute-start.16) | collective-permute-done | bytes 221216 | tf_op jit(solution)/shard_map/ppermute | solution.py:454
  153.2 10.6 %collective-permute-start.29 = (f32[432,128]{1,0:T(8,128)}, f32[432,128]{1,0:T(8,128)S(1)}, u32[]{:S(2)}, u32[]{:S(2)}) collective-permute-start(f32[432,128]{1,0:T(8,128)} %get-tuple-element.131), channel_id=1, source_target_pairs={{0,7},{1,6},{2,5},{3,4},{4,3},{5,2},{6,1},{7,0},{8,15},{9,14},{10,... | collective-permute-start | bytes 663560 | tf_op jit(solution)/shard_map/ppermute | solution.py:454
  163.8 4.0 %collective-permute-done.22.refs_7_ = f32[432,128]{1,0:T(8,128)S(1)} collective-permute-done((f32[432,128]{1,0:T(8,128)}, f32[432,128]{1,0:T(8,128)S(1)}, u32[]{:S(2)}, u32[]{:S(2)}) %collective-permute-start.22) | collective-permute-done | bytes 221216 | tf_op jit(solution)/shard_map/ppermute | solution.py:454
  171.5 9.4 %shard_map.90.along_ref = f32[3456,256]{1,0:T(8,128)} custom-call(s32[1]{0:T(128)} %bitcast.place_ref, f32[432,128]{1,0:T(8,128)} %get-tuple-element.74.refs_0_, f32[432,128]{1,0:T(8,128)} %copy-done.13, f32[432,128]{1,0:T(8,128)} %copy-done.9, f32[432,128]{1,0:T(8,128)} %copy-done.12, f32[432,128]{1,0:T(8,128)} %copy-done.11, f32[432,128]{1,0:T(8,128)} %copy-done.10, ...), custom_call_target="tpu_custom_call" | custom-call | flops 2038431744 | bytes 10485760 | tf_op jit(solution)/shard_map/pallas_call | solution.py:515
  181.0 4.4 %collective-permute-done.27.refs_12_ = f32[432,128]{1,0:T(8,128)S(1)} collective-permute-done((f32[432,128]{1,0:T(8,128)}, f32[432,128]{1,0:T(8,128)S(1)}, u32[]{:S(2)}, u32[]{:S(2)}) %collective-permute-start.27) | collective-permute-done | bytes 221216 | tf_op jit(solution)/shard_map/ppermute | solution.py:454
  185.3 8.6 %collective-permute-done.26.refs_11_ = f32[432,128]{1,0:T(8,128)S(1)} collective-permute-done((f32[432,128]{1,0:T(8,128)}, f32[432,128]{1,0:T(8,128)S(1)}, u32[]{:S(2)}, u32[]{:S(2)}) %collective-permute-start.26) | collective-permute-done | bytes 221216 | tf_op jit(solution)/shard_map/ppermute | solution.py:454
  194.6 8.2 %shard_map.91 = f32[6912,128]{1,0:T(8,128)} custom-call(s32[1]{0:T(128)} %bitcast.place_ref, f32[3456,256]{1,0:T(8,128)} %shard_map.90.along_ref, f32[192,192]{1,0:T(8,128)} %constant.23.clone.kin_ref.refs_18_, f32[432,128]{1,0:T(8,128)} %get-tuple-element.103.refs_0_, f32[432,128]{1,0:T(8,128)} %copy-done.27, f32[432,128]{1,0:T(8,128)} %copy-done.26, ...), custom_call_target="tpu_custom_call" | custom-call | flops 1019215872 | bytes 14680064 | tf_op jit(solution)/shard_map/pallas_call | solution.py:526
  202.8 5.1 %all-to-all-start.1 = ((f32[16,432,128]{2,1,0:T(8,128)}), f32[16,432,128]{2,1,0:T(8,128)S(1)}, u32[]{:S(2)}, u32[]{:S(2)}) async-start(f32[16,432,128]{2,1,0:T(8,128)} %bitcast.20), calls=%async_computation.1 | async-start | bytes 7077888 | tf_op jit(solution)/shard_map/all_to_all | solution.py:459
  208.5 65.6 %all-to-all-done.1 = f32[16,432,128]{2,1,0:T(8,128)S(1)} async-done(((f32[16,432,128]{2,1,0:T(8,128)}), f32[16,432,128]{2,1,0:T(8,128)S(1)}, u32[]{:S(2)}, u32[]{:S(2)}) %all-to-all-start.1) | async-done | bytes 3538976 | tf_op jit(solution)/shard_map/all_to_all | solution.py:459
  275.9 11.0 %shard_map.92 = (f32[1,2,12,192,192]{4,3,2,1,0:T(8,128)}, f32[1728,128]{1,0:T(8,128)}, f32[1728,128]{1,0:T(8,128)}, f32[3584,128]{1,0:T(8,128)}) custom-call(f32[1]{0:T(128)S(6)} %copy.14.occ_ref, f32[6912,128]{1,0:T(8,128)} %bitcast.19, f32[2,12,192,192]{3,2,1,0:T(8,128)} %get-tuple-element.82.base_ref, f32[2,192,192]{2,1,0:T(8,128)} %constant.24.clone.tables_ref), custom_call_target="tpu_custom_call" | custom-call | flops 2038431744 | bytes 16777216 | tf_op jit(solution)/shard_map/pallas_call | solution.py:543
  286.9 17.0 %all-to-all-start.2 = ((f32[32,112,128]{2,1,0:T(8,128)}), f32[32,112,128]{2,1,0:T(8,128)S(1)}, u32[]{:S(2)}, u32[]{:S(2)}) async-start(f32[32,112,128]{2,1,0:T(8,128)} %bitcast.25), calls=%async_computation.2 | async-start | bytes 3670016 | tf_op jit(solution)/shard_map/all_to_all | solution.py:463
  306.9 41.3 %all-to-all-done.2 = f32[32,112,128]{2,1,0:T(8,128)S(1)} async-done(((f32[32,112,128]{2,1,0:T(8,128)}), f32[32,112,128]{2,1,0:T(8,128)S(1)}, u32[]{:S(2)}, u32[]{:S(2)}) %all-to-all-start.2) | async-done | bytes 1835040 | tf_op jit(solution)/shard_map/all_to_all | solution.py:463
  351.3 3.6 all-to-all-start.4
  354.9 9.6 %collective-permute-done.31.lower_other = f32[1728,128]{1,0:T(8,128)} collective-permute-done((f32[1728,128]{1,0:T(8,128)}, f32[1728,128]{1,0:T(8,128)}, u32[]{:S(2)}, u32[]{:S(2)}) %collective-permute-start.31) | collective-permute-done | bytes 884768 | tf_op jit(solution)/shard_map/ppermute | solution.py:564
  364.5 3.6 all-to-all-done.4
  368.1 3.8 all-to-all-start.3
  372.9 12.3 %all-to-all-done.3 = f32[16,56,128]{2,1,0:T(8,128)S(1)} async-done(((f32[16,56,128]{2,1,0:T(8,128)}), f32[16,56,128]{2,1,0:T(8,128)S(1)}, u32[]{:S(2)}, u32[]{:S(2)}) %all-to-all-start.3) | async-done | bytes 458784 | tf_op jit(solution)/shard_map/all_to_all | solution.py:459
  386.8 4.3 %shard_map.94.refs_0_ = f32[12,192,192]{2,1,0:T(8,128)} custom-call(s32[1]{0:T(128)} %bitcast.place_ref, f32[896,128]{1,0:T(8,128)} %bitcast.24, f32[896,128]{1,0:T(8,128)} %copy-done.7, f32[1728,128]{1,0:T(8,128)} %get-tuple-element.139.upper_ref, f32[1728,128]{1,0:T(8,128)} %get-tuple-element.137.lower_ref, ...), custom_call_target="tpu_custom_call" | custom-call | flops 509607936 | bytes 4194304 | tf_op jit(solution)/shard_map/pallas_call | solution.py:586
  391.1 6.6 %collective-permute-done.32.far_ref = f32[896,128]{1,0:T(8,128)S(1)} collective-permute-done((f32[896,128]{1,0:T(8,128)S(1)}, f32[896,128]{1,0:T(8,128)S(1)}, u32[]{:S(2)}, u32[]{:S(2)}) %collective-permute-start.32) | collective-permute-done | bytes 458784 | tf_op jit(solution)/shard_map/ppermute | solution.py:606
  398.5 4.3 %shard_map.95 = f32[12,192,192]{2,1,0:T(8,128)} custom-call(s32[1]{0:T(128)} %bitcast.place_ref, f32[896,128]{1,0:T(8,128)} %bitcast.27, f32[896,128]{1,0:T(8,128)} %copy-done.8, f32[1728,128]{1,0:T(8,128)} %get-tuple-element.139.upper_ref, f32[1728,128]{1,0:T(8,128)} %get-tuple-element.137.lower_ref, ...), custom_call_target="tpu_custom_call", output_to_operand_aliasing={{}: (8, {})} | custom-call | flops 509607936 | bytes 4194304 | tf_op jit(solution)/shard_map/pallas_call | solution.py:586
  (142 shorter events, 57.5 us)
Async XLA Ops:
  4.8 76.4 %all-to-all-start = ((f32[16,112,128]{2,1,0:T(8,128)}), f32[16,112,128]{2,1,0:T(8,128)S(1)}, u32[]{:S(2)}, u32[]{:S(2)}) async-start(f32[16,112,128]{2,1,0:T(8,128)} %bitcast.22), calls=%async_computation | async-start | bytes 1835008 | tf_op jit(solution)/shard_map/all_to_all | solution.py:459
  17.9 38.3 %collective-permute-start.4 = (f32[432,128]{1,0:T(8,128)}, f32[432,128]{1,0:T(8,128)S(1)}, u32[]{:S(2)}, u32[]{:S(2)}) collective-permute-start(f32[432,128]{1,0:T(8,128)} %get-tuple-element.79), channel_id=1, source_target_pairs={{0,10},{1,11},{2,8},{3,9},{4,14},{5,15},{6,12},{7,13},{8,2},{9,3},... | collective-permute-start | bytes 663560 | tf_op jit(solution)/shard_map/ppermute | solution.py:454
  21.4 34.8 %collective-permute-start.3 = (f32[432,128]{1,0:T(8,128)}, f32[432,128]{1,0:T(8,128)S(1)}, u32[]{:S(2)}, u32[]{:S(2)}) collective-permute-start(f32[432,128]{1,0:T(8,128)} %get-tuple-element.78), channel_id=1, source_target_pairs={{0,2},{1,3},{2,0},{3,1},{4,6},{5,7},{6,4},{7,5},{8,10},{9,11},{10,... | collective-permute-start | bytes 663560 | tf_op jit(solution)/shard_map/ppermute | solution.py:454
  22.0 37.2 %collective-permute-start.2 = (f32[432,128]{1,0:T(8,128)}, f32[432,128]{1,0:T(8,128)S(1)}, u32[]{:S(2)}, u32[]{:S(2)}) collective-permute-start(f32[432,128]{1,0:T(8,128)} %get-tuple-element.77), channel_id=1, source_target_pairs={{0,9},{1,8},{2,11},{3,10},{4,13},{5,12},{6,15},{7,14},{8,1},{9,0},... | collective-permute-start | bytes 663560 | tf_op jit(solution)/shard_map/ppermute | solution.py:454
  22.0 47.6 %collective-permute-start = (f32[432,128]{1,0:T(8,128)}, f32[432,128]{1,0:T(8,128)S(1)}, u32[]{:S(2)}, u32[]{:S(2)}) collective-permute-start(f32[432,128]{1,0:T(8,128)} %get-tuple-element.75), channel_id=1, source_target_pairs={{0,8},{1,9},{2,10},{3,11},{4,12},{5,13},{6,14},{7,15},{8,0},{9,1},... | collective-permute-start | bytes 663560 | tf_op jit(solution)/shard_map/ppermute | solution.py:454
  56.2 17.6 %collective-permute-start.9 = (f32[432,128]{1,0:T(8,128)S(1)}, f32[432,128]{1,0:T(8,128)S(1)}, u32[]{:S(2)}, u32[]{:S(2)}) collective-permute-start(f32[432,128]{1,0:T(8,128)S(1)} %copy-done.40), channel_id=1, source_target_pairs={{0,5},{1,4},{2,7},{3,6},{4,1},{5,0},{6,3},{7,2},{8,13},{9,12},{10,... | collective-permute-start | bytes 663560 | tf_op jit(solution)/shard_map/ppermute | solution.py:454
  56.3 19.6 %collective-permute-start.8 = (f32[432,128]{1,0:T(8,128)S(1)}, f32[432,128]{1,0:T(8,128)S(1)}, u32[]{:S(2)}, u32[]{:S(2)}) collective-permute-start(f32[432,128]{1,0:T(8,128)S(1)} %copy-done.39), channel_id=1, source_target_pairs={{0,12},{1,13},{2,14},{3,15},{4,8},{5,9},{6,10},{7,11},{8,4},{9,5},... | collective-permute-start | bytes 663560 | tf_op jit(solution)/shard_map/ppermute | solution.py:454
  59.2 20.1 %collective-permute-start.7 = (f32[432,128]{1,0:T(8,128)S(1)}, f32[432,128]{1,0:T(8,128)S(1)}, u32[]{:S(2)}, u32[]{:S(2)}) collective-permute-start(f32[432,128]{1,0:T(8,128)S(1)} %copy-done.38), channel_id=1, source_target_pairs={{0,4},{1,5},{2,6},{3,7},{4,0},{5,1},{6,2},{7,3},{8,12},{9,13},{10,... | collective-permute-start | bytes 663560 | tf_op jit(solution)/shard_map/ppermute | solution.py:454
  59.2 29.3 %collective-permute-start.6 = (f32[432,128]{1,0:T(8,128)}, f32[432,128]{1,0:T(8,128)S(1)}, u32[]{:S(2)}, u32[]{:S(2)}) collective-permute-start(f32[432,128]{1,0:T(8,128)} %get-tuple-element.85), channel_id=1, source_target_pairs={{0,11},{1,10},{2,9},{3,8},{4,15},{5,14},{6,13},{7,12},{8,3},{9,2},... | collective-permute-start | bytes 663560 | tf_op jit(solution)/shard_map/ppermute | solution.py:454
  69.6 20.4 %collective-permute-start.5 = (f32[432,128]{1,0:T(8,128)}, f32[432,128]{1,0:T(8,128)S(1)}, u32[]{:S(2)}, u32[]{:S(2)}) collective-permute-start(f32[432,128]{1,0:T(8,128)} %get-tuple-element.83), channel_id=1, source_target_pairs={{0,3},{1,2},{2,1},{3,0},{4,7},{5,6},{6,5},{7,4},{8,11},{9,10},{10,... | collective-permute-start | bytes 663560 | tf_op jit(solution)/shard_map/ppermute | solution.py:454
  75.8 22.5 %collective-permute-start.13 = (f32[432,128]{1,0:T(8,128)}, f32[432,128]{1,0:T(8,128)S(1)}, u32[]{:S(2)}, u32[]{:S(2)}) collective-permute-start(f32[432,128]{1,0:T(8,128)} %get-tuple-element.99), channel_id=1, source_target_pairs={{0,7},{1,6},{2,5},{3,4},{4,3},{5,2},{6,1},{7,0},{8,15},{9,14},{10,... | collective-permute-start | bytes 663560 | tf_op jit(solution)/shard_map/ppermute | solution.py:454
  79.3 24.4 %collective-permute-start.12 = (f32[432,128]{1,0:T(8,128)}, f32[432,128]{1,0:T(8,128)}, u32[]{:S(2)}, u32[]{:S(2)}) collective-permute-start(f32[432,128]{1,0:T(8,128)} %get-tuple-element.97), channel_id=1, source_target_pairs={{0,14},{1,15},{2,12},{3,13},{4,10},{5,11},{6,8},{7,9},{8,6},{9,7},... | collective-permute-start | bytes 663560 | tf_op jit(solution)/shard_map/ppermute | solution.py:454
  88.5 82.1 %collective-permute-start.15 = (f32[1728,128]{1,0:T(8,128)}, f32[1728,128]{1,0:T(8,128)S(1)}, u32[]{:S(2)}, u32[]{:S(2)}) collective-permute-start(f32[1728,128]{1,0:T(8,128)} %shard_map.89.refs_16_), channel_id=1, source_target_pairs={{0,16},{16,0},{1,17},{17,1},{2,18},{18,2},{3,19},{19,3},{4,20},{20... | collective-permute-start | bytes 2654216 | tf_op jit(solution)/shard_map/ppermute | solution.py:513
  90.1 26.4 %collective-permute-start.10 = (f32[432,128]{1,0:T(8,128)}, f32[432,128]{1,0:T(8,128)S(1)}, u32[]{:S(2)}, u32[]{:S(2)}) collective-permute-start(f32[432,128]{1,0:T(8,128)} %get-tuple-element.93), channel_id=1, source_target_pairs={{0,13},{1,12},{2,15},{3,14},{4,9},{5,8},{6,11},{7,10},{8,5},{9,4},... | collective-permute-start | bytes 663560 | tf_op jit(solution)/shard_map/ppermute | solution.py:454
  98.4 32.3 %collective-permute-start.20 = (f32[432,128]{1,0:T(8,128)}, f32[432,128]{1,0:T(8,128)S(1)}, u32[]{:S(2)}, u32[]{:S(2)}) collective-permute-start(f32[432,128]{1,0:T(8,128)} %get-tuple-element.113), channel_id=1, source_target_pairs={{0,10},{1,11},{2,8},{3,9},{4,14},{5,15},{6,12},{7,13},{8,2},{9,3},... | collective-permute-start | bytes 663560 | tf_op jit(solution)/shard_map/ppermute | solution.py:454
  103.7 27.0 %collective-permute-start.19 = (f32[432,128]{1,0:T(8,128)}, f32[432,128]{1,0:T(8,128)S(1)}, u32[]{:S(2)}, u32[]{:S(2)}) collective-permute-start(f32[432,128]{1,0:T(8,128)} %get-tuple-element.111), channel_id=1, source_target_pairs={{0,2},{1,3},{2,0},{3,1},{4,6},{5,7},{6,4},{7,5},{8,10},{9,11},{10,... | collective-permute-start | bytes 663560 | tf_op jit(solution)/shard_map/ppermute | solution.py:454
  105.4 27.3 %collective-permute-start.18 = (f32[432,128]{1,0:T(8,128)}, f32[432,128]{1,0:T(8,128)S(1)}, u32[]{:S(2)}, u32[]{:S(2)}) collective-permute-start(f32[432,128]{1,0:T(8,128)} %get-tuple-element.109), channel_id=1, source_target_pairs={{0,9},{1,8},{2,11},{3,10},{4,13},{5,12},{6,15},{7,14},{8,1},{9,0},... | collective-permute-start | bytes 663560 | tf_op jit(solution)/shard_map/ppermute | solution.py:454
  116.5 18.0 %collective-permute-start.17 = (f32[432,128]{1,0:T(8,128)}, f32[432,128]{1,0:T(8,128)S(1)}, u32[]{:S(2)}, u32[]{:S(2)}) collective-permute-start(f32[432,128]{1,0:T(8,128)} %get-tuple-element.107), channel_id=1, source_target_pairs={{0,1},{1,0},{2,3},{3,2},{4,5},{5,4},{6,7},{7,6},{8,9},{9,8},{10,11... | collective-permute-start | bytes 663560 | tf_op jit(solution)/shard_map/ppermute | solution.py:454
  130.7 16.8 %collective-permute-start.16 = (f32[432,128]{1,0:T(8,128)}, f32[432,128]{1,0:T(8,128)S(1)}, u32[]{:S(2)}, u32[]{:S(2)}) collective-permute-start(f32[432,128]{1,0:T(8,128)} %get-tuple-element.105), channel_id=1, source_target_pairs={{0,8},{1,9},{2,10},{3,11},{4,12},{5,13},{6,14},{7,15},{8,0},{9,1},... | collective-permute-start | bytes 663560 | tf_op jit(solution)/shard_map/ppermute | solution.py:454
  130.7 16.8 %collective-permute-start.25 = (f32[432,128]{1,0:T(8,128)}, f32[432,128]{1,0:T(8,128)S(1)}, u32[]{:S(2)}, u32[]{:S(2)}) collective-permute-start(f32[432,128]{1,0:T(8,128)} %get-tuple-element.123), channel_id=1, source_target_pairs={{0,5},{1,4},{2,7},{3,6},{4,1},{5,0},{6,3},{7,2},{8,13},{9,12},{10,... | collective-permute-start | bytes 663560 | tf_op jit(solution)/shard_map/ppermute | solution.py:454
  132.7 18.0 %collective-permute-start.24 = (f32[432,128]{1,0:T(8,128)}, f32[432,128]{1,0:T(8,128)S(1)}, u32[]{:S(2)}, u32[]{:S(2)}) collective-permute-start(f32[432,128]{1,0:T(8,128)} %get-tuple-element.121), channel_id=1, source_target_pairs={{0,12},{1,13},{2,14},{3,15},{4,8},{5,9},{6,10},{7,11},{8,4},{9,5},... | collective-permute-start | bytes 663560 | tf_op jit(solution)/shard_map/ppermute | solution.py:454
  134.5 18.7 %collective-permute-start.23 = (f32[432,128]{1,0:T(8,128)}, f32[432,128]{1,0:T(8,128)S(1)}, u32[]{:S(2)}, u32[]{:S(2)}) collective-permute-start(f32[432,128]{1,0:T(8,128)} %get-tuple-element.119), channel_id=1, source_target_pairs={{0,4},{1,5},{2,6},{3,7},{4,0},{5,1},{6,2},{7,3},{8,12},{9,13},{10,... | collective-permute-start | bytes 663560 | tf_op jit(solution)/shard_map/ppermute | solution.py:454
  147.6 20.3 %collective-permute-start.22 = (f32[432,128]{1,0:T(8,128)}, f32[432,128]{1,0:T(8,128)S(1)}, u32[]{:S(2)}, u32[]{:S(2)}) collective-permute-start(f32[432,128]{1,0:T(8,128)} %get-tuple-element.117), channel_id=1, source_target_pairs={{0,11},{1,10},{2,9},{3,8},{4,15},{5,14},{6,13},{7,12},{8,3},{9,2},... | collective-permute-start | bytes 663560 | tf_op jit(solution)/shard_map/ppermute | solution.py:454
  147.6 23.0 %collective-permute-start.21 = (f32[432,128]{1,0:T(8,128)}, f32[432,128]{1,0:T(8,128)S(1)}, u32[]{:S(2)}, u32[]{:S(2)}) collective-permute-start(f32[432,128]{1,0:T(8,128)} %get-tuple-element.115), channel_id=1, source_target_pairs={{0,3},{1,2},{2,1},{3,0},{4,7},{5,6},{6,5},{7,4},{8,11},{9,10},{10,... | collective-permute-start | bytes 663560 | tf_op jit(solution)/shard_map/ppermute | solution.py:454
  150.7 30.2 %collective-permute-start.30 = (f32[432,128]{1,0:T(8,128)}, f32[432,128]{1,0:T(8,128)S(1)}, u32[]{:S(2)}, u32[]{:S(2)}) collective-permute-start(f32[432,128]{1,0:T(8,128)} %get-tuple-element.133), channel_id=1, source_target_pairs={{0,15},{1,14},{2,13},{3,12},{4,11},{5,10},{6,9},{7,8},{8,7},{9,6},... | collective-permute-start | bytes 663560 | tf_op jit(solution)/shard_map/ppermute | solution.py:454
  153.2 27.7 %collective-permute-start.29 = (f32[432,128]{1,0:T(8,128)}, f32[432,128]{1,0:T(8,128)S(1)}, u32[]{:S(2)}, u32[]{:S(2)}) collective-permute-start(f32[432,128]{1,0:T(8,128)} %get-tuple-element.131), channel_id=1, source_target_pairs={{0,7},{1,6},{2,5},{3,4},{4,3},{5,2},{6,1},{7,0},{8,15},{9,14},{10,... | collective-permute-start | bytes 663560 | tf_op jit(solution)/shard_map/ppermute | solution.py:454
  170.6 23.3 %collective-permute-start.26 = (f32[432,128]{1,0:T(8,128)}, f32[432,128]{1,0:T(8,128)S(1)}, u32[]{:S(2)}, u32[]{:S(2)}) collective-permute-start(f32[432,128]{1,0:T(8,128)} %get-tuple-element.125), channel_id=1, source_target_pairs={{0,13},{1,12},{2,15},{3,14},{4,9},{5,8},{6,11},{7,10},{8,5},{9,4},... | collective-permute-start | bytes 663560 | tf_op jit(solution)/shard_map/ppermute | solution.py:454
  202.8 71.3 %all-to-all-start.1 = ((f32[16,432,128]{2,1,0:T(8,128)}), f32[16,432,128]{2,1,0:T(8,128)S(1)}, u32[]{:S(2)}, u32[]{:S(2)}) async-start(f32[16,432,128]{2,1,0:T(8,128)} %bitcast.20), calls=%async_computation.1 | async-start | bytes 7077888 | tf_op jit(solution)/shard_map/all_to_all | solution.py:459
  286.9 61.2 %all-to-all-start.2 = ((f32[32,112,128]{2,1,0:T(8,128)}), f32[32,112,128]{2,1,0:T(8,128)S(1)}, u32[]{:S(2)}, u32[]{:S(2)}) async-start(f32[32,112,128]{2,1,0:T(8,128)} %bitcast.25), calls=%async_computation.2 | async-start | bytes 3670016 | tf_op jit(solution)/shard_map/all_to_all | solution.py:463
  304.0 47.3 %collective-permute-start.33 = (f32[1728,128]{1,0:T(8,128)S(1)}, f32[1728,128]{1,0:T(8,128)}, u32[]{:S(2)}, u32[]{:S(2)}) collective-permute-start(f32[1728,128]{1,0:T(8,128)S(1)} %copy-done.3), channel_id=1, source_target_pairs={{0,16},{16,0},{1,17},{17,1},{2,18},{18,2},{3,19},{19,3},{4,20},{20... | collective-permute-start | bytes 2654216 | tf_op jit(solution)/shard_map/ppermute | solution.py:563
  306.5 58.0 %collective-permute-start.31 = (f32[1728,128]{1,0:T(8,128)}, f32[1728,128]{1,0:T(8,128)}, u32[]{:S(2)}, u32[]{:S(2)}) collective-permute-start(f32[1728,128]{1,0:T(8,128)} %get-tuple-element.137.lower_ref), channel_id=1, source_target_pairs={{0,16},{16,0},{1,17},{17,1},{2,18},{18,2},{3,19},{19,3},{4,20},{20... | collective-permute-start | bytes 2654216 | tf_op jit(solution)/shard_map/ppermute | solution.py:564
  368.1 17.1 %all-to-all-start.3 = ((f32[16,56,128]{2,1,0:T(8,128)}), f32[16,56,128]{2,1,0:T(8,128)S(1)}, u32[]{:S(2)}, u32[]{:S(2)}) async-start(f32[16,56,128]{2,1,0:T(8,128)} %bitcast.7), calls=%async_computation.3 | async-start | bytes 917504 | tf_op jit(solution)/shard_map/all_to_all | solution.py:459
  (49 other events, 2018.6 us)

commit v13 on v8

--- a/solution.py
+++ b/solution.py
@@ -164,6 +164,14 @@
                 out_ref[pl.ds(to * chunk + used, chunk - used), :] = jnp.zeros((chunk - used, LANES), jnp.float32)
 
 
+def move(to_ref, to, from_ref, start, count, step=1):
+    if count < 8:
+        to_ref[pl.ds(to, count), :] = from_ref[pl.ds(start, count, stride=step), :]
+        return
+    for first in [*range(0, count - 7, 8)] + ([count - 8] if count % 8 else []):
+        to_ref[pl.ds(to + first, 8), :] = from_ref[pl.ds(start + first * step, 8, stride=step), :]
+
+
 def potential_kernel(sizes, bunch, place_ref, ion_ref, hxc_ref, out_ref, packed):
     planes, grid, rows, share = sizes
     chunk = chunk_rows(sizes)
@@ -175,7 +183,7 @@
         pack(ion_ref[inner] + hxc_ref[inner], slot)
         for to in range(grid):
             start = to * rows + band * share
-            out_ref[pl.ds(to * chunk + plane * share, share), :] = slot[pl.ds(start, share), :]
+            move(out_ref, to * chunk + plane * share, slot, start, share)
 
 
 def pack_kernel(sizes, bunch, turns, place_ref, psi_ref, *refs):
@@ -189,7 +197,7 @@
             pack(psi_ref[0, part, inner], slot)
             for turn, out_ref in zip(turns, out_refs):
                 start = (mine ^ turn) * rows
-                out_ref[pl.ds((plane * 2 + part) * rows, rows), :] = slot[pl.ds(start, rows), :]
+                move(out_ref, (plane * 2 + part) * rows, slot, start, rows)
 
 
 def plane_kernel(sizes, bunch, turns, place_ref, psi_ref, ion_ref, hxc_ref, kin_ref, *refs):
@@ -209,7 +217,7 @@
             pack(bare + applied[part], slot)
             for turn, out_ref in zip(turns, out_refs):
                 start = (mine ^ turn) * rows
-                out_ref[pl.ds((plane * 2 + part) * rows, rows), :] = slot[pl.ds(start, rows), :]
+                move(out_ref, (plane * 2 + part) * rows, slot, start, rows)
         for part in range(2):
             twice = kinetic(applied[part], kin) + (potential - 1.0) * applied[part]
             turned = applied[1] if part == 0 else -applied[0]
@@ -227,7 +235,7 @@
     for source in range(grid):
         for row in range(share):
             start = source * chunk + row
-            out_ref[pl.ds(row * length + source * planes, planes), :] = moved_ref[pl.ds(start, planes, stride=share), :]
+            move(out_ref, row * length + source * planes, moved_ref, start, planes, share)
 
 
 def along_kernel(sizes, steps, turns, place_ref, *refs):
@@ -241,7 +249,7 @@
         for turn, moved_ref in zip(turns, moved_refs):
             first = (place_ref[0] % grid ^ turn) * planes
             for part in range(2):
-                slot[part, pl.ds(first, planes), :] = moved_ref[pl.ds(part * rows + row, planes, stride=2 * rows), :]
+                move(slot.at[part], first, moved_ref, part * rows + row, planes, 2 * rows)
         field = jnp.concatenate([slot[0], slot[1]], axis=1)
         out_ref[inner * length : (inner + 1) * length, :] = product_of_parts(kin, split(field))
 
@@ -260,7 +268,7 @@
         for turn, mixed_ref in zip(turns, mixed_refs):
             first = (place_ref[0] % grid ^ turn) * planes
             for part in range(2):
-                slot[part, pl.ds(first, planes), :] = mixed_ref[pl.ds(part * rows + row, planes, stride=2 * rows), :]
+                move(slot.at[part], first, mixed_ref, part * rows + row, planes, 2 * rows)
         along = along_ref[here, :]
         again = product_of_parts(kin, split(jnp.concatenate([slot[0], slot[1]], axis=1) + along))
         potential = jnp.where(mine_here, own_ref[here, :], other_ref[here, :])
@@ -290,7 +298,7 @@
             slot = packed.at[inner * 4 + part]
             for source in range(grid):
                 start = ((source * planes + plane) * 2 + part) * rows
-                slot[pl.ds(source * rows, rows), :] = update_ref[pl.ds(start, rows), :]
+                move(slot, source * rows, update_ref, start, rows)
             fresh = base_ref[part, inner] + unpack(slot, length)
             fresh_ref[0, part, inner] = fresh
             part_sum = fresh * fresh if part_sum is None else part_sum + fresh * fresh
@@ -311,7 +319,7 @@
         slot = packed.at[inner * 4 + 3]
         pack(spectrum + jnp.where(first, means[inner] * length, 0.0), slot)
         for to in range(2 * grid):
-            out_ref[pl.ds(to * chunk + plane * share, share), :] = slot[pl.ds(to * share, share), :]
+            move(out_ref, to * chunk + plane * share, slot, to * share, share)
 
 
 def filter_kernel(sizes, spec_ref, cells_ref, tables_ref, upper_ref, lower_ref, lines):
@@ -367,7 +375,7 @@
             side = slot.at[pl.ds(pl.multiple_of(part * half, 8), half), :]
             for source in range(grid):
                 start = source * chunk + plane * share
-                side[pl.ds(source * share, share), :] = spec_ref[pl.ds(start, share), :]
+                move(side, source * share, spec_ref, start, share)
         lines.append(product_of_parts(turn, split(unpack(slot, length))))
     hartree = product_of_parts(split(jnp.concatenate(lines, axis=0)), basis)
     for inner in range(bunch):

time: 401 us -> 401 us (level)
  no operation moved by 1% of the time
where the time goes in v13:
time: 401 us; the launch traced here: 400 us
  waiting for transfers between devices  215 us (54%)
  starting transfers between devices  113 us (28%)
  Pallas kernels  63.9 us (16%)
  local copies, waits for them, and re-layouts  6.87 us (2%)
    all_to_all x4, waiting for transfers between devices, swap(): lax.all_to_all(flat, 'grid', split_axis=0, concat_axis=0)  81.5 us
    ppermute x30, waiting for transfers between devices, send(): lax.ppermute(piece, 'grid', [(spot, spot ^ turn) for spot in range(grid)])  76 us
    ppermute x30, starting transfers between devices, send(): lax.ppermute(piece, 'grid', [(spot, spot ^ turn) for spot in range(grid)])  65.6 us
    all_to_all x1, waiting for transfers between devices, swap_all(): lax.all_to_all(flat, ('band', 'grid'), split_axis=0, concat_axis=0)  41.3 us
    all_to_all x4, starting transfers between devices, swap(): lax.all_to_all(flat, 'grid', split_axis=0, concat_axis=0)  24.9 us
    all_to_all x1, starting transfers between devices, swap_all(): lax.all_to_all(flat, ('band', 'grid'), split_axis=0, concat_axis=0)  17 us
    pallas_call x1, Pallas kernels, packed_path(): pl.pallas_call(functools.partial(plane_kernel, sizes, bunch, turns), grid...  14 us
    pallas_call x1, Pallas kernels, packed_path(): pl.pallas_call(functools.partial(fresh_kernel, sizes, bunch), grid=(plane...  11 us
  transfers between devices with their start and end apart: 40, of which 21 were waited for; matrix products, arithmetic and copies ran while one was open for 0% of the time, Pallas kernels for 9%

profile of v13, /device:TPU:0, one launch (start us, length us, event | category | flops | bytes accessed | tf_op | source)
XLA Modules:
  0.0 400.4 jit_solution(13199862637791151928)
XLA Ops:
  0.6 4.1 %shard_map.86 = f32[1792,128]{1,0:T(8,128)} custom-call(s32[1]{0:T(128)} %bitcast.place_ref, f32[12,192,192]{2,1,0:T(8,128)} %ion_ref.3, f32[12,192,192]{2,1,0:T(8,128)} %hxc_ref.3), custom_call_target="tpu_custom_call" | custom-call | bytes 6291456 | tf_op jit(solution)/shard_map/pallas_call | solution.py:467
  4.8 7.4 %all-to-all-start = ((f32[16,112,128]{2,1,0:T(8,128)}), f32[16,112,128]{2,1,0:T(8,128)S(1)}, u32[]{:S(2)}, u32[]{:S(2)}) async-start(f32[16,112,128]{2,1,0:T(8,128)} %bitcast.22), calls=%async_computation | async-start | bytes 1835008 | tf_op jit(solution)/shard_map/all_to_all | solution.py:457
  12.1 5.4 %shard_map.87 = (f32[432,128]{1,0:T(8,128)}, f32[432,128]{1,0:T(8,128)}, f32[432,128]{1,0:T(8,128)}, f32[432,128]{1,0:T(8,128)}, f32[432,128]{1,0:T(8,128)}, /*i...) custom-call(s32[1]{0:T(128)} %bitcast.place_ref, ...), custom_call_target="tpu_custom_call" | custom-call | bytes 8388608 | tf_op jit(solution)/shard_map/pallas_call | solution.py:479
  17.9 3.5 collective-permute-start.4
  24.4 14.0 %shard_map.88 = (f32[432,128]{1,0:T(8,128)}, f32[432,128]{1,0:T(8,128)}, f32[432,128]{1,0:T(8,128)}, f32[432,128]{1,0:T(8,128)}, f32[432,128]{1,0:T(8,128)}, /*i...) custom-call(s32[1]{0:T(128)} %bitcast.place_ref, ...), custom_call_target="tpu_custom_call" | custom-call | flops 4076863488 | bytes 20971520 | tf_op jit(solution)/shard_map/pallas_call | solution.py:491
  38.4 17.8 %collective-permute-done.4.refs_5_ = f32[432,128]{1,0:T(8,128)S(1)} collective-permute-done((f32[432,128]{1,0:T(8,128)}, f32[432,128]{1,0:T(8,128)S(1)}, u32[]{:S(2)}, u32[]{:S(2)}) %collective-permute-start.4) | collective-permute-done | bytes 221216 | tf_op jit(solution)/shard_map/ppermute | solution.py:452
  62.2 7.4 %collective-permute-done.refs_1_ = f32[432,128]{1,0:T(8,128)S(1)} collective-permute-done((f32[432,128]{1,0:T(8,128)}, f32[432,128]{1,0:T(8,128)S(1)}, u32[]{:S(2)}, u32[]{:S(2)}) %collective-permute-start) | collective-permute-done | bytes 221216 | tf_op jit(solution)/shard_map/ppermute | solution.py:452
  69.8 4.0 %collective-permute-done.9.refs_10_ = f32[432,128]{1,0:T(8,128)S(1)} collective-permute-done((f32[432,128]{1,0:T(8,128)S(1)}, f32[432,128]{1,0:T(8,128)S(1)}, u32[]{:S(2)}, u32[]{:S(2)}) %collective-permute-start.9) | collective-permute-done | bytes 221216 | tf_op jit(solution)/shard_map/ppermute | solution.py:452
  79.3 6.5 %collective-permute-start.12 = (f32[432,128]{1,0:T(8,128)S(1)}, f32[432,128]{1,0:T(8,128)S(1)}, u32[]{:S(2)}, u32[]{:S(2)}) collective-permute-start(f32[432,128]{1,0:T(8,128)S(1)} %copy-done.34), channel_id=1, source_target_pairs={{0,14},{1,15},{2,12},{3,13},{4,10},{5,11},{6,8},{7,9},{8,6},{9,7},... | collective-permute-start | bytes 663560 | tf_op jit(solution)/shard_map/ppermute | solution.py:452
  88.5 6.6 %collective-permute-start.10 = (f32[432,128]{1,0:T(8,128)}, f32[432,128]{1,0:T(8,128)}, u32[]{:S(2)}, u32[]{:S(2)}) collective-permute-start(f32[432,128]{1,0:T(8,128)} %get-tuple-element.93), channel_id=1, source_target_pairs={{0,13},{1,12},{2,15},{3,14},{4,9},{5,8},{6,11},{7,10},{8,5},{9,4},... | collective-permute-start | bytes 663560 | tf_op jit(solution)/shard_map/ppermute | solution.py:452
  95.2 6.7 %collective-permute-start.20 = (f32[432,128]{1,0:T(8,128)}, f32[432,128]{1,0:T(8,128)}, u32[]{:S(2)}, u32[]{:S(2)}) collective-permute-start(f32[432,128]{1,0:T(8,128)} %get-tuple-element.113), channel_id=1, source_target_pairs={{0,10},{1,11},{2,8},{3,9},{4,14},{5,15},{6,12},{7,13},{8,2},{9,3},... | collective-permute-start | bytes 663560 | tf_op jit(solution)/shard_map/ppermute | solution.py:452
  104.6 11.9 %collective-permute-start.18 = (f32[432,128]{1,0:T(8,128)}, f32[432,128]{1,0:T(8,128)}, u32[]{:S(2)}, u32[]{:S(2)}) collective-permute-start(f32[432,128]{1,0:T(8,128)} %get-tuple-element.109), channel_id=1, source_target_pairs={{0,9},{1,8},{2,11},{3,10},{4,13},{5,12},{6,15},{7,14},{8,1},{9,0},... | collective-permute-start | bytes 663560 | tf_op jit(solution)/shard_map/ppermute | solution.py:452
  122.2 8.2 %collective-permute-done.20.refs_5_ = f32[432,128]{1,0:T(8,128)} collective-permute-done((f32[432,128]{1,0:T(8,128)}, f32[432,128]{1,0:T(8,128)}, u32[]{:S(2)}, u32[]{:S(2)}) %collective-permute-start.20) | collective-permute-done | bytes 221216 | tf_op jit(solution)/shard_map/ppermute | solution.py:452
  134.0 9.4 %collective-permute-done.16.refs_1_ = f32[432,128]{1,0:T(8,128)S(1)} collective-permute-done((f32[432,128]{1,0:T(8,128)}, f32[432,128]{1,0:T(8,128)S(1)}, u32[]{:S(2)}, u32[]{:S(2)}) %collective-permute-start.16) | collective-permute-done | bytes 221216 | tf_op jit(solution)/shard_map/ppermute | solution.py:452
  144.0 4.1 %collective-permute-done.24.refs_9_ = f32[432,128]{1,0:T(8,128)S(1)} collective-permute-done((f32[432,128]{1,0:T(8,128)}, f32[432,128]{1,0:T(8,128)S(1)}, u32[]{:S(2)}, u32[]{:S(2)}) %collective-permute-start.24) | collective-permute-done | bytes 221216 | tf_op jit(solution)/shard_map/ppermute | solution.py:452
  155.0 12.4 %collective-permute-done.22.refs_7_ = f32[432,128]{1,0:T(8,128)S(1)} collective-permute-done((f32[432,128]{1,0:T(8,128)}, f32[432,128]{1,0:T(8,128)S(1)}, u32[]{:S(2)}, u32[]{:S(2)}) %collective-permute-start.22) | collective-permute-done | bytes 221216 | tf_op jit(solution)/shard_map/ppermute | solution.py:452
  171.8 6.5 %shard_map.89.along_ref = f32[3456,256]{1,0:T(8,128)} custom-call(s32[1]{0:T(128)} %bitcast.place_ref, f32[432,128]{1,0:T(8,128)} %get-tuple-element.74.refs_0_, f32[432,128]{1,0:T(8,128)} %copy-done.13, f32[432,128]{1,0:T(8,128)} %copy-done.9, f32[432,128]{1,0:T(8,128)} %copy-done.12, f32[432,128]{1,0:T(8,128)} %copy-done.11, f32[432,128]{1,0:T(8,128)} %copy-done.10, ...), custom_call_target="tpu_custom_call" | custom-call | flops 1019215872 | bytes 8388608 | tf_op jit(solution)/shard_map/pallas_call | solution.py:512
  181.5 3.9 collective-permute-done.26.refs_11_
  186.3 9.0 %shard_map.91 = f32[6912,128]{1,0:T(8,128)} custom-call(s32[1]{0:T(128)} %bitcast.place_ref, f32[3456,256]{1,0:T(8,128)} %shard_map.89.along_ref, f32[1728,128]{1,0:T(8,128)} %shard_map.90.own_ref, f32[1728,128]{1,0:T(8,128)} %copy-done.6, f32[192,192]{1,0:T(8,128)} %constant.23.clone.kin_ref.refs_16_, f32[432,128]{1,0:T(8,128)} %get-tuple-element.103.refs_0_, ...), custom_call_target="tpu_custom_call" | custom-call | flops 1019215872 | bytes 14680064 | tf_op jit(solution)/shard_map/pallas_call | solution.py:524
  195.3 10.2 %all-to-all-start.1 = ((f32[16,432,128]{2,1,0:T(8,128)}), f32[16,432,128]{2,1,0:T(8,128)S(1)}, u32[]{:S(2)}, u32[]{:S(2)}) async-start(f32[16,432,128]{2,1,0:T(8,128)} %bitcast.19), calls=%async_computation.1 | async-start | bytes 7077888 | tf_op jit(solution)/shard_map/all_to_all | solution.py:457
  206.2 65.6 %all-to-all-done.1 = f32[16,432,128]{2,1,0:T(8,128)S(1)} async-done(((f32[16,432,128]{2,1,0:T(8,128)}), f32[16,432,128]{2,1,0:T(8,128)S(1)}, u32[]{:S(2)}, u32[]{:S(2)}) %all-to-all-start.1) | async-done | bytes 3538976 | tf_op jit(solution)/shard_map/all_to_all | solution.py:457
  273.6 11.0 %shard_map.92 = (f32[1,2,12,192,192]{4,3,2,1,0:T(8,128)}, f32[1728,128]{1,0:T(8,128)}, f32[1728,128]{1,0:T(8,128)}, f32[3584,128]{1,0:T(8,128)}) custom-call(f32[1]{0:T(128)S(6)} %copy.14.occ_ref, f32[6912,128]{1,0:T(8,128)} %bitcast.20, f32[2,12,192,192]{3,2,1,0:T(8,128)} %get-tuple-element.82.base_ref, f32[2,192,192]{2,1,0:T(8,128)} %constant.24.clone.tables_ref), custom_call_target="tpu_custom_call" | custom-call | flops 2038431744 | bytes 16777216 | tf_op jit(solution)/shard_map/pallas_call | solution.py:543
  284.6 17.0 %all-to-all-start.2 = ((f32[32,112,128]{2,1,0:T(8,128)}), f32[32,112,128]{2,1,0:T(8,128)S(1)}, u32[]{:S(2)}, u32[]{:S(2)}) async-start(f32[32,112,128]{2,1,0:T(8,128)} %bitcast.25), calls=%async_computation.2 | async-start | bytes 3670016 | tf_op jit(solution)/shard_map/all_to_all | solution.py:461
  304.5 41.3 %all-to-all-done.2 = f32[32,112,128]{2,1,0:T(8,128)S(1)} async-done(((f32[32,112,128]{2,1,0:T(8,128)}), f32[32,112,128]{2,1,0:T(8,128)S(1)}, u32[]{:S(2)}, u32[]{:S(2)}) %all-to-all-start.2) | async-done | bytes 1835040 | tf_op jit(solution)/shard_map/all_to_all | solution.py:461
  348.9 3.6 all-to-all-start.4
  352.5 9.6 %collective-permute-done.31.lower_other = f32[1728,128]{1,0:T(8,128)} collective-permute-done((f32[1728,128]{1,0:T(8,128)}, f32[1728,128]{1,0:T(8,128)}, u32[]{:S(2)}, u32[]{:S(2)}) %collective-permute-start.31) | collective-permute-done | bytes 884768 | tf_op jit(solution)/shard_map/ppermute | solution.py:564
  362.1 3.6 all-to-all-done.4
  365.7 3.8 all-to-all-start.3
  370.5 12.3 %all-to-all-done.3 = f32[16,56,128]{2,1,0:T(8,128)S(1)} async-done(((f32[16,56,128]{2,1,0:T(8,128)}), f32[16,56,128]{2,1,0:T(8,128)S(1)}, u32[]{:S(2)}, u32[]{:S(2)}) %all-to-all-start.3) | async-done | bytes 458784 | tf_op jit(solution)/shard_map/all_to_all | solution.py:457
  384.4 4.3 %shard_map.94.refs_0_ = f32[12,192,192]{2,1,0:T(8,128)} custom-call(s32[1]{0:T(128)} %bitcast.place_ref, f32[896,128]{1,0:T(8,128)} %bitcast.24, f32[896,128]{1,0:T(8,128)} %copy-done.7, f32[1728,128]{1,0:T(8,128)} %get-tuple-element.139.upper_ref, f32[1728,128]{1,0:T(8,128)} %get-tuple-element.137.lower_ref, ...), custom_call_target="tpu_custom_call" | custom-call | flops 509607936 | bytes 4194304 | tf_op jit(solution)/shard_map/pallas_call | solution.py:586
  388.7 6.6 %collective-permute-done.32.far_ref = f32[896,128]{1,0:T(8,128)S(1)} collective-permute-done((f32[896,128]{1,0:T(8,128)S(1)}, f32[896,128]{1,0:T(8,128)S(1)}, u32[]{:S(2)}, u32[]{:S(2)}) %collective-permute-start.32) | collective-permute-done | bytes 458784 | tf_op jit(solution)/shard_map/ppermute | solution.py:606
  396.1 4.3 %shard_map.95 = f32[12,192,192]{2,1,0:T(8,128)} custom-call(s32[1]{0:T(128)} %bitcast.place_ref, f32[896,128]{1,0:T(8,128)} %bitcast.27, f32[896,128]{1,0:T(8,128)} %copy-done.8, f32[1728,128]{1,0:T(8,128)} %get-tuple-element.139.upper_ref, f32[1728,128]{1,0:T(8,128)} %get-tuple-element.137.lower_ref, ...), custom_call_target="tpu_custom_call", output_to_operand_aliasing={{}: (8, {})} | custom-call | flops 509607936 | bytes 4194304 | tf_op jit(solution)/shard_map/pallas_call | solution.py:586
  (144 shorter events, 57.0 us)
Async XLA Ops:
  4.8 111.7 %all-to-all-start = ((f32[16,112,128]{2,1,0:T(8,128)}), f32[16,112,128]{2,1,0:T(8,128)S(1)}, u32[]{:S(2)}, u32[]{:S(2)}) async-start(f32[16,112,128]{2,1,0:T(8,128)} %bitcast.22), calls=%async_computation | async-start | bytes 1835008 | tf_op jit(solution)/shard_map/all_to_all | solution.py:457
  17.9 38.3 %collective-permute-start.4 = (f32[432,128]{1,0:T(8,128)}, f32[432,128]{1,0:T(8,128)S(1)}, u32[]{:S(2)}, u32[]{:S(2)}) collective-permute-start(f32[432,128]{1,0:T(8,128)} %get-tuple-element.79), channel_id=1, source_target_pairs={{0,10},{1,11},{2,8},{3,9},{4,14},{5,15},{6,12},{7,13},{8,2},{9,3},... | collective-permute-start | bytes 663560 | tf_op jit(solution)/shard_map/ppermute | solution.py:452
  21.4 34.8 %collective-permute-start.3 = (f32[432,128]{1,0:T(8,128)}, f32[432,128]{1,0:T(8,128)S(1)}, u32[]{:S(2)}, u32[]{:S(2)}) collective-permute-start(f32[432,128]{1,0:T(8,128)} %get-tuple-element.78), channel_id=1, source_target_pairs={{0,2},{1,3},{2,0},{3,1},{4,6},{5,7},{6,4},{7,5},{8,10},{9,11},{10,... | collective-permute-start | bytes 663560 | tf_op jit(solution)/shard_map/ppermute | solution.py:452
  22.0 37.2 %collective-permute-start.2 = (f32[432,128]{1,0:T(8,128)}, f32[432,128]{1,0:T(8,128)S(1)}, u32[]{:S(2)}, u32[]{:S(2)}) collective-permute-start(f32[432,128]{1,0:T(8,128)} %get-tuple-element.77), channel_id=1, source_target_pairs={{0,9},{1,8},{2,11},{3,10},{4,13},{5,12},{6,15},{7,14},{8,1},{9,0},... | collective-permute-start | bytes 663560 | tf_op jit(solution)/shard_map/ppermute | solution.py:452
  22.0 47.5 %collective-permute-start = (f32[432,128]{1,0:T(8,128)}, f32[432,128]{1,0:T(8,128)S(1)}, u32[]{:S(2)}, u32[]{:S(2)}) collective-permute-start(f32[432,128]{1,0:T(8,128)} %get-tuple-element.75), channel_id=1, source_target_pairs={{0,8},{1,9},{2,10},{3,11},{4,12},{5,13},{6,14},{7,15},{8,0},{9,1},... | collective-permute-start | bytes 663560 | tf_op jit(solution)/shard_map/ppermute | solution.py:452
  56.2 17.6 %collective-permute-start.9 = (f32[432,128]{1,0:T(8,128)S(1)}, f32[432,128]{1,0:T(8,128)S(1)}, u32[]{:S(2)}, u32[]{:S(2)}) collective-permute-start(f32[432,128]{1,0:T(8,128)S(1)} %copy-done.41), channel_id=1, source_target_pairs={{0,5},{1,4},{2,7},{3,6},{4,1},{5,0},{6,3},{7,2},{8,13},{9,12},{10,... | collective-permute-start | bytes 663560 | tf_op jit(solution)/shard_map/ppermute | solution.py:452
  56.3 19.6 %collective-permute-start.8 = (f32[432,128]{1,0:T(8,128)S(1)}, f32[432,128]{1,0:T(8,128)S(1)}, u32[]{:S(2)}, u32[]{:S(2)}) collective-permute-start(f32[432,128]{1,0:T(8,128)S(1)} %copy-done.40), channel_id=1, source_target_pairs={{0,12},{1,13},{2,14},{3,15},{4,8},{5,9},{6,10},{7,11},{8,4},{9,5},... | collective-permute-start | bytes 663560 | tf_op jit(solution)/shard_map/ppermute | solution.py:452
  59.2 20.1 %collective-permute-start.7 = (f32[432,128]{1,0:T(8,128)S(1)}, f32[432,128]{1,0:T(8,128)S(1)}, u32[]{:S(2)}, u32[]{:S(2)}) collective-permute-start(f32[432,128]{1,0:T(8,128)S(1)} %copy-done.39), channel_id=1, source_target_pairs={{0,4},{1,5},{2,6},{3,7},{4,0},{5,1},{6,2},{7,3},{8,12},{9,13},{10,... | collective-permute-start | bytes 663560 | tf_op jit(solution)/shard_map/ppermute | solution.py:452
  59.2 29.3 %collective-permute-start.6 = (f32[432,128]{1,0:T(8,128)S(1)}, f32[432,128]{1,0:T(8,128)S(1)}, u32[]{:S(2)}, u32[]{:S(2)}) collective-permute-start(f32[432,128]{1,0:T(8,128)S(1)} %copy-done.38), channel_id=1, source_target_pairs={{0,11},{1,10},{2,9},{3,8},{4,15},{5,14},{6,13},{7,12},{8,3},{9,2},... | collective-permute-start | bytes 663560 | tf_op jit(solution)/shard_map/ppermute | solution.py:452
  69.6 18.9 %collective-permute-start.5 = (f32[432,128]{1,0:T(8,128)S(1)}, f32[432,128]{1,0:T(8,128)S(1)}, u32[]{:S(2)}, u32[]{:S(2)}) collective-permute-start(f32[432,128]{1,0:T(8,128)S(1)} %copy-done.37), channel_id=1, source_target_pairs={{0,3},{1,2},{2,1},{3,0},{4,7},{5,6},{6,5},{7,4},{8,11},{9,10},{10,... | collective-permute-start | bytes 663560 | tf_op jit(solution)/shard_map/ppermute | solution.py:452
  73.9 21.3 %collective-permute-start.14 = (f32[432,128]{1,0:T(8,128)S(1)}, f32[432,128]{1,0:T(8,128)S(1)}, u32[]{:S(2)}, u32[]{:S(2)}) collective-permute-start(f32[432,128]{1,0:T(8,128)S(1)} %copy-done.36), channel_id=1, source_target_pairs={{0,15},{1,14},{2,13},{3,12},{4,11},{5,10},{6,9},{7,8},{8,7},{9,6},... | collective-permute-start | bytes 663560 | tf_op jit(solution)/shard_map/ppermute | solution.py:452
  75.8 26.0 %collective-permute-start.13 = (f32[432,128]{1,0:T(8,128)S(1)}, f32[432,128]{1,0:T(8,128)S(1)}, u32[]{:S(2)}, u32[]{:S(2)}) collective-permute-start(f32[432,128]{1,0:T(8,128)S(1)} %copy-done.35), channel_id=1, source_target_pairs={{0,7},{1,6},{2,5},{3,4},{4,3},{5,2},{6,1},{7,0},{8,15},{9,14},{10,... | collective-permute-start | bytes 663560 | tf_op jit(solution)/shard_map/ppermute | solution.py:452
  79.3 24.6 %collective-permute-start.12 = (f32[432,128]{1,0:T(8,128)S(1)}, f32[432,128]{1,0:T(8,128)S(1)}, u32[]{:S(2)}, u32[]{:S(2)}) collective-permute-start(f32[432,128]{1,0:T(8,128)S(1)} %copy-done.34), channel_id=1, source_target_pairs={{0,14},{1,15},{2,12},{3,13},{4,10},{5,11},{6,8},{7,9},{8,6},{9,7},... | collective-permute-start | bytes 663560 | tf_op jit(solution)/shard_map/ppermute | solution.py:452
  88.5 31.1 %collective-permute-start.11 = (f32[432,128]{1,0:T(8,128)}, f32[432,128]{1,0:T(8,128)}, u32[]{:S(2)}, u32[]{:S(2)}) collective-permute-start(f32[432,128]{1,0:T(8,128)} %get-tuple-element.95), channel_id=1, source_target_pairs={{0,6},{1,7},{2,4},{3,5},{4,2},{5,3},{6,0},{7,1},{8,14},{9,15},{10,... | collective-permute-start | bytes 663560 | tf_op jit(solution)/shard_map/ppermute | solution.py:452
  88.5 32.6 %collective-permute-start.10 = (f32[432,128]{1,0:T(8,128)}, f32[432,128]{1,0:T(8,128)}, u32[]{:S(2)}, u32[]{:S(2)}) collective-permute-start(f32[432,128]{1,0:T(8,128)} %get-tuple-element.93), channel_id=1, source_target_pairs={{0,13},{1,12},{2,15},{3,14},{4,9},{5,8},{6,11},{7,10},{8,5},{9,4},... | collective-permute-start | bytes 663560 | tf_op jit(solution)/shard_map/ppermute | solution.py:452
  95.2 35.2 %collective-permute-start.20 = (f32[432,128]{1,0:T(8,128)}, f32[432,128]{1,0:T(8,128)}, u32[]{:S(2)}, u32[]{:S(2)}) collective-permute-start(f32[432,128]{1,0:T(8,128)} %get-tuple-element.113), channel_id=1, source_target_pairs={{0,10},{1,11},{2,8},{3,9},{4,14},{5,15},{6,12},{7,13},{8,2},{9,3},... | collective-permute-start | bytes 663560 | tf_op jit(solution)/shard_map/ppermute | solution.py:452
  101.8 28.6 %collective-permute-start.19 = (f32[432,128]{1,0:T(8,128)}, f32[432,128]{1,0:T(8,128)}, u32[]{:S(2)}, u32[]{:S(2)}) collective-permute-start(f32[432,128]{1,0:T(8,128)} %get-tuple-element.111), channel_id=1, source_target_pairs={{0,2},{1,3},{2,0},{3,1},{4,6},{5,7},{6,4},{7,5},{8,10},{9,11},{10,... | collective-permute-start | bytes 663560 | tf_op jit(solution)/shard_map/ppermute | solution.py:452
  104.6 26.9 %collective-permute-start.18 = (f32[432,128]{1,0:T(8,128)}, f32[432,128]{1,0:T(8,128)}, u32[]{:S(2)}, u32[]{:S(2)}) collective-permute-start(f32[432,128]{1,0:T(8,128)} %get-tuple-element.109), channel_id=1, source_target_pairs={{0,9},{1,8},{2,11},{3,10},{4,13},{5,12},{6,15},{7,14},{8,1},{9,0},... | collective-permute-start | bytes 663560 | tf_op jit(solution)/shard_map/ppermute | solution.py:452
  119.6 65.7 %collective-permute-start.15 = (f32[1728,128]{1,0:T(8,128)}, f32[1728,128]{1,0:T(8,128)S(1)}, u32[]{:S(2)}, u32[]{:S(2)}) collective-permute-start(f32[1728,128]{1,0:T(8,128)} %shard_map.90.own_ref), channel_id=1, source_target_pairs={{0,16},{16,0},{1,17},{17,1},{2,18},{18,2},{3,19},{19,3},{4,20},{20... | collective-permute-start | bytes 2654216 | tf_op jit(solution)/shard_map/ppermute | solution.py:511
  131.5 16.6 %collective-permute-start.24 = (f32[432,128]{1,0:T(8,128)}, f32[432,128]{1,0:T(8,128)S(1)}, u32[]{:S(2)}, u32[]{:S(2)}) collective-permute-start(f32[432,128]{1,0:T(8,128)} %get-tuple-element.121), channel_id=1, source_target_pairs={{0,12},{1,13},{2,14},{3,15},{4,8},{5,9},{6,10},{7,11},{8,4},{9,5},... | collective-permute-start | bytes 663560 | tf_op jit(solution)/shard_map/ppermute | solution.py:452
  133.3 19.2 %collective-permute-start.23 = (f32[432,128]{1,0:T(8,128)}, f32[432,128]{1,0:T(8,128)S(1)}, u32[]{:S(2)}, u32[]{:S(2)}) collective-permute-start(f32[432,128]{1,0:T(8,128)} %get-tuple-element.119), channel_id=1, source_target_pairs={{0,4},{1,5},{2,6},{3,7},{4,0},{5,1},{6,2},{7,3},{8,12},{9,13},{10,... | collective-permute-start | bytes 663560 | tf_op jit(solution)/shard_map/ppermute | solution.py:452
  143.4 24.0 %collective-permute-start.22 = (f32[432,128]{1,0:T(8,128)}, f32[432,128]{1,0:T(8,128)S(1)}, u32[]{:S(2)}, u32[]{:S(2)}) collective-permute-start(f32[432,128]{1,0:T(8,128)} %get-tuple-element.117), channel_id=1, source_target_pairs={{0,11},{1,10},{2,9},{3,8},{4,15},{5,14},{6,13},{7,12},{8,3},{9,2},... | collective-permute-start | bytes 663560 | tf_op jit(solution)/shard_map/ppermute | solution.py:452
  143.5 25.5 %collective-permute-start.21 = (f32[432,128]{1,0:T(8,128)}, f32[432,128]{1,0:T(8,128)S(1)}, u32[]{:S(2)}, u32[]{:S(2)}) collective-permute-start(f32[432,128]{1,0:T(8,128)} %get-tuple-element.115), channel_id=1, source_target_pairs={{0,3},{1,2},{2,1},{3,0},{4,7},{5,6},{6,5},{7,4},{8,11},{9,10},{10,... | collective-permute-start | bytes 663560 | tf_op jit(solution)/shard_map/ppermute | solution.py:452
  148.1 20.9 %collective-permute-start.30 = (f32[432,128]{1,0:T(8,128)}, f32[432,128]{1,0:T(8,128)S(1)}, u32[]{:S(2)}, u32[]{:S(2)}) collective-permute-start(f32[432,128]{1,0:T(8,128)} %get-tuple-element.133), channel_id=1, source_target_pairs={{0,15},{1,14},{2,13},{3,12},{4,11},{5,10},{6,9},{7,8},{8,7},{9,6},... | collective-permute-start | bytes 663560 | tf_op jit(solution)/shard_map/ppermute | solution.py:452
  152.5 25.8 %collective-permute-start.29 = (f32[432,128]{1,0:T(8,128)}, f32[432,128]{1,0:T(8,128)S(1)}, u32[]{:S(2)}, u32[]{:S(2)}) collective-permute-start(f32[432,128]{1,0:T(8,128)} %get-tuple-element.131), channel_id=1, source_target_pairs={{0,7},{1,6},{2,5},{3,4},{4,3},{5,2},{6,1},{7,0},{8,15},{9,14},{10,... | collective-permute-start | bytes 663560 | tf_op jit(solution)/shard_map/ppermute | solution.py:452
  169.0 16.4 %collective-permute-start.26 = (f32[432,128]{1,0:T(8,128)}, f32[432,128]{1,0:T(8,128)S(1)}, u32[]{:S(2)}, u32[]{:S(2)}) collective-permute-start(f32[432,128]{1,0:T(8,128)} %get-tuple-element.125), channel_id=1, source_target_pairs={{0,13},{1,12},{2,15},{3,14},{4,9},{5,8},{6,11},{7,10},{8,5},{9,4},... | collective-permute-start | bytes 663560 | tf_op jit(solution)/shard_map/ppermute | solution.py:452
  195.3 76.4 %all-to-all-start.1 = ((f32[16,432,128]{2,1,0:T(8,128)}), f32[16,432,128]{2,1,0:T(8,128)S(1)}, u32[]{:S(2)}, u32[]{:S(2)}) async-start(f32[16,432,128]{2,1,0:T(8,128)} %bitcast.19), calls=%async_computation.1 | async-start | bytes 7077888 | tf_op jit(solution)/shard_map/all_to_all | solution.py:457
  284.6 61.2 %all-to-all-start.2 = ((f32[32,112,128]{2,1,0:T(8,128)}), f32[32,112,128]{2,1,0:T(8,128)S(1)}, u32[]{:S(2)}, u32[]{:S(2)}) async-start(f32[32,112,128]{2,1,0:T(8,128)} %bitcast.25), calls=%async_computation.2 | async-start | bytes 3670016 | tf_op jit(solution)/shard_map/all_to_all | solution.py:461
  301.6 47.3 %collective-permute-start.33 = (f32[1728,128]{1,0:T(8,128)S(1)}, f32[1728,128]{1,0:T(8,128)}, u32[]{:S(2)}, u32[]{:S(2)}) collective-permute-start(f32[1728,128]{1,0:T(8,128)S(1)} %copy-done.3), channel_id=1, source_target_pairs={{0,16},{16,0},{1,17},{17,1},{2,18},{18,2},{3,19},{19,3},{4,20},{20... | collective-permute-start | bytes 2654216 | tf_op jit(solution)/shard_map/ppermute | solution.py:563
  304.2 58.0 %collective-permute-start.31 = (f32[1728,128]{1,0:T(8,128)}, f32[1728,128]{1,0:T(8,128)}, u32[]{:S(2)}, u32[]{:S(2)}) collective-permute-start(f32[1728,128]{1,0:T(8,128)} %get-tuple-element.137.lower_ref), channel_id=1, source_target_pairs={{0,16},{16,0},{1,17},{17,1},{2,18},{18,2},{3,19},{19,3},{4,20},{20... | collective-permute-start | bytes 2654216 | tf_op jit(solution)/shard_map/ppermute | solution.py:564
  348.9 16.8 %all-to-all-start.4 = ((f32[16,56,128]{2,1,0:T(8,128)}), f32[16,56,128]{2,1,0:T(8,128)S(1)}, u32[]{:S(2)}, u32[]{:S(2)}) async-start(f32[16,56,128]{2,1,0:T(8,128)} %bitcast.9), calls=%async_computation.4 | async-start | bytes 917504 | tf_op jit(solution)/shard_map/all_to_all | solution.py:457
  365.7 17.1 %all-to-all-start.3 = ((f32[16,56,128]{2,1,0:T(8,128)}), f32[16,56,128]{2,1,0:T(8,128)S(1)}, u32[]{:S(2)}, u32[]{:S(2)}) async-start(f32[16,56,128]{2,1,0:T(8,128)} %bitcast.7), calls=%async_computation.3 | async-start | bytes 917504 | tf_op jit(solution)/shard_map/all_to_all | solution.py:457
  (50 other events, 1835.0 us)

commit v14 on v13

--- a/solution.py
+++ b/solution.py
@@ -594,7 +594,7 @@
             out_shape=shape(planes, length, length),
             scratch_shapes=scratch(2),
             input_output_aliases={8: 0} if made else {},
-            compiler_params=PARAMS,
+            compiler_params=SMALL,
             cost_estimate=cost(3 * work, 4 << 20),
         )(place, near, far, upper, lower, upper_other, lower_other, tables, *made)
 

time: 401 us -> 403 us (level)
  no operation moved by 1% of the time
where the time goes in v14:
time: 403 us; the launch traced here: 402 us
  waiting for transfers between devices  217 us (54%)
  starting transfers between devices  113 us (28%)
  Pallas kernels  63.3 us (16%)
  local copies, waits for them, and re-layouts  6.86 us (2%)
    all_to_all x4, waiting for transfers between devices, swap(): lax.all_to_all(flat, 'grid', split_axis=0, concat_axis=0)  83.7 us
    ppermute x30, waiting for transfers between devices, send(): lax.ppermute(piece, 'grid', [(spot, spot ^ turn) for spot in range(grid)])  76 us
    ppermute x30, starting transfers between devices, send(): lax.ppermute(piece, 'grid', [(spot, spot ^ turn) for spot in range(grid)])  65.6 us
    all_to_all x1, waiting for transfers between devices, swap_all(): lax.all_to_all(flat, ('band', 'grid'), split_axis=0, concat_axis=0)  41.3 us
    all_to_all x4, starting transfers between devices, swap(): lax.all_to_all(flat, 'grid', split_axis=0, concat_axis=0)  25.3 us
    all_to_all x1, starting transfers between devices, swap_all(): lax.all_to_all(flat, ('band', 'grid'), split_axis=0, concat_axis=0)  17.1 us
    pallas_call x1, Pallas kernels, packed_path(): pl.pallas_call(functools.partial(plane_kernel, sizes, bunch, turns), grid...  14 us
    pallas_call x1, Pallas kernels, packed_path(): pl.pallas_call(functools.partial(fresh_kernel, sizes, bunch), grid=(plane...  11 us
  transfers between devices with their start and end apart: 40, of which 21 were waited for; matrix products, arithmetic and copies ran while one was open for 0% of the time, Pallas kernels for 9%

profile of v14, /device:TPU:0, one launch (start us, length us, event | category | flops | bytes accessed | tf_op | source)
XLA Modules:
  0.0 401.9 jit_solution(7941120214253947847)
XLA Ops:
  0.6 4.1 %shard_map.86 = f32[1792,128]{1,0:T(8,128)} custom-call(s32[1]{0:T(128)} %bitcast.place_ref, f32[12,192,192]{2,1,0:T(8,128)} %ion_ref.3, f32[12,192,192]{2,1,0:T(8,128)} %hxc_ref.3), custom_call_target="tpu_custom_call" | custom-call | bytes 6291456 | tf_op jit(solution)/shard_map/pallas_call | solution.py:467
  4.8 7.4 %all-to-all-start = ((f32[16,112,128]{2,1,0:T(8,128)}), f32[16,112,128]{2,1,0:T(8,128)S(1)}, u32[]{:S(2)}, u32[]{:S(2)}) async-start(f32[16,112,128]{2,1,0:T(8,128)} %bitcast.25), calls=%async_computation | async-start | bytes 1835008 | tf_op jit(solution)/shard_map/all_to_all | solution.py:457
  12.1 5.4 %shard_map.87 = (f32[432,128]{1,0:T(8,128)}, f32[432,128]{1,0:T(8,128)}, f32[432,128]{1,0:T(8,128)}, f32[432,128]{1,0:T(8,128)}, f32[432,128]{1,0:T(8,128)}, /*i...) custom-call(s32[1]{0:T(128)} %bitcast.place_ref, ...), custom_call_target="tpu_custom_call" | custom-call | bytes 8388608 | tf_op jit(solution)/shard_map/pallas_call | solution.py:479
  24.4 14.0 %shard_map.88 = (f32[432,128]{1,0:T(8,128)}, f32[432,128]{1,0:T(8,128)}, f32[432,128]{1,0:T(8,128)}, f32[432,128]{1,0:T(8,128)}, f32[432,128]{1,0:T(8,128)}, /*i...) custom-call(s32[1]{0:T(128)} %bitcast.place_ref, ...), custom_call_target="tpu_custom_call" | custom-call | flops 4076863488 | bytes 20971520 | tf_op jit(solution)/shard_map/pallas_call | solution.py:491
  38.4 17.8 %collective-permute-done.4.refs_5_ = f32[432,128]{1,0:T(8,128)S(1)} collective-permute-done((f32[432,128]{1,0:T(8,128)}, f32[432,128]{1,0:T(8,128)S(1)}, u32[]{:S(2)}, u32[]{:S(2)}) %collective-permute-start.4) | collective-permute-done | bytes 221216 | tf_op jit(solution)/shard_map/ppermute | solution.py:452
  62.2 7.4 %collective-permute-done.refs_1_ = f32[432,128]{1,0:T(8,128)S(1)} collective-permute-done((f32[432,128]{1,0:T(8,128)}, f32[432,128]{1,0:T(8,128)S(1)}, u32[]{:S(2)}, u32[]{:S(2)}) %collective-permute-start) | collective-permute-done | bytes 221216 | tf_op jit(solution)/shard_map/ppermute | solution.py:452
  69.8 4.0 %collective-permute-done.9.refs_10_ = f32[432,128]{1,0:T(8,128)S(1)} collective-permute-done((f32[432,128]{1,0:T(8,128)S(1)}, f32[432,128]{1,0:T(8,128)S(1)}, u32[]{:S(2)}, u32[]{:S(2)}) %collective-permute-start.9) | collective-permute-done | bytes 221216 | tf_op jit(solution)/shard_map/ppermute | solution.py:452
  79.3 6.5 %collective-permute-start.12 = (f32[432,128]{1,0:T(8,128)S(1)}, f32[432,128]{1,0:T(8,128)S(1)}, u32[]{:S(2)}, u32[]{:S(2)}) collective-permute-start(f32[432,128]{1,0:T(8,128)S(1)} %copy-done.33), channel_id=1, source_target_pairs={{0,14},{1,15},{2,12},{3,13},{4,10},{5,11},{6,8},{7,9},{8,6},{9,7},... | collective-permute-start | bytes 663560 | tf_op jit(solution)/shard_map/ppermute | solution.py:452
  88.5 6.6 %collective-permute-start.10 = (f32[432,128]{1,0:T(8,128)}, f32[432,128]{1,0:T(8,128)}, u32[]{:S(2)}, u32[]{:S(2)}) collective-permute-start(f32[432,128]{1,0:T(8,128)} %get-tuple-element.93), channel_id=1, source_target_pairs={{0,13},{1,12},{2,15},{3,14},{4,9},{5,8},{6,11},{7,10},{8,5},{9,4},... | collective-permute-start | bytes 663560 | tf_op jit(solution)/shard_map/ppermute | solution.py:452
  95.2 6.7 %collective-permute-start.20 = (f32[432,128]{1,0:T(8,128)}, f32[432,128]{1,0:T(8,128)}, u32[]{:S(2)}, u32[]{:S(2)}) collective-permute-start(f32[432,128]{1,0:T(8,128)} %get-tuple-element.113), channel_id=1, source_target_pairs={{0,10},{1,11},{2,8},{3,9},{4,14},{5,15},{6,12},{7,13},{8,2},{9,3},... | collective-permute-start | bytes 663560 | tf_op jit(solution)/shard_map/ppermute | solution.py:452
  104.6 11.9 %collective-permute-start.18 = (f32[432,128]{1,0:T(8,128)}, f32[432,128]{1,0:T(8,128)}, u32[]{:S(2)}, u32[]{:S(2)}) collective-permute-start(f32[432,128]{1,0:T(8,128)} %get-tuple-element.109), channel_id=1, source_target_pairs={{0,9},{1,8},{2,11},{3,10},{4,13},{5,12},{6,15},{7,14},{8,1},{9,0},... | collective-permute-start | bytes 663560 | tf_op jit(solution)/shard_map/ppermute | solution.py:452
  122.2 8.2 %collective-permute-done.20.refs_5_ = f32[432,128]{1,0:T(8,128)} collective-permute-done((f32[432,128]{1,0:T(8,128)}, f32[432,128]{1,0:T(8,128)}, u32[]{:S(2)}, u32[]{:S(2)}) %collective-permute-start.20) | collective-permute-done | bytes 221216 | tf_op jit(solution)/shard_map/ppermute | solution.py:452
  134.0 9.4 %collective-permute-done.16.refs_1_ = f32[432,128]{1,0:T(8,128)S(1)} collective-permute-done((f32[432,128]{1,0:T(8,128)}, f32[432,128]{1,0:T(8,128)S(1)}, u32[]{:S(2)}, u32[]{:S(2)}) %collective-permute-start.16) | collective-permute-done | bytes 221216 | tf_op jit(solution)/shard_map/ppermute | solution.py:452
  144.0 4.1 %collective-permute-done.24.refs_9_ = f32[432,128]{1,0:T(8,128)S(1)} collective-permute-done((f32[432,128]{1,0:T(8,128)}, f32[432,128]{1,0:T(8,128)S(1)}, u32[]{:S(2)}, u32[]{:S(2)}) %collective-permute-start.24) | collective-permute-done | bytes 221216 | tf_op jit(solution)/shard_map/ppermute | solution.py:452
  155.0 12.4 %collective-permute-done.22.refs_7_ = f32[432,128]{1,0:T(8,128)S(1)} collective-permute-done((f32[432,128]{1,0:T(8,128)}, f32[432,128]{1,0:T(8,128)S(1)}, u32[]{:S(2)}, u32[]{:S(2)}) %collective-permute-start.22) | collective-permute-done | bytes 221216 | tf_op jit(solution)/shard_map/ppermute | solution.py:452
  171.8 6.5 %shard_map.89.along_ref = f32[3456,256]{1,0:T(8,128)} custom-call(s32[1]{0:T(128)} %bitcast.place_ref, f32[432,128]{1,0:T(8,128)} %get-tuple-element.74.refs_0_, f32[432,128]{1,0:T(8,128)} %copy-done.12, f32[432,128]{1,0:T(8,128)} %copy-done.8, f32[432,128]{1,0:T(8,128)} %copy-done.11, f32[432,128]{1,0:T(8,128)} %copy-done.10, f32[432,128]{1,0:T(8,128)} %copy-done.9, ...), custom_call_target="tpu_custom_call" | custom-call | flops 1019215872 | bytes 8388608 | tf_op jit(solution)/shard_map/pallas_call | solution.py:512
  181.5 3.9 collective-permute-done.26.refs_11_
  186.3 9.0 %shard_map.91 = f32[6912,128]{1,0:T(8,128)} custom-call(s32[1]{0:T(128)} %bitcast.place_ref, f32[3456,256]{1,0:T(8,128)} %shard_map.89.along_ref, f32[1728,128]{1,0:T(8,128)} %shard_map.90.own_ref, f32[1728,128]{1,0:T(8,128)} %copy-done.7, f32[192,192]{1,0:T(8,128)} %constant.23.clone.kin_ref.refs_16_, f32[432,128]{1,0:T(8,128)} %get-tuple-element.103.refs_0_, ...), custom_call_target="tpu_custom_call" | custom-call | flops 1019215872 | bytes 14680064 | tf_op jit(solution)/shard_map/pallas_call | solution.py:524
  195.3 10.2 %all-to-all-start.1 = ((f32[16,432,128]{2,1,0:T(8,128)}), f32[16,432,128]{2,1,0:T(8,128)S(1)}, u32[]{:S(2)}, u32[]{:S(2)}) async-start(f32[16,432,128]{2,1,0:T(8,128)} %bitcast.22), calls=%async_computation.1 | async-start | bytes 7077888 | tf_op jit(solution)/shard_map/all_to_all | solution.py:457
  206.2 65.6 %all-to-all-done.1 = f32[16,432,128]{2,1,0:T(8,128)S(1)} async-done(((f32[16,432,128]{2,1,0:T(8,128)}), f32[16,432,128]{2,1,0:T(8,128)S(1)}, u32[]{:S(2)}, u32[]{:S(2)}) %all-to-all-start.1) | async-done | bytes 3538976 | tf_op jit(solution)/shard_map/all_to_all | solution.py:457
  273.6 11.0 %shard_map.92 = (f32[1,2,12,192,192]{4,3,2,1,0:T(8,128)}, f32[1728,128]{1,0:T(8,128)}, f32[1728,128]{1,0:T(8,128)}, f32[3584,128]{1,0:T(8,128)}) custom-call(f32[1]{0:T(128)S(6)} %copy.14.occ_ref, f32[6912,128]{1,0:T(8,128)} %bitcast.23, f32[2,12,192,192]{3,2,1,0:T(8,128)} %get-tuple-element.82.base_ref, f32[2,192,192]{2,1,0:T(8,128)} %constant.24.clone.tables_ref), custom_call_target="tpu_custom_call" | custom-call | flops 2038431744 | bytes 16777216 | tf_op jit(solution)/shard_map/pallas_call | solution.py:543
  284.6 17.1 %all-to-all-start.2 = ((f32[32,112,128]{2,1,0:T(8,128)}), f32[32,112,128]{2,1,0:T(8,128)}, u32[]{:S(2)}, u32[]{:S(2)}) async-start(f32[32,112,128]{2,1,0:T(8,128)} %bitcast.26), calls=%async_computation.2 | async-start | bytes 3670016 | tf_op jit(solution)/shard_map/all_to_all | solution.py:461
  304.6 41.3 %all-to-all-done.2 = f32[32,112,128]{2,1,0:T(8,128)} async-done(((f32[32,112,128]{2,1,0:T(8,128)}), f32[32,112,128]{2,1,0:T(8,128)}, u32[]{:S(2)}, u32[]{:S(2)}) %all-to-all-start.2) | async-done | bytes 1835040 | tf_op jit(solution)/shard_map/all_to_all | solution.py:461
  345.9 3.7 shard_map.93
  351.2 3.6 all-to-all-start.4
  354.8 7.4 %collective-permute-done.31.lower_other = f32[1728,128]{1,0:T(8,128)} collective-permute-done((f32[1728,128]{1,0:T(8,128)S(1)}, f32[1728,128]{1,0:T(8,128)}, u32[]{:S(2)}, u32[]{:S(2)}) %collective-permute-start.31) | collective-permute-done | bytes 884768 | tf_op jit(solution)/shard_map/ppermute | solution.py:564
  362.2 5.8 %all-to-all-done.4 = f32[16,56,128]{2,1,0:T(8,128)S(1)} async-done(((f32[16,56,128]{2,1,0:T(8,128)}), f32[16,56,128]{2,1,0:T(8,128)S(1)}, u32[]{:S(2)}, u32[]{:S(2)}) %all-to-all-start.4) | async-done | bytes 458784 | tf_op jit(solution)/shard_map/all_to_all | solution.py:457
  368.0 4.2 %all-to-all-start.3 = ((f32[16,56,128]{2,1,0:T(8,128)}), f32[16,56,128]{2,1,0:T(8,128)}, u32[]{:S(2)}, u32[]{:S(2)}) async-start(f32[16,56,128]{2,1,0:T(8,128)} %bitcast.19), calls=%async_computation.3 | async-start | bytes 917504 | tf_op jit(solution)/shard_map/all_to_all | solution.py:457
  373.1 12.3 %all-to-all-done.3 = f32[16,56,128]{2,1,0:T(8,128)} async-done(((f32[16,56,128]{2,1,0:T(8,128)}), f32[16,56,128]{2,1,0:T(8,128)}, u32[]{:S(2)}, u32[]{:S(2)}) %all-to-all-start.3) | async-done | bytes 458784 | tf_op jit(solution)/shard_map/all_to_all | solution.py:457
  386.3 3.7 shard_map.94.refs_0_
  390.0 8.2 %collective-permute-done.32.far_ref = f32[896,128]{1,0:T(8,128)S(1)} collective-permute-done((f32[896,128]{1,0:T(8,128)}, f32[896,128]{1,0:T(8,128)S(1)}, u32[]{:S(2)}, u32[]{:S(2)}) %collective-permute-start.32) | collective-permute-done | bytes 458784 | tf_op jit(solution)/shard_map/ppermute | solution.py:606
  398.2 3.7 shard_map.95
  (142 shorter events, 57.3 us)
Async XLA Ops:
  4.8 111.7 %all-to-all-start = ((f32[16,112,128]{2,1,0:T(8,128)}), f32[16,112,128]{2,1,0:T(8,128)S(1)}, u32[]{:S(2)}, u32[]{:S(2)}) async-start(f32[16,112,128]{2,1,0:T(8,128)} %bitcast.25), calls=%async_computation | async-start | bytes 1835008 | tf_op jit(solution)/shard_map/all_to_all | solution.py:457
  17.9 38.3 %collective-permute-start.4 = (f32[432,128]{1,0:T(8,128)}, f32[432,128]{1,0:T(8,128)S(1)}, u32[]{:S(2)}, u32[]{:S(2)}) collective-permute-start(f32[432,128]{1,0:T(8,128)} %get-tuple-element.79), channel_id=1, source_target_pairs={{0,10},{1,11},{2,8},{3,9},{4,14},{5,15},{6,12},{7,13},{8,2},{9,3},... | collective-permute-start | bytes 663560 | tf_op jit(solution)/shard_map/ppermute | solution.py:452
  21.4 34.8 %collective-permute-start.3 = (f32[432,128]{1,0:T(8,128)}, f32[432,128]{1,0:T(8,128)S(1)}, u32[]{:S(2)}, u32[]{:S(2)}) collective-permute-start(f32[432,128]{1,0:T(8,128)} %get-tuple-element.78), channel_id=1, source_target_pairs={{0,2},{1,3},{2,0},{3,1},{4,6},{5,7},{6,4},{7,5},{8,10},{9,11},{10,... | collective-permute-start | bytes 663560 | tf_op jit(solution)/shard_map/ppermute | solution.py:452
  22.0 37.2 %collective-permute-start.2 = (f32[432,128]{1,0:T(8,128)}, f32[432,128]{1,0:T(8,128)S(1)}, u32[]{:S(2)}, u32[]{:S(2)}) collective-permute-start(f32[432,128]{1,0:T(8,128)} %get-tuple-element.77), channel_id=1, source_target_pairs={{0,9},{1,8},{2,11},{3,10},{4,13},{5,12},{6,15},{7,14},{8,1},{9,0},... | collective-permute-start | bytes 663560 | tf_op jit(solution)/shard_map/ppermute | solution.py:452
  22.0 47.6 %collective-permute-start = (f32[432,128]{1,0:T(8,128)}, f32[432,128]{1,0:T(8,128)S(1)}, u32[]{:S(2)}, u32[]{:S(2)}) collective-permute-start(f32[432,128]{1,0:T(8,128)} %get-tuple-element.75), channel_id=1, source_target_pairs={{0,8},{1,9},{2,10},{3,11},{4,12},{5,13},{6,14},{7,15},{8,0},{9,1},... | collective-permute-start | bytes 663560 | tf_op jit(solution)/shard_map/ppermute | solution.py:452
  56.2 17.6 %collective-permute-start.9 = (f32[432,128]{1,0:T(8,128)S(1)}, f32[432,128]{1,0:T(8,128)S(1)}, u32[]{:S(2)}, u32[]{:S(2)}) collective-permute-start(f32[432,128]{1,0:T(8,128)S(1)} %copy-done.40), channel_id=1, source_target_pairs={{0,5},{1,4},{2,7},{3,6},{4,1},{5,0},{6,3},{7,2},{8,13},{9,12},{10,... | collective-permute-start | bytes 663560 | tf_op jit(solution)/shard_map/ppermute | solution.py:452
  56.3 19.6 %collective-permute-start.8 = (f32[432,128]{1,0:T(8,128)S(1)}, f32[432,128]{1,0:T(8,128)S(1)}, u32[]{:S(2)}, u32[]{:S(2)}) collective-permute-start(f32[432,128]{1,0:T(8,128)S(1)} %copy-done.39), channel_id=1, source_target_pairs={{0,12},{1,13},{2,14},{3,15},{4,8},{5,9},{6,10},{7,11},{8,4},{9,5},... | collective-permute-start | bytes 663560 | tf_op jit(solution)/shard_map/ppermute | solution.py:452
  59.2 20.1 %collective-permute-start.7 = (f32[432,128]{1,0:T(8,128)S(1)}, f32[432,128]{1,0:T(8,128)S(1)}, u32[]{:S(2)}, u32[]{:S(2)}) collective-permute-start(f32[432,128]{1,0:T(8,128)S(1)} %copy-done.38), channel_id=1, source_target_pairs={{0,4},{1,5},{2,6},{3,7},{4,0},{5,1},{6,2},{7,3},{8,12},{9,13},{10,... | collective-permute-start | bytes 663560 | tf_op jit(solution)/shard_map/ppermute | solution.py:452
  59.2 29.3 %collective-permute-start.6 = (f32[432,128]{1,0:T(8,128)S(1)}, f32[432,128]{1,0:T(8,128)S(1)}, u32[]{:S(2)}, u32[]{:S(2)}) collective-permute-start(f32[432,128]{1,0:T(8,128)S(1)} %copy-done.37), channel_id=1, source_target_pairs={{0,11},{1,10},{2,9},{3,8},{4,15},{5,14},{6,13},{7,12},{8,3},{9,2},... | collective-permute-start | bytes 663560 | tf_op jit(solution)/shard_map/ppermute | solution.py:452
  69.6 18.9 %collective-permute-start.5 = (f32[432,128]{1,0:T(8,128)S(1)}, f32[432,128]{1,0:T(8,128)S(1)}, u32[]{:S(2)}, u32[]{:S(2)}) collective-permute-start(f32[432,128]{1,0:T(8,128)S(1)} %copy-done.36), channel_id=1, source_target_pairs={{0,3},{1,2},{2,1},{3,0},{4,7},{5,6},{6,5},{7,4},{8,11},{9,10},{10,... | collective-permute-start | bytes 663560 | tf_op jit(solution)/shard_map/ppermute | solution.py:452
  73.9 21.3 %collective-permute-start.14 = (f32[432,128]{1,0:T(8,128)S(1)}, f32[432,128]{1,0:T(8,128)S(1)}, u32[]{:S(2)}, u32[]{:S(2)}) collective-permute-start(f32[432,128]{1,0:T(8,128)S(1)} %copy-done.35), channel_id=1, source_target_pairs={{0,15},{1,14},{2,13},{3,12},{4,11},{5,10},{6,9},{7,8},{8,7},{9,6},... | collective-permute-start | bytes 663560 | tf_op jit(solution)/shard_map/ppermute | solution.py:452
  75.8 26.0 %collective-permute-start.13 = (f32[432,128]{1,0:T(8,128)S(1)}, f32[432,128]{1,0:T(8,128)S(1)}, u32[]{:S(2)}, u32[]{:S(2)}) collective-permute-start(f32[432,128]{1,0:T(8,128)S(1)} %copy-done.34), channel_id=1, source_target_pairs={{0,7},{1,6},{2,5},{3,4},{4,3},{5,2},{6,1},{7,0},{8,15},{9,14},{10,... | collective-permute-start | bytes 663560 | tf_op jit(solution)/shard_map/ppermute | solution.py:452
  79.3 24.6 %collective-permute-start.12 = (f32[432,128]{1,0:T(8,128)S(1)}, f32[432,128]{1,0:T(8,128)S(1)}, u32[]{:S(2)}, u32[]{:S(2)}) collective-permute-start(f32[432,128]{1,0:T(8,128)S(1)} %copy-done.33), channel_id=1, source_target_pairs={{0,14},{1,15},{2,12},{3,13},{4,10},{5,11},{6,8},{7,9},{8,6},{9,7},... | collective-permute-start | bytes 663560 | tf_op jit(solution)/shard_map/ppermute | solution.py:452
  88.5 31.1 %collective-permute-start.11 = (f32[432,128]{1,0:T(8,128)}, f32[432,128]{1,0:T(8,128)}, u32[]{:S(2)}, u32[]{:S(2)}) collective-permute-start(f32[432,128]{1,0:T(8,128)} %get-tuple-element.95), channel_id=1, source_target_pairs={{0,6},{1,7},{2,4},{3,5},{4,2},{5,3},{6,0},{7,1},{8,14},{9,15},{10,... | collective-permute-start | bytes 663560 | tf_op jit(solution)/shard_map/ppermute | solution.py:452
  88.5 32.7 %collective-permute-start.10 = (f32[432,128]{1,0:T(8,128)}, f32[432,128]{1,0:T(8,128)}, u32[]{:S(2)}, u32[]{:S(2)}) collective-permute-start(f32[432,128]{1,0:T(8,128)} %get-tuple-element.93), channel_id=1, source_target_pairs={{0,13},{1,12},{2,15},{3,14},{4,9},{5,8},{6,11},{7,10},{8,5},{9,4},... | collective-permute-start | bytes 663560 | tf_op jit(solution)/shard_map/ppermute | solution.py:452
  95.2 35.2 %collective-permute-start.20 = (f32[432,128]{1,0:T(8,128)}, f32[432,128]{1,0:T(8,128)}, u32[]{:S(2)}, u32[]{:S(2)}) collective-permute-start(f32[432,128]{1,0:T(8,128)} %get-tuple-element.113), channel_id=1, source_target_pairs={{0,10},{1,11},{2,8},{3,9},{4,14},{5,15},{6,12},{7,13},{8,2},{9,3},... | collective-permute-start | bytes 663560 | tf_op jit(solution)/shard_map/ppermute | solution.py:452
  101.8 28.6 %collective-permute-start.19 = (f32[432,128]{1,0:T(8,128)}, f32[432,128]{1,0:T(8,128)}, u32[]{:S(2)}, u32[]{:S(2)}) collective-permute-start(f32[432,128]{1,0:T(8,128)} %get-tuple-element.111), channel_id=1, source_target_pairs={{0,2},{1,3},{2,0},{3,1},{4,6},{5,7},{6,4},{7,5},{8,10},{9,11},{10,... | collective-permute-start | bytes 663560 | tf_op jit(solution)/shard_map/ppermute | solution.py:452
  104.6 26.9 %collective-permute-start.18 = (f32[432,128]{1,0:T(8,128)}, f32[432,128]{1,0:T(8,128)}, u32[]{:S(2)}, u32[]{:S(2)}) collective-permute-start(f32[432,128]{1,0:T(8,128)} %get-tuple-element.109), channel_id=1, source_target_pairs={{0,9},{1,8},{2,11},{3,10},{4,13},{5,12},{6,15},{7,14},{8,1},{9,0},... | collective-permute-start | bytes 663560 | tf_op jit(solution)/shard_map/ppermute | solution.py:452
  119.6 65.7 %collective-permute-start.15 = (f32[1728,128]{1,0:T(8,128)}, f32[1728,128]{1,0:T(8,128)S(1)}, u32[]{:S(2)}, u32[]{:S(2)}) collective-permute-start(f32[1728,128]{1,0:T(8,128)} %shard_map.90.own_ref), channel_id=1, source_target_pairs={{0,16},{16,0},{1,17},{17,1},{2,18},{18,2},{3,19},{19,3},{4,20},{20... | collective-permute-start | bytes 2654216 | tf_op jit(solution)/shard_map/ppermute | solution.py:511
  131.5 16.6 %collective-permute-start.24 = (f32[432,128]{1,0:T(8,128)}, f32[432,128]{1,0:T(8,128)S(1)}, u32[]{:S(2)}, u32[]{:S(2)}) collective-permute-start(f32[432,128]{1,0:T(8,128)} %get-tuple-element.121), channel_id=1, source_target_pairs={{0,12},{1,13},{2,14},{3,15},{4,8},{5,9},{6,10},{7,11},{8,4},{9,5},... | collective-permute-start | bytes 663560 | tf_op jit(solution)/shard_map/ppermute | solution.py:452
  133.3 19.2 %collective-permute-start.23 = (f32[432,128]{1,0:T(8,128)}, f32[432,128]{1,0:T(8,128)S(1)}, u32[]{:S(2)}, u32[]{:S(2)}) collective-permute-start(f32[432,128]{1,0:T(8,128)} %get-tuple-element.119), channel_id=1, source_target_pairs={{0,4},{1,5},{2,6},{3,7},{4,0},{5,1},{6,2},{7,3},{8,12},{9,13},{10,... | collective-permute-start | bytes 663560 | tf_op jit(solution)/shard_map/ppermute | solution.py:452
  143.4 24.0 %collective-permute-start.22 = (f32[432,128]{1,0:T(8,128)}, f32[432,128]{1,0:T(8,128)S(1)}, u32[]{:S(2)}, u32[]{:S(2)}) collective-permute-start(f32[432,128]{1,0:T(8,128)} %get-tuple-element.117), channel_id=1, source_target_pairs={{0,11},{1,10},{2,9},{3,8},{4,15},{5,14},{6,13},{7,12},{8,3},{9,2},... | collective-permute-start | bytes 663560 | tf_op jit(solution)/shard_map/ppermute | solution.py:452
  143.5 25.5 %collective-permute-start.21 = (f32[432,128]{1,0:T(8,128)}, f32[432,128]{1,0:T(8,128)S(1)}, u32[]{:S(2)}, u32[]{:S(2)}) collective-permute-start(f32[432,128]{1,0:T(8,128)} %get-tuple-element.115), channel_id=1, source_target_pairs={{0,3},{1,2},{2,1},{3,0},{4,7},{5,6},{6,5},{7,4},{8,11},{9,10},{10,... | collective-permute-start | bytes 663560 | tf_op jit(solution)/shard_map/ppermute | solution.py:452
  148.1 20.9 %collective-permute-start.30 = (f32[432,128]{1,0:T(8,128)}, f32[432,128]{1,0:T(8,128)S(1)}, u32[]{:S(2)}, u32[]{:S(2)}) collective-permute-start(f32[432,128]{1,0:T(8,128)} %get-tuple-element.133), channel_id=1, source_target_pairs={{0,15},{1,14},{2,13},{3,12},{4,11},{5,10},{6,9},{7,8},{8,7},{9,6},... | collective-permute-start | bytes 663560 | tf_op jit(solution)/shard_map/ppermute | solution.py:452
  152.5 25.8 %collective-permute-start.29 = (f32[432,128]{1,0:T(8,128)}, f32[432,128]{1,0:T(8,128)S(1)}, u32[]{:S(2)}, u32[]{:S(2)}) collective-permute-start(f32[432,128]{1,0:T(8,128)} %get-tuple-element.131), channel_id=1, source_target_pairs={{0,7},{1,6},{2,5},{3,4},{4,3},{5,2},{6,1},{7,0},{8,15},{9,14},{10,... | collective-permute-start | bytes 663560 | tf_op jit(solution)/shard_map/ppermute | solution.py:452
  169.0 16.4 %collective-permute-start.26 = (f32[432,128]{1,0:T(8,128)}, f32[432,128]{1,0:T(8,128)S(1)}, u32[]{:S(2)}, u32[]{:S(2)}) collective-permute-start(f32[432,128]{1,0:T(8,128)} %get-tuple-element.125), channel_id=1, source_target_pairs={{0,13},{1,12},{2,15},{3,14},{4,9},{5,8},{6,11},{7,10},{8,5},{9,4},... | collective-permute-start | bytes 663560 | tf_op jit(solution)/shard_map/ppermute | solution.py:452
  195.3 76.4 %all-to-all-start.1 = ((f32[16,432,128]{2,1,0:T(8,128)}), f32[16,432,128]{2,1,0:T(8,128)S(1)}, u32[]{:S(2)}, u32[]{:S(2)}) async-start(f32[16,432,128]{2,1,0:T(8,128)} %bitcast.22), calls=%async_computation.1 | async-start | bytes 7077888 | tf_op jit(solution)/shard_map/all_to_all | solution.py:457
  284.6 61.3 %all-to-all-start.2 = ((f32[32,112,128]{2,1,0:T(8,128)}), f32[32,112,128]{2,1,0:T(8,128)}, u32[]{:S(2)}, u32[]{:S(2)}) async-start(f32[32,112,128]{2,1,0:T(8,128)} %bitcast.26), calls=%async_computation.2 | async-start | bytes 3670016 | tf_op jit(solution)/shard_map/all_to_all | solution.py:461
  301.7 49.5 %collective-permute-start.33 = (f32[1728,128]{1,0:T(8,128)S(1)}, f32[1728,128]{1,0:T(8,128)S(1)}, u32[]{:S(2)}, u32[]{:S(2)}) collective-permute-start(f32[1728,128]{1,0:T(8,128)S(1)} %copy-done.1), channel_id=1, source_target_pairs={{0,16},{16,0},{1,17},{17,1},{2,18},{18,2},{3,19},{19,3},{4,20},{20... | collective-permute-start | bytes 2654216 | tf_op jit(solution)/shard_map/ppermute | solution.py:563
  304.2 57.9 %collective-permute-start.31 = (f32[1728,128]{1,0:T(8,128)S(1)}, f32[1728,128]{1,0:T(8,128)}, u32[]{:S(2)}, u32[]{:S(2)}) collective-permute-start(f32[1728,128]{1,0:T(8,128)S(1)} %copy-done.2), channel_id=1, source_target_pairs={{0,16},{16,0},{1,17},{17,1},{2,18},{18,2},{3,19},{19,3},{4,20},{20... | collective-permute-start | bytes 2654216 | tf_op jit(solution)/shard_map/ppermute | solution.py:564
  351.2 16.8 %all-to-all-start.4 = ((f32[16,56,128]{2,1,0:T(8,128)}), f32[16,56,128]{2,1,0:T(8,128)S(1)}, u32[]{:S(2)}, u32[]{:S(2)}) async-start(f32[16,56,128]{2,1,0:T(8,128)} %bitcast.20), calls=%async_computation.4 | async-start | bytes 917504 | tf_op jit(solution)/shard_map/all_to_all | solution.py:457
  368.0 17.5 %all-to-all-start.3 = ((f32[16,56,128]{2,1,0:T(8,128)}), f32[16,56,128]{2,1,0:T(8,128)}, u32[]{:S(2)}, u32[]{:S(2)}) async-start(f32[16,56,128]{2,1,0:T(8,128)} %bitcast.19), calls=%async_computation.3 | async-start | bytes 917504 | tf_op jit(solution)/shard_map/all_to_all | solution.py:457
  (49 other events, 1831.2 us)
